TPU v7x, 32 devices: a whole 2x2x4 slice. The times are simulated.
32 devices in a mesh: seq: 4 (over z), head: 8 (over y, x, core).
Axes of the slice: x: 2, y: 2, z: 4, core: 2. Of those that a mesh axis runs over, the one named last changes fastest.
Arguments:
- inputs: bfloat16 [8192, 2048], P(('seq', 'head')), may hold values from -6 to 6
- doc_lengths: int32 [3], replicated, may hold values from 65 to 6080, as said below
- first_gain: float32 [2048], replicated, may hold values from 0.5 to 1.5
- w_query: bfloat16 [2048, 2048], P(None, 'head'), may hold values from -0.125 to 0.125
- w_key: bfloat16 [2048, 2048], P(None, 'head'), may hold values from -0.125 to 0.125
- w_value: bfloat16 [2048, 4096], P(None, 'head'), may hold values from -0.125 to 0.125
- w_outgate: bfloat16 [2048, 4096], P(None, 'head'), may hold values from -0.125 to 0.125
- w_decay: bfloat16 [2048, 16], P(None, 'head'), may hold values from -0.125 to 0.125
- w_beta: bfloat16 [2048, 16], P(None, 'head'), may hold values from -0.125 to 0.125
- conv_query: float32 [4, 2048], P(None, 'head'), may hold values from -3 to 3
- conv_key: float32 [4, 2048], P(None, 'head'), may hold values from -3 to 3
- conv_value: float32 [4, 4096], P(None, 'head'), may hold values from -3 to 3
- decay_log: float32 [16], P('head'), may hold values from -4 to 1
- decay_bias: float32 [16], P('head'), may hold values from -3 to 1
- head_gain: float32 [256], replicated, may hold values from 0.5 to 1.5
- w_output: bfloat16 [4096, 2048], P('head'), may hold values from -0.09375 to 0.09375
- second_gain: float32 [2048], replicated, may hold values from 0.5 to 1.5
- w_gate: bfloat16 [2048, 5632], P(None, 'seq'), may hold values from -0.125 to 0.125
- w_up: bfloat16 [2048, 5632], P(None, 'seq'), may hold values from -0.125 to 0.125
- w_down: bfloat16 [5632, 2048], P('seq'), may hold values from -0.078125 to 0.078125
- cotangent: bfloat16 [8192, 2048], P(('seq', 'head')), may hold values from -6 to 6
Outputs:
- output: bfloat16 [8192, 2048], P(('seq', 'head'))
- grad_inputs: float32 [8192, 2048], P(('seq', 'head'))
- grad_first_gain: float32 [2048], replicated
- grad_w_query: float32 [2048, 2048], P(None, 'head')
- grad_w_key: float32 [2048, 2048], P(None, 'head')
- grad_w_value: float32 [2048, 4096], P(None, 'head')
- grad_w_outgate: float32 [2048, 4096], P(None, 'head')
- grad_w_decay: float32 [2048, 16], P(None, 'head')
- grad_w_beta: float32 [2048, 16], P(None, 'head')
- grad_conv_query: float32 [4, 2048], P(None, 'head')
- grad_conv_key: float32 [4, 2048], P(None, 'head')
- grad_conv_value: float32 [4, 4096], P(None, 'head')
- grad_decay_log: float32 [16], P('head')
- grad_decay_bias: float32 [16], P('head')
- grad_head_gain: float32 [256], replicated
- grad_w_output: float32 [4096, 2048], P('head')
- grad_second_gain: float32 [2048], replicated
- grad_w_gate: float32 [2048, 5632], P(None, 'seq')
- grad_w_up: float32 [2048, 5632], P(None, 'seq')
- grad_w_down: float32 [5632, 2048], P('seq')
Inputs may be any that keep to these rules, and one draw needn't show every extreme that they name: Document i occupies a slot of doc_lengths[i] rounded up to a multiple of 64; the slots lie end to end and fill all 8192 tokens; the second document starts within the first 2048 tokens, ends within the last 2048, and is 6080 tokens long.
All inputs are finite; a program needn't handle non-finite values.
Results may differ from a plain program's by a relative error of at most 0.025.
Values may be sent and summed in bfloat16 or wider, within the bound.
A program may use at most 384 MiB of HBM per device.

v0:
```python
import jax
import jax.numpy as jnp
from jax import lax
from jax.sharding import PartitionSpec as P

GROUP = 64


epsilon = 1e-06
highest_precision = lax.Precision.HIGHEST


def shifted_2(shard, axis, by):
    devices = lax.axis_size(axis)
    pairs = [(i, i + by) for i in range(devices) if 0 <= i + by < devices]
    return lax.ppermute(shard, axis, pairs)


def prefix(shard, axis, combine, identity, reverse):
    devices, mine = (lax.axis_size(axis), lax.axis_index(axis))
    everything = jax.tree.map(
        lambda part, kind: lax.all_gather(part.astype(kind), axis),
        shard,
        (jnp.bfloat16, jnp.bfloat16),
    )
    start = jax.tree.map(
        lambda part, zero: jnp.broadcast_to(jnp.asarray(zero, part.dtype), part.shape),
        shard,
        identity,
    )

    def step(k, before):
        at = devices - 1 - k if reverse else k
        reached = at > mine if reverse else at < mine
        new = combine(
            before, jax.tree.map(lambda part, own: part[at].astype(own.dtype), everything, shard)
        )
        return jax.tree.map(lambda a, b: jnp.where(reached, a, b), new, before)

    return lax.fori_loop(0, devices, step, start)


def matmul(left, right):
    return jnp.dot(left, right, precision=highest_precision, preferred_element_type=jnp.float32)


def product(left, right):
    return jnp.dot(left, right, preferred_element_type=jnp.float32)


def product_t(left, right):
    return lax.dot_general(
        left, right, (((0,), (0,)), ((), ())), preferred_element_type=jnp.float32
    )


def product_nt(left, right):
    return lax.dot_general(
        left, right, (((1,), (1,)), ((), ())), preferred_element_type=jnp.float32
    )


def layout(doc_lengths, first_row, row_total):
    slot_sizes = (doc_lengths + (GROUP - 1)) // GROUP * GROUP
    starts = jnp.cumsum(slot_sizes, dtype=jnp.int32) - slot_sizes
    places = first_row + jnp.arange(row_total, dtype=jnp.int32)
    owners = jnp.sum(
        (places[:, None] >= starts[None, 1:]).astype(jnp.int32), axis=1, dtype=jnp.int32
    )
    picked = (owners[:, None] == jnp.arange(doc_lengths.shape[0], dtype=jnp.int32)[None, :]).astype(
        jnp.int32
    )
    begins = jnp.sum(picked * starts[None, :], axis=1, dtype=jnp.int32)
    length = jnp.sum(picked * doc_lengths[None, :], axis=1, dtype=jnp.int32)
    offset = places - begins
    return (offset, offset < length)


def rms_scale(values, gain):
    return values * lax.rsqrt(jnp.mean(values * values, axis=-1, keepdims=True) + epsilon) * gain


def rms_back(values, gain, grad_in):
    scale = lax.rsqrt(jnp.mean(values * values, axis=-1, keepdims=True) + epsilon)
    weighted = grad_in * gain
    grad_values = scale * weighted - values * scale**3 * jnp.mean(
        weighted * values, axis=-1, keepdims=True
    )
    grad_gain = jnp.sum((grad_in * values * scale).reshape(-1, values.shape[-1]), axis=0)
    return (grad_values, grad_gain)


def unit_rows(values):
    return values * lax.rsqrt(jnp.sum(values * values, axis=-1, keepdims=True) + epsilon)


def unit_back(values, grad_in):
    scale = lax.rsqrt(jnp.sum(values * values, axis=-1, keepdims=True) + epsilon)
    return scale * grad_in - values * scale**3 * jnp.sum(grad_in * values, axis=-1, keepdims=True)


def silu_slope(values):
    sigma = jax.nn.sigmoid(values)
    return sigma * (1.0 + values * (1.0 - sigma))


def conv_forward(extended, kernel, offset):
    taps = kernel.shape[0]
    length = offset.shape[0]
    summed = jnp.zeros((length, extended.shape[1]), jnp.float32)
    for lag_at in range(taps):
        window = extended[taps - 1 - lag_at : taps - 1 - lag_at + length]
        summed = summed + kernel[lag_at] * window * (offset >= lag_at).astype(jnp.float32)[:, None]
    return summed


def conv_backward(grad_ext, kernel, offsets):
    taps = kernel.shape[0]
    length = grad_ext.shape[0] - (taps - 1)
    summed = jnp.zeros((length, grad_ext.shape[1]), jnp.float32)
    for lag_at in range(taps):
        masked = grad_ext * (offsets >= lag_at).astype(jnp.float32)[:, None]
        summed = summed + kernel[lag_at] * masked[lag_at : lag_at + length]
    return summed


def conv_kernel_grad(grad_conv, extended, offset, taps):
    length = offset.shape[0]
    rows_out = []
    for lag_at in range(taps):
        window = extended[taps - 1 - lag_at : taps - 1 - lag_at + length]
        rows_out.append(
            jnp.sum(grad_conv * window * (offset >= lag_at).astype(jnp.float32)[:, None], axis=0)
        )
    return jnp.stack(rows_out, axis=0)


def group_parts(queries, key_rows, values, decay, strength):
    cumul = jnp.cumsum(decay)
    length = cumul.shape[0]
    gaps = cumul[:, None] - cumul[None, :]
    inclusive = jnp.tril(jnp.ones((length, length), jnp.bool_))
    strictly = jnp.tril(jnp.ones((length, length), jnp.bool_), -1)
    within = jnp.where(inclusive, jnp.exp(jnp.minimum(gaps, 0.0)), 0.0)
    keys_gram = matmul(key_rows, key_rows.T)
    system = jnp.eye(length, dtype=jnp.float32) + jnp.where(
        strictly, strength[:, None] * keys_gram * within, 0.0
    )
    weights_w = jax.scipy.linalg.solve_triangular(
        system, (strength * jnp.exp(cumul))[:, None] * key_rows, lower=True
    )
    values_u = jax.scipy.linalg.solve_triangular(system, strength[:, None] * values, lower=True)
    scores = matmul(queries, key_rows.T) * within
    scaled_queries = jnp.exp(cumul)[:, None] * queries
    tail_keys = key_rows * jnp.exp(cumul[-1] - cumul)[:, None]
    return (weights_w, values_u, scores, scaled_queries, tail_keys, jnp.exp(cumul[-1]))


def state_step(memory_state, block):
    weights_w, values_u, scores, scaled_queries, tail_keys, total_decay, reset = block
    memory_state = memory_state * (1.0 - reset)
    fresh = values_u - matmul(weights_w, memory_state)
    outs = matmul(scaled_queries, memory_state) + matmul(scores, fresh)
    memory_state = total_decay * memory_state + matmul(tail_keys.T, fresh)
    return (memory_state, outs)


def run_core(queries, key_rows, values, decay, strength, resets, state_zero):
    parts = jax.vmap(jax.vmap(group_parts))(queries, key_rows, values, decay, strength)
    stepper = jax.checkpoint(state_step)

    def one_head(weights_w, values_u, scores, scaled_queries, tail_keys, total_decay, state_h):
        return lax.scan(
            stepper,
            state_h,
            (weights_w, values_u, scores, scaled_queries, tail_keys, total_decay, resets),
        )

    final, outs = jax.vmap(one_head)(
        parts[0], parts[1], parts[2], parts[3], parts[4], parts[5], state_zero
    )
    return (outs, final)


def combine_states(earlier, later):
    joined = jnp.einsum("hij,hjk->hik", later[0], earlier[0], precision=highest_precision)
    carried_state = (
        jnp.einsum("hij,hjk->hik", later[0], earlier[1], precision=highest_precision) + later[1]
    )
    return (joined, carried_state)


def shards(
    inputs,
    doc_lengths,
    first_gain,
    w_query,
    w_key,
    w_value,
    w_outgate,
    w_decay,
    w_beta,
    conv_query,
    conv_key,
    conv_value,
    decay_log,
    decay_bias,
    head_gain,
    w_output,
    second_gain,
    w_gate,
    w_up,
    w_down,
    cotangent,
):
    row_count = inputs.shape[0]
    model_width = inputs.shape[1]
    heads_here = decay_log.shape[0]
    key_width = w_query.shape[1] // heads_here
    value_width = w_value.shape[1] // heads_here
    taps = conv_query.shape[0]
    seq_index = lax.axis_index("seq")
    head_index = lax.axis_index("head")
    head_total = lax.axis_size("head")
    inputs_f = inputs.astype(jnp.float32)
    normed = rms_scale(inputs_f, first_gain).astype(jnp.bfloat16)
    block_rows = lax.all_gather(normed, "head", axis=0, tiled=True)
    seq_rows = block_rows.shape[0]
    groups_here = seq_rows // GROUP
    offsets, _ = layout(doc_lengths, seq_index * seq_rows, seq_rows + taps - 1)
    offset = offsets[:seq_rows]
    _, own_valid = layout(doc_lengths, (seq_index * head_total + head_index) * row_count, row_count)
    pre_query = product(block_rows, w_query)
    pre_key = product(block_rows, w_key)
    pre_value = product(block_rows, w_value)
    pre_gate = product(block_rows, w_outgate)
    pre_decay = product(block_rows, w_decay)
    pre_beta = product(block_rows, w_beta)
    cut_at = seq_rows - taps + 1
    rim_query, rim_key, rim_value = shifted_2(
        (pre_query[cut_at:], pre_key[cut_at:], pre_value[cut_at:]), "seq", 1
    )
    ext_query = jnp.concatenate([rim_query, pre_query], axis=0)
    ext_key = jnp.concatenate([rim_key, pre_key], axis=0)
    ext_value = jnp.concatenate([rim_value, pre_value], axis=0)
    conv_q = conv_forward(ext_query, conv_query, offset)
    conv_k = conv_forward(ext_key, conv_key, offset)
    conv_v = conv_forward(ext_value, conv_value, offset)
    act_query = jax.nn.silu(conv_q).reshape(seq_rows, heads_here, key_width)
    act_key = jax.nn.silu(conv_k).reshape(seq_rows, heads_here, key_width)
    queries = (unit_rows(act_query) * key_width ** (-0.5)).astype(jnp.bfloat16)
    key_rows = unit_rows(act_key).astype(jnp.bfloat16)
    values = jax.nn.silu(conv_v).reshape(seq_rows, heads_here, value_width).astype(jnp.bfloat16)
    strength = jax.nn.sigmoid(pre_beta)
    rate = jnp.exp(decay_log)
    shifted = pre_decay + decay_bias
    decay = -rate * jax.nn.softplus(shifted)

    def to_groups(array):
        return (
            array.astype(jnp.float32)
            .reshape(groups_here, GROUP, heads_here, -1)
            .transpose(2, 0, 1, 3)
        )

    def scalar_groups(array):
        return array.reshape(groups_here, GROUP, heads_here).transpose(2, 0, 1)

    def from_groups(array):
        return array.transpose(1, 2, 0, 3).reshape(seq_rows, heads_here, -1)

    resets = (offset[::GROUP] == 0).astype(jnp.float32)
    query_c = to_groups(queries)
    key_c = to_groups(key_rows)
    value_c = to_groups(values)
    decay_c = scalar_groups(decay)
    strength_c = scalar_groups(strength)
    identity = jnp.broadcast_to(
        jnp.eye(key_width, dtype=jnp.float32), (heads_here, key_width, key_width)
    )
    zero_state = jnp.zeros((heads_here, key_width, value_width), jnp.float32)
    widened = jnp.concatenate(
        [jnp.zeros(value_c.shape[:-1] + (key_width,), jnp.float32), value_c], axis=-1
    )
    outs, final = run_core(
        query_c,
        key_c,
        widened,
        decay_c,
        strength_c,
        resets,
        jnp.concatenate([identity, zero_state], axis=-1),
    )
    carried_state = outs[..., :key_width]
    intra_block_output = outs[..., key_width:]
    passing = final[..., :key_width]
    added = final[..., key_width:]
    _, incoming_state = prefix(
        (passing, added), "seq", combine_states, (identity, zero_state), False
    )
    recurrent_output = intra_block_output + jnp.einsum(
        "pbsa,pax->pbsx", carried_state, incoming_state, precision=highest_precision
    )
    mixed_heads = from_groups(recurrent_output)
    head_normed = rms_scale(mixed_heads, head_gain)
    gate_heads = pre_gate.reshape(seq_rows, heads_here, value_width)
    gate_act = jax.nn.silu(gate_heads)
    gated = (
        (head_normed * gate_act).reshape(seq_rows, heads_here * value_width).astype(jnp.bfloat16)
    )
    mixer_out = lax.psum_scatter(product(gated, w_output), "head", scatter_dimension=0, tiled=True)
    hidden_in = inputs_f + mixer_out
    normed_two = rms_scale(hidden_in, second_gain).astype(jnp.bfloat16)
    mlp_block = lax.all_gather(normed_two, "seq", axis=0, tiled=True)
    gate_pre = product(mlp_block, w_gate)
    up_pre = product(mlp_block, w_up)
    hidden = (jax.nn.silu(gate_pre) * up_pre).astype(jnp.bfloat16)
    mlp_out = lax.psum_scatter(
        product(hidden, w_down).astype(jnp.bfloat16), "seq", scatter_dimension=0, tiled=True
    ).astype(jnp.float32)
    output = (hidden_in + mlp_out).astype(jnp.bfloat16)
    grad_out = cotangent.astype(jnp.float32) * own_valid.astype(jnp.float32)[:, None]
    grad_low = grad_out.astype(jnp.bfloat16)
    grad_block_two = lax.all_gather(grad_low, "seq", axis=0, tiled=True)
    grad_hidden = product_nt(grad_block_two, w_down)
    grad_w_down = product_t(hidden, grad_block_two)
    grad_gate = (grad_hidden * up_pre * silu_slope(gate_pre)).astype(jnp.bfloat16)
    grad_up = (grad_hidden * jax.nn.silu(gate_pre)).astype(jnp.bfloat16)
    grad_normed_two = lax.psum_scatter(
        (product_nt(grad_gate, w_gate) + product_nt(grad_up, w_up)).astype(jnp.bfloat16),
        "seq",
        scatter_dimension=0,
        tiled=True,
    ).astype(jnp.float32)
    grad_w_gate = product_t(mlp_block, grad_gate)
    grad_w_up = product_t(mlp_block, grad_up)
    grad_hidden_norm, grad_second = rms_back(hidden_in, second_gain, grad_normed_two)
    grad_hidden_in = grad_out + grad_hidden_norm
    grad_mix = grad_hidden_in.astype(jnp.bfloat16)
    grad_block = lax.all_gather(grad_mix, "head", axis=0, tiled=True)
    grad_gated = product_nt(grad_block, w_output).reshape(seq_rows, heads_here, value_width)
    grad_w_output = product_t(gated, grad_block)
    grad_head_normed = grad_gated * gate_act
    grad_gate_pre = (
        (grad_gated * head_normed * silu_slope(gate_heads))
        .reshape(seq_rows, heads_here * value_width)
        .astype(jnp.bfloat16)
    )
    grad_core, grad_head = rms_back(mixed_heads, head_gain, grad_head_normed)
    grad_recurrent_block = to_groups(grad_core)
    pulled_back = jnp.einsum(
        "mqao,mqap->mop", carried_state, grad_recurrent_block, precision=highest_precision
    )
    _, grad_state_out = prefix(
        (jnp.swapaxes(passing, 1, 2), pulled_back),
        "seq",
        combine_states,
        (identity, zero_state),
        True,
    )

    def local_core(query_a, key_a, value_a, decay_a, strength_a, state_a):
        return run_core(query_a, key_a, value_a, decay_a, strength_a, resets, state_a)

    _, pullback = jax.vjp(local_core, query_c, key_c, value_c, decay_c, strength_c, incoming_state)
    grad_query_c, grad_key_c, grad_value_c, grad_decay_c, grad_strength_c, _ = pullback(
        (grad_recurrent_block, grad_state_out)
    )
    grad_act_query = unit_back(act_query, from_groups(grad_query_c) * key_width ** (-0.5))
    grad_act_key = unit_back(act_key, from_groups(grad_key_c))
    grad_conv_q = grad_act_query.reshape(seq_rows, -1) * silu_slope(conv_q)
    grad_conv_k = grad_act_key.reshape(seq_rows, -1) * silu_slope(conv_k)
    grad_conv_v = from_groups(grad_value_c).reshape(seq_rows, -1) * silu_slope(conv_v)
    next_query, next_key, next_value = shifted_2(
        (grad_conv_q[: taps - 1], grad_conv_k[: taps - 1], grad_conv_v[: taps - 1]), "seq", -1
    )
    grad_pre_query = conv_backward(
        jnp.concatenate([grad_conv_q, next_query], axis=0), conv_query, offsets
    ).astype(jnp.bfloat16)
    grad_pre_key = conv_backward(
        jnp.concatenate([grad_conv_k, next_key], axis=0), conv_key, offsets
    ).astype(jnp.bfloat16)
    grad_pre_value = conv_backward(
        jnp.concatenate([grad_conv_v, next_value], axis=0), conv_value, offsets
    ).astype(jnp.bfloat16)
    grad_conv_query = conv_kernel_grad(grad_conv_q, ext_query, offset, taps)
    grad_conv_key = conv_kernel_grad(grad_conv_k, ext_key, offset, taps)
    grad_conv_value = conv_kernel_grad(grad_conv_v, ext_value, offset, taps)
    grad_decay = grad_decay_c.transpose(1, 2, 0).reshape(seq_rows, heads_here)
    grad_strength = grad_strength_c.transpose(1, 2, 0).reshape(seq_rows, heads_here)
    grad_shifted = grad_decay * -rate * jax.nn.sigmoid(shifted)
    grad_pre_decay = grad_shifted.astype(jnp.bfloat16)
    grad_decay_bias = jnp.sum(grad_shifted, axis=0)
    grad_decay_log = jnp.sum(grad_decay * decay, axis=0)
    grad_pre_beta = (grad_strength * strength * (1.0 - strength)).astype(jnp.bfloat16)
    grad_pieces = (
        grad_pre_query,
        grad_pre_key,
        grad_pre_value,
        grad_gate_pre,
        grad_pre_decay,
        grad_pre_beta,
    )
    weight_mats = (w_query, w_key, w_value, w_outgate, w_decay, w_beta)
    summed = jnp.zeros((lax.axis_size("head") * row_count, model_width), jnp.float32)
    for grad_piece, weight_mat in zip(grad_pieces, weight_mats):
        summed = summed + product_nt(grad_piece, weight_mat)
    grad_normed = lax.psum_scatter(
        summed.astype(jnp.bfloat16), "head", scatter_dimension=0, tiled=True
    ).astype(jnp.float32)
    grad_input_norm, grad_first = rms_back(inputs_f, first_gain, grad_normed)
    grad_inputs = grad_hidden_in + grad_input_norm
    grad_w_query = product_t(block_rows, grad_pre_query)
    grad_w_key = product_t(block_rows, grad_pre_key)
    grad_w_value = product_t(block_rows, grad_pre_value)
    grad_w_outgate = product_t(block_rows, grad_gate_pre)
    grad_w_decay = product_t(block_rows, grad_pre_decay)
    grad_w_beta = product_t(block_rows, grad_pre_beta)
    grad_w_gate, grad_w_up, grad_w_down, first_part, second_part, head_part = (
        lax.psum(grad_w_gate.astype(jnp.bfloat16), "head").astype(jnp.float32),
        lax.psum(grad_w_up.astype(jnp.bfloat16), "head").astype(jnp.float32),
        lax.psum(grad_w_down.astype(jnp.bfloat16), "head").astype(jnp.float32),
        lax.psum(grad_first.astype(jnp.bfloat16), "head").astype(jnp.float32),
        lax.psum(grad_second.astype(jnp.bfloat16), "head").astype(jnp.float32),
        lax.psum(grad_head.astype(jnp.bfloat16), "head").astype(jnp.float32),
    )
    summed_seq = (
        lax.psum(grad_w_query.astype(jnp.bfloat16), "seq").astype(jnp.float32),
        lax.psum(grad_w_key.astype(jnp.bfloat16), "seq").astype(jnp.float32),
        lax.psum(grad_w_value.astype(jnp.bfloat16), "seq").astype(jnp.float32),
        lax.psum(grad_w_outgate.astype(jnp.bfloat16), "seq").astype(jnp.float32),
        lax.psum(grad_w_decay.astype(jnp.bfloat16), "seq").astype(jnp.float32),
        lax.psum(grad_w_beta.astype(jnp.bfloat16), "seq").astype(jnp.float32),
        lax.psum(grad_conv_query.astype(jnp.bfloat16), "seq").astype(jnp.float32),
        lax.psum(grad_conv_key.astype(jnp.bfloat16), "seq").astype(jnp.float32),
        lax.psum(grad_conv_value.astype(jnp.bfloat16), "seq").astype(jnp.float32),
        lax.psum(grad_decay_log.astype(jnp.bfloat16), "seq").astype(jnp.float32),
        lax.psum(grad_decay_bias.astype(jnp.bfloat16), "seq").astype(jnp.float32),
        lax.psum(grad_w_output.astype(jnp.bfloat16), "seq").astype(jnp.float32),
        lax.psum(first_part.astype(jnp.bfloat16), "seq").astype(jnp.float32),
        lax.psum(second_part.astype(jnp.bfloat16), "seq").astype(jnp.float32),
        lax.psum(head_part.astype(jnp.bfloat16), "seq").astype(jnp.float32),
    )
    return (
        output,
        grad_inputs,
        summed_seq[12],
        summed_seq[0],
        summed_seq[1],
        summed_seq[2],
        summed_seq[3],
        summed_seq[4],
        summed_seq[5],
        summed_seq[6],
        summed_seq[7],
        summed_seq[8],
        summed_seq[9],
        summed_seq[10],
        summed_seq[14],
        summed_seq[11],
        summed_seq[13],
        grad_w_gate,
        grad_w_up,
        grad_w_down,
    )


def solution(mesh):
    in_specs = (
        P(("seq", "head"), None),
        P(),
        P(),
        P(None, "head"),
        P(None, "head"),
        P(None, "head"),
        P(None, "head"),
        P(None, "head"),
        P(None, "head"),
        P(None, "head"),
        P(None, "head"),
        P(None, "head"),
        P("head"),
        P("head"),
        P(),
        P("head", None),
        P(),
        P(None, "seq"),
        P(None, "seq"),
        P("seq", None),
        P(("seq", "head"), None),
    )
    out_specs = (
        P(("seq", "head"), None),
        P(("seq", "head"), None),
        P(),
        P(None, "head"),
        P(None, "head"),
        P(None, "head"),
        P(None, "head"),
        P(None, "head"),
        P(None, "head"),
        P(None, "head"),
        P(None, "head"),
        P(None, "head"),
        P("head"),
        P("head"),
        P(),
        P("head", None),
        P(),
        P(None, "seq"),
        P(None, "seq"),
        P("seq", None),
    )
    return jax.shard_map(shards, mesh=mesh, in_specs=in_specs, out_specs=out_specs, check_vma=False)
```

profile of v0, /device:TPU:0, one launch (start us, length us, event | category | flops | bytes accessed | tf_op | source)
XLA Modules:
  0.0 2439.9 jit_solution(15817840317215919354)
XLA Ops:
  15.0 54.3 %all-gather.9.cloned.1.call-done = bf16[2048,2048]{1,0:T(8,128)(2,1)} async-done(((bf16[256,2048]{1,0:T(8,128)(2,1)}), bf16[2048,2048]{1,0:T(8,128)(2,1)}) %all-gather.9.cloned.1.call-update) | async-done | bytes 8388624 | tf_op jit(solution)/shard_map/all_gather | solution.py:227
  90.3 7.4 fusion.247
  97.8 9.5 fusion.248
  115.9 8.5 fusion.183
  131.0 8.2 fusion.233
  179.6 7.5 fusion.75
  187.1 134.0 %custom-call.19 = f32[2,32,1,64,64]{1,3,4,2,0:T(8,128)} custom-call(f32[2,32,1,64,64]{1,4,3,2,0:T(8,128)} %fusion.75), custom_call_target="InvertDiagBlocksLowerTriangular" | custom-call | tf_op jit(solution)/shard_map/vmap(vmap(jit(_solve_triangular)))/triangular_solve | solution.py:152
  355.1 7.5 fusion.105
  362.7 227.4 %while.80 = (s32[]{:T(128)}, f32[2,128,384]{2,1,0:T(8,128)S(1)}, f32[32,2,64,384]{3,2,0,1:T(8,128)}, f32[32,2]{1,0:T(8,128)S(1)}, f32[32]{0:T(128)S(1)}, /*index...) while((s32[]{:T(128)}, f32[2,128,384]{2,1,0:T(8,128)S(1)}, ...), condition=%wide.region_8.10_spmd, body=%wide.region_7.9_spmd.sunk | while | flops 264830976 | bytes 3215033 | solution.py:173
  590.6 15.0 all-gather
  605.6 14.7 all-gather.1
  648.1 10.8 multiply_convert_fusion.4
  660.2 8.2 fusion.250
  668.6 114.3 %reduce-scatter.5.cloned.1.call-done = f32[256,2048]{1,0:T(8,128)} async-done(((f32[2048,2048]{1,0:T(8,128)}), f32[256,2048]{1,0:T(8,128)}) %reduce-scatter.5.cloned.1.call-update) | async-done | bytes 2097168 | tf_op jit(solution)/shard_map/reduce_scatter | solution.py:311
  790.5 78.0 %all-gather.11.cloned.1.call-done = bf16[1024,2048]{1,0:T(8,128)(2,1)} async-done(((bf16[256,2048]{1,0:T(8,128)(2,1)}), bf16[1024,2048]{1,0:T(8,128)(2,1)}) %all-gather.11.cloned.1.call-update) | async-done | bytes 4194320 | tf_op jit(solution)/shard_map/all_gather | solution.py:314
  868.5 12.3 fusion.251
  880.8 10.2 fusion.252
  891.0 58.3 %all-gather.13.cloned.1.call-done = bf16[1024,2048]{1,0:T(8,128)(2,1)} async-done(((bf16[256,2048]{1,0:T(8,128)(2,1)}), bf16[1024,2048]{1,0:T(8,128)(2,1)}) %all-gather.13.cloned.1.call-update) | async-done | bytes 4194320 | tf_op jit(solution)/shard_map/all_gather | solution.py:324
  949.3 15.5 multiply_convert_fusion
  964.8 10.8 fusion.253
  975.6 11.2 add_convert_fusion.1
  986.9 11.0 convolution_convert_fusion.3
  1014.6 7.3 fusion.97
  1026.2 36.0 %reduce-scatter.9.cloned.1.call-done = bf16[256,2048]{1,0:T(8,128)(2,1)} async-done(((bf16[1024,2048]{1,0:T(8,128)(2,1)}), bf16[256,2048]{1,0:T(8,128)(2,1)}) %reduce-scatter.9.cloned.1.call-update) | async-done | bytes 1048592 | tf_op jit(solution)/shard_map/reduce_scatter | solution.py:329
  1065.3 76.5 %reduce-scatter.7.cloned.1.call-done = bf16[256,2048]{1,0:T(8,128)(2,1)} async-done(((bf16[1024,2048]{1,0:T(8,128)(2,1)}), bf16[256,2048]{1,0:T(8,128)(2,1)}) %reduce-scatter.7.cloned.1.call-update) | async-done | bytes 1048592 | tf_op jit(solution)/shard_map/reduce_scatter | solution.py:318
  1147.3 144.3 %while.81 = (s32[]{:T(128)}, f32[2,128,256]{2,1,0:T(8,128)S(1)}, f32[32,2,128,256]{3,2,1,0:T(8,128)}, f32[32,2]{1,0:T(8,128)S(1)}, f32[32]{0:T(128)S(1)}, /*inde...) while((s32[]{:T(128)}, f32[2,128,256]{2,1,0:T(8,128)S(1)}, ...), condition=%wide.region_24.26_spmd, body=%wide.region_23.25_spmd.sunk | while | flops 100958208 | bytes 1837225 | solution.py:173
  1297.6 14.4 all-gather.2
  1312.0 10.8 convolution_convert_fusion
  1322.9 8.7 convolution_convert_fusion.2
  1331.5 8.7 convolution_convert_fusion.1
  1340.9 15.0 multiply_convert_fusion.3
  1361.9 6.9 multiply_reduce_fusion.1
  1379.1 14.7 all-gather.3
  1404.4 422.8 %while.82 = (s32[]{:T(128)}, f32[2,128,256]{2,1,0:T(8,128)S(1)}, f32[32,2,64,128]{3,2,1,0:T(8,128)}, f32[32,2,64,256]{3,2,1,0:T(8,128)}, f32[32,2,64,64]{3,2,1,0...) while((s32[]{:T(128)}, f32[2,128,256]{2,1,0:T(8,128)S(1)}, ...), condition=%wide.region_27.29_spmd, body=%wide.region_25.28_spmd.sunk | while | flops 403439616 | bytes 6848865 | solution.py:173
  1846.0 8.0 fusion.101
  1863.2 7.6 fusion.104
  1877.5 10.3 multiply_reduce_fusion.7
  2023.1 8.7 fusion.226
  2031.9 8.1 fusion.245
  2040.0 8.3 fusion.258
  2048.3 8.3 fusion.254
  2056.6 8.3 fusion.257
  2064.9 31.1 %add_convert_fusion = bf16[2048,2048]{1,0:T(8,128)(2,1)} fusion(f32[2048,2048]{1,0:T(8,128)} %fusion.245, f32[2048,2048]{1,0:T(8,128)} %fusion.226, f32[2048,2048]{1,0:T(8,128)} %fusion.258, f32[2048,2048]{1,0:T(8,128)} %fusion.257, f32[2048,2048]{1,0:T(8,128)} %fusion.254, bf16[2048,256]{1,0:T(8,128)(2,1)S(1)} %copy-done.43, ...), kind=kOutput, calls=%fused_computation.88 | convolution fusion | flops 2172649472 | bytes 94371840 | tf_op jit(solution)/shard_map/dot_general | solution.py:58
  2096.1 8.9 convert_element_type.416
  2119.6 195.5 %all-reduce.13.cloned.1.call-done = (bf16[2048,256]{1,0:T(8,128)(2,1)}, bf16[2048,256]{1,0:T(8,128)(2,1)}, bf16[2048,512]{1,0:T(8,128)(2,1)}, bf16[2048,512]{1,0:T(8,128)(2,1)}, bf16[512,2048]{1,0:T(8,128)(2,1)}) async-done(((bf16[2048,256]{1,0:T(8,128)(2,1)}, bf16[2048,256]{1,0:T(8,128)(2,1)}, bf16[2048,512]{1,0:T(8,128)(2,1)}, bf16[2048,512]{1,0:T(8,128)(2,1)}, bf16[512,2048]{1,0:T(8,128)(2,1)}), ...) | async-done | bytes 8388624 | tf_op jit(solution)/shard_map/psum | solution.py:428
  2328.4 60.2 %reduce-scatter.11.cloned.1.call-done = bf16[256,2048]{1,0:T(8,128)(2,1)} async-done(((bf16[2048,2048]{1,0:T(8,128)(2,1)}), bf16[256,2048]{1,0:T(8,128)(2,1)}) %reduce-scatter.11.cloned.1.call-update) | async-done | bytes 1048592 | tf_op jit(solution)/shard_map/reduce_scatter | solution.py:408
  2390.5 13.3 all-reduce.4
  2403.8 19.3 all-reduce.6
  (1642 shorter events, 1160.0 us)
Async XLA Ops:
  7.2 653.1 %copy-start = (bf16[512,2048]{1,0:T(8,128)(2,1)S(1)}, bf16[512,2048]{1,0:T(8,128)(2,1)}, u32[]{:S(2)}) copy-start(bf16[512,2048]{1,0:T(8,128)(2,1)} %param.50) | copy-start | bytes 6291460
  7.2 62.1 %all-gather.9.cloned.1.call-start = ((), (), s32[]{:S(2)}) async-start(), calls=%async_computation.4 | async-start | bytes 9437184 | tf_op jit(solution)/shard_map/all_gather | solution.py:227
  9.5 59.8 %copy-start.146 = (f32[2]{0:T(128)S(1)}, f32[2]{0:T(128)}, u32[]{:S(2)}) copy-start(f32[2]{0:T(128)} %param.48) | copy-start | bytes 28
  12.1 770.8 %reduce-scatter.5.cloned.1.call-start = ((), (), s32[]{:S(2)}) async-start(), calls=%async_computation.5 | async-start | bytes 18874368 | tf_op jit(solution)/shard_map/reduce_scatter | solution.py:311
  14.6 60.9 %copy-start.144 = (f32[2]{0:T(128)}, f32[2]{0:T(128)S(1)}, u32[]{:S(2)}) copy-start(f32[2]{0:T(128)S(1)} %exponential_negate_fusion) | copy-start | bytes 28
  14.7 116.3 %copy-start.127 = (f32[1,256]{1,0:T(1,128)}, f32[1,256]{1,0:T(1,128)S(1)}, u32[]{:S(2)}) copy-start(f32[1,256]{1,0:T(1,128)S(1)} %get-tuple-element.1145) | copy-start | bytes 3076
  14.7 116.3 %copy-start.129 = (f32[1,256]{1,0:T(1,128)}, f32[1,256]{1,0:T(1,128)S(1)}, u32[]{:S(2)}) copy-start(f32[1,256]{1,0:T(1,128)S(1)} %get-tuple-element.1146) | copy-start | bytes 3076
  14.7 116.3 %copy-start.131 = (f32[1,256]{1,0:T(1,128)}, f32[1,256]{1,0:T(1,128)S(1)}, u32[]{:S(2)}) copy-start(f32[1,256]{1,0:T(1,128)S(1)} %get-tuple-element.1147) | copy-start | bytes 3076
  14.7 116.3 %copy-start.133 = (f32[1,256]{1,0:T(1,128)}, f32[1,256]{1,0:T(1,128)S(1)}, u32[]{:S(2)}) copy-start(f32[1,256]{1,0:T(1,128)S(1)} %get-tuple-element.1148) | copy-start | bytes 3076
  14.8 101.1 %copy-start.135 = (f32[1,256]{1,0:T(1,128)}, f32[1,256]{1,0:T(1,128)S(1)}, u32[]{:S(2)}) copy-start(f32[1,256]{1,0:T(1,128)S(1)} %get-tuple-element.1141) | copy-start | bytes 3076
  14.8 101.1 %copy-start.137 = (f32[1,256]{1,0:T(1,128)}, f32[1,256]{1,0:T(1,128)S(1)}, u32[]{:S(2)}) copy-start(f32[1,256]{1,0:T(1,128)S(1)} %get-tuple-element.1142) | copy-start | bytes 3076
  14.8 101.1 %copy-start.139 = (f32[1,256]{1,0:T(1,128)}, f32[1,256]{1,0:T(1,128)S(1)}, u32[]{:S(2)}) copy-start(f32[1,256]{1,0:T(1,128)S(1)} %get-tuple-element.1143) | copy-start | bytes 3076
  14.8 101.1 %copy-start.141 = (f32[1,256]{1,0:T(1,128)}, f32[1,256]{1,0:T(1,128)S(1)}, u32[]{:S(2)}) copy-start(f32[1,256]{1,0:T(1,128)S(1)} %get-tuple-element.1144) | copy-start | bytes 3076
  14.8 324.4 %copy-start.112 = (f32[1,512]{1,0:T(1,128)}, f32[1,512]{1,0:T(1,128)S(1)}, u32[]{:S(2)}) copy-start(f32[1,512]{1,0:T(1,128)S(1)} %get-tuple-element.1137) | copy-start | bytes 6148
  14.8 324.4 %copy-start.114 = (f32[1,512]{1,0:T(1,128)}, f32[1,512]{1,0:T(1,128)S(1)}, u32[]{:S(2)}) copy-start(f32[1,512]{1,0:T(1,128)S(1)} %get-tuple-element.1138) | copy-start | bytes 6148
  14.8 324.4 %copy-start.116 = (f32[1,512]{1,0:T(1,128)}, f32[1,512]{1,0:T(1,128)S(1)}, u32[]{:S(2)}) copy-start(f32[1,512]{1,0:T(1,128)S(1)} %get-tuple-element.1139) | copy-start | bytes 6148
  14.8 324.4 %copy-start.118 = (f32[1,512]{1,0:T(1,128)}, f32[1,512]{1,0:T(1,128)S(1)}, u32[]{:S(2)}) copy-start(f32[1,512]{1,0:T(1,128)S(1)} %get-tuple-element.1140) | copy-start | bytes 6148
  14.9 164.7 %copy-start.94 = (pred[64,64]{1,0:T(8,128)(4,1)}, pred[64,64]{1,0:T(8,128)(4,1)S(1)}, u32[]{:S(2)}) copy-start(pred[64,64]{1,0:T(8,128)(4,1)S(1)} %get-tuple-element.1172) | copy-start | bytes 12292
  14.9 311.8 %copy-start.81 = (pred[64,64]{1,0:T(8,128)(4,1)}, pred[64,64]{1,0:T(8,128)(4,1)S(1)}, u32[]{:S(2)}) copy-start(pred[64,64]{1,0:T(8,128)(4,1)S(1)} %get-tuple-element.1173) | copy-start | bytes 12292
  15.0 324.3 %copy-start.70 = (f32[2048]{0:T(1024)}, f32[2048]{0:T(1024)S(1)}, u32[]{:S(2)}) copy-start(f32[2048]{0:T(1024)S(1)} %get-tuple-element.1133) | copy-start | bytes 24580
  15.0 324.3 %copy-start.72 = (f32[2048]{0:T(1024)}, f32[2048]{0:T(1024)S(1)}, u32[]{:S(2)}) copy-start(f32[2048]{0:T(1024)S(1)} %get-tuple-element.1134) | copy-start | bytes 24580
  15.0 324.3 %copy-start.74 = (f32[2048]{0:T(1024)}, f32[2048]{0:T(1024)S(1)}, u32[]{:S(2)}) copy-start(f32[2048]{0:T(1024)S(1)} %get-tuple-element.1135) | copy-start | bytes 24580
  15.0 324.3 %copy-start.76 = (f32[2048]{0:T(1024)}, f32[2048]{0:T(1024)S(1)}, u32[]{:S(2)}) copy-start(f32[2048]{0:T(1024)S(1)} %get-tuple-element.1136) | copy-start | bytes 24580
  76.6 250.1 %copy-start.52 = (f32[2,32,64]{2,1,0:T(8,128)}, f32[2,32,64]{2,1,0:T(8,128)S(1)}, u32[]{:S(2)}) copy-start(f32[2,32,64]{2,1,0:T(8,128)S(1)} %reduce_window_sum.34) | copy-start | bytes 49156
  84.5 31.3 %collective-permute-start.2 = (f32[3,256]{1,0:T(4,128)S(1)}, f32[3,256]{1,0:T(4,128)S(1)}, u32[]{:S(2)}, u32[]{:S(2)}) collective-permute-start(f32[3,256]{1,0:T(4,128)S(1)} %slice.254), channel_id=1, source_target_pairs={{0,8},{8,16},{16,24},{1,9},{9,17},{17,25},{2,10},{10,18},{18,26},{... | collective-permute-start | bytes 9224 | tf_op jit(solution)/shard_map/ppermute | solution.py:16
  90.3 264.8 %copy-start.56 = (f32[32,64,2]{1,0,2:T(8,128)}, f32[32,64,2]{1,0,2:T(8,128)S(1)}, u32[]{:S(2)}) copy-start(f32[32,64,2]{1,0,2:T(8,128)S(1)} %reshape.425) | copy-start | bytes 49156
  107.4 72.2 %copy-start.54 = (f32[2,32,64]{1,2,0:T(8,128)}, f32[2,32,64]{1,2,0:T(8,128)S(1)}, u32[]{:S(2)}) copy-start(f32[2,32,64]{1,2,0:T(8,128)S(1)} %copy.403) | copy-start | bytes 49156
  108.2 22.7 collective-permute-start
  111.7 67.9 %copy-start.64 = (f32[2,32,64]{1,2,0:T(8,128)}, f32[2,32,64]{1,2,0:T(8,128)S(1)}, u32[]{:S(2)}) copy-start(f32[2,32,64]{1,2,0:T(8,128)S(1)} %copy.401) | copy-start | bytes 49156
  112.5 226.8 %collective-permute-start.1 = (f32[3,512]{1,0:T(4,128)S(1)}, f32[3,512]{1,0:T(4,128)S(1)}, u32[]{:S(2)}, u32[]{:S(2)}) collective-permute-start(f32[3,512]{1,0:T(4,128)S(1)} %slice.249), channel_id=1, source_target_pairs={{0,8},{8,16},{16,24},{1,9},{9,17},{17,25},{2,10},{10,18},{18,26},{... | collective-permute-start | bytes 18440 | tf_op jit(solution)/shard_map/ppermute | solution.py:16
  668.5 117.9 %copy-start.96 = (f32[2048]{0:T(1024)S(1)}, f32[2048]{0:T(1024)}, u32[]{:S(2)}) copy-start(f32[2048]{0:T(1024)} %param.51) | copy-start | bytes 24580
  668.5 200.0 %all-gather.11.cloned.1.call-start = ((), (), s32[]{:S(2)}) async-start(), calls=%async_computation.6 | async-start | bytes 5242880 | tf_op jit(solution)/shard_map/all_gather | solution.py:314
  787.6 161.6 %all-gather.13.cloned.1.call-start = ((), (), s32[]{:S(2)}) async-start(), calls=%async_computation.8 | async-start | bytes 5242880 | tf_op jit(solution)/shard_map/all_gather | solution.py:324
  790.5 271.8 %reduce-scatter.9.cloned.1.call-start = ((), (), s32[]{:S(2)}) async-start(), calls=%async_computation.9 | async-start | bytes 5242880 | tf_op jit(solution)/shard_map/reduce_scatter | solution.py:329
  986.8 155.0 %reduce-scatter.7.cloned.1.call-start = ((), (), s32[]{:S(2)}) async-start(), calls=%async_computation.7 | async-start | bytes 5242880 | tf_op jit(solution)/shard_map/reduce_scatter | solution.py:318
  997.8 342.5 %all-gather.15.cloned.1.call-start = ((), (), s32[]{:S(2)}) async-start(), calls=%async_computation.10 | async-start | bytes 9437184 | tf_op jit(solution)/shard_map/all_gather | solution.py:340
  1147.2 948.8 %all-reduce.11.cloned.1.call-start = ((), (), s32[]{:S(2)}) async-start(), calls=%async_computation.12 | async-start | bytes 34603008 | tf_op jit(solution)/shard_map/psum | solution.py:420
  1340.3 974.8 %all-reduce.13.cloned.1.call-start = ((), (), s32[]{:S(2)}) async-start(), calls=%async_computation.13 | async-start | bytes 16777216 | tf_op jit(solution)/shard_map/psum | solution.py:428
  1909.7 96.1 %collective-permute-start.5 = (f32[3,512]{1,0:T(4,128)S(1)}, f32[3,512]{1,0:T(4,128)S(1)}, u32[]{:S(2)}, u32[]{:S(2)}) collective-permute-start(f32[3,512]{1,0:T(4,128)S(1)} %slice.284), channel_id=1, source_target_pairs={{8,0},{16,8},{24,16},{9,1},{17,9},{25,17},{10,2},{18,10},{26,18},{... | collective-permute-start | bytes 18440 | tf_op jit(solution)/shard_map/ppermute | solution.py:16
  1940.9 51.3 %collective-permute-start.3 = (f32[3,256]{1,0:T(4,128)S(1)}, f32[3,256]{1,0:T(4,128)S(1)}, u32[]{:S(2)}, u32[]{:S(2)}) collective-permute-start(f32[3,256]{1,0:T(4,128)S(1)} %slice.262), channel_id=1, source_target_pairs={{8,0},{16,8},{24,16},{9,1},{17,9},{25,17},{10,2},{18,10},{26,18},{... | collective-permute-start | bytes 9224 | tf_op jit(solution)/shard_map/ppermute | solution.py:16
  1978.8 16.5 collective-permute-start.4
  2017.2 371.4 %reduce-scatter.11.cloned.1.call-start = ((), (), s32[]{:S(2)}) async-start(), calls=%async_computation.11 | async-start | bytes 9437184 | tf_op jit(solution)/shard_map/reduce_scatter | solution.py:408
  2325.6 63.0 %copy-start.14 = (bf16[256,2048]{1,0:T(8,128)(2,1)S(1)}, bf16[256,2048]{1,0:T(8,128)(2,1)}, u32[]{:S(2)}) copy-start(bf16[256,2048]{1,0:T(8,128)(2,1)} %param.35) | copy-start | bytes 3145732
  2325.6 63.0 %copy-start.97 = (f32[2048]{0:T(1024)S(1)}, f32[2048]{0:T(1024)}, u32[]{:S(2)}) copy-start(f32[2048]{0:T(1024)} %param.37) | copy-start | bytes 24580
  2325.6 63.0 %copy-start.121 = (f32[256]{0:T(256)S(1)}, f32[256]{0:T(256)}, u32[]{:S(2)}) copy-start(f32[256]{0:T(256)} %copy-done.120) | copy-start | bytes 3076
  2328.4 62.1 %copy-start.126 = (bf16[2048]{0:T(1024)(128)(2,1)S(1)}, bf16[2048]{0:T(1024)(128)(2,1)}, u32[]{:S(2)}) copy-start(bf16[2048]{0:T(1024)(128)(2,1)} %get-tuple-element.962) | copy-start | bytes 12292
  2328.4 62.1 %copy-start.154 = (bf16[256]{0:T(256)(128)(2,1)S(1)}, bf16[256]{0:T(256)(128)(2,1)}, u32[]{:S(2)}) copy-start(bf16[256]{0:T(256)(128)(2,1)} %get-tuple-element.949) | copy-start | bytes 1540
  2328.4 100.5 %copy-start.147 = (f32[256]{0:T(256)S(1)}, f32[256]{0:T(256)}, u32[]{:S(2)}) copy-start(f32[256]{0:T(256)} %get-tuple-element.1149) | copy-start | bytes 3076
  (160 other events, 948.2 us)
Sparse Core Ops, SparseCore 0:
  12.2 57.0 all-gather.8
  668.6 114.1 reduce-scatter.4
  787.8 80.7 all-gather.10
  870.0 79.2 all-gather.12
  986.9 75.2 reduce-scatter.8
  1064.5 77.2 reduce-scatter.6
  1147.3 54.8 all-gather.14
  1340.4 223.6 all-reduce.10
  2017.3 297.7 all-reduce.12
  2318.4 70.1 reduce-scatter.10
where the time goes:
time: 2470 us; the launch traced here: 2440 us
  matrix products  827 us (33%)
  waiting for transfers between devices  673 us (27%)
  local copies, waits for them, and re-layouts  436 us (18%)
  other arithmetic  313 us (13%)
  blocking collectives  91.4 us (4%)
  loops' own time  67.3 us (3%)
    dot_general x486, matrix products, matmul(): jnp.dot(left, right, precision=highest_precision, preferred_element_type=...  489 us
    psum x1, waiting for transfers between devices, shards(): lax.psum(grad_w_query.astype(jnp.bfloat16), 'seq').astype(jnp.float32)  196 us
    squeeze x192, local copies, waits for them, and re-layouts, one_head(): lax.scan(stepper, state_h, (weights_w, values_u, scores, scaled_queries,...  146 us
    another operation x2, other arithmetic, group_parts(): jax.scipy.linalg.solve_triangular(system, strength[:, None] * values, low...  141 us
    dot_general x10, matrix products, product_nt(): lax.dot_general(left, right, (((1,), (1,)), ((), ())), preferred_element_...  125 us
    reduce_scatter x1, waiting for transfers between devices, shards(): lax.psum_scatter(product(gated, w_output), 'head', scatter_dimension=0, t...  114 us
    dynamic_slice x160, local copies, waits for them, and re-layouts, one_head(): lax.scan(stepper, state_h, (weights_w, values_u, scores, scaled_queries,...  86.1 us
    dot_general x10, matrix products, product(): return jnp.dot(left, right, preferred_element_type=jnp.float32)  84.2 us
  transfers between devices with their start and end apart: 16, of which 8 were waited for; matrix products, arithmetic and copies ran while one was open for 49% of the time, Pallas kernels for 0%

commit v1 on v0

v1 whole, which is shorter than its diff:
```python
import functools

import jax
import jax.numpy as jnp
from jax import lax
from jax.experimental import pallas as pl
from jax.experimental.pallas import tpu as pltpu
from jax.sharding import PartitionSpec as P

GROUP = 64
BLOCK = 256
LANES = 128
HALO = 8

epsilon = 1e-06
f32 = jnp.float32
bf16 = jnp.bfloat16
VMEM_LIMIT = 56 * 1024 * 1024


def dot(left, right):
    return jnp.dot(left, right, preferred_element_type=f32)


def dot_tn(left, right):
    return lax.dot_general(left, right, (((0,), (0,)), ((), ())), preferred_element_type=f32)


def dot_nt(left, right):
    return lax.dot_general(left, right, (((1,), (1,)), ((), ())), preferred_element_type=f32)


def halves(values):
    top = values.astype(bf16)
    return top, (values - top.astype(f32)).astype(bf16)


def exact_left(left, right):
    top = right.astype(bf16)
    rest = right - top.astype(f32)
    middle = rest.astype(bf16)
    low = (rest - middle.astype(f32)).astype(bf16)
    return dot(left, top) + dot(left, middle) + dot(left, low)


def dot_fine(left, right):
    left_top, left_low = halves(left)
    right_top, right_low = halves(right)
    return dot(left_top, right_top) + (dot(left_top, right_low) + dot(left_low, right_top))


def sigmoid(values):
    return jax.nn.sigmoid(values)


def silu_slope(values):
    sigma = sigmoid(values)
    return sigma * (1.0 + values * (1.0 - sigma))


def softplus(values):
    return jnp.maximum(values, 0.0) + jnp.log1p(jnp.exp(-jnp.abs(values)))


def slot_starts(doc_lengths):
    slot_sizes = (doc_lengths + (GROUP - 1)) // GROUP * GROUP
    return jnp.cumsum(slot_sizes, dtype=jnp.int32) - slot_sizes


def layout(doc_lengths, first_row, row_total):
    starts = slot_starts(doc_lengths)
    places = first_row + jnp.arange(row_total, dtype=jnp.int32)
    owners = jnp.sum(
        (places[:, None] >= starts[None, 1:]).astype(jnp.int32), axis=1, dtype=jnp.int32
    )
    picked = (owners[:, None] == jnp.arange(doc_lengths.shape[0], dtype=jnp.int32)[None, :]).astype(
        jnp.int32
    )
    begins = jnp.sum(picked * starts[None, :], axis=1, dtype=jnp.int32)
    length = jnp.sum(picked * doc_lengths[None, :], axis=1, dtype=jnp.int32)
    offset = places - begins
    return (offset, offset < length)


def rms_scale(values, gain):
    return values * lax.rsqrt(jnp.mean(values * values, axis=-1, keepdims=True) + epsilon) * gain


def rms_back(values, gain, grad_in):
    scale = lax.rsqrt(jnp.mean(values * values, axis=-1, keepdims=True) + epsilon)
    weighted = grad_in * gain
    grad_values = scale * weighted - values * scale**3 * jnp.mean(
        weighted * values, axis=-1, keepdims=True
    )
    grad_gain = jnp.sum((grad_in * values * scale).reshape(-1, values.shape[-1]), axis=0)
    return (grad_values, grad_gain)


def owner_of(meta, docs, places):
    total = jnp.zeros_like(places)
    for doc in range(1, docs):
        total = total + jnp.where(places >= meta[1 + doc], 1, 0)
    return total


def offset_of(meta, docs, places):
    begin = jnp.zeros_like(places)
    for doc in range(1, docs):
        begin = jnp.where(places >= meta[1 + doc], meta[1 + doc], begin)
    return places - begin


class Masks:
    def __init__(self, meta, docs, chunk):
        base = meta[0] + chunk * BLOCK
        rows = lax.broadcasted_iota(jnp.int32, (BLOCK, BLOCK), 0)
        cols = lax.broadcasted_iota(jnp.int32, (BLOCK, BLOCK), 1)
        same = owner_of(meta, docs, base + rows) == owner_of(meta, docs, base + cols)
        self.inclusive = same & (rows >= cols)
        self.strictly = same & (rows > cols)
        self.level = rows ^ cols
        self.lower = jnp.where(rows >= cols, 1.0, 0.0).astype(bf16)
        self.upper = jnp.where(rows <= cols, 1.0, 0.0).astype(bf16)
        self.eye = jnp.where(rows == cols, 1.0, 0.0)
        place = base + lax.broadcasted_iota(jnp.int32, (BLOCK, 1), 0)
        owner = owner_of(meta, docs, place)
        before = jnp.int32(0)
        last = jnp.int32(0)
        for doc in range(1, docs):
            before = before + jnp.where(base - 1 >= meta[1 + doc], 1, 0)
            last = last + jnp.where(base + BLOCK - 1 >= meta[1 + doc], 1, 0)
        self.enters = jnp.where(owner == before, 1.0, 0.0)
        self.leaves = jnp.where(owner == last, 1.0, 0.0)
        self.through = jnp.where(before == last, 1.0, 0.0).astype(f32)
        self.offset = offset_of(meta, docs, place)


def decays(masks, scal, scal_t, head):
    column = scal[:, head : head + 1]
    row = scal_t[head : head + 1, :]
    within = jnp.where(masks.inclusive, jnp.exp(jnp.minimum(column - row, 0.0)), 0.0)
    last = column[BLOCK - 1 : BLOCK, :]
    entry = jnp.exp(column) * masks.enters
    leave = jnp.exp(last - column) * masks.leaves
    through = jnp.exp(last) * masks.through
    return within, entry, leave, through


def unit_lower_inverse(masks, system):
    inverse = masks.eye - jnp.where(masks.level == 1, system, 0.0)
    width = 2
    while width < BLOCK:
        part = jnp.where((masks.level >= width) & (masks.level < 2 * width), system, 0.0)
        low = inverse.astype(bf16)
        inverse = inverse - dot(low, dot(part.astype(bf16), low).astype(bf16))
        width *= 2
    return inverse


def forward_kernel(
    heads, key_width, value_width, docs, taps,
    meta, rows_ref, tail_ref, w_ref, conv_ref, dvec_ref,
    pre_ref, act_ref, gate_ref, small_ref, scal_ref, qkv_ref, inv_ref, w_out_ref, u_ref, starts_ref, drop_ref, map_ref,
    ext, state,
):
    chunk = pl.program_id(0)
    qw, vw = heads * key_width, heads * value_width
    mixed = 2 * qw + vw
    masks = Masks(meta, docs, chunk)
    rows = rows_ref[...]

    @pl.when(chunk == 0)
    def _():
        halo = dot(tail_ref[...], w_ref[:, :mixed])
        ext[0:HALO, :] = halo[HALO : 2 * HALO, :]
        ident = jnp.where(
            lax.broadcasted_iota(jnp.int32, (key_width, key_width + value_width), 0)
            == lax.broadcasted_iota(jnp.int32, (key_width, key_width + value_width), 1),
            1.0, 0.0,
        )
        for head in range(heads):
            state[head] = ident

    @pl.when(chunk > 0)
    def _():
        ext[0:HALO, :] = ext[BLOCK : BLOCK + HALO, :]

    pre = dot(rows, w_ref[...])
    ext[HALO : HALO + BLOCK, :] = pre[:, :mixed]
    pre_ref[...] = pre[:, :mixed]
    gate_ref[...] = pre[:, mixed : mixed + vw]
    small = pre[:, mixed + vw :]
    small_ref[...] = small

    conv = jnp.zeros((BLOCK, mixed), f32)
    for lag in range(taps):
        keep = jnp.where(masks.offset >= lag, 1.0, 0.0)
        conv = conv + conv_ref[lag : lag + 1, :] * (ext[HALO - lag : HALO - lag + BLOCK, :] * keep)
    act_ref[...] = conv
    act = conv * sigmoid(conv)

    lane = lax.broadcasted_iota(jnp.int32, (BLOCK, LANES), 1)
    decay = dvec_ref[1:2, :] * softplus(small + dvec_ref[0:1, :])
    cumul = exact_left(masks.lower, decay)
    scal = jnp.where(lane < heads, cumul, sigmoid(small))
    scal_ref[...] = scal
    scal_t = scal.T

    for head in range(heads):
        act_q = act[:, head * key_width : (head + 1) * key_width]
        act_k = act[:, qw + head * key_width : qw + (head + 1) * key_width]
        value = act[:, 2 * qw + head * value_width : 2 * qw + (head + 1) * value_width].astype(bf16)
        norm_q = lax.rsqrt(jnp.sum(act_q * act_q, axis=1, keepdims=True) + epsilon)
        norm_k = lax.rsqrt(jnp.sum(act_k * act_k, axis=1, keepdims=True) + epsilon)
        query = (act_q * norm_q * key_width ** (-0.5)).astype(bf16)
        key = (act_k * norm_k).astype(bf16)
        qkv_ref[:, head * key_width : (head + 1) * key_width] = query
        qkv_ref[:, qw + head * key_width : qw + (head + 1) * key_width] = key
        qkv_ref[:, 2 * qw + head * value_width : 2 * qw + (head + 1) * value_width] = value
        within, entry, leave, through = decays(masks, scal, scal_t, head)
        beta = scal[:, heads + head : heads + head + 1]
        system = jnp.where(masks.strictly, beta * dot_nt(key, key) * within, 0.0)
        inverse = unit_lower_inverse(masks, system).astype(bf16)
        inv_ref[0, head] = inverse
        key_f = key.astype(f32)
        w_part = dot(inverse, (beta * entry * key_f).astype(bf16)).astype(bf16)
        u_part = dot(inverse, (beta * value.astype(f32)).astype(bf16))
        w_out_ref[0, head] = w_part
        u_ref[0, head] = u_part
        tail_key = (leave * key_f).astype(bf16)
        drop = dot_tn(tail_key, w_part)
        added = dot_tn(tail_key, u_part.astype(bf16))
        drop_ref[0, head] = drop
        before = state[head]
        starts_ref[0, head] = before
        after = through * before - dot(drop.astype(bf16), before.astype(bf16))
        after = after + jnp.concatenate([jnp.zeros((key_width, key_width), f32), added], axis=1)
        state[head] = after
        map_ref[head] = after


def output_kernel(
    heads, key_width, value_width, docs, others,
    meta, maps_ref, starts_ref, w_in_ref, u_ref, qkv_ref, scal_ref, gate_ref, gain_ref, w_output_ref,
    core_ref, gated_ref, mixed_ref, fresh_ref, state_ref,
    incoming,
):
    chunk = pl.program_id(0)
    qw = heads * key_width

    @pl.when(chunk == 0)
    def _():
        for head in range(heads):
            state = jnp.zeros((key_width, value_width), f32)
            for other in range(others):
                passing = maps_ref[other, head, :, :key_width]
                top, low = halves(state)
                state = dot(passing, top) + dot(passing, low) + maps_ref[other, head, :, key_width:].astype(f32)
            incoming[head] = state

    masks = Masks(meta, docs, chunk)
    scal = scal_ref[...]
    scal_t = scal.T
    gain = gain_ref[...]
    for head in range(heads):
        query = qkv_ref[:, head * key_width : (head + 1) * key_width]
        key = qkv_ref[:, qw + head * key_width : qw + (head + 1) * key_width]
        within, entry, leave, through = decays(masks, scal, scal_t, head)
        begun = starts_ref[0, head]
        state = dot_fine(begun[:, :key_width], incoming[head]) + begun[:, key_width:]
        state_ref[0, head] = state
        state_low = state.astype(bf16)
        fresh = (u_ref[0, head] - dot(w_in_ref[0, head], state_low)).astype(bf16)
        fresh_ref[0, head] = fresh
        scores = (dot_nt(query, key) * within).astype(bf16)
        core = dot((query.astype(f32) * entry).astype(bf16), state_low) + dot(scores, fresh)
        span = slice(head * value_width, (head + 1) * value_width)
        core_ref[:, span] = core
        scale = lax.rsqrt(jnp.mean(core * core, axis=1, keepdims=True) + epsilon)
        gate = gate_ref[:, span]
        gated_ref[:, span] = (core * scale * gain * (gate * sigmoid(gate))).astype(bf16)
    mixed_ref[...] = dot(gated_ref[...], w_output_ref[...]).astype(bf16)


def core_grad_kernel(
    heads, key_width, value_width, docs, chunks,
    meta, grad_ref, w_output_ref, core_ref, gate_ref, gain_ref, qkv_ref, scal_ref, w_in_ref, drop_ref,
    grad_core_ref, inner_ref, pull_ref, grad_gate_ref, grad_gain_ref, total_ref,
):
    step = pl.program_id(0)
    chunk = chunks - 1 - step
    qw = heads * key_width
    masks = Masks(meta, docs, chunk)
    scal = scal_ref[...]
    scal_t = scal.T
    gain = gain_ref[...]

    @pl.when(step == 0)
    def _():
        grad_gain_ref[...] = jnp.zeros_like(grad_gain_ref)
        total_ref[...] = jnp.zeros_like(total_ref)

    grad_gated = dot_nt(grad_ref[...], w_output_ref[...])
    for head in range(heads):
        span = slice(head * value_width, (head + 1) * value_width)
        core = core_ref[:, span]
        gate = gate_ref[:, span]
        grad_in = grad_gated[:, span]
        scale = lax.rsqrt(jnp.mean(core * core, axis=1, keepdims=True) + epsilon)
        sigma = sigmoid(gate)
        normed = core * scale
        grad_gate_ref[:, span] = (
            grad_in * (normed * gain) * (sigma * (1.0 + gate * (1.0 - sigma)))
        ).astype(bf16)
        grad_normed = grad_in * (gate * sigma)
        weighted = grad_normed * gain
        grad_core = scale * (weighted - normed * jnp.mean(weighted * normed, axis=1, keepdims=True))
        grad_gain_ref[0:1, :] += jnp.sum(grad_normed * normed, axis=0, keepdims=True)
        grad_core = grad_core.astype(bf16)
        grad_core_ref[0, head] = grad_core
        query = qkv_ref[:, head * key_width : (head + 1) * key_width]
        key = qkv_ref[:, qw + head * key_width : qw + (head + 1) * key_width]
        within, entry, leave, through = decays(masks, scal, scal_t, head)
        scores = (dot_nt(query, key) * within).astype(bf16)
        inner = dot_tn(scores, grad_core)
        inner_ref[0, head] = inner
        pull = dot_tn((query.astype(f32) * entry).astype(bf16), grad_core) - dot_tn(
            w_in_ref[0, head], inner.astype(bf16)
        )
        pull_ref[0, head] = pull
        total = total_ref[head]
        total_ref[head] = (
            through * total - dot_tn(drop_ref[0, head].astype(bf16), total.astype(bf16)) + pull
        )


def backward_kernel(
    heads, key_width, value_width, docs, chunks, others,
    meta, maps_ref, qkv_ref, act_ref, scal_ref, small_ref, inv_ref, fresh_ref, state_ref,
    grad_core_ref, inner_ref, pull_ref, drop_ref, dvec_ref,
    grad_conv_ref, grad_small_ref, sums_ref,
    carried,
):
    step = pl.program_id(0)
    chunk = chunks - 1 - step
    qw = heads * key_width

    @pl.when(step == 0)
    def _():
        sums_ref[...] = jnp.zeros_like(sums_ref)
        for head in range(heads):
            state = jnp.zeros((key_width, value_width), f32)
            for other in range(others):
                passing = maps_ref[other, head, :, :key_width]
                top, low = halves(state)
                state = dot_tn(passing, top) + dot_tn(passing, low) + maps_ref[other, head, :, key_width:].astype(f32)
            carried[head] = state

    masks = Masks(meta, docs, chunk)
    scal = scal_ref[...]
    scal_t = scal.T
    lane = lax.broadcasted_iota(jnp.int32, (BLOCK, LANES), 1)
    slopes = jnp.zeros((BLOCK, LANES), f32)
    tails = jnp.zeros((1, LANES), f32)
    betas = jnp.zeros((BLOCK, LANES), f32)
    for head in range(heads):
        q_span = slice(head * key_width, (head + 1) * key_width)
        k_span = slice(qw + head * key_width, qw + (head + 1) * key_width)
        v_span = slice(2 * qw + head * value_width, 2 * qw + (head + 1) * value_width)
        query, key, value = qkv_ref[:, q_span], qkv_ref[:, k_span], qkv_ref[:, v_span]
        query_f, key_f = query.astype(f32), key.astype(f32)
        within, entry, leave, through = decays(masks, scal, scal_t, head)
        beta = scal[:, heads + head : heads + head + 1]
        later = carried[head]
        later_low = later.astype(bf16)
        state = state_ref[0, head]
        state_low = state.astype(bf16)
        grad_core = grad_core_ref[0, head]
        fresh = fresh_ref[0, head]
        carried[head] = through * later - dot_tn(drop_ref[0, head].astype(bf16), later_low) + pull_ref[0, head]
        grad_fresh = inner_ref[0, head] + dot((leave * key_f).astype(bf16), later_low)
        grad_x = dot_tn(inv_ref[0, head], grad_fresh.astype(bf16))
        grad_x_low = grad_x.astype(bf16)
        grad_x_beta = beta * grad_x
        recalled = dot(key, state_low)
        grad_beta = jnp.sum(grad_x * (value.astype(f32) - entry * recalled), axis=1, keepdims=True)
        from_state_q = dot_nt(grad_core, state_low)
        from_state_k = dot_nt(grad_x_beta.astype(bf16), state_low)
        grad_scores = (dot_nt(grad_core, fresh) * within).astype(bf16)
        gram = dot_nt(key, key)
        grad_system = jnp.where(masks.strictly, dot_nt(grad_x_low, fresh) * within, 0.0)
        grad_beta = grad_beta - jnp.sum(grad_system * gram, axis=1, keepdims=True)
        grad_gram = (-beta * grad_system).astype(bf16)
        grad_query = dot(grad_scores, key) + entry * from_state_q
        grad_row = dot(grad_gram, key) - entry * from_state_k
        passed = leave * dot_nt(fresh, later_low)
        grad_col = dot_tn(grad_gram, key) + dot_tn(grad_scores, query) + passed
        slope = jnp.sum(query_f * grad_query + key_f * (grad_row - grad_col), axis=1, keepdims=True)
        kept = jnp.sum(jnp.sum(state * later, axis=1, keepdims=True), axis=0, keepdims=True)
        moved = jnp.sum(jnp.sum(key_f * passed, axis=1, keepdims=True), axis=0, keepdims=True)
        tail = through * kept + moved
        slopes = jnp.where(lane == head, slope, slopes)
        tails = jnp.where(lane[0:1, :] == head, tail, tails)
        betas = jnp.where(lane == heads + head, grad_beta, betas)

        conv_q, conv_k, conv_v = act_ref[:, q_span], act_ref[:, k_span], act_ref[:, v_span]
        for span, conv, grad, factor in (
            (q_span, conv_q, grad_query, key_width ** (-0.5)),
            (k_span, conv_k, grad_row + grad_col, 1.0),
        ):
            sigma = sigmoid(conv)
            act = conv * sigma
            norm = lax.rsqrt(jnp.sum(act * act, axis=1, keepdims=True) + epsilon)
            unit = act * norm
            grad_act = (factor * norm) * (grad - unit * jnp.sum(grad * unit, axis=1, keepdims=True))
            grad_conv_ref[:, span] = grad_act * (sigma * (1.0 + conv * (1.0 - sigma)))
        grad_conv_ref[:, v_span] = grad_x_beta * silu_slope(conv_v)

    grad_decay = jnp.where(lane < heads, exact_left(masks.upper, slopes) + tails, 0.0)
    shifted = small_ref[...] + dvec_ref[0:1, :]
    rate = dvec_ref[1:2, :]
    grad_z = grad_decay * rate * sigmoid(shifted)
    sums_ref[0:1, :] += jnp.sum(grad_z, axis=0, keepdims=True)
    sums_ref[1:2, :] += jnp.sum(grad_decay * (rate * softplus(shifted)), axis=0, keepdims=True)
    strength = sigmoid(small_ref[...])
    grad_small_ref[...] = jnp.where(lane < heads, grad_z, betas * strength * (1.0 - strength)).astype(bf16)


def projection_grad_kernel(
    mixed, docs, chunks, taps,
    meta, grad_conv_ref, later_ref, edge_ref, pre_ref, grad_gate_ref, grad_small_ref, conv_ref, w_ref,
    grad_pre_ref, grad_taps_ref, grad_rows_ref,
    ext,
):
    chunk = pl.program_id(0)

    @pl.when(chunk == 0)
    def _():
        grad_taps_ref[...] = jnp.zeros_like(grad_taps_ref)

    ext[0:BLOCK, :] = grad_conv_ref[...]

    @pl.when(chunk == chunks - 1)
    def _():
        ext[BLOCK : BLOCK + HALO, :] = edge_ref[...]

    @pl.when(chunk < chunks - 1)
    def _():
        ext[BLOCK : BLOCK + HALO, :] = later_ref[...]

    place = meta[0] + chunk * BLOCK + lax.broadcasted_iota(jnp.int32, (BLOCK, 1), 0)
    pre = pre_ref[...]
    total = jnp.zeros((BLOCK, mixed), f32)
    for lag in range(taps):
        keep = jnp.where(offset_of(meta, docs, place + lag) >= lag, 1.0, 0.0)
        moved = ext[lag : lag + BLOCK, :] * keep
        total = total + conv_ref[lag : lag + 1, :] * moved
        grad_taps_ref[lag : lag + 1, :] += jnp.sum(pre * moved, axis=0, keepdims=True)
    width = grad_gate_ref.shape[1]
    grad_pre_ref[:, :mixed] = total.astype(bf16)
    grad_pre_ref[:, mixed : mixed + width] = grad_gate_ref[...]
    grad_pre_ref[:, mixed + width :] = grad_small_ref[...]
    grad_rows_ref[...] = dot_nt(grad_pre_ref[...], w_ref[...]).astype(bf16)


def whole(shape):
    zeros = (0,) * len(shape)
    return pl.BlockSpec(tuple(shape), lambda step: zeros)


def by_rows(width, chunks=None):
    if chunks is None:
        return pl.BlockSpec((BLOCK, width), lambda step: (step, 0))
    return pl.BlockSpec((BLOCK, width), lambda step: (chunks - 1 - step, 0))


def by_chunk(shape, chunks=None):
    rest = (0,) * len(shape)
    if chunks is None:
        return pl.BlockSpec((1,) + tuple(shape), lambda step: (step,) + rest)
    return pl.BlockSpec((1,) + tuple(shape), lambda step: (chunks - 1 - step,) + rest)


SCALARS = pl.BlockSpec(memory_space=pltpu.SMEM)


def params():
    return pltpu.CompilerParams(dimension_semantics=("arbitrary",), vmem_limit_bytes=VMEM_LIMIT)


def struct(shape, dtype):
    return jax.ShapeDtypeStruct(tuple(shape), dtype)


def from_earlier(array, axis):
    devices = lax.axis_size(axis)
    parts = [
        lax.ppermute(array, axis, [(i, i + by) for i in range(devices - by)])
        for by in range(devices - 1, 0, -1)
    ]
    return jnp.stack(parts) if parts else jnp.zeros((1,) + array.shape, array.dtype)


def from_later(array, axis):
    devices = lax.axis_size(axis)
    parts = [
        lax.ppermute(array, axis, [(i + by, i) for i in range(devices - by)])
        for by in range(devices - 1, 0, -1)
    ]
    return jnp.stack(parts) if parts else jnp.zeros((1,) + array.shape, array.dtype)


def shards(
    inputs,
    doc_lengths,
    first_gain,
    w_query,
    w_key,
    w_value,
    w_outgate,
    w_decay,
    w_beta,
    conv_query,
    conv_key,
    conv_value,
    decay_log,
    decay_bias,
    head_gain,
    w_output,
    second_gain,
    w_gate,
    w_up,
    w_down,
    cotangent,
):
    row_count, model_width = inputs.shape
    heads = decay_log.shape[0]
    qw, vw = w_query.shape[1], w_value.shape[1]
    key_width, value_width = qw // heads, vw // heads
    mixed_width = 2 * qw + vw
    taps = conv_query.shape[0]
    docs = doc_lengths.shape[0]
    seq_index = lax.axis_index("seq")
    head_index = lax.axis_index("head")
    head_total = lax.axis_size("head")
    seq_rows = row_count * head_total
    chunks = seq_rows // BLOCK
    others = max(lax.axis_size("seq") - 1, 1)
    sizes = (heads, key_width, value_width, docs)

    inputs_f = inputs.astype(f32)
    normed = rms_scale(inputs_f, first_gain).astype(bf16)
    block_rows = lax.all_gather(normed, "head", axis=0, tiled=True)
    tail = from_previous(block_rows[seq_rows - 2 * HALO :])
    meta = jnp.concatenate(
        [(seq_index * seq_rows).astype(jnp.int32)[None], slot_starts(doc_lengths)]
    )
    _, own_valid = layout(doc_lengths, (seq_index * head_total + head_index) * row_count, row_count)

    w_all = jnp.concatenate(
        [
            w_query, w_key, w_value, w_outgate, w_decay, w_beta,
            jnp.zeros((model_width, LANES - 2 * heads), bf16),
        ],
        axis=1,
    )
    all_width = w_all.shape[1]
    conv_all = jnp.concatenate([conv_query, conv_key, conv_value], axis=1)
    dvec = jnp.zeros((8, LANES), f32)
    dvec = dvec.at[0, :heads].set(decay_bias).at[1, :heads].set(-jnp.exp(decay_log))
    map_shape = (heads, key_width, key_width + value_width)

    (pre, conv, gate, small, scal, qkv, inverse, w_part, u_part, starts, drop, block_map) = pl.pallas_call(
        functools.partial(forward_kernel, *sizes, taps),
        grid=(chunks,),
        in_specs=[
            SCALARS, by_rows(model_width), whole((2 * HALO, model_width)),
            whole(w_all.shape), whole(conv_all.shape), whole(dvec.shape),
        ],
        out_specs=[
            by_rows(mixed_width), by_rows(mixed_width), by_rows(vw), by_rows(LANES), by_rows(LANES),
            by_rows(mixed_width),
            by_chunk((heads, BLOCK, BLOCK)), by_chunk((heads, BLOCK, key_width)),
            by_chunk((heads, BLOCK, value_width)), by_chunk(map_shape),
            by_chunk((heads, key_width, key_width)), whole(map_shape),
        ],
        out_shape=[
            struct((seq_rows, mixed_width), f32), struct((seq_rows, mixed_width), f32),
            struct((seq_rows, vw), f32), struct((seq_rows, LANES), f32), struct((seq_rows, LANES), f32),
            struct((seq_rows, mixed_width), bf16),
            struct((chunks, heads, BLOCK, BLOCK), bf16), struct((chunks, heads, BLOCK, key_width), bf16),
            struct((chunks, heads, BLOCK, value_width), f32), struct((chunks,) + map_shape, f32),
            struct((chunks, heads, key_width, key_width), f32), struct(map_shape, f32),
        ],
        scratch_shapes=[pltpu.VMEM((BLOCK + HALO, mixed_width), f32), pltpu.VMEM(map_shape, f32)],
        compiler_params=params(),
        name="mixer_forward",
    )(meta, block_rows, tail, w_all, conv_all, dvec)

    earlier = from_earlier(block_map.astype(bf16), "seq")
    gain_row = head_gain[None, :]
    core, gated, mixed_part, fresh, states = pl.pallas_call(
        functools.partial(output_kernel, *sizes, others),
        grid=(chunks,),
        in_specs=[
            SCALARS, whole(earlier.shape), by_chunk(map_shape), by_chunk((heads, BLOCK, key_width)),
            by_chunk((heads, BLOCK, value_width)), by_rows(mixed_width), by_rows(LANES), by_rows(vw),
            whole(gain_row.shape), whole(w_output.shape),
        ],
        out_specs=[
            by_rows(vw), by_rows(vw), by_rows(model_width), by_chunk((heads, BLOCK, value_width)),
            by_chunk((heads, key_width, value_width)),
        ],
        out_shape=[
            struct((seq_rows, vw), f32), struct((seq_rows, vw), bf16), struct((seq_rows, model_width), bf16),
            struct((chunks, heads, BLOCK, value_width), bf16),
            struct((chunks, heads, key_width, value_width), f32),
        ],
        scratch_shapes=[pltpu.VMEM((heads, key_width, value_width), f32)],
        compiler_params=params(),
        name="mixer_output",
    )(meta, earlier, starts, w_part, u_part, qkv, scal, gate, gain_row, w_output)

    mixer_out = lax.psum_scatter(mixed_part, "head", scatter_dimension=0, tiled=True).astype(f32)
    hidden_in = inputs_f + mixer_out
    normed_two = rms_scale(hidden_in, second_gain).astype(bf16)
    mlp_block = lax.all_gather(normed_two, "seq", axis=0, tiled=True)
    gate_pre = dot(mlp_block, w_gate)
    up_pre = dot(mlp_block, w_up)
    hidden = (jax.nn.silu(gate_pre) * up_pre).astype(bf16)
    mlp_out = lax.psum_scatter(
        dot(hidden, w_down).astype(bf16), "seq", scatter_dimension=0, tiled=True
    ).astype(f32)
    output = (hidden_in + mlp_out).astype(bf16)
    grad_out = cotangent.astype(f32) * own_valid.astype(f32)[:, None]
    grad_low = grad_out.astype(bf16)
    grad_block_two = lax.all_gather(grad_low, "seq", axis=0, tiled=True)
    grad_hidden = dot_nt(grad_block_two, w_down)
    grad_w_down = dot_tn(hidden, grad_block_two)
    grad_gate = (grad_hidden * up_pre * silu_slope(gate_pre)).astype(bf16)
    grad_up = (grad_hidden * jax.nn.silu(gate_pre)).astype(bf16)
    grad_normed_two = lax.psum_scatter(
        (dot_nt(grad_gate, w_gate) + dot_nt(grad_up, w_up)).astype(bf16),
        "seq",
        scatter_dimension=0,
        tiled=True,
    ).astype(f32)
    grad_w_gate = dot_tn(mlp_block, grad_gate)
    grad_w_up = dot_tn(mlp_block, grad_up)
    grad_hidden_norm, grad_second = rms_back(hidden_in, second_gain, grad_normed_two)
    grad_hidden_in = grad_out + grad_hidden_norm
    grad_mix = grad_hidden_in.astype(bf16)
    grad_block = lax.all_gather(grad_mix, "head", axis=0, tiled=True)

    grad_core, inner, pull, grad_gate_pre, grad_head, pulled = pl.pallas_call(
        functools.partial(core_grad_kernel, *sizes, chunks),
        grid=(chunks,),
        in_specs=[
            SCALARS, by_rows(model_width, chunks), whole(w_output.shape), by_rows(vw, chunks), by_rows(vw, chunks),
            whole(gain_row.shape), by_rows(mixed_width, chunks), by_rows(LANES, chunks),
            by_chunk((heads, BLOCK, key_width), chunks), by_chunk((heads, key_width, key_width), chunks),
        ],
        out_specs=[
            by_chunk((heads, BLOCK, value_width), chunks), by_chunk((heads, BLOCK, value_width), chunks),
            by_chunk((heads, key_width, value_width), chunks), by_rows(vw, chunks),
            whole((8, value_width)), whole((heads, key_width, value_width)),
        ],
        out_shape=[
            struct((chunks, heads, BLOCK, value_width), bf16), struct((chunks, heads, BLOCK, value_width), f32),
            struct((chunks, heads, key_width, value_width), f32), struct((seq_rows, vw), bf16),
            struct((8, value_width), f32), struct((heads, key_width, value_width), f32),
        ],
        compiler_params=params(),
        name="mixer_core_grad",
    )(meta, grad_block, w_output, core, gate, gain_row, qkv, scal, w_part, drop)
    grad_w_output = dot_tn(gated, grad_block)

    later = from_later(
        jnp.concatenate([block_map[:, :, :key_width], pulled], axis=2).astype(bf16), "seq"
    )
    grad_conv, grad_small, sums = pl.pallas_call(
        functools.partial(backward_kernel, *sizes, chunks, others),
        grid=(chunks,),
        in_specs=[
            SCALARS, whole(later.shape), by_rows(mixed_width, chunks), by_rows(mixed_width, chunks),
            by_rows(LANES, chunks), by_rows(LANES, chunks), by_chunk((heads, BLOCK, BLOCK), chunks),
            by_chunk((heads, BLOCK, value_width), chunks), by_chunk((heads, key_width, value_width), chunks),
            by_chunk((heads, BLOCK, value_width), chunks), by_chunk((heads, BLOCK, value_width), chunks),
            by_chunk((heads, key_width, value_width), chunks), by_chunk((heads, key_width, key_width), chunks),
            whole(dvec.shape),
        ],
        out_specs=[by_rows(mixed_width, chunks), by_rows(LANES, chunks), whole((8, LANES))],
        out_shape=[
            struct((seq_rows, mixed_width), f32), struct((seq_rows, LANES), bf16), struct((8, LANES), f32),
        ],
        scratch_shapes=[pltpu.VMEM((heads, key_width, value_width), f32)],
        compiler_params=params(),
        name="mixer_backward",
    )(meta, later, qkv, conv, scal, small, inverse, fresh, states, grad_core, inner, pull, drop, dvec)

    edge = from_next(grad_conv[:HALO])
    step_rows = BLOCK // HALO
    last_halo = seq_rows // HALO - 1
    grad_pre, grad_taps, grad_rows = pl.pallas_call(
        functools.partial(projection_grad_kernel, mixed_width, docs, chunks, taps),
        grid=(chunks,),
        in_specs=[
            SCALARS, by_rows(mixed_width),
            pl.BlockSpec(
                (HALO, mixed_width), lambda step: (jnp.minimum((step + 1) * step_rows, last_halo), 0)
            ),
            whole(edge.shape), by_rows(mixed_width), by_rows(vw), by_rows(LANES),
            whole(conv_all.shape), whole(w_all.shape),
        ],
        out_specs=[by_rows(all_width), whole((8, mixed_width)), by_rows(model_width)],
        out_shape=[
            struct((seq_rows, all_width), bf16), struct((8, mixed_width), f32),
            struct((seq_rows, model_width), bf16),
        ],
        scratch_shapes=[pltpu.VMEM((BLOCK + HALO, mixed_width), f32)],
        compiler_params=params(),
        name="projection_grad",
    )(meta, grad_conv, grad_conv, edge, pre, grad_gate_pre, grad_small, conv_all, w_all)

    grad_normed = lax.psum_scatter(grad_rows, "head", scatter_dimension=0, tiled=True).astype(f32)
    grad_input_norm, grad_first = rms_back(inputs_f, first_gain, grad_normed)
    grad_inputs = grad_hidden_in + grad_input_norm
    grad_w_all = dot_tn(block_rows, grad_pre).astype(bf16)

    grad_w_gate, grad_w_up, grad_w_down, first_part, second_part, head_part = (
        lax.psum(grad_w_gate.astype(bf16), "head").astype(f32),
        lax.psum(grad_w_up.astype(bf16), "head").astype(f32),
        lax.psum(grad_w_down.astype(bf16), "head").astype(f32),
        lax.psum(grad_first.astype(bf16), "head").astype(f32),
        lax.psum(grad_second.astype(bf16), "head").astype(f32),
        lax.psum(grad_head[0].astype(bf16), "head").astype(f32),
    )
    grad_w_all, grad_w_output, grad_taps, sums, first_part, second_part, head_part = (
        lax.psum(part.astype(bf16), "seq").astype(f32)
        for part in (
            grad_w_all, grad_w_output, grad_taps[:taps], sums[:2, :heads], first_part, second_part, head_part,
        )
    )
    gate_at = mixed_width
    small_at = mixed_width + vw
    return (
        output,
        grad_inputs,
        first_part,
        grad_w_all[:, :qw],
        grad_w_all[:, qw : 2 * qw],
        grad_w_all[:, 2 * qw : gate_at],
        grad_w_all[:, gate_at:small_at],
        grad_w_all[:, small_at : small_at + heads],
        grad_w_all[:, small_at + heads : small_at + 2 * heads],
        grad_taps[:, :qw],
        grad_taps[:, qw : 2 * qw],
        grad_taps[:, 2 * qw :],
        sums[1],
        sums[0],
        head_part,
        grad_w_output,
        second_part,
        grad_w_gate,
        grad_w_up,
        grad_w_down,
    )


def from_previous(array):
    devices = lax.axis_size("seq")
    return lax.ppermute(array, "seq", [(i, i + 1) for i in range(devices - 1)])


def from_next(array):
    devices = lax.axis_size("seq")
    return lax.ppermute(array, "seq", [(i + 1, i) for i in range(devices - 1)])


def solution(mesh):
    in_specs = (
        P(("seq", "head"), None),
        P(),
        P(),
        P(None, "head"),
        P(None, "head"),
        P(None, "head"),
        P(None, "head"),
        P(None, "head"),
        P(None, "head"),
        P(None, "head"),
        P(None, "head"),
        P(None, "head"),
        P("head"),
        P("head"),
        P(),
        P("head", None),
        P(),
        P(None, "seq"),
        P(None, "seq"),
        P("seq", None),
        P(("seq", "head"), None),
    )
    out_specs = (
        P(("seq", "head"), None),
        P(("seq", "head"), None),
        P(),
        P(None, "head"),
        P(None, "head"),
        P(None, "head"),
        P(None, "head"),
        P(None, "head"),
        P(None, "head"),
        P(None, "head"),
        P(None, "head"),
        P(None, "head"),
        P("head"),
        P("head"),
        P(),
        P("head", None),
        P(),
        P(None, "seq"),
        P(None, "seq"),
        P("seq", None),
    )
    return jax.shard_map(shards, mesh=mesh, in_specs=in_specs, out_specs=out_specs, check_vma=False)
```

time: 2470 us -> 1320 us (0.53)
  matrix products: 827 us -> 129 us
  local copies, waits for them, and re-layouts: 436 us -> 35.8 us
  other arithmetic: 313 us -> 54.1 us
  waiting for transfers between devices: 673 us -> 850 us
  Pallas kernels: 0 us -> 176 us
  loops' own time: 67.3 us -> 0 us
  blocking collectives: 91.4 us -> 33.7 us
    dot_general x528 -> x11, matrix products: 788 us -> 129 us  [the longest x5 58.3 us: dot_tn(): lax.dot_general(left, right, (((0,), (0,)), ((), ())), preferred_element_...]
    pallas_call x0 -> x5, Pallas kernels: none -> 176 us  [the longest x1 77.7 us: shards(): pl.pallas_call(functools.partial(forward_kernel, *sizes, taps), grid=(chu...]
    psum x2, waiting for transfers between devices: 196 us -> 370 us  [the longest x1 290 us: shards(): lax.psum(part.astype(bf16), 'seq').astype(f32)]
    squeeze x192 -> x1, local copies, waits for them, and re-layouts: 146 us -> 0.52 us  [shards(): sums[0]]
    another operation x10 -> x7, other arithmetic: 147 us -> 2.97 us  [the longest x2 141 us: group_parts(): jax.scipy.linalg.solve_triangular(system, strength[:, None] * values, low...]
    dynamic_slice x160 -> x0, local copies, waits for them, and re-layouts: 86.1 us -> none  [one_head(): lax.scan(stepper, state_h, (weights_w, values_u, scores, scaled_queries,...]
    another operation x5 -> x0, loops' own time: 67.3 us -> none  [the longest x3 66.7 us: one_head(): lax.scan(stepper, state_h, (weights_w, values_u, scores, scaled_queries,...]
    all_gather x4 -> x0, blocking collectives: 58.8 us -> none  [prefix(): lax.all_gather(part.astype(kind), axis)]
  transfers between devices with their start and end apart: 16 -> 18, of which waited for: 8 -> 15; matrix products, arithmetic and copies ran while one was open for 49% -> 12% of each run, Pallas kernels for 0% -> 6%
where the time goes in v1:
time: 1320 us; the launch traced here: 1310 us
  waiting for transfers between devices  850 us (64%)
  Pallas kernels  176 us (13%)
  matrix products  129 us (10%)
  other arithmetic  54.1 us (4%)
  local copies, waits for them, and re-layouts  35.8 us (3%)
  blocking collectives  33.7 us (3%)
  starting transfers between devices  19.2 us (1%)
  between operations  15.1 us (1%)
    psum x1, waiting for transfers between devices, shards(): lax.psum(part.astype(bf16), 'seq').astype(f32)  290 us
    psum x1, waiting for transfers between devices, shards(): lax.psum(grad_w_gate.astype(bf16), 'head').astype(f32)  79.9 us
    all_gather x1, waiting for transfers between devices, shards(): mlp_block = lax.all_gather(normed_two, 'seq', axis=0, tiled=True)  78.9 us
    pallas_call x1, Pallas kernels, shards(): pl.pallas_call(functools.partial(forward_kernel, *sizes, taps), grid=(chu...  77.7 us
    reduce_scatter x1, waiting for transfers between devices, shards(): lax.psum_scatter(mixed_part, 'head', scatter_dimension=0, tiled=True)  76.5 us
    reduce_scatter x1, waiting for transfers between devices, shards(): lax.psum_scatter((dot_nt(grad_gate, w_gate) + dot_nt(grad_up, w_up)).asty...  75.4 us
    all_gather x1, waiting for transfers between devices, shards(): grad_block_two = lax.all_gather(grad_low, 'seq', axis=0, tiled=True)  58.7 us
    dot_general x5, matrix products, dot_tn(): lax.dot_general(left, right, (((0,), (0,)), ((), ())), preferred_element_...  58.3 us
  transfers between devices with their start and end apart: 18, of which 15 were waited for; matrix products, arithmetic and copies ran while one was open for 12% of the time, Pallas kernels for 6%

profile of v1, /device:TPU:0, one launch (start us, length us, event | category | flops | bytes accessed | tf_op | source)
XLA Modules:
  0.0 1313.1 jit_solution(1437458928445481408)
XLA Ops:
  10.1 2.5 fusion.13
  14.7 11.0 concatenate.18.w_ref
  25.7 44.2 %all-gather.5.cloned.1.call-done.rows_ref = bf16[2048,2048]{1,0:T(8,128)(2,1)} async-done(((bf16[256,2048]{1,0:T(8,128)(2,1)}), bf16[2048,2048]{1,0:T(8,128)(2,1)}) %all-gather.5.cloned.1.call-update) | async-done | bytes 8388624 | tf_op jit(solution)/shard_map/all_gather | solution.py:553
  70.7 3.4 collective-permute-start
  76.6 77.7 %mixer_forward.1 = (f32[2048,1024]{1,0:T(8,128)}, f32[2048,1024]{1,0:T(8,128)}, f32[2048,512]{1,0:T(8,128)}, f32[2048,128]{1,0:T(8,128)}, f32[2048,128]{1,0:T(8,...) custom-call(s32[4]{0:T(128)} %pad_add_fusion.meta, ...), custom_call_target="tpu_custom_call" | custom-call | tf_op jit(solution)/shard_map/mixer_forward/pallas_call | solution.py:573
  155.3 4.3 collective-permute-start.3
  159.6 4.3 collective-permute-start.2
  165.3 4.0 collective-permute-done.2
  169.3 2.2 collective-permute-done.1
  172.4 19.8 %mixer_output.1 = (f32[2048,512]{1,0:T(8,128)}, bf16[2048,512]{1,0:T(8,128)(2,1)}, bf16[2048,2048]{1,0:T(8,128)(2,1)}, bf16[8,2,256,256]{3,2,1,0:T(8,128)(2,1)}, f32[8,2,128,256]{3,2,1,0:T(8,128)}) custom-call(s32[4]{0:T(128)} %pad_add_fusion.meta, bf16[3,2,128,384]{3,2,1,0:T(8,128)(2,1)} %pad_maximum_fusion.maps_ref, ...), custom_call_target="tpu_custom_call" | custom-call | tf_op jit(solution)/shard_map/mixer_output/pallas_call | solution.py:602
  192.3 76.5 %reduce-scatter.5.cloned.1.call-done = bf16[256,2048]{1,0:T(8,128)(2,1)} async-done(((bf16[2048,2048]{1,0:T(8,128)(2,1)}), bf16[256,2048]{1,0:T(8,128)(2,1)}) %reduce-scatter.5.cloned.1.call-update) | async-done | bytes 1048592 | tf_op jit(solution)/shard_map/reduce_scatter | solution.py:624
  270.5 2.6 multiply_convert_fusion.3
  275.0 78.9 %all-gather.7.cloned.1.call-done = bf16[1024,2048]{1,0:T(8,128)(2,1)} async-done(((bf16[256,2048]{1,0:T(8,128)(2,1)}), bf16[1024,2048]{1,0:T(8,128)(2,1)}) %all-gather.7.cloned.1.call-update) | async-done | bytes 4194320 | tf_op jit(solution)/shard_map/all_gather | solution.py:627
  354.0 11.8 fusion.27
  365.8 10.3 fusion.28
  376.1 58.7 %all-gather.9.cloned.1.call-done = bf16[1024,2048]{1,0:T(8,128)(2,1)} async-done(((bf16[256,2048]{1,0:T(8,128)(2,1)}), bf16[1024,2048]{1,0:T(8,128)(2,1)}) %all-gather.9.cloned.1.call-update) | async-done | bytes 4194320 | tf_op jit(solution)/shard_map/all_gather | solution.py:637
  434.8 15.5 %multiply_convert_fusion = (bf16[1024,1408]{1,0:T(8,128)(2,1)S(1)}, bf16[1024,1408]{1,0:T(8,128)(2,1)S(1)}, bf16[1024,1408]{1,0:T(8,128)(2,1)}) fusion(f32[1024,1408]{1,0:T(8,128)} %fusion.27, f32[1024,1408]{1,0:T(8,128)} %fusion.28, bf16[1024,2048]{1,0:T(8,128)(2,1)} %all-gather.9.cloned.1.call-done, bf16[1408,2048]{1,0:T(8,128)(2,1)} %param.44), kind=kOutput, calls=%fused_computation.5 | convolution fusion | flops 5927206912 | bytes 30146560 | tf_op jit(solution)/shard_map/dot_general | solution.py:30
  450.3 10.8 fusion.29
  461.2 11.0 add_convert_fusion
  472.2 75.4 %reduce-scatter.9.cloned.1.call-done = bf16[256,2048]{1,0:T(8,128)(2,1)} async-done(((bf16[1024,2048]{1,0:T(8,128)(2,1)}), bf16[256,2048]{1,0:T(8,128)(2,1)}) %reduce-scatter.9.cloned.1.call-update) | async-done | bytes 1048592 | tf_op jit(solution)/shard_map/reduce_scatter | solution.py:642
  549.7 3.1 fusion.22
  552.9 10.8 convolution_convert_fusion
  563.8 8.7 convolution_convert_fusion.2
  572.4 8.6 convolution_convert_fusion.1
  581.1 26.7 %all-gather.11.cloned.1.call-done.grad_ref = bf16[2048,2048]{1,0:T(8,128)(2,1)} async-done(((bf16[256,2048]{1,0:T(8,128)(2,1)}), bf16[2048,2048]{1,0:T(8,128)(2,1)}) %all-gather.11.cloned.1.call-update) | async-done | bytes 8388624 | tf_op jit(solution)/shard_map/all_gather | solution.py:653
  607.9 20.6 %mixer_core_grad.1 = (bf16[8,2,256,256]{3,2,1,0:T(8,128)(2,1)}, f32[8,2,256,256]{3,2,1,0:T(8,128)}, f32[8,2,128,256]{3,2,1,0:T(8,128)}, bf16[2048,512]{1,0:T(8,1...) custom-call(s32[4]{0:T(128)} %pad_add_fusion.meta, bf16[2048,2048]{1,0:T(8,128)(2,1)} %all-gather.11.cloned.1.call-done.grad_ref, ...), custom_call_target="tpu_custom_call" | custom-call | tf_op jit(solution)/shard_map/mixer_core_grad/pallas_call | solution.py:655
  633.4 5.1 collective-permute-done.6
  638.6 13.5 %collective-permute-done.5 = bf16[2,128,384]{2,1,0:T(8,128)(2,1)S(1)} collective-permute-done((bf16[2,128,384]{2,1,0:T(8,128)(2,1)S(1)}, bf16[2,128,384]{2,1,0:T(8,128)(2,1)S(1)}, u32[]{:S(2)}, u32[]{:S(2)}) %collective-permute-start.5) | collective-permute-done | bytes 196640 | tf_op jit(solution)/shard_map/ppermute | solution.py:507
  653.0 26.2 %mixer_backward.1 = (f32[2048,1024]{1,0:T(8,128)}, bf16[2048,128]{1,0:T(8,128)(2,1)}, f32[8,128]{1,0:T(8,128)}) custom-call(s32[4]{0:T(128)} %pad_add_fusion.meta, bf16[3,2,128,384]{3,2,1,0:T(8,128)(2,1)} %pad_maximum_fusion.1.maps_ref, bf16[2048,1024]{1,0:T(8,128)(2,1)} %get-tuple-element.77.qkv_ref, f32[2048,1024]{1,0:T(8,128)} %get-tuple-element.84.act_ref, ...), custom_call_target="tpu_custom_call" | custom-call | tf_op jit(solution)/shard_map/mixer_backward/pallas_call | solution.py:681
  681.3 9.2 convolution_convert_fusion.5
  691.1 31.5 %projection_grad.1 = (bf16[2048,1664]{1,0:T(8,128)(2,1)}, f32[8,1024]{1,0:T(8,128)}, bf16[2048,2048]{1,0:T(8,128)(2,1)}) custom-call(s32[4]{0:T(128)} %pad_add_fusion.meta, f32[2048,1024]{1,0:T(8,128)} %get-tuple-element.92.grad_conv_ref.later_ref, f32[2048,1024]{1,0:T(8,128)} %get-tuple-element.92.grad_conv_ref.later_ref, f32[8,1024]{1,0:T(8,128)} %copy-done.11, ...), custom_call_target="tpu_custom_call" | custom-call | tf_op jit(solution)/shard_map/projection_grad/pallas_call | solution.py:704
  722.5 21.0 %convolution_convert_fusion.3 = bf16[2048,1664]{1,0:T(8,128)(2,1)} fusion(bf16[2048,2048]{1,0:T(8,128)(2,1)} %all-gather.5.cloned.1.call-done.rows_ref, bf16[2048,1664]{1,0:T(8,128)(2,1)} %get-tuple-element.97), kind=kOutput, calls=%fused_computation.4 | convolution fusion | flops 13962051584 | bytes 22020096 | tf_op jit(solution)/shard_map/dot_general | solution.py:26
  744.3 11.3 convolution_convert_fusion.4
  755.6 79.9 %all-reduce.8.cloned.1.call-done = (bf16[2048,1408]{1,0:T(8,128)(2,1)}, bf16[2048,1408]{1,0:T(8,128)(2,1)}, bf16[1408,2048]{1,0:T(8,128)(2,1)}) async-done(((bf16[2048,1408]{1,0:T(8,128)(2,1)}, bf16[2048,1408]{1,0:T(8,128)(2,1)}, bf16[1408,2048]{1,0:T(8,128)(2,1)}), (bf16[2048,1408]{1,0:T(8,128)(2,1)}, bf16[2048,1408]{1,0:T(8,128)(2,1)}, bf16[1408,2048]{1,0:T(8,128)(2,1)})) %all-reduce.8.cloned.1.call-update) | async-done | bytes 17301520 | tf_op jit(solution)/shard_map/psum | solution.py:731
  835.5 9.4 convert_element_type.158
  844.9 5.2 convert_element_type.160
  850.1 6.0 convert_element_type.162
  857.6 289.7 %all-reduce.10.cloned.1.call-done = (bf16[2048,1664]{1,0:T(8,128)(2,1)}, bf16[512,2048]{1,0:T(8,128)(2,1)}) async-done(((bf16[2048,1664]{1,0:T(8,128)(2,1)}, bf16[512,2048]{1,0:T(8,128)(2,1)}), (bf16[2048,1664]{1,0:T(8,128)(2,1)}, bf16[512,2048]{1,0:T(8,128)(2,1)})) %all-reduce.10.cloned.1.call-update) | async-done | bytes 8912912 | tf_op jit(solution)/shard_map/psum | solution.py:739
  1147.3 2.8 fusion.23
  1150.1 2.2 copy.47
  1154.4 5.1 convert_element_type.154
  1159.5 4.7 fusion.25
  1164.2 4.5 fusion.24
  1168.7 52.4 %reduce-scatter.11.cloned.1.call-done = bf16[256,2048]{1,0:T(8,128)(2,1)} async-done(((bf16[2048,2048]{1,0:T(8,128)(2,1)}), bf16[256,2048]{1,0:T(8,128)(2,1)}) %reduce-scatter.11.cloned.1.call-update) | async-done | bytes 1048592 | tf_op jit(solution)/shard_map/reduce_scatter | solution.py:725
  1222.9 13.3 %all-reduce.1 = (bf16[2048]{0:T(1024)(128)(2,1)S(1)}, bf16[256]{0:T(256)(128)(2,1)S(1)}, bf16[2048]{0:T(1024)(128)(2,1)S(1)}) all-reduce(bf16[2048]{0:T(1024)(128)(2,1)S(1)} %get-tuple-element.144, bf16[256]{0:T(256)(128)(2,1)S(1)} %fusion.20, bf16[2048]{0:T(1024)(128)(2,1)S(1)} %get-tuple-element.142), channel_id=1, replica_groups=mesh['seq'=4,'head'=8] {'head'}, use_global_device_ids=true, to_apply=%region_13.14 | all-reduce | flops 4352 | bytes 17408 | tf_op jit(solution)/shard_map/psum | solution.py:734
  1236.2 20.4 %all-reduce.3 = (bf16[4,1024]{1,0:T(4,128)(2,1)S(1)}, bf16[2048]{0:T(1024)(128)(2,1)S(1)}, bf16[2,2]{1,0:T(2,128)(2,1)S(1)}, bf16[256]{0:T(256)(128)(2,1)S(1)}, bf16[2048]{0:T(1024)(128)(2,1)S(1)}) all-reduce(bf16[4,1024]{1,0:T(4,128)(2,1)S(1)} %slice.130, ...), channel_id=1, replica_groups=mesh['seq'=4,'head'=8] {'seq'}, use_global_device_ids=true, to_apply=%region_16.17 | all-reduce | flops 8452 | bytes 33808 | tf_op jit(solution)/shard_map/psum | solution.py:739
  1260.1 41.0 %reduce-scatter.7.cloned.1.call-done = bf16[256,2048]{1,0:T(8,128)(2,1)} async-done(((bf16[1024,2048]{1,0:T(8,128)(2,1)}), bf16[256,2048]{1,0:T(8,128)(2,1)}) %reduce-scatter.7.cloned.1.call-update) | async-done | bytes 1048592 | tf_op jit(solution)/shard_map/reduce_scatter | solution.py:631
  1301.1 4.7 fusion.5
  (148 shorter events, 35.6 us)
Async XLA Ops:
  7.2 5.5 copy-start.14
  7.2 5.8 copy-start.15
  7.2 6.1 copy-start.22
  7.2 6.3 copy-start.21
  7.2 6.3 copy-start.26
  7.2 7.4 copy-start.5
  7.3 62.6 %all-gather.5.cloned.1.call-start = ((), (), s32[]{:S(2)}) async-start(), calls=%async_computation.4 | async-start | bytes 9437184 | tf_op jit(solution)/shard_map/all_gather | solution.py:553
  12.6 256.2 %reduce-scatter.5.cloned.1.call-start = ((), (), s32[]{:S(2)}) async-start(), calls=%async_computation.5 | async-start | bytes 9437184 | tf_op jit(solution)/shard_map/reduce_scatter | solution.py:624
  13.8 11.9 copy-start.10
  14.6 11.0 copy-start.19
  14.6 11.0 copy-start.20
  14.6 11.0 copy-start.16
  25.7 50.3 %copy-start.7 = (f32[4,1024]{1,0:T(4,128)}, f32[4,1024]{1,0:T(4,128)S(1)}, u32[]{:S(2)}) copy-start(f32[4,1024]{1,0:T(4,128)S(1)} %constant_dynamic-update-slice_fusion.conv_ref) | copy-start | bytes 49156
  70.7 5.3 collective-permute-start
  155.3 9.9 collective-permute-start.3
  159.6 9.7 collective-permute-start.2
  163.9 7.6 collective-permute-start.1
  192.2 76.6 %copy-start = (bf16[256,2048]{1,0:T(8,128)(2,1)S(1)}, bf16[256,2048]{1,0:T(8,128)(2,1)}, u32[]{:S(2)}) copy-start(bf16[256,2048]{1,0:T(8,128)(2,1)} %param.25) | copy-start | bytes 3145732
  192.2 78.3 %copy-start.6 = (f32[2048]{0:T(1024)S(1)}, f32[2048]{0:T(1024)}, u32[]{:S(2)}) copy-start(f32[2048]{0:T(1024)} %param.41) | copy-start | bytes 24580
  192.2 81.2 %copy-start.3 = (bf16[256,2048]{1,0:T(8,128)(2,1)S(1)}, bf16[256,2048]{1,0:T(8,128)(2,1)}, u32[]{:S(2)}) copy-start(bf16[256,2048]{1,0:T(8,128)(2,1)} %param.45) | copy-start | bytes 3145732
  192.2 161.7 %all-gather.7.cloned.1.call-start = ((), (), s32[]{:S(2)}) async-start(), calls=%async_computation.6 | async-start | bytes 5242880 | tf_op jit(solution)/shard_map/all_gather | solution.py:627
  273.1 161.7 %all-gather.9.cloned.1.call-start = ((), (), s32[]{:S(2)}) async-start(), calls=%async_computation.8 | async-start | bytes 5242880 | tf_op jit(solution)/shard_map/all_gather | solution.py:637
  274.6 273.0 %reduce-scatter.9.cloned.1.call-start = ((), (), s32[]{:S(2)}) async-start(), calls=%async_computation.9 | async-start | bytes 5242880 | tf_op jit(solution)/shard_map/reduce_scatter | solution.py:642
  354.0 11.8 copy-start.23
  450.3 10.8 copy-start.27
  450.3 10.8 copy-start.29
  472.2 75.5 %copy-start.1 = (bf16[256,2048]{1,0:T(8,128)(2,1)S(1)}, bf16[256,2048]{1,0:T(8,128)(2,1)}, u32[]{:S(2)}) copy-start(bf16[256,2048]{1,0:T(8,128)(2,1)} %reduce-scatter.5.cloned.1.call-done) | copy-start | bytes 3145732
  472.2 135.7 %all-gather.11.cloned.1.call-start = ((), (), s32[]{:S(2)}) async-start(), calls=%async_computation.10 | async-start | bytes 9437184 | tf_op jit(solution)/shard_map/all_gather | solution.py:653
  552.9 282.7 %all-reduce.8.cloned.1.call-start = ((), (), s32[]{:S(2)}) async-start(), calls=%async_computation.12 | async-start | bytes 34603008 | tf_op jit(solution)/shard_map/psum | solution.py:731
  552.9 10.8 copy-start.24
  552.9 10.8 copy-start.28
  563.7 8.7 copy-start.30
  581.1 566.2 %all-reduce.10.cloned.1.call-start = ((), (), s32[]{:S(2)}) async-start(), calls=%async_computation.13 | async-start | bytes 17825792 | tf_op jit(solution)/shard_map/psum | solution.py:739
  629.5 9.0 collective-permute-start.6
  630.8 21.2 %collective-permute-start.5 = (bf16[2,128,384]{2,1,0:T(8,128)(2,1)S(1)}, bf16[2,128,384]{2,1,0:T(8,128)(2,1)S(1)}, u32[]{:S(2)}, u32[]{:S(2)}) collective-permute-start(bf16[2,128,384]{2,1,0:T(8,128)(2,1)S(1)} %pad_maximum_fusion.2), channel_id=1, source_target_pairs={{16,0},{24,8},{17,1},{25,9},{18,2},{26,10},{19,3},{27,11},{20,4},{... | collective-permute-start | bytes 589832 | tf_op jit(solution)/shard_map/ppermute | solution.py:507
  632.1 19.9 %collective-permute-start.4 = (bf16[2,128,384]{2,1,0:T(8,128)(2,1)S(1)}, bf16[2,128,384]{2,1,0:T(8,128)(2,1)S(1)}, u32[]{:S(2)}, u32[]{:S(2)}) collective-permute-start(bf16[2,128,384]{2,1,0:T(8,128)(2,1)S(1)} %pad_maximum_fusion.2), channel_id=1, source_target_pairs={{24,0},{25,1},{26,2},{27,3},{28,4},{29,5},{30,6},{31,7}} | collective-permute-start | bytes 589832 | tf_op jit(solution)/shard_map/ppermute | solution.py:507
  653.0 28.3 %copy-start.25 = (bf16[2048,512]{1,0:T(8,128)(2,1)S(1)}, bf16[2048,512]{1,0:T(8,128)(2,1)}, u32[]{:S(2)}) copy-start(bf16[2048,512]{1,0:T(8,128)(2,1)} %get-tuple-element.101) | copy-start | bytes 6291460
  680.0 10.5 collective-permute-start.7
  743.5 477.5 %reduce-scatter.11.cloned.1.call-start = ((), (), s32[]{:S(2)}) async-start(), calls=%async_computation.11 | async-start | bytes 9437184 | tf_op jit(solution)/shard_map/reduce_scatter | solution.py:725
  744.3 556.9 %reduce-scatter.7.cloned.1.call-start = ((), (), s32[]{:S(2)}) async-start(), calls=%async_computation.7 | async-start | bytes 5242880 | tf_op jit(solution)/shard_map/reduce_scatter | solution.py:631
  835.5 9.4 copy-start.4
  835.5 14.6 %slice-start.2 = ((s8[5767168]{0:T(1024)(128)(4,1)}), s8[4194304]{0:T(1024)(128)(4,1)S(1)}, s32[]{:S(2)}) async-start(s8[5767168]{0:T(1024)(128)(4,1)} %bitcast.43), calls=%async_computation.16 | async-start | bytes 8388608
  844.9 5.2 slice-start.3
  850.1 6.7 copy-start.18
  1154.4 9.7 slice-start
  1164.1 56.9 %copy-start.8 = (f32[2048]{0:T(1024)S(1)}, f32[2048]{0:T(1024)}, u32[]{:S(2)}) copy-start(f32[2048]{0:T(1024)} %param.27) | copy-start | bytes 24580
  1164.2 56.9 %copy-start.13 = (f32[256]{0:T(256)S(1)}, f32[256]{0:T(256)}, u32[]{:S(2)}) copy-start(f32[256]{0:T(256)} %copy-done.12) | copy-start | bytes 3076
  1164.2 137.0 %copy-start.17 = (f32[256]{0:T(256)S(1)}, f32[256]{0:T(256)}, u32[]{:S(2)}) copy-start(f32[256]{0:T(256)} %get-tuple-element.176) | copy-start | bytes 3076
  (5 other events, 8.5 us)
Sparse Core Ops, SparseCore 0:
  12.8 57.0 all-gather.4
  192.3 76.4 reduce-scatter.4
  273.2 80.7 all-gather.6
  355.5 79.2 all-gather.8
  472.3 75.2 reduce-scatter.8
  553.0 54.8 all-gather.10
  612.1 223.4 all-reduce.7
  838.7 308.5 all-reduce.9
  1150.8 70.2 reduce-scatter.10
  1223.3 77.7 reduce-scatter.6

commit v2 on v1

--- a/solution.py
+++ b/solution.py
@@ -158,21 +158,35 @@
 
 
 def forward_kernel(
-    heads, key_width, value_width, docs, taps,
-    meta, rows_ref, tail_ref, w_ref, conv_ref, dvec_ref,
-    pre_ref, act_ref, gate_ref, small_ref, scal_ref, qkv_ref, inv_ref, w_out_ref, u_ref, starts_ref, drop_ref, map_ref,
-    ext, state,
+    heads, key_width, value_width, docs, taps, chunks,
+    meta, rows_ref, tail_ref, wq_ref, wk_ref, wv_ref, wg_ref, ws_ref, conv_ref, dvec_ref, block_ref,
+    pre_ref, act_ref, gate_ref, small_ref, scal_ref, qkv_ref, inv_ref, w_out_ref, u_ref, starts_ref, drop_ref, map_ref, blocks_ref,
+    ext, state, own_sem, send_sem, recv_sem,
 ):
     chunk = pl.program_id(0)
+    gather = LineGather("seq", block_ref, blocks_ref, own_sem, send_sem, recv_sem)
+
+    @pl.when(chunk == 0)
+    def _():
+        gather.enter()
+        gather.advance(0)
+
+    for hop in range(1, gather.devices):
+        @pl.when(chunk == min(hop * chunks // gather.devices + 1, chunks - 1))
+        def _():
+            gather.advance(hop)
+
     qw, vw = heads * key_width, heads * value_width
     mixed = 2 * qw + vw
     masks = Masks(meta, docs, chunk)
     rows = rows_ref[...]
+    mixed_weights = ((slice(0, qw), wq_ref), (slice(qw, 2 * qw), wk_ref), (slice(2 * qw, mixed), wv_ref))
 
     @pl.when(chunk == 0)
     def _():
-        halo = dot(tail_ref[...], w_ref[:, :mixed])
-        ext[0:HALO, :] = halo[HALO : 2 * HALO, :]
+        for span, ref in mixed_weights:
+            ext[0:HALO, span] = dot(tail_ref[...], ref[...])[HALO : 2 * HALO, :]
+
         ident = jnp.where(
             lax.broadcasted_iota(jnp.int32, (key_width, key_width + value_width), 0)
             == lax.broadcasted_iota(jnp.int32, (key_width, key_width + value_width), 1),
@@ -185,11 +199,12 @@
     def _():
         ext[0:HALO, :] = ext[BLOCK : BLOCK + HALO, :]
 
-    pre = dot(rows, w_ref[...])
-    ext[HALO : HALO + BLOCK, :] = pre[:, :mixed]
-    pre_ref[...] = pre[:, :mixed]
-    gate_ref[...] = pre[:, mixed : mixed + vw]
-    small = pre[:, mixed + vw :]
+    for span, ref in mixed_weights:
+        pre = dot(rows, ref[...])
+        ext[HALO : HALO + BLOCK, span] = pre
+        pre_ref[:, span] = pre
+    gate_ref[...] = dot(rows, wg_ref[...])
+    small = dot(rows, ws_ref[...])
     small_ref[...] = small
 
     conv = jnp.zeros((BLOCK, mixed), f32)
@@ -237,6 +252,10 @@
         after = after + jnp.concatenate([jnp.zeros((key_width, key_width), f32), added], axis=1)
         state[head] = after
         map_ref[head] = after
+
+    @pl.when(chunk == chunks - 1)
+    def _():
+        gather.leave()
 
 
 def output_kernel(
@@ -428,8 +447,9 @@
 
 def projection_grad_kernel(
     mixed, docs, chunks, taps,
-    meta, grad_conv_ref, later_ref, edge_ref, pre_ref, grad_gate_ref, grad_small_ref, conv_ref, w_ref,
-    grad_pre_ref, grad_taps_ref, grad_rows_ref,
+    meta, grad_conv_ref, later_ref, edge_ref, pre_ref, grad_gate_ref, grad_small_ref, conv_ref, rows_ref,
+    wq_ref, wk_ref, wv_ref, wg_ref, ws_ref,
+    grad_pre_ref, grad_taps_ref, grad_rows_ref, gain_sum_ref,
     ext,
 ):
     chunk = pl.program_id(0)
@@ -437,6 +457,7 @@
     @pl.when(chunk == 0)
     def _():
         grad_taps_ref[...] = jnp.zeros_like(grad_taps_ref)
+        gain_sum_ref[...] = jnp.zeros_like(gain_sum_ref)
 
     ext[0:BLOCK, :] = grad_conv_ref[...]
 
@@ -460,7 +481,240 @@
     grad_pre_ref[:, :mixed] = total.astype(bf16)
     grad_pre_ref[:, mixed : mixed + width] = grad_gate_ref[...]
     grad_pre_ref[:, mixed + width :] = grad_small_ref[...]
-    grad_rows_ref[...] = dot_nt(grad_pre_ref[...], w_ref[...]).astype(bf16)
+    grad = jnp.zeros(grad_rows_ref.shape, f32)
+    begin = 0
+    for ref in (wq_ref, wk_ref, wv_ref, wg_ref, ws_ref):
+        grad = grad + dot_nt(grad_pre_ref[:, begin : begin + ref.shape[1]], ref[...])
+        begin += ref.shape[1]
+    grad_rows_ref[...] = grad.astype(bf16)
+    gain_sum_ref[0:1, :] += jnp.sum(grad * rows_ref[...].astype(f32), axis=0, keepdims=True)
+
+
+MESH = pl.DeviceIdType.MESH
+ANYWHERE = pl.BlockSpec(memory_space=pl.ANY)
+
+
+def line_barrier(axis):
+    devices, place = lax.axis_size(axis), lax.axis_index(axis)
+    barrier = pltpu.get_barrier_semaphore()
+
+    @pl.when(place > 0)
+    def _():
+        pl.semaphore_signal(barrier, inc=1, device_id={axis: place - 1}, device_id_type=MESH)
+
+    @pl.when(place < devices - 1)
+    def _():
+        pl.semaphore_signal(barrier, inc=1, device_id={axis: place + 1}, device_id_type=MESH)
+
+    @pl.when((place > 0) & (place < devices - 1))
+    def _():
+        pl.semaphore_wait(barrier, 2)
+
+    @pl.when((place == 0) | (place == devices - 1))
+    def _():
+        pl.semaphore_wait(barrier, 1)
+
+
+def line_sum_kernel(axis, counts, depths, *refs):
+    total = len(counts)
+    parts, sums = refs[:total], refs[total : 2 * total]
+    arrived, passed = refs[2 * total : 3 * total], refs[3 * total : 4 * total]
+    semaphores = refs[4 * total :]
+    devices = lax.axis_size(axis)
+    place = lax.axis_index(axis)
+
+    line_barrier(axis)
+
+    def rows_of(index, half, at):
+        return pl.ds(pl.multiple_of((half * counts[index] + at) * depths[index], depths[index]), depths[index])
+
+    def copy(index, half, at, target, back):
+        rows = rows_of(index, half, at)
+        slot = half * counts[index] + at
+        sent = semaphores[4 * index + 2 * back].at[slot]
+        received = semaphores[4 * index + 2 * back + 1].at[slot]
+        source, landing = (sums, sums) if back else (passed, arrived)
+        return pltpu.make_async_remote_copy(
+            source[index].at[rows, :], landing[index].at[rows, :], sent, received,
+            device_id={axis: target}, device_id_type=MESH,
+        )
+
+    def each(step, handle):
+        for half in range(2):
+            first, last = (devices - 1, 0) if half == 0 else (0, devices - 1)
+            toward = place - 1 if half == 0 else place + 1
+            away = place + 1 if half == 0 else place - 1
+            for index in range(total):
+                handle(half, index, step, toward, away, place == first, place == last)
+
+    steps = max(counts)
+    skew = 2
+    window = 2
+
+    def send(half, index, at, target, back):
+        @pl.when(at >= window)
+        def _():
+            copy(index, half, at - window, target, back).wait_send()
+
+        copy(index, half, at, target, back).start()
+
+    def reduce_step(step, carry):
+        def handle(half, index, step, toward, away, begin, end):
+            at = step - skew * ((devices - 1 - place) if half == 0 else place)
+
+            @pl.when((at >= 0) & (at < counts[index]))
+            def _():
+                rows = rows_of(index, half, at)
+
+                @pl.when(begin)
+                def _():
+                    passed[index][rows, :] = parts[index][rows, :]
+                    send(half, index, at, toward, 0)
+
+                @pl.when(jnp.logical_not(begin))
+                def _():
+                    copy(index, half, at, toward, 0).wait_recv()
+                    added = (parts[index][rows, :].astype(f32) + arrived[index][rows, :].astype(f32)).astype(bf16)
+
+                    @pl.when(jnp.logical_not(end))
+                    def _():
+                        passed[index][rows, :] = added
+                        send(half, index, at, toward, 0)
+
+                    @pl.when(end)
+                    def _():
+                        sums[index][rows, :] = added
+
+        each(step, handle)
+        return carry
+
+    lax.fori_loop(0, steps + skew * (devices - 1), reduce_step, 0)
+
+    def back_step(step, carry):
+        def handle(half, index, step, toward, away, begin, end):
+            at = step - skew * (place if half == 0 else (devices - 1 - place))
+
+            @pl.when((at >= 0) & (at < counts[index]))
+            def _():
+                @pl.when(jnp.logical_not(end))
+                def _():
+                    copy(index, half, at, away, 1).wait_recv()
+
+                @pl.when(jnp.logical_not(begin))
+                def _():
+                    send(half, index, at, away, 1)
+
+        each(step, handle)
+        return carry
+
+    lax.fori_loop(0, steps + skew * (devices - 1), back_step, 0)
+
+    def last_step(step, carry):
+        def handle(half, index, step, toward, away, begin, end):
+            at = counts[index] - min(window, counts[index]) + step
+
+            @pl.when(at < counts[index])
+            def _():
+                @pl.when(jnp.logical_not(end))
+                def _():
+                    copy(index, half, at, toward, 0).wait_send()
+
+                @pl.when(jnp.logical_not(begin))
+                def _():
+                    copy(index, half, at, away, 1).wait_send()
+
+        each(step, handle)
+        return carry
+
+    lax.fori_loop(0, window, last_step, 0)
+
+
+def line_sum(arrays, depths, axis, collective_id):
+    if lax.axis_size(axis) == 1:
+        return arrays
+    counts = tuple(array.shape[0] // (2 * depth) for array, depth in zip(arrays, depths))
+    vmem = pl.BlockSpec(memory_space=pltpu.VMEM)
+    scratch = [pltpu.VMEM(array.shape, bf16) for array in arrays] * 2
+    for count in counts:
+        scratch += [pltpu.SemaphoreType.DMA((2 * count,))] * 4
+    return pl.pallas_call(
+        functools.partial(line_sum_kernel, axis, counts, tuple(depths)),
+        in_specs=[vmem] * len(arrays),
+        out_specs=[vmem] * len(arrays),
+        out_shape=[struct(array.shape, bf16) for array in arrays],
+        scratch_shapes=scratch,
+        compiler_params=pltpu.CompilerParams(
+            collective_id=collective_id, has_side_effects=True, vmem_limit_bytes=VMEM_LIMIT
+        ),
+        cost_estimate=pl.CostEstimate(flops=10**8, bytes_accessed=600 * 10**6, transcendentals=0),
+        name="line_sum",
+    )(*arrays)
+
+
+class LineGather:
+    def __init__(self, axis, block, blocks, own_sem, send_sem, recv_sem):
+        self.axis, self.block, self.blocks = axis, block, blocks
+        self.own_sem, self.send_sem, self.recv_sem = own_sem, send_sem, recv_sem
+        self.devices, self.place = lax.axis_size(axis), lax.axis_index(axis)
+        self.rows = block.shape[0]
+
+    def at(self, owner):
+        return self.blocks.at[pl.ds(pl.multiple_of(owner * self.rows, self.rows), self.rows), :]
+
+    def enter(self):
+        line_barrier(self.axis)
+
+    def copy(self, hop, way):
+        owner = self.place - hop if way == 0 else self.place + hop
+        target = self.place + 1 if way == 0 else self.place - 1
+        slot = 2 * hop + way
+        return pltpu.make_async_remote_copy(
+            self.block if hop == 0 else self.at(owner), self.at(owner),
+            self.send_sem.at[slot], self.recv_sem.at[slot],
+            device_id={self.axis: target}, device_id_type=MESH,
+        )
+
+    def arrival(self, hop, way):
+        owner = self.place - hop if way == 0 else self.place + hop
+        target = self.place + 1 if way == 0 else self.place - 1
+        slot = 2 * (hop - 1) + way
+        return pltpu.make_async_remote_copy(
+            self.at(owner), self.at(owner), self.send_sem.at[slot], self.recv_sem.at[slot],
+            device_id={self.axis: target}, device_id_type=MESH,
+        )
+
+    def sends(self, hop, way):
+        if way == 0:
+            return (self.place >= hop) & (self.place < self.devices - 1)
+        return (self.place + hop < self.devices) & (self.place > 0)
+
+    def comes(self, hop, way):
+        return self.place >= hop if way == 0 else self.place + hop < self.devices
+
+    def own(self):
+        return pltpu.make_async_copy(self.block, self.at(self.place), self.own_sem)
+
+    def advance(self, hop):
+        if hop == 0:
+            self.own().start()
+        for way in range(2):
+            if hop:
+                @pl.when(self.comes(hop, way))
+                def _():
+                    self.arrival(hop, way).wait_recv()
+
+            if hop < self.devices - 1:
+                @pl.when(self.sends(hop, way))
+                def _():
+                    self.copy(hop, way).start()
+
+    def leave(self):
+        self.own().wait()
+        for hop in range(self.devices - 1):
+            for way in range(2):
+                @pl.when(self.sends(hop, way))
+                def _():
+                    self.copy(hop, way).wait_send()
 
 
 def whole(shape):
@@ -484,8 +738,467 @@
 SCALARS = pl.BlockSpec(memory_space=pltpu.SMEM)
 
 
-def params():
-    return pltpu.CompilerParams(dimension_semantics=("arbitrary",), vmem_limit_bytes=VMEM_LIMIT)
+def feed_kernel(
+    axis, devices, rows,
+    own_ref, grad_hidden_ref, w_gate_ref, w_up_ref,
+    blocks_ref, hidden_ref, grad_gate_ref, grad_up_ref, total_ref,
+    parts, arrived, gather_send, gather_recv, chain_send, chain_recv,
+):
+    place = lax.axis_index(axis)
+    piece = rows // 2
+    line_barrier(axis)
+
+    def span(block, half):
+        return pl.ds(pl.multiple_of(block * rows + half * piece, piece), piece)
+
+    def full(block):
+        return pl.ds(pl.multiple_of(block * rows, rows), rows)
+
+    def gather(owner, hop, way, half):
+        target = place + 1 - 2 * way
+        slot = (hop * 2 + way) * 2 + half
+        return pltpu.make_async_remote_copy(
+            blocks_ref.at[span(owner, half), :], blocks_ref.at[span(owner, half), :],
+            gather_send.at[slot], gather_recv.at[slot], device_id={axis: target}, device_id_type=MESH,
+        )
+
+    def chain(block, way, half, at):
+        target = at + 1 - 2 * way
+        landing = jnp.where((block == target) & (way == 0), devices, block)
+        slot = (way * devices + block) * 2 + half
+        return pltpu.make_async_remote_copy(
+            parts.at[span(block, half), :], arrived.at[span(landing, half), :],
+            chain_send.at[slot], chain_recv.at[slot], device_id={axis: target}, device_id_type=MESH,
+        )
+
+    blocks_ref[full(place), :] = own_ref[...]
+
+    def event(step, carry):
+        hop = (step + 1) // 2
+        way = (step + 1) % 2
+        owner = jnp.where(way == 0, place - hop, place + hop)
+        target = place + 1 - 2 * way
+
+        @pl.when(step == 0)
+        def _():
+            for side in range(2):
+                @pl.when((place + 1 - 2 * side >= 0) & (place + 1 - 2 * side < devices))
+                def _():
+                    for half in range(2):
+                        gather(place, 0, side, half).start()
+
+        @pl.when((owner >= 0) & (owner < devices))
+        def _():
+            @pl.when(step > 0)
+            def _():
+                for half in range(2):
+                    gather(owner, hop - 1, way, half).wait_recv()
+
+                    @pl.when((target >= 0) & (target < devices))
+                    def _():
+                        gather(owner, hop, way, half).start()
+
+            here = full(owner)
+            block = blocks_ref[here, :]
+            gate_pre = dot(block, w_gate_ref[...])
+            up_pre = dot(block, w_up_ref[...])
+            sigma = sigmoid(gate_pre)
+            act = gate_pre * sigma
+            hidden_ref[here, :] = (act * up_pre).astype(bf16)
+            grad_hidden = grad_hidden_ref[here, :]
+            grad_gate_ref[here, :] = (grad_hidden * up_pre * (sigma * (1.0 + gate_pre * (1.0 - sigma)))).astype(bf16)
+            grad_up_ref[here, :] = (grad_hidden * act).astype(bf16)
+            grad = dot_nt(grad_gate_ref[here, :], w_gate_ref[...]) + dot_nt(grad_up_ref[here, :], w_up_ref[...])
+
+            @pl.when(step == 0)
+            def _():
+                total_ref[...] = grad
+
+            @pl.when(step > 0)
+            def _():
+                parts[here, :] = grad.astype(bf16)
+
+        @pl.when((way == 1) & (step > 0))
+        def _():
+            for side in (1, 0):
+                block = devices - 1 - hop if side == 1 else hop
+                begins = place == devices - 1 if side == 1 else place == 0
+                valid = (block >= 0) & (block < place) if side == 1 else (block < devices) & (block > place)
+
+                @pl.when(valid)
+                def _():
+                    for half in range(2):
+                        @pl.when(jnp.logical_not(begins))
+                        def _():
+                            chain(block, side, half, place + 2 * side - 1).wait_recv()
+                            at = span(block, half)
+                            parts[at, :] = (parts[at, :].astype(f32) + arrived[at, :].astype(f32)).astype(bf16)
+
+                        chain(block, side, half, place).start()
+
+        return carry
+
+    lax.fori_loop(0, 2 * devices - 1, event, 0)
+
+    for side, landing, comes in ((1, place, place < devices - 1), (0, devices, place > 0)):
+        @pl.when(comes)
+        def _():
+            for half in range(2):
+                chain(place, side, half, place + 2 * side - 1).wait_recv()
+                at = pl.ds(half * piece, piece)
+                total_ref[at, :] += arrived[span(landing, half), :].astype(f32)
+
+    def gather_end(step, carry):
+        hop = step // 2
+        way = step % 2
+        owner = jnp.where(way == 0, place - hop, place + hop)
+        target = place + 1 - 2 * way
+
+        @pl.when((owner >= 0) & (owner < devices) & (target >= 0) & (target < devices))
+        def _():
+            for half in range(2):
+                gather(owner, hop, way, half).wait_send()
+
+        return carry
+
+    lax.fori_loop(0, 2 * (devices - 1), gather_end, 0)
+
+    def chain_end(block, carry):
+        @pl.when(block < place)
+        def _():
+            for half in range(2):
+                chain(block, 1, half, place).wait_send()
+
+        @pl.when(block > place)
+        def _():
+            for half in range(2):
+                chain(block, 0, half, place).wait_send()
+
+        return carry
+
+    lax.fori_loop(0, devices, chain_end, 0)
+
+
+def feed(own, grad_hidden, w_gate, w_up, axis, collective_id):
+    devices = lax.axis_size(axis)
+    rows, width = own.shape
+    units = w_gate.shape[1]
+    vmem = pl.BlockSpec(memory_space=pltpu.VMEM)
+    moves = pltpu.SemaphoreType.DMA((4 * devices,))
+    return pl.pallas_call(
+        functools.partial(feed_kernel, axis, devices, rows),
+        in_specs=[vmem] * 4,
+        out_specs=[vmem] * 5,
+        out_shape=[struct((devices * rows, width), bf16)]
+        + [struct((devices * rows, units), bf16)] * 3
+        + [struct((rows, width), f32)],
+        scratch_shapes=[
+            pltpu.VMEM((devices * rows, width), bf16), pltpu.VMEM(((devices + 1) * rows, width), bf16),
+            moves, moves, moves, moves,
+        ],
+        compiler_params=pltpu.CompilerParams(
+            collective_id=collective_id, has_side_effects=True, vmem_limit_bytes=60 * 1024 * 1024
+        ),
+        name="feed",
+    )(own, grad_hidden, w_gate, w_up)
+
+
+def flip(index, mask):
+    for bit in (1, 2, 4):
+        if mask & bit:
+            index = index + bit * (1 - 2 * ((index // bit) % 2))
+    return index
+
+
+def cube_barrier(axis, place):
+    barrier = pltpu.get_barrier_semaphore()
+    for mask in (1, 2, 4):
+        pl.semaphore_signal(barrier, inc=1, device_id={axis: flip(place, mask)}, device_id_type=MESH)
+    pl.semaphore_wait(barrier, 3)
+
+
+class CubeGather:
+    FIRST = ((0, 0, 2), (0, 1, 4), (0, 1, 2), (0, 0, 4), (0, 0, 1), (0, 1, 1))
+    SECOND = ((2, 0, 4), (4, 1, 2), (2, 0, 1), (4, 1, 1))
+    THIRD = ((2, 1, 1), (4, 0, 1))
+    FOURTH = ((6, 0, 1), (6, 1, 1))
+
+    def __init__(self, axis, own_ref, all_ref, own_sem, send_sem, recv_sem):
+        self.axis, self.own_ref, self.all_ref = axis, own_ref, all_ref
+        self.own_sem, self.send_sem, self.recv_sem = own_sem, send_sem, recv_sem
+        self.place = lax.axis_index(axis)
+        self.rows = own_ref.shape[0]
+        self.piece = self.rows // 2
+
+    def part(self, mask, half):
+        start = flip(self.place, mask) * self.rows + half * self.piece
+        return self.all_ref.at[pl.ds(pl.multiple_of(start, self.piece), self.piece), :]
+
+    def copy(self, mask, half, toward):
+        source = self.part(mask, half) if mask else self.own_ref.at[pl.ds(half * self.piece, self.piece), :]
+        return pltpu.make_async_remote_copy(
+            source, self.part(mask, half),
+            self.send_sem.at[toward * 2 + half, mask // 2], self.recv_sem.at[(mask ^ toward) * 2 + half],
+            device_id={self.axis: flip(self.place, toward)}, device_id_type=MESH,
+        )
+
+    def wait(self, mask, half):
+        pltpu.make_async_remote_copy(
+            self.part(mask, half), self.part(mask, half), self.send_sem.at[0, 0], self.recv_sem.at[mask * 2 + half],
+            device_id={self.axis: flip(self.place, 1)}, device_id_type=MESH,
+        ).wait_recv()
+
+    def own(self):
+        start = pl.multiple_of(self.place * self.rows, self.rows)
+        return pltpu.make_async_copy(self.own_ref, self.all_ref.at[pl.ds(start, self.rows), :], self.own_sem)
+
+    def first(self):
+        cube_barrier(self.axis, self.place)
+        for move in self.FIRST:
+            self.copy(*move).start()
+        self.own().start()
+
+    def second(self):
+        self.wait(2, 0)
+        self.copy(*self.SECOND[0]).start()
+        self.wait(4, 1)
+        for move in self.SECOND[1:]:
+            self.copy(*move).start()
+
+    def third(self):
+        for move in self.THIRD:
+            self.wait(*move[:2])
+            self.copy(*move).start()
+
+    def fourth(self):
+        for move in self.FOURTH:
+            self.wait(*move[:2])
+            self.copy(*move).start()
+
+    def last(self):
+        for mask in (1, 3, 5, 7):
+            for half in range(2):
+                self.wait(mask, half)
+        self.own().wait()
+        for move in self.FIRST + self.SECOND + self.THIRD + self.FOURTH:
+            self.copy(*move).wait_send()
+
+
+CUBE_SEMAPHORES = [pltpu.SemaphoreType.DMA, pltpu.SemaphoreType.DMA((10, 4)), pltpu.SemaphoreType.DMA((16,))]
+
+
+def cube_gather_kernel(axis, own_ref, all_ref, *semaphores):
+    gather = CubeGather(axis, own_ref, all_ref, *semaphores)
+    gather.first()
+    gather.second()
+    gather.third()
+    gather.fourth()
+    gather.last()
+
+
+def cube_gather(own, axis, collective_id):
+    if lax.axis_size(axis) != 8:
+        return lax.all_gather(own, axis, axis=0, tiled=True)
+    rows, width = own.shape
+    return pl.pallas_call(
+        functools.partial(cube_gather_kernel, axis),
+        in_specs=[ANYWHERE],
+        out_specs=ANYWHERE,
+        out_shape=struct((8 * rows, width), own.dtype),
+        scratch_shapes=CUBE_SEMAPHORES,
+        compiler_params=pltpu.CompilerParams(
+            collective_id=collective_id, has_side_effects=True, vmem_limit_bytes=VMEM_LIMIT
+        ),
+        name="cube_gather",
+    )(own)
+
+
+def feed_grads_kernel(
+    axis, cube,
+    own_ref, blocks_ref, grads_ref, w_down_ref, hidden_ref, grad_gate_ref, grad_up_ref,
+    *refs,
+):
+    outs = refs[: 5 if cube else 4]
+    down_ref, gate_ref, up_ref, part_ref = outs[:4]
+    step = pl.program_id(0)
+    steps = pl.num_programs(0)
+    if cube:
+        gather = CubeGather(axis, own_ref, outs[4], *refs[5:])
+        for at, phase in ((0, gather.first), (2, gather.second), (4, gather.third), (6, gather.fourth)):
+            @pl.when(step == at)
+            def _():
+                phase()
+
+    gate_ref[...] = dot_tn(blocks_ref[...], grad_gate_ref[...]).astype(bf16)
+    up_ref[...] = dot_tn(blocks_ref[...], grad_up_ref[...]).astype(bf16)
+    down_ref[...] = dot_tn(hidden_ref[...], grads_ref[...]).astype(bf16)
+    part_ref[...] = dot(hidden_ref[...], w_down_ref[...]).astype(bf16)
+    if cube:
+        @pl.when(step == steps - 1)
+        def _():
+            gather.last()
+
+
+def feed_grads(own, blocks, grads, w_down, hidden, grad_gate, grad_up, axis, collective_id):
+    cube = lax.axis_size(axis) == 8
+    rows, width = blocks.shape
+    units = hidden.shape[1]
+    tall = pl.BlockSpec((rows, BLOCK), lambda step: (0, step))
+    down = pl.BlockSpec((units, BLOCK), lambda step: (0, step))
+    flat = pl.BlockSpec((BLOCK, units), lambda step: (step, 0))
+    held = pl.BlockSpec((rows, units), lambda step: (0, 0), pipeline_mode=pl.Buffered(1))
+    *results, gathered = pl.pallas_call(
+        functools.partial(feed_grads_kernel, axis, cube),
+        grid=(width // BLOCK,),
+        in_specs=[ANYWHERE, tall, tall, down, held, held, held],
+        out_specs=[down, flat, flat, tall] + [ANYWHERE] * cube,
+        out_shape=[
+            struct((units, width), bf16), struct((width, units), bf16), struct((width, units), bf16),
+            struct((rows, width), bf16),
+        ] + [struct((8 * own.shape[0], width), bf16)] * cube,
+        scratch_shapes=CUBE_SEMAPHORES if cube else [],
+        compiler_params=params(collective_id if cube else None),
+        name="feed_grads",
+    )(own, blocks, grads, w_down, hidden, grad_gate, grad_up)
+    if not cube:
+        results, gathered = [*results, gathered], lax.all_gather(own, axis, axis=0, tiled=True)
+    return (*results, gathered)
+
+
+def cube_sum_kernel(axis, part_ref, total_ref, held, arrived, send_sem, recv_sem):
+    place = lax.axis_index(axis)
+    cube_barrier(axis, place)
+    held[0] = part_ref[...]
+    for stage, mask in enumerate((1, 2, 4)):
+        copy = pltpu.make_async_remote_copy(
+            held.at[stage], arrived.at[stage], send_sem.at[stage], recv_sem.at[stage],
+            device_id={axis: flip(place, mask)}, device_id_type=MESH,
+        )
+        copy.start()
+        copy.wait()
+        if stage < 2:
+            held[stage + 1] = held[stage] + arrived[stage]
+        else:
+            total_ref[...] = held[stage] + arrived[stage]
+
+
+def cube_sum(part, axis, collective_id):
+    if lax.axis_size(axis) != 8:
+        return lax.psum(part, axis)
+    vmem = pl.BlockSpec(memory_space=pltpu.VMEM)
+    return pl.pallas_call(
+        functools.partial(cube_sum_kernel, axis),
+        in_specs=[vmem],
+        out_specs=vmem,
+        out_shape=struct(part.shape, f32),
+        scratch_shapes=[
+            pltpu.VMEM((3,) + part.shape, f32), pltpu.VMEM((3,) + part.shape, f32),
+            pltpu.SemaphoreType.DMA((3,)), pltpu.SemaphoreType.DMA((3,)),
+        ],
+        compiler_params=pltpu.CompilerParams(collective_id=collective_id, has_side_effects=True),
+        name="cube_sum",
+    )(part)
+
+
+def cube_scatter_kernel(axis, rows, parts_ref, total_ref, other, leaving, coming, send_sem, recv_sem):
+    place = lax.axis_index(axis)
+    piece = rows // 2
+
+    def span(mask, half):
+        return pl.ds(pl.multiple_of(flip(place, mask) * rows + half * piece, piece), piece)
+
+    def slot(index, half):
+        return pl.ds((2 * index + half) * piece, piece)
+
+    def core_copy(mask, half):
+        return pltpu.make_async_remote_copy(
+            parts_ref.at[span(mask, half), :], other.at[slot(mask // 2, half), :],
+            send_sem.at[0, mask // 2, half], recv_sem.at[0, mask // 2, half],
+            device_id={axis: flip(place, 1)}, device_id_type=MESH,
+        )
+
+    def chip_copy(index, half, toward):
+        landing = (toward // 2 - 1) * 2 + (1 if index else 0)
+        return pltpu.make_async_remote_copy(
+            leaving.at[slot(index, half), :], coming.at[slot(landing, half), :],
+            send_sem.at[toward // 2, index, half], recv_sem.at[toward // 2, 1 if index else 0, half],
+            device_id={axis: flip(place, toward)}, device_id_type=MESH,
+        )
+
+    cube_barrier(axis, place)
+    for mask in (7, 3, 5, 1):
+        for half in range(2):
+            core_copy(mask, half).start()
+
+    def chip_part(mask, half):
+        core_copy(mask + 1, half).wait_recv()
+        return parts_ref[span(mask, half), :].astype(f32) + other[slot(mask // 2, half), :].astype(f32)
+
+    def arrived(index, half, toward):
+        chip_copy(index, half, toward).wait_recv()
+        landing = (toward // 2 - 1) * 2 + (1 if index else 0)
+        return coming[slot(landing, half), :].astype(f32)
+
+    leaving[slot(0, 0), :] = chip_part(6, 0).astype(bf16)
+    chip_copy(0, 0, 2).start()
+    leaving[slot(0, 1), :] = chip_part(6, 1).astype(bf16)
+    chip_copy(0, 1, 4).start()
+    leaving[slot(1, 0), :] = chip_part(2, 0).astype(bf16)
+    chip_copy(1, 0, 2).start()
+    leaving[slot(2, 1), :] = chip_part(4, 1).astype(bf16)
+    chip_copy(2, 1, 4).start()
+    by_x = chip_part(2, 1)
+    leaving[slot(1, 1), :] = (by_x + arrived(0, 1, 4)).astype(bf16)
+    chip_copy(1, 1, 2).start()
+    by_y = chip_part(4, 0)
+    leaving[slot(2, 0), :] = (by_y + arrived(0, 0, 2)).astype(bf16)
+    chip_copy(2, 0, 4).start()
+    for half in range(2):
+        total_ref[half * piece : (half + 1) * piece, :] = chip_part(0, half)
+    for half in (0, 1):
+        at = slice(half * piece, (half + 1) * piece)
+        if half == 0:
+            total_ref[at, :] += arrived(1, 0, 2)
+            total_ref[at, :] += arrived(2, 0, 4)
+        else:
+            total_ref[at, :] += arrived(2, 1, 4)
+            total_ref[at, :] += arrived(1, 1, 2)
+    for mask in (7, 3, 5, 1):
+        for half in range(2):
+            core_copy(mask, half).wait_send()
+    for index, half, toward in ((0, 0, 2), (0, 1, 4), (1, 0, 2), (2, 1, 4), (1, 1, 2), (2, 0, 4)):
+        chip_copy(index, half, toward).wait_send()
+
+
+def cube_scatter(parts, axis, collective_id):
+    if lax.axis_size(axis) != 8:
+        return lax.psum_scatter(parts, axis, scatter_dimension=0, tiled=True).astype(f32)
+    rows, width = parts.shape[0] // 8, parts.shape[1]
+    vmem = pl.BlockSpec(memory_space=pltpu.VMEM)
+    return pl.pallas_call(
+        functools.partial(cube_scatter_kernel, axis, rows),
+        in_specs=[vmem],
+        out_specs=vmem,
+        out_shape=struct((rows, width), f32),
+        scratch_shapes=[
+            pltpu.VMEM((4 * rows, width), bf16), pltpu.VMEM((3 * rows, width), bf16),
+            pltpu.VMEM((4 * rows, width), bf16),
+            pltpu.SemaphoreType.DMA((3, 4, 2)), pltpu.SemaphoreType.DMA((3, 4, 2)),
+        ],
+        compiler_params=pltpu.CompilerParams(
+            collective_id=collective_id, has_side_effects=True, vmem_limit_bytes=VMEM_LIMIT
+        ),
+        name="cube_scatter",
+    )(parts)
+
+
+def params(collective_id=None):
+    return pltpu.CompilerParams(
+        dimension_semantics=("arbitrary",),
+        vmem_limit_bytes=VMEM_LIMIT,
+        collective_id=collective_id,
+        has_side_effects=collective_id is not None,
+    )
 
 
 def struct(shape, dtype):
@@ -550,39 +1263,36 @@
 
     inputs_f = inputs.astype(f32)
     normed = rms_scale(inputs_f, first_gain).astype(bf16)
-    block_rows = lax.all_gather(normed, "head", axis=0, tiled=True)
+    block_rows = cube_gather(normed, "head", 4)
     tail = from_previous(block_rows[seq_rows - 2 * HALO :])
     meta = jnp.concatenate(
         [(seq_index * seq_rows).astype(jnp.int32)[None], slot_starts(doc_lengths)]
     )
     _, own_valid = layout(doc_lengths, (seq_index * head_total + head_index) * row_count, row_count)
 
-    w_all = jnp.concatenate(
-        [
-            w_query, w_key, w_value, w_outgate, w_decay, w_beta,
-            jnp.zeros((model_width, LANES - 2 * heads), bf16),
-        ],
-        axis=1,
-    )
-    all_width = w_all.shape[1]
+    grad_out = cotangent.astype(f32) * own_valid.astype(f32)[:, None]
+    grad_low = grad_out.astype(bf16)
+    w_small = jnp.concatenate([w_decay, w_beta, jnp.zeros((model_width, LANES - 2 * heads), bf16)], axis=1)
+    weights = (w_query, w_key, w_value, w_outgate, w_small)
+    all_width = mixed_width + vw + LANES
     conv_all = jnp.concatenate([conv_query, conv_key, conv_value], axis=1)
     dvec = jnp.zeros((8, LANES), f32)
     dvec = dvec.at[0, :heads].set(decay_bias).at[1, :heads].set(-jnp.exp(decay_log))
     map_shape = (heads, key_width, key_width + value_width)
 
-    (pre, conv, gate, small, scal, qkv, inverse, w_part, u_part, starts, drop, block_map) = pl.pallas_call(
-        functools.partial(forward_kernel, *sizes, taps),
+    (pre, conv, gate, small, scal, qkv, inverse, w_part, u_part, starts, drop, block_map, grad_block_two) = pl.pallas_call(
+        functools.partial(forward_kernel, *sizes, taps, chunks),
         grid=(chunks,),
         in_specs=[
             SCALARS, by_rows(model_width), whole((2 * HALO, model_width)),
-            whole(w_all.shape), whole(conv_all.shape), whole(dvec.shape),
+            *(whole(weight.shape) for weight in weights), whole(conv_all.shape), whole(dvec.shape), ANYWHERE,
         ],
         out_specs=[
             by_rows(mixed_width), by_rows(mixed_width), by_rows(vw), by_rows(LANES), by_rows(LANES),
             by_rows(mixed_width),
             by_chunk((heads, BLOCK, BLOCK)), by_chunk((heads, BLOCK, key_width)),
             by_chunk((heads, BLOCK, value_width)), by_chunk(map_shape),
-            by_chunk((heads, key_width, key_width)), whole(map_shape),
+            by_chunk((heads, key_width, key_width)), whole(map_shape), ANYWHERE,
         ],
         out_shape=[
             struct((seq_rows, mixed_width), f32), struct((seq_rows, mixed_width), f32),
@@ -591,11 +1301,15 @@
             struct((chunks, heads, BLOCK, BLOCK), bf16), struct((chunks, heads, BLOCK, key_width), bf16),
             struct((chunks, heads, BLOCK, value_width), f32), struct((chunks,) + map_shape, f32),
             struct((chunks, heads, key_width, key_width), f32), struct(map_shape, f32),
-        ],
-        scratch_shapes=[pltpu.VMEM((BLOCK + HALO, mixed_width), f32), pltpu.VMEM(map_shape, f32)],
-        compiler_params=params(),
+            struct((lax.axis_size("seq") * row_count, model_width), bf16),
+        ],
+        scratch_shapes=[
+            pltpu.VMEM((BLOCK + HALO, mixed_width), f32), pltpu.VMEM(map_shape, f32), pltpu.SemaphoreType.DMA,
+            pltpu.SemaphoreType.DMA((2 * lax.axis_size("seq"),)), pltpu.SemaphoreType.DMA((2 * lax.axis_size("seq"),)),
+        ],
+        compiler_params=params(2),
         name="mixer_forward",
-    )(meta, block_rows, tail, w_all, conv_all, dvec)
+    )(meta, block_rows, tail, *weights, conv_all, dvec, grad_low)
 
     earlier = from_earlier(block_map.astype(bf16), "seq")
     gain_row = head_gain[None, :]
@@ -621,37 +1335,19 @@
         name="mixer_output",
     )(meta, earlier, starts, w_part, u_part, qkv, scal, gate, gain_row, w_output)
 
-    mixer_out = lax.psum_scatter(mixed_part, "head", scatter_dimension=0, tiled=True).astype(f32)
+    mixer_out = cube_scatter(mixed_part, "head", 5)
     hidden_in = inputs_f + mixer_out
     normed_two = rms_scale(hidden_in, second_gain).astype(bf16)
-    mlp_block = lax.all_gather(normed_two, "seq", axis=0, tiled=True)
-    gate_pre = dot(mlp_block, w_gate)
-    up_pre = dot(mlp_block, w_up)
-    hidden = (jax.nn.silu(gate_pre) * up_pre).astype(bf16)
-    mlp_out = lax.psum_scatter(
-        dot(hidden, w_down).astype(bf16), "seq", scatter_dimension=0, tiled=True
-    ).astype(f32)
-    output = (hidden_in + mlp_out).astype(bf16)
-    grad_out = cotangent.astype(f32) * own_valid.astype(f32)[:, None]
-    grad_low = grad_out.astype(bf16)
-    grad_block_two = lax.all_gather(grad_low, "seq", axis=0, tiled=True)
     grad_hidden = dot_nt(grad_block_two, w_down)
-    grad_w_down = dot_tn(hidden, grad_block_two)
-    grad_gate = (grad_hidden * up_pre * silu_slope(gate_pre)).astype(bf16)
-    grad_up = (grad_hidden * jax.nn.silu(gate_pre)).astype(bf16)
-    grad_normed_two = lax.psum_scatter(
-        (dot_nt(grad_gate, w_gate) + dot_nt(grad_up, w_up)).astype(bf16),
-        "seq",
-        scatter_dimension=0,
-        tiled=True,
-    ).astype(f32)
-    grad_w_gate = dot_tn(mlp_block, grad_gate)
-    grad_w_up = dot_tn(mlp_block, grad_up)
+    mlp_block, hidden, grad_gate, grad_up, grad_normed_two = feed(
+        normed_two, grad_hidden, w_gate, w_up, "seq", 3
+    )
     grad_hidden_norm, grad_second = rms_back(hidden_in, second_gain, grad_normed_two)
     grad_hidden_in = grad_out + grad_hidden_norm
     grad_mix = grad_hidden_in.astype(bf16)
-    grad_block = lax.all_gather(grad_mix, "head", axis=0, tiled=True)
-
+    *ff_grads, mlp_part, grad_block = feed_grads(
+        grad_mix, mlp_block, grad_block_two, w_down, hidden, grad_gate, grad_up, "head", 6
+    )
     grad_core, inner, pull, grad_gate_pre, grad_head, pulled = pl.pallas_call(
         functools.partial(core_grad_kernel, *sizes, chunks),
         grid=(chunks,),
@@ -673,11 +1369,13 @@
         compiler_params=params(),
         name="mixer_core_grad",
     )(meta, grad_block, w_output, core, gate, gain_row, qkv, scal, w_part, drop)
-    grad_w_output = dot_tn(gated, grad_block)
+    grad_w_output = dot_tn(gated, grad_block).astype(bf16)
 
     later = from_later(
         jnp.concatenate([block_map[:, :, :key_width], pulled], axis=2).astype(bf16), "seq"
     )
+    mlp_part, later = lax.optimization_barrier((mlp_part, later))
+    mlp_out = lax.psum_scatter(mlp_part, "seq", scatter_dimension=0, tiled=True)
     grad_conv, grad_small, sums = pl.pallas_call(
         functools.partial(backward_kernel, *sizes, chunks, others),
         grid=(chunks,),
@@ -701,7 +1399,7 @@
     edge = from_next(grad_conv[:HALO])
     step_rows = BLOCK // HALO
     last_halo = seq_rows // HALO - 1
-    grad_pre, grad_taps, grad_rows = pl.pallas_call(
+    grad_pre, grad_taps, grad_rows, gain_sum = pl.pallas_call(
         functools.partial(projection_grad_kernel, mixed_width, docs, chunks, taps),
         grid=(chunks,),
         in_specs=[
@@ -710,37 +1408,53 @@
                 (HALO, mixed_width), lambda step: (jnp.minimum((step + 1) * step_rows, last_halo), 0)
             ),
             whole(edge.shape), by_rows(mixed_width), by_rows(vw), by_rows(LANES),
-            whole(conv_all.shape), whole(w_all.shape),
-        ],
-        out_specs=[by_rows(all_width), whole((8, mixed_width)), by_rows(model_width)],
+            whole(conv_all.shape), by_rows(model_width), *(whole(weight.shape) for weight in weights),
+        ],
+        out_specs=[by_rows(all_width), whole((8, mixed_width)), by_rows(model_width), whole((8, model_width))],
         out_shape=[
             struct((seq_rows, all_width), bf16), struct((8, mixed_width), f32),
-            struct((seq_rows, model_width), bf16),
+            struct((seq_rows, model_width), bf16), struct((8, model_width), f32),
         ],
         scratch_shapes=[pltpu.VMEM((BLOCK + HALO, mixed_width), f32)],
         compiler_params=params(),
         name="projection_grad",
-    )(meta, grad_conv, grad_conv, edge, pre, grad_gate_pre, grad_small, conv_all, w_all)
+    )(meta, grad_conv, grad_conv, edge, pre, grad_gate_pre, grad_small, conv_all, block_rows, *weights)
 
     grad_normed = lax.psum_scatter(grad_rows, "head", scatter_dimension=0, tiled=True).astype(f32)
-    grad_input_norm, grad_first = rms_back(inputs_f, first_gain, grad_normed)
+    grad_input_norm, _ = rms_back(inputs_f, first_gain, grad_normed)
     grad_inputs = grad_hidden_in + grad_input_norm
     grad_w_all = dot_tn(block_rows, grad_pre).astype(bf16)
 
-    grad_w_gate, grad_w_up, grad_w_down, first_part, second_part, head_part = (
-        lax.psum(grad_w_gate.astype(bf16), "head").astype(f32),
-        lax.psum(grad_w_up.astype(bf16), "head").astype(f32),
-        lax.psum(grad_w_down.astype(bf16), "head").astype(f32),
-        lax.psum(grad_first.astype(bf16), "head").astype(f32),
-        lax.psum(grad_second.astype(bf16), "head").astype(f32),
-        lax.psum(grad_head[0].astype(bf16), "head").astype(f32),
+    gains = cube_sum(
+        jnp.concatenate([gain_sum[0] / first_gain, grad_second, grad_head[0]]).reshape(2, -1).repeat(4, axis=0),
+        "head",
+        7,
     )
-    grad_w_all, grad_w_output, grad_taps, sums, first_part, second_part, head_part = (
-        lax.psum(part.astype(bf16), "seq").astype(f32)
-        for part in (
-            grad_w_all, grad_w_output, grad_taps[:taps], sums[:2, :heads], first_part, second_part, head_part,
-        )
+    mlp_out, *ff_grads = lax.optimization_barrier((mlp_out, *ff_grads))
+    ff_grads = [lax.psum(part, "head") for part in ff_grads]
+    grad_w_all, grad_w_output, small_sums, gains = line_sum(
+        (
+            grad_w_all,
+            grad_w_output,
+            jnp.pad(
+                jnp.concatenate([grad_taps, sums], axis=1), ((0, 24), (0, all_width - mixed_width - LANES))
+            ).astype(bf16),
+            jnp.pad(gains, ((0, 24), (0, 0))).astype(bf16),
+        ),
+        (32, 16, 16, 16),
+        "seq",
+        1,
     )
+    gains = jnp.concatenate([gains[0], gains[4]]).astype(f32)
+    first_part, second_part = gains[:model_width], gains[model_width : 2 * model_width]
+    head_part = gains[2 * model_width :]
+    grad_w_all, *ff_grads = lax.optimization_barrier((grad_w_all, *ff_grads))
+    grad_w_down, grad_w_gate, grad_w_up = (part.astype(f32) for part in ff_grads)
+    grad_w_all = grad_w_all.astype(f32)
+    grad_w_output = grad_w_output.astype(f32)
+    grad_taps = small_sums[:taps, :mixed_width].astype(f32)
+    sums = small_sums[:2, mixed_width : mixed_width + heads].astype(f32)
+    output = (hidden_in + mlp_out.astype(f32)).astype(bf16)
     gate_at = mixed_width
     small_at = mixed_width + vw
     return (

time: 1320 us -> 925 us (0.70)
  waiting for transfers between devices: 850 us -> 56.5 us
  Pallas kernels: 176 us -> 712 us
  matrix products: 129 us -> 41 us
  blocking collectives: 33.7 us -> 0 us
  local copies, waits for them, and re-layouts: 35.8 us -> 22.3 us
    pallas_call x1 -> x7, Pallas kernels: 77.7 us -> 615 us  [the longest x1 237 us: line_sum(): pl.pallas_call(functools.partial(line_sum_kernel, axis, counts, tuple(dep...]
    psum x2 -> x1, waiting for transfers between devices: 370 us -> 3.76 us  [shards(): ff_grads = [lax.psum(part, 'head') for part in ff_grads]]
    all_gather x4 -> x0, waiting for transfers between devices: 209 us -> none  [the longest x1 78.9 us: shards(): mlp_block = lax.all_gather(normed_two, 'seq', axis=0, tiled=True)]
    reduce_scatter x3 -> x1, waiting for transfers between devices: 193 us -> 12.6 us  [shards(): mlp_out = lax.psum_scatter(mlp_part, 'seq', scatter_dimension=0, tiled=True)]
    reduce_scatter x1, waiting for transfers between devices: 52.4 us -> 0.01 us  [shards(): lax.psum_scatter(grad_rows, 'head', scatter_dimension=0, tiled=True)]
    psum x2 -> x0, blocking collectives: 33.7 us -> none  [the longest x1 20.4 us: shards(): lax.psum(part.astype(bf16), 'seq').astype(f32)]
    dot_general x3 -> x0, matrix products: 33.4 us -> none  [dot(): return jnp.dot(left, right, preferred_element_type=f32)]
    dot_general x5 -> x2, matrix products: 58.3 us -> 30.9 us  [dot_tn(): lax.dot_general(left, right, (((0,), (0,)), ((), ())), preferred_element_...]
  transfers between devices with their start and end apart: 18 -> 11, of which waited for: 15 -> 5; matrix products, arithmetic and copies ran while one was open for 12% -> 7% of each run, Pallas kernels for 6% -> 33%
where the time goes in v2:
time: 925 us; the launch traced here: 916 us
  Pallas kernels  712 us (77%)
  waiting for transfers between devices  56.5 us (6%)
  other arithmetic  52.9 us (6%)
  matrix products  41 us (4%)
  local copies, waits for them, and re-layouts  22.3 us (2%)
  starting transfers between devices  17.3 us (2%)
  between operations  14.6 us (2%)
    pallas_call x1, Pallas kernels, line_sum(): pl.pallas_call(functools.partial(line_sum_kernel, axis, counts, tuple(dep...  237 us
    pallas_call x1, Pallas kernels, feed(): pl.pallas_call(functools.partial(feed_kernel, axis, devices, rows), in_sp...  139 us
    pallas_call x1, Pallas kernels, shards(): pl.pallas_call(functools.partial(forward_kernel, *sizes, taps, chunks), g...  93.6 us
    pallas_call x1, Pallas kernels, feed_grads(): pl.pallas_call(functools.partial(feed_grads_kernel, axis, cube), grid=(wi...  48.5 us
    pallas_call x1, Pallas kernels, cube_scatter(): pl.pallas_call(functools.partial(cube_scatter_kernel, axis, rows), in_spe...  43.5 us
    pallas_call x1, Pallas kernels, cube_gather(): pl.pallas_call(functools.partial(cube_gather_kernel, axis), in_specs=[ANY...  42.1 us
    ppermute x3, waiting for transfers between devices, from_later(): lax.ppermute(array, axis, [(i + by, i) for i in range(devices - by)])  34.8 us
    pallas_call x1, Pallas kernels, shards(): pl.pallas_call(functools.partial(projection_grad_kernel, mixed_width, doc...  31.8 us
  transfers between devices with their start and end apart: 11, of which 5 were waited for; matrix products, arithmetic and copies ran while one was open for 7% of the time, Pallas kernels for 33%

profile of v2, /device:TPU:0, one launch (start us, length us, event | category | flops | bytes accessed | tf_op | source)
XLA Modules:
  0.0 916.3 jit_solution(18101807033406713762)
XLA Ops:
  7.2 1.5 fusion
  8.8 2.5 fusion.2.own_ref
  11.3 42.1 %cube_gather.1.rows_ref = bf16[2048,2048]{1,0:T(8,128)(2,1)} custom-call(bf16[256,2048]{1,0:T(8,128)(2,1)} %fusion.2.own_ref), custom_call_target="tpu_custom_call" | custom-call | tf_op jit(solution)/shard_map/cube_gather/pallas_call | solution.py:1003
  54.2 3.5 collective-permute-start
  59.1 1.2 fusion.7.block_ref
  60.4 1.1 maximum_maximum_fusion.ws_ref
  62.7 93.6 %mixer_forward.1 = (f32[2048,1024]{1,0:T(8,128)}, f32[2048,1024]{1,0:T(8,128)}, f32[2048,512]{1,0:T(8,128)}, f32[2048,128]{1,0:T(8,128)}, f32[2048,128]{1,0:T(8,...) custom-call(s32[4]{0:T(128)} %pad_add_fusion.meta, ...), custom_call_target="tpu_custom_call" | custom-call | tf_op jit(solution)/shard_map/mixer_forward/pallas_call | solution.py:1283
  156.3 1.0 convert_element_type.84
  157.3 1.3 collective-permute-start.3
  158.6 5.5 collective-permute-start.2
  164.2 1.5 collective-permute-start.1
  165.7 10.1 %fusion.21.grad_hidden_ref = f32[1024,1408]{1,0:T(8,128)} fusion(bf16[1024,2048]{1,0:T(8,128)(2,1)} %get-tuple-element.107.grads_ref, bf16[1408,2048]{1,0:T(8,128)(2,1)S(1)} %bitcast.34), kind=kOutput, calls=%fused_computation.74 | convolution fusion | flops 5905580032 | bytes 15728640 | tf_op jit(solution)/shard_map/dot_general | solution.py:30
  176.7 19.8 %mixer_output.1 = (f32[2048,512]{1,0:T(8,128)}, bf16[2048,512]{1,0:T(8,128)(2,1)}, bf16[2048,2048]{1,0:T(8,128)(2,1)}, bf16[8,2,256,256]{3,2,1,0:T(8,128)(2,1)}, f32[8,2,128,256]{3,2,1,0:T(8,128)}) custom-call(s32[4]{0:T(128)} %pad_add_fusion.meta, bf16[3,2,128,384]{3,2,1,0:T(8,128)(2,1)} %pad_maximum_fusion.maps_ref, ...), custom_call_target="tpu_custom_call" | custom-call | tf_op jit(solution)/shard_map/mixer_output/pallas_call | solution.py:1316
  196.5 43.5 %cube_scatter.1 = f32[256,2048]{1,0:T(8,128)} custom-call(bf16[2048,2048]{1,0:T(8,128)(2,1)} %get-tuple-element.106.parts_ref), custom_call_target="tpu_custom_call" | custom-call | tf_op jit(solution)/shard_map/cube_scatter/pallas_call | solution.py:1178
  240.0 2.0 multiply_reduce_fusion.2
  242.0 1.2 multiply_convert_fusion.own_ref
  243.2 139.3 %feed.1 = (bf16[1024,2048]{1,0:T(8,128)(2,1)}, bf16[1024,1408]{1,0:T(8,128)(2,1)}, bf16[1024,1408]{1,0:T(8,128)(2,1)}, bf16[1024,1408]{1,0:T(8,128)(2,1)}, f32[256,2048]{1,0:T(8,128)}) custom-call(bf16[256,2048]{1,0:T(8,128)(2,1)} %multiply_convert_fusion.own_ref, f32[1024,1408]{1,0:T(8,128)} %fusion.21.grad_hidden_ref, bf16[2048,1408]{1,0:T(8,128)(2,1)} %w_gate_ref.1, ...), custom_call_target="tpu_custom_call" | custom-call | tf_op jit(solution)/shard_map/feed/pallas_call | solution.py:888
  382.5 2.3 multiply_reduce_fusion
  385.0 2.4 fusion.16
  387.4 48.5 %feed_grads.1 = (bf16[1408,2048]{1,0:T(8,128)(2,1)}, bf16[2048,1408]{1,0:T(8,128)(2,1)}, bf16[2048,1408]{1,0:T(8,128)(2,1)}, bf16[1024,2048]{1,0:T(8,128)(2,1)}, bf16[2048,2048]{1,0:T(8,128)(2,1)}) custom-call(bf16[256,2048]{1,0:T(8,128)(2,1)} %get-tuple-element.203.own_ref, bf16[1024,2048]{1,0:T(8,128)(2,1)} %get-tuple-element.109.blocks_ref, ...), custom_call_target="tpu_custom_call" | custom-call | tf_op jit(solution)/shard_map/feed_grads/pallas_call | solution.py:1050
  435.9 19.6 %mixer_core_grad.1 = (bf16[8,2,256,256]{3,2,1,0:T(8,128)(2,1)}, f32[8,2,256,256]{3,2,1,0:T(8,128)}, f32[8,2,128,256]{3,2,1,0:T(8,128)}, bf16[2048,512]{1,0:T(8,1...) custom-call(s32[4]{0:T(128)} %pad_add_fusion.meta, bf16[2048,2048]{1,0:T(8,128)(2,1)} %get-tuple-element.114.grad_ref, ...), custom_call_target="tpu_custom_call" | custom-call | tf_op jit(solution)/shard_map/mixer_core_grad/pallas_call | solution.py:1351
  455.4 1.0 convert.17
  456.4 1.3 collective-permute-start.6
  457.7 1.3 collective-permute-start.5
  459.0 1.3 collective-permute-start.4
  460.3 11.9 %collective-permute-done.6 = bf16[2,128,384]{2,1,0:T(8,128)(2,1)S(1)} collective-permute-done((bf16[2,128,384]{2,1,0:T(8,128)(2,1)S(1)}, bf16[2,128,384]{2,1,0:T(8,128)(2,1)S(1)}, u32[]{:S(2)}, u32[]{:S(2)}) %collective-permute-start.6) | collective-permute-done | bytes 196640 | tf_op jit(solution)/shard_map/ppermute | solution.py:1220
  472.2 23.0 %collective-permute-done.5 = bf16[2,128,384]{2,1,0:T(8,128)(2,1)S(1)} collective-permute-done((bf16[2,128,384]{2,1,0:T(8,128)(2,1)S(1)}, bf16[2,128,384]{2,1,0:T(8,128)(2,1)S(1)}, u32[]{:S(2)}, u32[]{:S(2)}) %collective-permute-start.5) | collective-permute-done | bytes 196640 | tf_op jit(solution)/shard_map/ppermute | solution.py:1220
  496.1 25.8 %mixer_backward.1 = (f32[2048,1024]{1,0:T(8,128)}, bf16[2048,128]{1,0:T(8,128)(2,1)}, f32[8,128]{1,0:T(8,128)}) custom-call(s32[4]{0:T(128)} %pad_add_fusion.meta, bf16[3,2,128,384]{3,2,1,0:T(8,128)(2,1)} %pad_maximum_fusion.1.maps_ref, bf16[2048,1024]{1,0:T(8,128)(2,1)} %get-tuple-element.103.qkv_ref, f32[2048,1024]{1,0:T(8,128)} %get-tuple-element.124.act_ref, ...), custom_call_target="tpu_custom_call" | custom-call | tf_op jit(solution)/shard_map/mixer_backward/pallas_call | solution.py:1379
  522.6 1.5 collective-permute-start.7
  524.1 5.2 collective-permute-done.7.edge_ref
  529.9 31.8 %projection_grad.1 = (bf16[2048,1664]{1,0:T(8,128)(2,1)}, f32[8,1024]{1,0:T(8,128)}, bf16[2048,2048]{1,0:T(8,128)(2,1)}, f32[8,2048]{1,0:T(8,128)}) custom-call(s32[4]{0:T(128)} %pad_add_fusion.meta, f32[2048,1024]{1,0:T(8,128)} %get-tuple-element.132.grad_conv_ref.later_ref, f32[2048,1024]{1,0:T(8,128)} %get-tuple-element.132.grad_conv_ref.later_ref, ...), custom_call_target="tpu_custom_call" | custom-call | tf_op jit(solution)/shard_map/projection_grad/pallas_call | solution.py:1402
  561.8 12.6 %reduce-scatter.3.cloned.1.call-done = bf16[256,2048]{1,0:T(8,128)(2,1)} async-done(((bf16[1024,2048]{1,0:T(8,128)(2,1)}), bf16[256,2048]{1,0:T(8,128)(2,1)}) %reduce-scatter.3.cloned.1.call-update) | async-done | bytes 1048592 | tf_op jit(solution)/shard_map/reduce_scatter | solution.py:1378
  575.1 10.0 %convolution_convert_fusion.1.refs_1_ = bf16[512,2048]{1,0:T(8,128)(2,1)} fusion(bf16[2048,512]{1,0:T(8,128)(2,1)} %get-tuple-element.138, bf16[2048,2048]{1,0:T(8,128)(2,1)} %get-tuple-element.114.grad_ref), kind=kOutput, calls=%fused_computation.6 | convolution fusion | flops 4296015872 | bytes 12582912 | tf_op jit(solution)/shard_map/dot_general | solution.py:26
  586.7 11.0 %cube_sum.1 = f32[8,2176]{1,0:T(8,128)} custom-call(f32[8,2176]{1,0:T(8,128)} %reshape.191.part_ref), custom_call_target="tpu_custom_call" | custom-call | tf_op jit(solution)/shard_map/cube_sum/pallas_call | solution.py:1089
  599.9 20.9 %convolution_convert_fusion.refs_0_ = bf16[2048,1664]{1,0:T(8,128)(2,1)} fusion(bf16[2048,2048]{1,0:T(8,128)(2,1)} %cube_gather.1.rows_ref, bf16[2048,1664]{1,0:T(8,128)(2,1)} %get-tuple-element.137), kind=kOutput, calls=%fused_computation | convolution fusion | flops 13962051584 | bytes 22020096 | tf_op jit(solution)/shard_map/dot_general | solution.py:26
  620.9 237.1 %line_sum.1 = (bf16[2048,1664]{1,0:T(8,128)(2,1)}, bf16[512,2048]{1,0:T(8,128)(2,1)}, bf16[32,1664]{1,0:T(8,128)(2,1)}, bf16[32,2176]{1,0:T(8,128)(2,1)}) custom-call(bf16[2048,1664]{1,0:T(8,128)(2,1)} %convolution_convert_fusion.refs_0_, bf16[512,2048]{1,0:T(8,128)(2,1)} %convolution_convert_fusion.1.refs_1_, bf16[32,1664]{1,0:T(8,128)(2,1)} %fusion.13.refs_2_, ...), custom_call_target="tpu_custom_call" | custom-call | flops 100000000 | bytes 600000000 | tf_op jit(solution)/shard_map/line_sum/pallas_call | solution.py:640
  860.9 4.3 convert_element_type.96
  868.1 1.3 add_convert_fusion
  869.4 1.8 fusion.6
  871.3 3.2 fusion.5
  874.5 3.8 all-reduce.6.cloned.1.call-done
  878.3 1.6 fusion.17
  879.9 4.0 fusion.19
  883.9 4.5 fusion.18
  888.5 0.9 copy.48
  890.3 8.0 convert_element_type.97
  898.4 5.2 convert_element_type.98
  903.5 6.0 convert_element_type.99
  (128 shorter events, 18.3 us)
Async XLA Ops:
  7.2 567.2 %reduce-scatter.3.cloned.1.call-start = ((), (), s32[]{:S(2)}) async-start(), calls=%async_computation.2 | async-start | bytes 5242880 | tf_op jit(solution)/shard_map/reduce_scatter | solution.py:1378
  11.3 46.5 %copy-start.21 = (f32[2]{0:T(128)S(1)}, f32[2]{0:T(128)}, u32[]{:S(2)}) copy-start(f32[2]{0:T(128)} %param.37) | copy-start | bytes 28
  11.3 46.5 %copy-start.20 = (s32[3]{0:T(128)S(1)}, s32[3]{0:T(128)}, u32[]{:S(2)}) copy-start(s32[3]{0:T(128)} %param.26) | copy-start | bytes 40
  11.3 47.0 %copy-start.17 = (f32[4,256]{1,0:T(4,128)S(1)}, f32[4,256]{1,0:T(4,128)}, u32[]{:S(2)}) copy-start(f32[4,256]{1,0:T(4,128)} %param.34) | copy-start | bytes 12292
  11.3 47.0 %copy-start.13 = (bf16[2048,2]{0,1:T(2,128)(2,1)S(1)}, bf16[2048,2]{0,1:T(2,128)(2,1)}, u32[]{:S(2)}) copy-start(bf16[2048,2]{0,1:T(2,128)(2,1)} %param.32) | copy-start | bytes 24580
  11.3 47.3 %copy-start.14 = (bf16[2048,2]{0,1:T(2,128)(2,1)S(1)}, bf16[2048,2]{0,1:T(2,128)(2,1)}, u32[]{:S(2)}) copy-start(bf16[2048,2]{0,1:T(2,128)(2,1)} %param.33) | copy-start | bytes 24580
  11.3 47.7 %copy-start.19 = (f32[2]{0:T(128)S(1)}, f32[2]{0:T(128)}, u32[]{:S(2)}) copy-start(f32[2]{0:T(128)} %param.38) | copy-start | bytes 28
  11.3 47.7 %copy-start.18 = (f32[4,256]{1,0:T(4,128)S(1)}, f32[4,256]{1,0:T(4,128)}, u32[]{:S(2)}) copy-start(f32[4,256]{1,0:T(4,128)} %param.35) | copy-start | bytes 12292
  11.3 47.7 %copy-start.15 = (f32[4,512]{1,0:T(4,128)S(1)}, f32[4,512]{1,0:T(4,128)}, u32[]{:S(2)}) copy-start(f32[4,512]{1,0:T(4,128)} %param.36) | copy-start | bytes 24580
  11.3 47.7 %copy-start.3 = (bf16[256,2048]{1,0:T(8,128)(2,1)S(1)}, bf16[256,2048]{1,0:T(8,128)(2,1)}, u32[]{:S(2)}) copy-start(bf16[256,2048]{1,0:T(8,128)(2,1)} %param.45) | copy-start | bytes 3145732
  54.2 7.8 collective-permute-start
  59.1 3.0 copy-start.7
  60.4 1.7 copy-start.10
  61.5 104.2 %slice-start.6 = ((s8[5767168]{0:T(1024)(128)(4,1)}), s8[4194304]{0:T(1024)(128)(4,1)S(1)}, s32[]{:S(2)}) async-start(s8[5767168]{0:T(1024)(128)(4,1)} %bitcast.33), calls=%async_computation.11 | async-start | bytes 8388608
  62.1 103.6 %slice-start.7 = ((s8[5767168]{0:T(1024)(128)(4,1)}), s8[1572864]{0:T(1024)(128)(4,1)S(1)}, s32[]{:S(2)}) async-start(s8[5767168]{0:T(1024)(128)(4,1)} %bitcast.33), calls=%async_computation.12 | async-start | bytes 3145728
  62.1 0.6 copy-start.9
  157.3 18.5 %collective-permute-start.3 = (bf16[2,128,384]{2,1,0:T(8,128)(2,1)S(1)}, bf16[2,128,384]{2,1,0:T(8,128)(2,1)S(1)}, u32[]{:S(2)}, u32[]{:S(2)}) collective-permute-start(bf16[2,128,384]{2,1,0:T(8,128)(2,1)S(1)} %convert_element_type.84), channel_id=1, source_target_pairs={{0,8},{8,16},{16,24},{1,9},{9,17},{17,25},{2,10},{10,18},{18,26},{... | collective-permute-start | bytes 589832 | tf_op jit(solution)/shard_map/ppermute | solution.py:1211
  158.6 17.2 %collective-permute-start.2 = (bf16[2,128,384]{2,1,0:T(8,128)(2,1)S(1)}, bf16[2,128,384]{2,1,0:T(8,128)(2,1)S(1)}, u32[]{:S(2)}, u32[]{:S(2)}) collective-permute-start(bf16[2,128,384]{2,1,0:T(8,128)(2,1)S(1)} %convert_element_type.84), channel_id=1, source_target_pairs={{0,16},{8,24},{1,17},{9,25},{2,18},{10,26},{3,19},{11,27},{4,20},{... | collective-permute-start | bytes 589832 | tf_op jit(solution)/shard_map/ppermute | solution.py:1211
  164.2 11.6 %collective-permute-start.1 = (bf16[2,128,384]{2,1,0:T(8,128)(2,1)S(1)}, bf16[2,128,384]{2,1,0:T(8,128)(2,1)S(1)}, u32[]{:S(2)}, u32[]{:S(2)}) collective-permute-start(bf16[2,128,384]{2,1,0:T(8,128)(2,1)S(1)} %convert_element_type.84), channel_id=1, source_target_pairs={{0,24},{1,25},{2,26},{3,27},{4,28},{5,29},{6,30},{7,31}} | collective-permute-start | bytes 589832 | tf_op jit(solution)/shard_map/ppermute | solution.py:1211
  196.5 43.5 %copy-start = (bf16[256,2048]{1,0:T(8,128)(2,1)S(1)}, bf16[256,2048]{1,0:T(8,128)(2,1)}, u32[]{:S(2)}) copy-start(bf16[256,2048]{1,0:T(8,128)(2,1)} %param.25) | copy-start | bytes 3145732
  240.0 2.0 copy-start.8
  382.5 2.3 copy-start.2
  382.5 2.5 copy-start.4
  456.4 15.8 %collective-permute-start.6 = (bf16[2,128,384]{2,1,0:T(8,128)(2,1)S(1)}, bf16[2,128,384]{2,1,0:T(8,128)(2,1)S(1)}, u32[]{:S(2)}, u32[]{:S(2)}) collective-permute-start(bf16[2,128,384]{2,1,0:T(8,128)(2,1)S(1)} %pad_maximum_fusion.2), channel_id=1, source_target_pairs={{8,0},{16,8},{24,16},{9,1},{17,9},{25,17},{10,2},{18,10},{26,18},{... | collective-permute-start | bytes 589832 | tf_op jit(solution)/shard_map/ppermute | solution.py:1220
  457.7 37.4 %collective-permute-start.5 = (bf16[2,128,384]{2,1,0:T(8,128)(2,1)S(1)}, bf16[2,128,384]{2,1,0:T(8,128)(2,1)S(1)}, u32[]{:S(2)}, u32[]{:S(2)}) collective-permute-start(bf16[2,128,384]{2,1,0:T(8,128)(2,1)S(1)} %pad_maximum_fusion.2), channel_id=1, source_target_pairs={{16,0},{24,8},{17,1},{25,9},{18,2},{26,10},{19,3},{27,11},{20,4},{... | collective-permute-start | bytes 589832 | tf_op jit(solution)/shard_map/ppermute | solution.py:1220
  459.0 36.1 %collective-permute-start.4 = (bf16[2,128,384]{2,1,0:T(8,128)(2,1)S(1)}, bf16[2,128,384]{2,1,0:T(8,128)(2,1)S(1)}, u32[]{:S(2)}, u32[]{:S(2)}) collective-permute-start(bf16[2,128,384]{2,1,0:T(8,128)(2,1)S(1)} %pad_maximum_fusion.2), channel_id=1, source_target_pairs={{24,0},{25,1},{26,2},{27,3},{28,4},{29,5},{30,6},{31,7}} | collective-permute-start | bytes 589832 | tf_op jit(solution)/shard_map/ppermute | solution.py:1220
  496.1 373.4 %reduce-scatter.5.cloned.1.call-start = ((), (), s32[]{:S(2)}) async-start(), calls=%async_computation.3 | async-start | bytes 9437184 | tf_op jit(solution)/shard_map/reduce_scatter | solution.py:1423
  522.6 6.7 collective-permute-start.7
  529.3 0.6 copy-start.11
  561.7 316.5 %all-reduce.6.cloned.1.call-start = ((), (), s32[]{:S(2)}) async-start(), calls=%async_computation.4 | async-start | bytes 34603008 | tf_op jit(solution)/shard_map/psum | solution.py:1434
  575.1 10.0 %copy-start.16 = (f32[8,128]{1,0:T(8,128)S(1)}, f32[8,128]{1,0:T(8,128)}, u32[]{:S(2)}) copy-start(f32[8,128]{1,0:T(8,128)} %get-tuple-element.140) | copy-start | bytes 12292
  575.1 10.8 %copy-start.6 = (f32[2048]{0:T(1024)S(1)}, f32[2048]{0:T(1024)}, u32[]{:S(2)}) copy-start(f32[2048]{0:T(1024)} %param.27) | copy-start | bytes 24580
  575.1 10.9 %copy-start.12 = (f32[8,1024]{1,0:T(8,128)S(1)}, f32[8,1024]{1,0:T(8,128)}, u32[]{:S(2)}) copy-start(f32[8,1024]{1,0:T(8,128)} %get-tuple-element.139) | copy-start | bytes 98308
  860.9 7.3 copy-start.5
  869.4 1.9 copy-start.1
  878.3 5.7 slice-start
  879.9 4.1 slice-start.1
  889.4 9.0 slice-start.4
  890.3 8.0 slice-start.5
  890.3 13.2 %slice-start.2 = ((s8[5767168]{0:T(1024)(128)(4,1)}), s8[4194304]{0:T(1024)(128)(4,1)S(1)}, s32[]{:S(2)}) async-start(s8[5767168]{0:T(1024)(128)(4,1)} %bitcast.29), calls=%async_computation.7 | async-start | bytes 8388608
  898.4 5.2 slice-start.3
Sparse Core Ops, SparseCore 0:
  496.2 78.1 reduce-scatter.2
  578.8 71.7 reduce-scatter.4
  654.8 223.4 all-reduce.5

commit v3 on v2

--- a/solution.py
+++ b/solution.py
@@ -146,71 +146,215 @@
     return within, entry, leave, through
 
 
-def unit_lower_inverse(masks, system):
-    inverse = masks.eye - jnp.where(masks.level == 1, system, 0.0)
+def unit_lower_inverses(systems):
+    half = BLOCK // 2
+    rows = lax.broadcasted_iota(jnp.int32, (half, half), 0)
+    cols = lax.broadcasted_iota(jnp.int32, (half, half), 1)
+    level = rows ^ cols
+    eye = jnp.where(rows == cols, 1.0, 0.0)
+    parts = [system[at : at + half, at : at + half] for system in systems for at in (0, half)]
+    solved = [eye - jnp.where(level == 1, part, 0.0) for part in parts]
     width = 2
-    while width < BLOCK:
-        part = jnp.where((masks.level >= width) & (masks.level < 2 * width), system, 0.0)
-        low = inverse.astype(bf16)
-        inverse = inverse - dot(low, dot(part.astype(bf16), low).astype(bf16))
+    while width < half:
+        keep = (level >= width) & (level < 2 * width)
+        low = [inverse.astype(bf16) for inverse in solved]
+        moved = [dot(jnp.where(keep, part, 0.0).astype(bf16), inverse) for part, inverse in zip(parts, low)]
+        solved = [
+            whole_part - dot(inverse, part.astype(bf16))
+            for whole_part, inverse, part in zip(solved, low, moved)
+        ]
         width *= 2
-    return inverse
+    solved = [inverse.astype(bf16) for inverse in solved]
+    results = []
+    for index, system in enumerate(systems):
+        upper, lower = solved[2 * index], solved[2 * index + 1]
+        corner = -dot(lower, dot(system[half:, :half].astype(bf16), upper).astype(bf16))
+        results.append((upper, corner.astype(bf16), lower))
+    return results
+
+
+LEAD = 2 * HALO
+STRIDE = BLOCK + LEAD
+
+
+def cube_order(axis, step):
+    place = lax.axis_index(axis)
+    chunk = 0
+    for bit in (1, 2, 4):
+        chunk = chunk + bit * ((place // bit + step // bit) % 2)
+    return chunk
+
+
+class EdgeRows:
+    def __init__(self, line, axis, own_ref, rows_ref, edge_ref, line_sem, send_sem, recv_sem):
+        self.line, self.axis = line, axis
+        self.group, self.place = lax.axis_index(line), lax.axis_index(axis)
+        self.groups, self.last = lax.axis_size(line), lax.axis_size(axis) - 1
+        self.own_ref, self.rows_ref, self.edge_ref = own_ref, rows_ref, edge_ref
+        self.line_sem, self.send_sem, self.recv_sem = line_sem, send_sem, recv_sem
+
+    def enter(self):
+        barrier = pltpu.get_barrier_semaphore()
+        for mask in (1, 2, 4, 6):
+            pl.semaphore_signal(barrier, inc=1, device_id={self.axis: flip(self.place, mask)}, device_id_type=MESH)
+
+        @pl.when(self.receives())
+        def _():
+            pl.semaphore_signal(barrier, inc=1, device_id={self.line: self.group - 1}, device_id_type=MESH)
+
+        @pl.when(self.hands_on())
+        def _():
+            pl.semaphore_wait(barrier, 5)
+
+        @pl.when(jnp.logical_not(self.hands_on()))
+        def _():
+            pl.semaphore_wait(barrier, 4)
+
+    def hands_on(self):
+        return (self.place == self.last) & (self.group < self.groups - 1)
+
+    def receives(self):
+        return (self.place == self.last) & (self.group > 0)
+
+    def landing(self, mask):
+        block = lax.rem(flip(self.place, mask) + 1, self.last + 1)
+        return self.rows_ref.at[pl.ds(pl.multiple_of(block * STRIDE, LEAD), LEAD), :]
+
+    def onward(self):
+        return pltpu.make_async_remote_copy(
+            self.own_ref.at[pl.ds(BLOCK - LEAD, LEAD), :], self.edge_ref, self.line_sem.at[0], self.line_sem.at[1],
+            device_id={self.line: self.group + 1}, device_id_type=MESH,
+        )
+
+    def copy(self, mask, toward):
+        return pltpu.make_async_remote_copy(
+            self.landing(mask) if mask else self.edge_ref, self.landing(mask),
+            self.send_sem.at[mask + toward if mask else toward], self.recv_sem.at[mask ^ toward],
+            device_id={self.axis: flip(self.place, toward)}, device_id_type=MESH,
+        )
+
+    def wait(self, mask):
+        pltpu.make_async_remote_copy(
+            self.landing(mask), self.landing(mask), self.send_sem.at[0], self.recv_sem.at[mask],
+            device_id={self.axis: flip(self.place, 1)}, device_id_type=MESH,
+        ).wait_recv()
+
+    def start(self):
+        @pl.when(self.hands_on())
+        def _():
+            self.onward().start()
+
+        @pl.when(self.place < self.last)
+        def _():
+            self.edge_ref[...] = self.own_ref[BLOCK - LEAD :, :]
+
+        @pl.when((self.place == self.last) & (self.group == 0))
+        def _():
+            self.edge_ref[...] = jnp.zeros(self.edge_ref.shape, bf16)
+
+        @pl.when(self.receives())
+        def _():
+            pltpu.make_async_remote_copy(
+                self.edge_ref, self.edge_ref, self.line_sem.at[0], self.line_sem.at[1],
+                device_id={self.line: self.group - 1}, device_id_type=MESH,
+            ).wait_recv()
+
+        for toward in (6, 2, 4, 1):
+            self.copy(0, toward).start()
+        self.landing(0)[...] = self.edge_ref[...]
+
+    def spread(self):
+        for mask in (2, 4, 6):
+            self.wait(mask)
+            self.copy(mask, 1).start()
+        for mask in (1, 3, 5, 7):
+            self.wait(mask)
+
+    def end(self):
+        @pl.when(self.hands_on())
+        def _():
+            self.onward().wait_send()
+
+        for toward in (6, 2, 4, 1):
+            self.copy(0, toward).wait_send()
+        for mask in (2, 4, 6):
+            self.copy(mask, 1).wait_send()
 
 
 def forward_kernel(
-    heads, key_width, value_width, docs, taps, chunks,
-    meta, rows_ref, tail_ref, wq_ref, wk_ref, wv_ref, wg_ref, ws_ref, conv_ref, dvec_ref, block_ref,
-    pre_ref, act_ref, gate_ref, small_ref, scal_ref, qkv_ref, inv_ref, w_out_ref, u_ref, starts_ref, drop_ref, map_ref, blocks_ref,
-    ext, state, own_sem, send_sem, recv_sem,
+    heads, key_width, value_width, docs, taps, chunks, cube,
+    meta, rows_ref, wq_ref, wk_ref, wv_ref, wg_ref, ws_ref, conv_ref, dvec_ref,
+    pre_ref, act_ref, gate_ref, small_ref, scal_ref, qkv_ref, inv_ref, w_out_ref, u_ref, drop_ref,
+    starts_ref, map_ref, *refs,
 ):
-    chunk = pl.program_id(0)
-    gather = LineGather("seq", block_ref, blocks_ref, own_sem, send_sem, recv_sem)
-
-    @pl.when(chunk == 0)
-    def _():
-        gather.enter()
-        gather.advance(0)
-
-    for hop in range(1, gather.devices):
-        @pl.when(chunk == min(hop * chunks // gather.devices + 1, chunks - 1))
-        def _():
-            gather.advance(hop)
+    step = pl.program_id(0)
+    ext, state, drops, adds, throughs = refs[cube : cube + 5]
+    if cube:
+        all_ref = refs[0]
+        held, copy_sem, edge_ref, line_sem, edge_send, edge_recv, cube_send, cube_recv = refs[6:]
+        chunk = cube_order("head", step)
+        rows_in = CubeGather("head", rows_ref, held, None, cube_send, cube_recv, STRIDE, LEAD)
+        edges = EdgeRows("seq", "head", rows_ref, held, edge_ref, line_sem, edge_send, edge_recv)
+
+        def kept(block):
+            start = pl.multiple_of(block * STRIDE + LEAD, LEAD)
+            return pltpu.make_async_copy(
+                held.at[pl.ds(start, BLOCK), :],
+                all_ref.at[pl.ds(pl.multiple_of(block * BLOCK, BLOCK), BLOCK), :],
+                copy_sem.at[block],
+            )
+
+        @pl.when(step == 0)
+        def _():
+            edges.enter()
+            edges.start()
+            rows_in.first()
+            held[pl.ds(pl.multiple_of(chunk * STRIDE + LEAD, LEAD), BLOCK), :] = rows_ref[...]
+
+        @pl.when(step == 2)
+        def _():
+            rows_in.second()
+            rows_in.third()
+
+        @pl.when(step == 4)
+        def _():
+            rows_in.fourth()
+
+        for odd in (1, 3, 5, 7):
+            @pl.when(step == odd)
+            def _():
+                for half in range(2):
+                    rows_in.wait(odd, half)
+
+        kept(chunk).start()
+        rows = held[pl.ds(pl.multiple_of(chunk * STRIDE + LEAD, LEAD), BLOCK), :]
+    else:
+        chunk = step
+        rows = rows_ref[LEAD:, :]
 
     qw, vw = heads * key_width, heads * value_width
     mixed = 2 * qw + vw
     masks = Masks(meta, docs, chunk)
-    rows = rows_ref[...]
-    mixed_weights = ((slice(0, qw), wq_ref), (slice(qw, 2 * qw), wk_ref), (slice(2 * qw, mixed), wv_ref))
-
-    @pl.when(chunk == 0)
-    def _():
-        for span, ref in mixed_weights:
-            ext[0:HALO, span] = dot(tail_ref[...], ref[...])[HALO : 2 * HALO, :]
-
-        ident = jnp.where(
-            lax.broadcasted_iota(jnp.int32, (key_width, key_width + value_width), 0)
-            == lax.broadcasted_iota(jnp.int32, (key_width, key_width + value_width), 1),
-            1.0, 0.0,
-        )
-        for head in range(heads):
-            state[head] = ident
-
-    @pl.when(chunk > 0)
-    def _():
-        ext[0:HALO, :] = ext[BLOCK : BLOCK + HALO, :]
-
-    for span, ref in mixed_weights:
-        pre = dot(rows, ref[...])
-        ext[HALO : HALO + BLOCK, span] = pre
-        pre_ref[:, span] = pre
     gate_ref[...] = dot(rows, wg_ref[...])
     small = dot(rows, ws_ref[...])
     small_ref[...] = small
+    if cube:
+        @pl.when(step == 0)
+        def _():
+            edges.spread()
+
+        rows_ext = held[pl.ds(pl.multiple_of(chunk * STRIDE, LEAD), STRIDE), :]
+    else:
+        rows_ext = rows_ref[...]
+    for span, ref in ((slice(0, qw), wq_ref), (slice(qw, 2 * qw), wk_ref), (slice(2 * qw, mixed), wv_ref)):
+        pre = dot(rows_ext, ref[...])
+        ext[:, span] = pre
+        pre_ref[:, span] = pre[LEAD:, :]
 
     conv = jnp.zeros((BLOCK, mixed), f32)
     for lag in range(taps):
         keep = jnp.where(masks.offset >= lag, 1.0, 0.0)
-        conv = conv + conv_ref[lag : lag + 1, :] * (ext[HALO - lag : HALO - lag + BLOCK, :] * keep)
+        conv = conv + conv_ref[lag : lag + 1, :] * (ext[LEAD - lag : LEAD - lag + BLOCK, :] * keep)
     act_ref[...] = conv
     act = conv * sigmoid(conv)
 
@@ -221,6 +365,7 @@
     scal_ref[...] = scal
     scal_t = scal.T
 
+    held_heads = []
     for head in range(heads):
         act_q = act[:, head * key_width : (head + 1) * key_width]
         act_k = act[:, qw + head * key_width : qw + (head + 1) * key_width]
@@ -235,8 +380,17 @@
         within, entry, leave, through = decays(masks, scal, scal_t, head)
         beta = scal[:, heads + head : heads + head + 1]
         system = jnp.where(masks.strictly, beta * dot_nt(key, key) * within, 0.0)
-        inverse = unit_lower_inverse(masks, system).astype(bf16)
-        inv_ref[0, head] = inverse
+        held_heads.append((system, key, value, beta, entry, leave, through))
+
+    half = BLOCK // 2
+    inverses = unit_lower_inverses([part[0] for part in held_heads])
+    for head, (upper, corner, lower) in enumerate(inverses):
+        inv_ref[0, head, :half, :half] = upper
+        inv_ref[0, head, :half, half:] = jnp.zeros((half, half), bf16)
+        inv_ref[0, head, half:, :half] = corner
+        inv_ref[0, head, half:, half:] = lower
+    for head, (_, key, value, beta, entry, leave, through) in enumerate(held_heads):
+        inverse = inv_ref[0, head]
         key_f = key.astype(f32)
         w_part = dot(inverse, (beta * entry * key_f).astype(bf16)).astype(bf16)
         u_part = dot(inverse, (beta * value.astype(f32)).astype(bf16))
@@ -244,30 +398,49 @@
         u_ref[0, head] = u_part
         tail_key = (leave * key_f).astype(bf16)
         drop = dot_tn(tail_key, w_part)
-        added = dot_tn(tail_key, u_part.astype(bf16))
         drop_ref[0, head] = drop
-        before = state[head]
-        starts_ref[0, head] = before
-        after = through * before - dot(drop.astype(bf16), before.astype(bf16))
-        after = after + jnp.concatenate([jnp.zeros((key_width, key_width), f32), added], axis=1)
-        state[head] = after
-        map_ref[head] = after
-
-    @pl.when(chunk == chunks - 1)
+        drops[chunk, head] = drop.astype(bf16)
+        adds[chunk, head] = dot_tn(tail_key, u_part.astype(bf16))
+        throughs[chunk, head] = jnp.broadcast_to(through, (8, LANES))
+
+    @pl.when(step == chunks - 1)
     def _():
-        gather.leave()
+        shape = (key_width, key_width + value_width)
+        ident = jnp.where(lax.broadcasted_iota(jnp.int32, shape, 0) == lax.broadcasted_iota(jnp.int32, shape, 1), 1.0, 0.0)
+        for head in range(heads):
+            state[head] = ident
+
+        def pass_on(at, carry):
+            for head in range(heads):
+                before = state[head]
+                starts_ref[at, head] = before
+                after = throughs[at, head][0:1, 0:1] * before - dot(drops[at, head], before.astype(bf16))
+                state[head] = after + jnp.concatenate(
+                    [jnp.zeros((key_width, key_width), f32), adds[at, head]], axis=1
+                )
+            return carry
+
+        lax.fori_loop(0, chunks, pass_on, 0)
+        for head in range(heads):
+            map_ref[head] = state[head]
+        if cube:
+            rows_in.last()
+            edges.end()
+            for block in range(chunks):
+                kept(block).wait()
 
 
 def output_kernel(
-    heads, key_width, value_width, docs, others,
+    heads, key_width, value_width, docs, others, cube,
     meta, maps_ref, starts_ref, w_in_ref, u_ref, qkv_ref, scal_ref, gate_ref, gain_ref, w_output_ref,
-    core_ref, gated_ref, mixed_ref, fresh_ref, state_ref,
-    incoming,
+    core_ref, gated_ref, fresh_ref, state_ref, mixed_ref,
+    incoming, *refs,
 ):
-    chunk = pl.program_id(0)
+    step = pl.program_id(0)
+    chunk = cube_order("head", 7 - step) if cube else step
     qw = heads * key_width
 
-    @pl.when(chunk == 0)
+    @pl.when(step == 0)
     def _():
         for head in range(heads):
             state = jnp.zeros((key_width, value_width), f32)
@@ -298,7 +471,12 @@
         scale = lax.rsqrt(jnp.mean(core * core, axis=1, keepdims=True) + epsilon)
         gate = gate_ref[:, span]
         gated_ref[:, span] = (core * scale * gain * (gate * sigmoid(gate))).astype(bf16)
-    mixed_ref[...] = dot(gated_ref[...], w_output_ref[...]).astype(bf16)
+    mixed = dot(gated_ref[...], w_output_ref[...])
+    if not cube:
+        mixed_ref[...] = mixed.astype(bf16)
+        return
+
+    scatter_block(step, CubeScatter("head", mixed_ref, *refs), mixed)
 
 
 def core_grad_kernel(
@@ -446,15 +624,16 @@
 
 
 def projection_grad_kernel(
-    mixed, docs, chunks, taps,
+    mixed, docs, chunks, taps, cube,
     meta, grad_conv_ref, later_ref, edge_ref, pre_ref, grad_gate_ref, grad_small_ref, conv_ref, rows_ref,
     wq_ref, wk_ref, wv_ref, wg_ref, ws_ref,
     grad_pre_ref, grad_taps_ref, grad_rows_ref, gain_sum_ref,
-    ext,
+    ext, *refs,
 ):
-    chunk = pl.program_id(0)
-
-    @pl.when(chunk == 0)
+    step = pl.program_id(0)
+    chunk = cube_order("head", 7 - step) if cube else step
+
+    @pl.when(step == 0)
     def _():
         grad_taps_ref[...] = jnp.zeros_like(grad_taps_ref)
         gain_sum_ref[...] = jnp.zeros_like(gain_sum_ref)
@@ -486,15 +665,18 @@
     for ref in (wq_ref, wk_ref, wv_ref, wg_ref, ws_ref):
         grad = grad + dot_nt(grad_pre_ref[:, begin : begin + ref.shape[1]], ref[...])
         begin += ref.shape[1]
-    grad_rows_ref[...] = grad.astype(bf16)
     gain_sum_ref[0:1, :] += jnp.sum(grad * rows_ref[...].astype(f32), axis=0, keepdims=True)
+    if cube:
+        scatter_block(step, CubeScatter("head", grad_rows_ref, *refs), grad)
+    else:
+        grad_rows_ref[...] = grad.astype(bf16)
 
 
 MESH = pl.DeviceIdType.MESH
 ANYWHERE = pl.BlockSpec(memory_space=pl.ANY)
 
 
-def line_barrier(axis):
+def line_barrier(axis, cube=None):
     devices, place = lax.axis_size(axis), lax.axis_index(axis)
     barrier = pltpu.get_barrier_semaphore()
 
@@ -506,220 +688,241 @@
     def _():
         pl.semaphore_signal(barrier, inc=1, device_id={axis: place + 1}, device_id_type=MESH)
 
+    more = 0
+    if cube is not None:
+        for mask in (1, 2, 4):
+            pl.semaphore_signal(
+                barrier, inc=1, device_id={cube: flip(lax.axis_index(cube), mask)}, device_id_type=MESH
+            )
+        more = 3
+
     @pl.when((place > 0) & (place < devices - 1))
     def _():
-        pl.semaphore_wait(barrier, 2)
+        pl.semaphore_wait(barrier, 2 + more)
 
     @pl.when((place == 0) | (place == devices - 1))
     def _():
-        pl.semaphore_wait(barrier, 1)
-
-
-def line_sum_kernel(axis, counts, depths, *refs):
-    total = len(counts)
-    parts, sums = refs[:total], refs[total : 2 * total]
-    arrived, passed = refs[2 * total : 3 * total], refs[3 * total : 4 * total]
-    semaphores = refs[4 * total :]
-    devices = lax.axis_size(axis)
-    place = lax.axis_index(axis)
-
-    line_barrier(axis)
-
-    def rows_of(index, half, at):
-        return pl.ds(pl.multiple_of((half * counts[index] + at) * depths[index], depths[index]), depths[index])
-
-    def copy(index, half, at, target, back):
-        rows = rows_of(index, half, at)
-        slot = half * counts[index] + at
-        sent = semaphores[4 * index + 2 * back].at[slot]
-        received = semaphores[4 * index + 2 * back + 1].at[slot]
-        source, landing = (sums, sums) if back else (passed, arrived)
+        pl.semaphore_wait(barrier, 1 + more)
+
+
+class LineSum:
+    skew = 2
+    window = 4
+
+    def __init__(self, axis, counts, depths, parts, passed, arrived, sums, reduce_sems, back_sems):
+        self.axis, self.counts, self.depths = axis, counts, depths
+        self.parts, self.passed, self.arrived, self.sums = parts, passed, arrived, sums
+        self.sems = (reduce_sems, back_sems)
+        self.devices, self.place = lax.axis_size(axis), lax.axis_index(axis)
+        self.steps = max(counts) + self.skew * (self.devices - 1)
+
+    def rows_of(self, half, index, at):
+        depth = self.depths[index]
+        return pl.ds(pl.multiple_of((half * self.counts[index] + at) * depth, depth), depth)
+
+    def copy(self, half, index, at, target, back):
+        rows = self.rows_of(half, index, at)
+        slot = half * self.counts[index] + at
+        source, landing = (self.sums, self.sums) if back else (self.passed, self.arrived)
+        sent, received = self.sems[back][2 * index], self.sems[back][2 * index + 1]
         return pltpu.make_async_remote_copy(
-            source[index].at[rows, :], landing[index].at[rows, :], sent, received,
-            device_id={axis: target}, device_id_type=MESH,
+            source[index].at[rows, :], landing[index].at[rows, :], sent.at[slot], received.at[slot],
+            device_id={self.axis: target}, device_id_type=MESH,
         )
 
-    def each(step, handle):
+    def send(self, half, index, at, target, back):
+        @pl.when(at >= self.window)
+        def _():
+            self.copy(half, index, at - self.window, target, back).wait_send()
+
+        self.copy(half, index, at, target, back).start()
+
+    def each(self, handle):
+        place, last = self.place, self.devices - 1
         for half in range(2):
-            first, last = (devices - 1, 0) if half == 0 else (0, devices - 1)
+            ends = (last, 0) if half == 0 else (0, last)
             toward = place - 1 if half == 0 else place + 1
             away = place + 1 if half == 0 else place - 1
-            for index in range(total):
-                handle(half, index, step, toward, away, place == first, place == last)
-
-    steps = max(counts)
-    skew = 2
-    window = 2
-
-    def send(half, index, at, target, back):
-        @pl.when(at >= window)
-        def _():
-            copy(index, half, at - window, target, back).wait_send()
-
-        copy(index, half, at, target, back).start()
-
-    def reduce_step(step, carry):
-        def handle(half, index, step, toward, away, begin, end):
-            at = step - skew * ((devices - 1 - place) if half == 0 else place)
-
-            @pl.when((at >= 0) & (at < counts[index]))
+            for index in range(len(self.counts)):
+                handle(half, index, toward, away, place == ends[0], place == ends[1])
+
+    def reduce(self, step):
+        def handle(half, index, toward, away, begin, end):
+            late = (self.devices - 1 - self.place) if half == 0 else self.place
+            at = step - self.skew * late
+
+            @pl.when((at >= 0) & (at < self.counts[index]))
             def _():
-                rows = rows_of(index, half, at)
+                rows = self.rows_of(half, index, at)
 
                 @pl.when(begin)
                 def _():
-                    passed[index][rows, :] = parts[index][rows, :]
-                    send(half, index, at, toward, 0)
+                    self.passed[index][rows, :] = self.parts[index][rows, :]
+                    self.send(half, index, at, toward, 0)
 
                 @pl.when(jnp.logical_not(begin))
                 def _():
-                    copy(index, half, at, toward, 0).wait_recv()
-                    added = (parts[index][rows, :].astype(f32) + arrived[index][rows, :].astype(f32)).astype(bf16)
+                    self.copy(half, index, at, toward, 0).wait_recv()
+                    added = (
+                        self.parts[index][rows, :].astype(f32) + self.arrived[index][rows, :].astype(f32)
+                    ).astype(bf16)
 
                     @pl.when(jnp.logical_not(end))
                     def _():
-                        passed[index][rows, :] = added
-                        send(half, index, at, toward, 0)
+                        self.passed[index][rows, :] = added
+                        self.send(half, index, at, toward, 0)
 
                     @pl.when(end)
                     def _():
-                        sums[index][rows, :] = added
-
-        each(step, handle)
-        return carry
-
-    lax.fori_loop(0, steps + skew * (devices - 1), reduce_step, 0)
-
-    def back_step(step, carry):
-        def handle(half, index, step, toward, away, begin, end):
-            at = step - skew * (place if half == 0 else (devices - 1 - place))
-
-            @pl.when((at >= 0) & (at < counts[index]))
+                        self.sums[index][rows, :] = added
+
+        self.each(handle)
+
+    def back(self, step, given=None):
+        def handle(half, index, toward, away, begin, end):
+            late = self.place if half == 0 else (self.devices - 1 - self.place)
+            at = step - self.skew * late
+
+            @pl.when((at >= 0) & (at < self.counts[index]))
             def _():
+                if given is not None:
+                    @pl.when(end)
+                    def _():
+                        rows = self.rows_of(half, index, at)
+                        self.sums[index][rows, :] = given[index][rows, :]
+
                 @pl.when(jnp.logical_not(end))
                 def _():
-                    copy(index, half, at, away, 1).wait_recv()
+                    self.copy(half, index, at, away, 1).wait_recv()
 
                 @pl.when(jnp.logical_not(begin))
                 def _():
-                    send(half, index, at, away, 1)
-
-        each(step, handle)
+                    self.send(half, index, at, away, 1)
+
+        self.each(handle)
+
+    def settle(self, back):
+        def handle(half, index, toward, away, begin, end):
+            count = self.counts[index]
+            for at in range(max(count - self.window, 0), count):
+                @pl.when(jnp.logical_not(begin if back else end))
+                def _():
+                    self.copy(half, index, at, away if back else toward, back).wait_send()
+
+        self.each(handle)
+
+
+def line_sum_kernel(axis, cube, counts, depths, *refs):
+    total = len(counts)
+    rows_ref, grads_ref, *refs = refs
+    parts, sums, refs = refs[: total - 1], refs[total - 1 : 2 * total - 1], refs[2 * total - 1 :]
+    if cube:
+        whole_ref, refs = refs[0], refs[1:]
+    product, *refs = refs
+    parts = (product, *parts)
+    arrived, passed, refs = refs[:total], refs[total : 2 * total], refs[2 * total :]
+    share = BLOCK // depths[0]
+    tiles = counts[0] // share
+    line = LineSum(axis, counts, depths, parts, passed, arrived, sums, refs[: 2 * total], refs[2 * total : 4 * total])
+    line_barrier(axis, "head" if cube else None)
+
+    begin = max(counts)
+    final = CubeTotal(*refs[4 * total :]) if cube else None
+
+    def step_on(step, carry):
+        @pl.when((step % share == 0) & (step < tiles * share))
+        def _():
+            for half in range(2):
+                columns = pl.ds(pl.multiple_of((half * tiles + step // share) * BLOCK, BLOCK), BLOCK)
+                product[columns, :] = dot_tn(rows_ref[:, columns], grads_ref[...]).astype(bf16)
+
+        @pl.when(step < line.steps)
+        def _():
+            line.reduce(step)
+
+        @pl.when(step >= begin)
+        def _():
+            line.back(step - begin)
+
+        if cube:
+            after = begin + line.skew * line.devices
+            for stage in range(4):
+                @pl.when(step == after + 3 * stage)
+                def _():
+                    if stage:
+                        final.end(stage - 1, whole_ref)
+                    else:
+                        final.held[0] = sums[-1][: whole_ref.shape[0], :].astype(f32)
+                    if stage < 3:
+                        final.copy(stage).start()
+
         return carry
 
-    lax.fori_loop(0, steps + skew * (devices - 1), back_step, 0)
-
-    def last_step(step, carry):
-        def handle(half, index, step, toward, away, begin, end):
-            at = counts[index] - min(window, counts[index]) + step
-
-            @pl.when(at < counts[index])
-            def _():
-                @pl.when(jnp.logical_not(end))
-                def _():
-                    copy(index, half, at, toward, 0).wait_send()
-
-                @pl.when(jnp.logical_not(begin))
-                def _():
-                    copy(index, half, at, away, 1).wait_send()
-
-        each(step, handle)
-        return carry
-
-    lax.fori_loop(0, window, last_step, 0)
-
-
-def line_sum(arrays, depths, axis, collective_id):
-    if lax.axis_size(axis) == 1:
-        return arrays
+    lax.fori_loop(0, begin + line.steps, step_on, 0)
+    line.settle(0)
+    line.settle(1)
+
+
+class CubeTotal:
+    def __init__(self, held, arrived, send_sem, recv_sem):
+        self.held, self.arrived, self.send_sem, self.recv_sem = held, arrived, send_sem, recv_sem
+
+    def copy(self, stage):
+        return pltpu.make_async_remote_copy(
+            self.held.at[stage], self.arrived.at[stage], self.send_sem.at[stage], self.recv_sem.at[stage],
+            device_id={"head": flip(lax.axis_index("head"), (1, 2, 4)[stage])}, device_id_type=MESH,
+        )
+
+    def end(self, stage, total_ref):
+        self.copy(stage).wait()
+        if stage < 2:
+            self.held[stage + 1] = self.held[stage] + self.arrived[stage]
+        else:
+            total_ref[...] = self.held[stage] + self.arrived[stage]
+
+
+def line_scratch(arrays, depths, moves):
     counts = tuple(array.shape[0] // (2 * depth) for array, depth in zip(arrays, depths))
+    semaphores = []
+    for count in counts:
+        semaphores += [pltpu.SemaphoreType.DMA((2 * count,))] * 2
+    return counts, semaphores * moves
+
+
+def line_sum(rows, grads, given, depths, axis, collective_id):
+    cube = lax.axis_size("head") == 8
+    arrays = (struct((rows.shape[1], grads.shape[1]), bf16), *given)
+    counts, semaphores = line_scratch(arrays, depths, 2)
     vmem = pl.BlockSpec(memory_space=pltpu.VMEM)
-    scratch = [pltpu.VMEM(array.shape, bf16) for array in arrays] * 2
-    for count in counts:
-        scratch += [pltpu.SemaphoreType.DMA((2 * count,))] * 4
-    return pl.pallas_call(
-        functools.partial(line_sum_kernel, axis, counts, tuple(depths)),
-        in_specs=[vmem] * len(arrays),
-        out_specs=[vmem] * len(arrays),
-        out_shape=[struct(array.shape, bf16) for array in arrays],
+    scratch = [pltpu.VMEM(array.shape, bf16) for array in (arrays[0], *arrays, *arrays)] + semaphores
+    total = (8, arrays[-1].shape[1])
+    if cube:
+        scratch += [pltpu.VMEM((3,) + total, f32)] * 2 + [pltpu.SemaphoreType.DMA((3,))] * 2
+    results = pl.pallas_call(
+        functools.partial(line_sum_kernel, axis, cube, counts, tuple(depths)),
+        in_specs=[vmem] * (len(arrays) + 1),
+        out_specs=[vmem] * (len(arrays) + cube),
+        out_shape=[struct(array.shape, bf16) for array in arrays] + [struct(total, f32)] * cube,
         scratch_shapes=scratch,
         compiler_params=pltpu.CompilerParams(
             collective_id=collective_id, has_side_effects=True, vmem_limit_bytes=VMEM_LIMIT
         ),
-        cost_estimate=pl.CostEstimate(flops=10**8, bytes_accessed=600 * 10**6, transcendentals=0),
+        cost_estimate=pl.CostEstimate(flops=10**8, bytes_accessed=40 * 10**6, transcendentals=0),
         name="line_sum",
-    )(*arrays)
-
-
-class LineGather:
-    def __init__(self, axis, block, blocks, own_sem, send_sem, recv_sem):
-        self.axis, self.block, self.blocks = axis, block, blocks
-        self.own_sem, self.send_sem, self.recv_sem = own_sem, send_sem, recv_sem
-        self.devices, self.place = lax.axis_size(axis), lax.axis_index(axis)
-        self.rows = block.shape[0]
-
-    def at(self, owner):
-        return self.blocks.at[pl.ds(pl.multiple_of(owner * self.rows, self.rows), self.rows), :]
-
-    def enter(self):
-        line_barrier(self.axis)
-
-    def copy(self, hop, way):
-        owner = self.place - hop if way == 0 else self.place + hop
-        target = self.place + 1 if way == 0 else self.place - 1
-        slot = 2 * hop + way
-        return pltpu.make_async_remote_copy(
-            self.block if hop == 0 else self.at(owner), self.at(owner),
-            self.send_sem.at[slot], self.recv_sem.at[slot],
-            device_id={self.axis: target}, device_id_type=MESH,
-        )
-
-    def arrival(self, hop, way):
-        owner = self.place - hop if way == 0 else self.place + hop
-        target = self.place + 1 if way == 0 else self.place - 1
-        slot = 2 * (hop - 1) + way
-        return pltpu.make_async_remote_copy(
-            self.at(owner), self.at(owner), self.send_sem.at[slot], self.recv_sem.at[slot],
-            device_id={self.axis: target}, device_id_type=MESH,
-        )
-
-    def sends(self, hop, way):
-        if way == 0:
-            return (self.place >= hop) & (self.place < self.devices - 1)
-        return (self.place + hop < self.devices) & (self.place > 0)
-
-    def comes(self, hop, way):
-        return self.place >= hop if way == 0 else self.place + hop < self.devices
-
-    def own(self):
-        return pltpu.make_async_copy(self.block, self.at(self.place), self.own_sem)
-
-    def advance(self, hop):
-        if hop == 0:
-            self.own().start()
-        for way in range(2):
-            if hop:
-                @pl.when(self.comes(hop, way))
-                def _():
-                    self.arrival(hop, way).wait_recv()
-
-            if hop < self.devices - 1:
-                @pl.when(self.sends(hop, way))
-                def _():
-                    self.copy(hop, way).start()
-
-    def leave(self):
-        self.own().wait()
-        for hop in range(self.devices - 1):
-            for way in range(2):
-                @pl.when(self.sends(hop, way))
-                def _():
-                    self.copy(hop, way).wait_send()
+    )(rows, grads, *given)
+    if not cube:
+        results = [*results, lax.psum(results[-1][:8].astype(f32), "head")]
+    return results
 
 
 def whole(shape):
     zeros = (0,) * len(shape)
     return pl.BlockSpec(tuple(shape), lambda step: zeros)
+
+
+def held(shape):
+    zeros = (0,) * len(shape)
+    return pl.BlockSpec(tuple(shape), lambda step: zeros, pipeline_mode=pl.Buffered(1))
 
 
 def by_rows(width, chunks=None):
@@ -740,12 +943,26 @@
 
 def feed_kernel(
     axis, devices, rows,
-    own_ref, grad_hidden_ref, w_gate_ref, w_up_ref,
-    blocks_ref, hidden_ref, grad_gate_ref, grad_up_ref, total_ref,
-    parts, arrived, gather_send, gather_recv, chain_send, chain_recv,
+    own_ref, *refs,
 ):
+    given, kept, refs = refs[:4], refs[4:9], refs[9:]
+    total_ref, *refs = refs
+    inside, refs = refs[:8], refs[8:]
+    inside = (*inside, inside[0])
+    grads_ref, w_gate_ref, w_up_ref, w_down_ref = inside[:4]
+    blocks_ref, hidden_ref, grad_gate_ref, grad_up_ref, part_ref = inside[4:]
+    parts, arrived, gather_send, gather_recv, chain_send, chain_recv, load_sem, store_sem = refs
     place = lax.axis_index(axis)
     piece = rows // 2
+
+    def load(index):
+        return pltpu.make_async_copy(given[index], inside[index], load_sem.at[index])
+
+    def store(index):
+        return pltpu.make_async_copy(inside[4 + index], kept[index], store_sem.at[index])
+
+    for index in (3, 0, 1, 2):
+        load(index).start()
     line_barrier(axis)
 
     def span(block, half):
@@ -762,12 +979,15 @@
             gather_send.at[slot], gather_recv.at[slot], device_id={axis: target}, device_id_type=MESH,
         )
 
-    def chain(block, way, half, at):
+    def quarter(block, part):
+        return pl.ds(pl.multiple_of(block * rows + part * (rows // 4), rows // 4), rows // 4)
+
+    def chain(block, way, part, at):
         target = at + 1 - 2 * way
         landing = jnp.where((block == target) & (way == 0), devices, block)
-        slot = (way * devices + block) * 2 + half
+        slot = (way * devices + block) * 4 + part
         return pltpu.make_async_remote_copy(
-            parts.at[span(block, half), :], arrived.at[span(landing, half), :],
+            parts.at[quarter(block, part), :], arrived.at[quarter(landing, part), :],
             chain_send.at[slot], chain_recv.at[slot], device_id={axis: target}, device_id_type=MESH,
         )
 
@@ -787,8 +1007,14 @@
                     for half in range(2):
                         gather(place, 0, side, half).start()
 
+            for index in range(4):
+                load(index).wait()
+
         @pl.when((owner >= 0) & (owner < devices))
         def _():
+            here = full(owner)
+            grad_hidden = dot_nt(grads_ref[here, :], w_down_ref[...])
+
             @pl.when(step > 0)
             def _():
                 for half in range(2):
@@ -798,14 +1024,12 @@
                     def _():
                         gather(owner, hop, way, half).start()
 
-            here = full(owner)
             block = blocks_ref[here, :]
             gate_pre = dot(block, w_gate_ref[...])
             up_pre = dot(block, w_up_ref[...])
             sigma = sigmoid(gate_pre)
             act = gate_pre * sigma
             hidden_ref[here, :] = (act * up_pre).astype(bf16)
-            grad_hidden = grad_hidden_ref[here, :]
             grad_gate_ref[here, :] = (grad_hidden * up_pre * (sigma * (1.0 + gate_pre * (1.0 - sigma)))).astype(bf16)
             grad_up_ref[here, :] = (grad_hidden * act).astype(bf16)
             grad = dot_nt(grad_gate_ref[here, :], w_gate_ref[...]) + dot_nt(grad_up_ref[here, :], w_up_ref[...])
@@ -820,33 +1044,44 @@
 
         @pl.when((way == 1) & (step > 0))
         def _():
-            for side in (1, 0):
-                block = devices - 1 - hop if side == 1 else hop
-                begins = place == devices - 1 if side == 1 else place == 0
-                valid = (block >= 0) & (block < place) if side == 1 else (block < devices) & (block > place)
+            for turn in range(2):
+                side = jnp.where(2 * place < devices, turn, 1 - turn)
+                block = jnp.where(side == 1, devices - 1 - hop, hop)
+                begins = place == jnp.where(side == 1, devices - 1, 0)
+                valid = jnp.where(side == 1, block < place, block > place)
 
                 @pl.when(valid)
                 def _():
-                    for half in range(2):
+                    for part in range(4):
                         @pl.when(jnp.logical_not(begins))
                         def _():
-                            chain(block, side, half, place + 2 * side - 1).wait_recv()
-                            at = span(block, half)
+                            chain(block, side, part, place + 2 * side - 1).wait_recv()
+                            at = quarter(block, part)
                             parts[at, :] = (parts[at, :].astype(f32) + arrived[at, :].astype(f32)).astype(bf16)
 
-                        chain(block, side, half, place).start()
+                        chain(block, side, part, place).start()
 
         return carry
 
     lax.fori_loop(0, 2 * devices - 1, event, 0)
+
+    for index in range(4):
+        store(index).start()
+
+    def feed_part(block, carry):
+        part_ref[full(block), :] = dot(hidden_ref[full(block), :], w_down_ref[...]).astype(bf16)
+        return carry
+
+    lax.fori_loop(0, devices, feed_part, 0)
+    store(4).start()
 
     for side, landing, comes in ((1, place, place < devices - 1), (0, devices, place > 0)):
         @pl.when(comes)
         def _():
-            for half in range(2):
-                chain(place, side, half, place + 2 * side - 1).wait_recv()
-                at = pl.ds(half * piece, piece)
-                total_ref[at, :] += arrived[span(landing, half), :].astype(f32)
+            for part in range(4):
+                chain(place, side, part, place + 2 * side - 1).wait_recv()
+                at = pl.ds(part * (rows // 4), rows // 4)
+                total_ref[at, :] += arrived[quarter(landing, part), :].astype(f32)
 
     def gather_end(step, carry):
         hop = step // 2
@@ -866,41 +1101,46 @@
     def chain_end(block, carry):
         @pl.when(block < place)
         def _():
-            for half in range(2):
-                chain(block, 1, half, place).wait_send()
+            for part in range(4):
+                chain(block, 1, part, place).wait_send()
 
         @pl.when(block > place)
         def _():
-            for half in range(2):
-                chain(block, 0, half, place).wait_send()
+            for part in range(4):
+                chain(block, 0, part, place).wait_send()
 
         return carry
 
     lax.fori_loop(0, devices, chain_end, 0)
-
-
-def feed(own, grad_hidden, w_gate, w_up, axis, collective_id):
+    for index in range(5):
+        store(index).wait()
+
+
+def feed(own, grads, w_gate, w_up, w_down, axis, collective_id):
     devices = lax.axis_size(axis)
     rows, width = own.shape
     units = w_gate.shape[1]
     vmem = pl.BlockSpec(memory_space=pltpu.VMEM)
     moves = pltpu.SemaphoreType.DMA((4 * devices,))
+    chains = pltpu.SemaphoreType.DMA((8 * devices,))
+    given = (grads, w_gate, w_up, w_down)
+    kept = [struct((devices * rows, width), bf16)] + [struct((devices * rows, units), bf16)] * 3
+    kept += [struct((devices * rows, width), bf16)]
     return pl.pallas_call(
         functools.partial(feed_kernel, axis, devices, rows),
-        in_specs=[vmem] * 4,
-        out_specs=[vmem] * 5,
-        out_shape=[struct((devices * rows, width), bf16)]
-        + [struct((devices * rows, units), bf16)] * 3
-        + [struct((rows, width), f32)],
+        in_specs=[vmem] + [ANYWHERE] * 4,
+        out_specs=[ANYWHERE] * 5 + [vmem],
+        out_shape=kept + [struct((rows, width), f32)],
         scratch_shapes=[
+            *(pltpu.VMEM(array.shape, array.dtype) for array in (*given, *kept[:4])),
             pltpu.VMEM((devices * rows, width), bf16), pltpu.VMEM(((devices + 1) * rows, width), bf16),
-            moves, moves, moves, moves,
+            moves, moves, chains, chains, pltpu.SemaphoreType.DMA((4,)), pltpu.SemaphoreType.DMA((5,)),
         ],
         compiler_params=pltpu.CompilerParams(
-            collective_id=collective_id, has_side_effects=True, vmem_limit_bytes=60 * 1024 * 1024
+            collective_id=collective_id, has_side_effects=True, vmem_limit_bytes=61 * 1024 * 1024
         ),
         name="feed",
-    )(own, grad_hidden, w_gate, w_up)
+    )(own, grads, w_gate, w_up, w_down)
 
 
 def flip(index, mask):
@@ -923,16 +1163,17 @@
     THIRD = ((2, 1, 1), (4, 0, 1))
     FOURTH = ((6, 0, 1), (6, 1, 1))
 
-    def __init__(self, axis, own_ref, all_ref, own_sem, send_sem, recv_sem):
+    def __init__(self, axis, own_ref, all_ref, own_sem, send_sem, recv_sem, stride=None, lead=0):
         self.axis, self.own_ref, self.all_ref = axis, own_ref, all_ref
+        self.stride, self.lead = stride or own_ref.shape[0], lead
         self.own_sem, self.send_sem, self.recv_sem = own_sem, send_sem, recv_sem
         self.place = lax.axis_index(axis)
         self.rows = own_ref.shape[0]
         self.piece = self.rows // 2
 
     def part(self, mask, half):
-        start = flip(self.place, mask) * self.rows + half * self.piece
-        return self.all_ref.at[pl.ds(pl.multiple_of(start, self.piece), self.piece), :]
+        start = flip(self.place, mask) * self.stride + self.lead + half * self.piece
+        return self.all_ref.at[pl.ds(pl.multiple_of(start, LEAD), self.piece), :]
 
     def copy(self, mask, half, toward):
         source = self.part(mask, half) if mask else self.own_ref.at[pl.ds(half * self.piece, self.piece), :]
@@ -953,10 +1194,11 @@
         return pltpu.make_async_copy(self.own_ref, self.all_ref.at[pl.ds(start, self.rows), :], self.own_sem)
 
     def first(self):
-        cube_barrier(self.axis, self.place)
+        if self.own_sem is not None:
+            cube_barrier(self.axis, self.place)
+            self.own().start()
         for move in self.FIRST:
             self.copy(*move).start()
-        self.own().start()
 
     def second(self):
         self.wait(2, 0)
@@ -976,10 +1218,11 @@
             self.copy(*move).start()
 
     def last(self):
-        for mask in (1, 3, 5, 7):
-            for half in range(2):
-                self.wait(mask, half)
-        self.own().wait()
+        if self.own_sem is not None:
+            for mask in (1, 3, 5, 7):
+                for half in range(2):
+                    self.wait(mask, half)
+            self.own().wait()
         for move in self.FIRST + self.SECOND + self.THIRD + self.FOURTH:
             self.copy(*move).wait_send()
 
@@ -1015,15 +1258,14 @@
 
 def feed_grads_kernel(
     axis, cube,
-    own_ref, blocks_ref, grads_ref, w_down_ref, hidden_ref, grad_gate_ref, grad_up_ref,
+    own_ref, blocks_ref, grads_ref, hidden_ref, grad_gate_ref, grad_up_ref,
     *refs,
 ):
-    outs = refs[: 5 if cube else 4]
-    down_ref, gate_ref, up_ref, part_ref = outs[:4]
+    down_ref, gate_ref, up_ref = refs[:3]
     step = pl.program_id(0)
     steps = pl.num_programs(0)
     if cube:
-        gather = CubeGather(axis, own_ref, outs[4], *refs[5:])
+        gather = CubeGather(axis, own_ref, refs[3], *refs[4:])
         for at, phase in ((0, gather.first), (2, gather.second), (4, gather.third), (6, gather.fourth)):
             @pl.when(step == at)
             def _():
@@ -1032,164 +1274,137 @@
     gate_ref[...] = dot_tn(blocks_ref[...], grad_gate_ref[...]).astype(bf16)
     up_ref[...] = dot_tn(blocks_ref[...], grad_up_ref[...]).astype(bf16)
     down_ref[...] = dot_tn(hidden_ref[...], grads_ref[...]).astype(bf16)
-    part_ref[...] = dot(hidden_ref[...], w_down_ref[...]).astype(bf16)
     if cube:
         @pl.when(step == steps - 1)
         def _():
             gather.last()
 
 
-def feed_grads(own, blocks, grads, w_down, hidden, grad_gate, grad_up, axis, collective_id):
+def feed_grads(own, blocks, grads, hidden, grad_gate, grad_up, axis, collective_id):
     cube = lax.axis_size(axis) == 8
     rows, width = blocks.shape
     units = hidden.shape[1]
     tall = pl.BlockSpec((rows, BLOCK), lambda step: (0, step))
     down = pl.BlockSpec((units, BLOCK), lambda step: (0, step))
     flat = pl.BlockSpec((BLOCK, units), lambda step: (step, 0))
-    held = pl.BlockSpec((rows, units), lambda step: (0, 0), pipeline_mode=pl.Buffered(1))
-    *results, gathered = pl.pallas_call(
+    fixed = held((rows, units))
+    results = pl.pallas_call(
         functools.partial(feed_grads_kernel, axis, cube),
         grid=(width // BLOCK,),
-        in_specs=[ANYWHERE, tall, tall, down, held, held, held],
-        out_specs=[down, flat, flat, tall] + [ANYWHERE] * cube,
+        in_specs=[ANYWHERE, tall, tall, fixed, fixed, fixed],
+        out_specs=[down, flat, flat] + [ANYWHERE] * cube,
         out_shape=[
             struct((units, width), bf16), struct((width, units), bf16), struct((width, units), bf16),
-            struct((rows, width), bf16),
         ] + [struct((8 * own.shape[0], width), bf16)] * cube,
         scratch_shapes=CUBE_SEMAPHORES if cube else [],
         compiler_params=params(collective_id if cube else None),
         name="feed_grads",
-    )(own, blocks, grads, w_down, hidden, grad_gate, grad_up)
-    if not cube:
-        results, gathered = [*results, gathered], lax.all_gather(own, axis, axis=0, tiled=True)
-    return (*results, gathered)
-
-
-def cube_sum_kernel(axis, part_ref, total_ref, held, arrived, send_sem, recv_sem):
-    place = lax.axis_index(axis)
-    cube_barrier(axis, place)
-    held[0] = part_ref[...]
-    for stage, mask in enumerate((1, 2, 4)):
-        copy = pltpu.make_async_remote_copy(
-            held.at[stage], arrived.at[stage], send_sem.at[stage], recv_sem.at[stage],
-            device_id={axis: flip(place, mask)}, device_id_type=MESH,
+    )(own, blocks, grads, hidden, grad_gate, grad_up)
+    return results if cube else (*results, lax.all_gather(own, axis, axis=0, tiled=True))
+
+
+class CubeScatter:
+    def __init__(self, axis, total_ref, given, other, leaving, coming, waiting, send_sem, recv_sem):
+        self.axis, self.total_ref = axis, total_ref
+        self.given, self.other, self.leaving, self.coming, self.waiting = given, other, leaving, coming, waiting
+        self.send_sem, self.recv_sem = send_sem, recv_sem
+        self.place = lax.axis_index(axis)
+        self.piece = total_ref.shape[0] // 2
+
+    def slot(self, index, half):
+        return pl.ds((2 * index + half) * self.piece, self.piece)
+
+    def core_copy(self, mask, half):
+        at = self.slot(mask // 2, half)
+        return pltpu.make_async_remote_copy(
+            self.given.at[at, :], self.other.at[at, :],
+            self.send_sem.at[0, mask // 2, half], self.recv_sem.at[0, mask // 2, half],
+            device_id={self.axis: flip(self.place, 1)}, device_id_type=MESH,
         )
-        copy.start()
-        copy.wait()
-        if stage < 2:
-            held[stage + 1] = held[stage] + arrived[stage]
+
+    def landing(self, index, toward):
+        return (toward // 2 - 1) * 2 + (1 if index else 0)
+
+    def chip_copy(self, index, half, toward):
+        return pltpu.make_async_remote_copy(
+            self.leaving.at[self.slot(index, half), :],
+            self.coming.at[self.slot(self.landing(index, toward), half), :],
+            self.send_sem.at[toward // 2, index, half], self.recv_sem.at[toward // 2, 1 if index else 0, half],
+            device_id={self.axis: flip(self.place, toward)}, device_id_type=MESH,
+        )
+
+    def arrived(self, index, half, toward):
+        self.chip_copy(index, half, toward).wait_recv()
+        return self.coming[self.slot(self.landing(index, toward), half), :].astype(f32)
+
+    def send(self, index, half, toward, values):
+        self.leaving[self.slot(index, half), :] = values.astype(bf16)
+        self.chip_copy(index, half, toward).start()
+
+    def take(self, mask, block):
+        piece = self.piece
+        if mask % 2:
+            self.given[pl.ds(mask // 2 * 2 * piece, 2 * piece), :] = block.astype(bf16)
+            for half in range(2):
+                self.core_copy(mask, half).start()
+            return
+        parts = []
+        for half in range(2):
+            self.core_copy(mask + 1, half).wait_recv()
+            parts.append(
+                block[half * piece : (half + 1) * piece, :]
+                + self.other[self.slot(mask // 2, half), :].astype(f32)
+            )
+        if mask == 6:
+            self.send(0, 0, 2, parts[0])
+            self.send(0, 1, 4, parts[1])
+        elif mask == 4:
+            self.send(2, 1, 4, parts[1])
+            self.waiting[0] = parts[0]
+        elif mask == 2:
+            self.send(1, 0, 2, parts[0])
+            self.waiting[1] = parts[1]
         else:
-            total_ref[...] = held[stage] + arrived[stage]
-
-
-def cube_sum(part, axis, collective_id):
-    if lax.axis_size(axis) != 8:
-        return lax.psum(part, axis)
-    vmem = pl.BlockSpec(memory_space=pltpu.VMEM)
-    return pl.pallas_call(
-        functools.partial(cube_sum_kernel, axis),
-        in_specs=[vmem],
-        out_specs=vmem,
-        out_shape=struct(part.shape, f32),
-        scratch_shapes=[
-            pltpu.VMEM((3,) + part.shape, f32), pltpu.VMEM((3,) + part.shape, f32),
-            pltpu.SemaphoreType.DMA((3,)), pltpu.SemaphoreType.DMA((3,)),
-        ],
-        compiler_params=pltpu.CompilerParams(collective_id=collective_id, has_side_effects=True),
-        name="cube_sum",
-    )(part)
-
-
-def cube_scatter_kernel(axis, rows, parts_ref, total_ref, other, leaving, coming, send_sem, recv_sem):
-    place = lax.axis_index(axis)
-    piece = rows // 2
-
-    def span(mask, half):
-        return pl.ds(pl.multiple_of(flip(place, mask) * rows + half * piece, piece), piece)
-
-    def slot(index, half):
-        return pl.ds((2 * index + half) * piece, piece)
-
-    def core_copy(mask, half):
-        return pltpu.make_async_remote_copy(
-            parts_ref.at[span(mask, half), :], other.at[slot(mask // 2, half), :],
-            send_sem.at[0, mask // 2, half], recv_sem.at[0, mask // 2, half],
-            device_id={axis: flip(place, 1)}, device_id_type=MESH,
-        )
-
-    def chip_copy(index, half, toward):
-        landing = (toward // 2 - 1) * 2 + (1 if index else 0)
-        return pltpu.make_async_remote_copy(
-            leaving.at[slot(index, half), :], coming.at[slot(landing, half), :],
-            send_sem.at[toward // 2, index, half], recv_sem.at[toward // 2, 1 if index else 0, half],
-            device_id={axis: flip(place, toward)}, device_id_type=MESH,
-        )
-
-    cube_barrier(axis, place)
-    for mask in (7, 3, 5, 1):
-        for half in range(2):
-            core_copy(mask, half).start()
-
-    def chip_part(mask, half):
-        core_copy(mask + 1, half).wait_recv()
-        return parts_ref[span(mask, half), :].astype(f32) + other[slot(mask // 2, half), :].astype(f32)
-
-    def arrived(index, half, toward):
-        chip_copy(index, half, toward).wait_recv()
-        landing = (toward // 2 - 1) * 2 + (1 if index else 0)
-        return coming[slot(landing, half), :].astype(f32)
-
-    leaving[slot(0, 0), :] = chip_part(6, 0).astype(bf16)
-    chip_copy(0, 0, 2).start()
-    leaving[slot(0, 1), :] = chip_part(6, 1).astype(bf16)
-    chip_copy(0, 1, 4).start()
-    leaving[slot(1, 0), :] = chip_part(2, 0).astype(bf16)
-    chip_copy(1, 0, 2).start()
-    leaving[slot(2, 1), :] = chip_part(4, 1).astype(bf16)
-    chip_copy(2, 1, 4).start()
-    by_x = chip_part(2, 1)
-    leaving[slot(1, 1), :] = (by_x + arrived(0, 1, 4)).astype(bf16)
-    chip_copy(1, 1, 2).start()
-    by_y = chip_part(4, 0)
-    leaving[slot(2, 0), :] = (by_y + arrived(0, 0, 2)).astype(bf16)
-    chip_copy(2, 0, 4).start()
-    for half in range(2):
-        total_ref[half * piece : (half + 1) * piece, :] = chip_part(0, half)
-    for half in (0, 1):
-        at = slice(half * piece, (half + 1) * piece)
-        if half == 0:
-            total_ref[at, :] += arrived(1, 0, 2)
-            total_ref[at, :] += arrived(2, 0, 4)
-        else:
-            total_ref[at, :] += arrived(2, 1, 4)
-            total_ref[at, :] += arrived(1, 1, 2)
-    for mask in (7, 3, 5, 1):
-        for half in range(2):
-            core_copy(mask, half).wait_send()
-    for index, half, toward in ((0, 0, 2), (0, 1, 4), (1, 0, 2), (2, 1, 4), (1, 1, 2), (2, 0, 4)):
-        chip_copy(index, half, toward).wait_send()
-
-
-def cube_scatter(parts, axis, collective_id):
-    if lax.axis_size(axis) != 8:
-        return lax.psum_scatter(parts, axis, scatter_dimension=0, tiled=True).astype(f32)
-    rows, width = parts.shape[0] // 8, parts.shape[1]
-    vmem = pl.BlockSpec(memory_space=pltpu.VMEM)
-    return pl.pallas_call(
-        functools.partial(cube_scatter_kernel, axis, rows),
-        in_specs=[vmem],
-        out_specs=vmem,
-        out_shape=struct((rows, width), f32),
-        scratch_shapes=[
-            pltpu.VMEM((4 * rows, width), bf16), pltpu.VMEM((3 * rows, width), bf16),
-            pltpu.VMEM((4 * rows, width), bf16),
-            pltpu.SemaphoreType.DMA((3, 4, 2)), pltpu.SemaphoreType.DMA((3, 4, 2)),
-        ],
-        compiler_params=pltpu.CompilerParams(
-            collective_id=collective_id, has_side_effects=True, vmem_limit_bytes=VMEM_LIMIT
-        ),
-        name="cube_scatter",
-    )(parts)
+            self.total_ref[0:piece, :] = parts[0]
+            self.total_ref[piece:, :] = parts[1]
+
+    def finish(self):
+        piece = self.piece
+        self.send(2, 0, 4, self.waiting[0] + self.arrived(0, 0, 2))
+        self.send(1, 1, 2, self.waiting[1] + self.arrived(0, 1, 4))
+        self.total_ref[0:piece, :] += self.arrived(1, 0, 2)
+        self.total_ref[piece:, :] += self.arrived(2, 1, 4)
+        self.total_ref[0:piece, :] += self.arrived(2, 0, 4)
+        self.total_ref[piece:, :] += self.arrived(1, 1, 2)
+        for mask in (7, 5, 3, 1):
+            for half in range(2):
+                self.core_copy(mask, half).wait_send()
+        for index, half, toward in ((0, 0, 2), (0, 1, 4), (1, 0, 2), (2, 1, 4), (1, 1, 2), (2, 0, 4)):
+            self.chip_copy(index, half, toward).wait_send()
+
+
+def scatter_block(step, scatter, block):
+    @pl.when(step == 0)
+    def _():
+        cube_barrier("head", scatter.place)
+
+    for mask in range(8):
+        @pl.when(step == 7 - mask)
+        def _():
+            scatter.take(mask, block)
+
+    @pl.when(step == 7)
+    def _():
+        scatter.finish()
+
+
+def cube_scatter_scratch(rows, width):
+    return [
+        pltpu.VMEM((4 * rows, width), bf16), pltpu.VMEM((4 * rows, width), bf16),
+        pltpu.VMEM((3 * rows, width), bf16), pltpu.VMEM((4 * rows, width), bf16),
+        pltpu.VMEM((2, rows // 2, width), f32),
+        pltpu.SemaphoreType.DMA((3, 4, 2)), pltpu.SemaphoreType.DMA((3, 4, 2)),
+    ]
 
 
 def params(collective_id=None):
@@ -1199,6 +1414,35 @@
         collective_id=collective_id,
         has_side_effects=collective_id is not None,
     )
+
+
+def widen_kernel(cuts, down_in, gate_in, up_in, all_in, output_in, down, gate, up, *refs):
+    *columns, output = refs
+    for source, result in ((down_in, down), (gate_in, gate), (up_in, up), (output_in, output)):
+        result[...] = source[...].astype(f32)
+    begin = 0
+    for cut, result in zip(cuts, columns):
+        result[...] = all_in[:, begin : begin + cut].astype(f32)
+        begin += cut
+
+
+def widen(ff_grads, grad_w_all, cuts, grad_w_output):
+    sources = (*ff_grads, grad_w_all, grad_w_output)
+    steps = 8 if ff_grads[0].shape[0] % 128 == 0 else 4
+    shapes = [array.shape for array in ff_grads] + [(grad_w_all.shape[0], cut) for cut in cuts] + [grad_w_output.shape]
+
+    def part(shape):
+        return pl.BlockSpec((shape[0] // steps, shape[1]), lambda step: (step, 0))
+
+    return pl.pallas_call(
+        functools.partial(widen_kernel, cuts),
+        grid=(steps,),
+        in_specs=[part(array.shape) for array in sources],
+        out_specs=[part(shape) for shape in shapes],
+        out_shape=[struct(shape, f32) for shape in shapes],
+        compiler_params=params(),
+        name="widen",
+    )(*sources)
 
 
 def struct(shape, dtype):
@@ -1263,8 +1507,6 @@
 
     inputs_f = inputs.astype(f32)
     normed = rms_scale(inputs_f, first_gain).astype(bf16)
-    block_rows = cube_gather(normed, "head", 4)
-    tail = from_previous(block_rows[seq_rows - 2 * HALO :])
     meta = jnp.concatenate(
         [(seq_index * seq_rows).astype(jnp.int32)[None], slot_starts(doc_lengths)]
     )
@@ -1280,73 +1522,121 @@
     dvec = dvec.at[0, :heads].set(decay_bias).at[1, :heads].set(-jnp.exp(decay_log))
     map_shape = (heads, key_width, key_width + value_width)
 
-    (pre, conv, gate, small, scal, qkv, inverse, w_part, u_part, starts, drop, block_map, grad_block_two) = pl.pallas_call(
-        functools.partial(forward_kernel, *sizes, taps, chunks),
+    cube = head_total == 8 and chunks == 8 and row_count == BLOCK
+    if cube:
+        rows_given, rows_spec = normed, held(normed.shape)
+
+        def at_step(step):
+            return cube_order("head", step)
+    else:
+        block_rows = lax.all_gather(normed, "head", axis=0, tiled=True)
+        tail = from_previous(block_rows[seq_rows - LEAD :])
+        blocks = block_rows.reshape(chunks, BLOCK, model_width)
+        leads = jnp.concatenate([tail[None], blocks[:-1, BLOCK - LEAD :]], axis=0)
+        rows_given = jnp.concatenate([leads, blocks], axis=1).reshape(chunks * STRIDE, model_width)
+        rows_spec = pl.BlockSpec((STRIDE, model_width), lambda step: (step, 0))
+
+        def at_step(step):
+            return step
+
+    def rows_out(width):
+        return pl.BlockSpec((BLOCK, width), lambda step: (at_step(step), 0))
+
+    def chunk_out(shape):
+        return pl.BlockSpec((1,) + tuple(shape), lambda step: (at_step(step),) + (0,) * len(shape))
+
+    results = pl.pallas_call(
+        functools.partial(forward_kernel, *sizes, taps, chunks, cube),
         grid=(chunks,),
         in_specs=[
-            SCALARS, by_rows(model_width), whole((2 * HALO, model_width)),
-            *(whole(weight.shape) for weight in weights), whole(conv_all.shape), whole(dvec.shape), ANYWHERE,
+            SCALARS, rows_spec, *(held(weight.shape) for weight in weights), whole(conv_all.shape),
+            whole(dvec.shape),
         ],
         out_specs=[
-            by_rows(mixed_width), by_rows(mixed_width), by_rows(vw), by_rows(LANES), by_rows(LANES),
-            by_rows(mixed_width),
-            by_chunk((heads, BLOCK, BLOCK)), by_chunk((heads, BLOCK, key_width)),
-            by_chunk((heads, BLOCK, value_width)), by_chunk(map_shape),
-            by_chunk((heads, key_width, key_width)), whole(map_shape), ANYWHERE,
-        ],
+            rows_out(mixed_width), rows_out(mixed_width), rows_out(vw), rows_out(LANES), rows_out(LANES),
+            rows_out(mixed_width),
+            chunk_out((heads, BLOCK, BLOCK)), chunk_out((heads, BLOCK, key_width)),
+            chunk_out((heads, BLOCK, value_width)), chunk_out((heads, key_width, key_width)),
+            whole((chunks,) + map_shape), whole(map_shape),
+        ] + [ANYWHERE] * cube,
         out_shape=[
             struct((seq_rows, mixed_width), f32), struct((seq_rows, mixed_width), f32),
             struct((seq_rows, vw), f32), struct((seq_rows, LANES), f32), struct((seq_rows, LANES), f32),
             struct((seq_rows, mixed_width), bf16),
             struct((chunks, heads, BLOCK, BLOCK), bf16), struct((chunks, heads, BLOCK, key_width), bf16),
-            struct((chunks, heads, BLOCK, value_width), f32), struct((chunks,) + map_shape, f32),
-            struct((chunks, heads, key_width, key_width), f32), struct(map_shape, f32),
-            struct((lax.axis_size("seq") * row_count, model_width), bf16),
-        ],
+            struct((chunks, heads, BLOCK, value_width), f32),
+            struct((chunks, heads, key_width, key_width), f32),
+            struct((chunks,) + map_shape, f32), struct(map_shape, f32),
+        ] + [struct((seq_rows, model_width), bf16)] * cube,
         scratch_shapes=[
-            pltpu.VMEM((BLOCK + HALO, mixed_width), f32), pltpu.VMEM(map_shape, f32), pltpu.SemaphoreType.DMA,
-            pltpu.SemaphoreType.DMA((2 * lax.axis_size("seq"),)), pltpu.SemaphoreType.DMA((2 * lax.axis_size("seq"),)),
-        ],
-        compiler_params=params(2),
+            pltpu.VMEM((STRIDE, mixed_width), f32), pltpu.VMEM(map_shape, f32),
+            pltpu.VMEM((chunks, heads, key_width, key_width), bf16),
+            pltpu.VMEM((chunks, heads, key_width, value_width), f32),
+            pltpu.VMEM((chunks, heads, 8, LANES), f32),
+        ] + [
+            pltpu.VMEM((chunks * STRIDE, model_width), bf16), pltpu.SemaphoreType.DMA((chunks,)),
+            pltpu.VMEM((LEAD, model_width), bf16), pltpu.SemaphoreType.DMA((2,)),
+            pltpu.SemaphoreType.DMA((8,)), pltpu.SemaphoreType.DMA((8,)), *CUBE_SEMAPHORES[1:],
+        ] * cube,
+        compiler_params=params(2 if cube else None),
         name="mixer_forward",
-    )(meta, block_rows, tail, *weights, conv_all, dvec, grad_low)
+    )(meta, rows_given, *weights, conv_all, dvec)
+    (pre, conv, gate, small, scal, qkv, inverse, w_part, u_part, drop, starts, block_map) = results[:12]
+    if cube:
+        block_rows = results[12]
 
     earlier = from_earlier(block_map.astype(bf16), "seq")
+    grad_block_two = lax.all_gather(grad_low, "seq", axis=0, tiled=True)
     gain_row = head_gain[None, :]
-    core, gated, mixed_part, fresh, states = pl.pallas_call(
-        functools.partial(output_kernel, *sizes, others),
+    def last_first(step):
+        return cube_order("head", 7 - step) if cube else step
+
+    def rows_back(width):
+        return pl.BlockSpec((BLOCK, width), lambda step: (last_first(step), 0))
+
+    def chunk_back(shape):
+        return pl.BlockSpec((1,) + tuple(shape), lambda step: (last_first(step),) + (0,) * len(shape))
+
+    core, gated, fresh, states, mixed_part = pl.pallas_call(
+        functools.partial(output_kernel, *sizes, others, cube),
         grid=(chunks,),
         in_specs=[
-            SCALARS, whole(earlier.shape), by_chunk(map_shape), by_chunk((heads, BLOCK, key_width)),
-            by_chunk((heads, BLOCK, value_width)), by_rows(mixed_width), by_rows(LANES), by_rows(vw),
-            whole(gain_row.shape), whole(w_output.shape),
+            SCALARS, whole(earlier.shape), chunk_back(map_shape), chunk_back((heads, BLOCK, key_width)),
+            chunk_back((heads, BLOCK, value_width)), rows_back(mixed_width), rows_back(LANES), rows_back(vw),
+            whole(gain_row.shape), held(w_output.shape),
         ],
         out_specs=[
-            by_rows(vw), by_rows(vw), by_rows(model_width), by_chunk((heads, BLOCK, value_width)),
-            by_chunk((heads, key_width, value_width)),
+            rows_back(vw), rows_back(vw), chunk_back((heads, BLOCK, value_width)),
+            chunk_back((heads, key_width, value_width)),
+            whole((row_count, model_width)) if cube else rows_back(model_width),
         ],
         out_shape=[
-            struct((seq_rows, vw), f32), struct((seq_rows, vw), bf16), struct((seq_rows, model_width), bf16),
+            struct((seq_rows, vw), f32), struct((seq_rows, vw), bf16),
             struct((chunks, heads, BLOCK, value_width), bf16),
             struct((chunks, heads, key_width, value_width), f32),
+            struct((row_count, model_width), f32) if cube else struct((seq_rows, model_width), bf16),
         ],
-        scratch_shapes=[pltpu.VMEM((heads, key_width, value_width), f32)],
-        compiler_params=params(),
+        scratch_shapes=[pltpu.VMEM((heads, key_width, value_width), f32)]
+        + (cube_scatter_scratch(row_count, model_width) if cube else []),
+        compiler_params=params(5 if cube else None),
         name="mixer_output",
     )(meta, earlier, starts, w_part, u_part, qkv, scal, gate, gain_row, w_output)
-
-    mixer_out = cube_scatter(mixed_part, "head", 5)
+    if cube:
+        mixer_out = mixed_part
+    else:
+        mixer_out = lax.psum_scatter(mixed_part, "head", scatter_dimension=0, tiled=True).astype(f32)
+
     hidden_in = inputs_f + mixer_out
     normed_two = rms_scale(hidden_in, second_gain).astype(bf16)
-    grad_hidden = dot_nt(grad_block_two, w_down)
-    mlp_block, hidden, grad_gate, grad_up, grad_normed_two = feed(
-        normed_two, grad_hidden, w_gate, w_up, "seq", 3
+    mlp_block, hidden, grad_gate, grad_up, mlp_part, grad_normed_two = feed(
+        normed_two, grad_block_two, w_gate, w_up, w_down, "seq", 3
     )
+    mlp_out = lax.psum_scatter(mlp_part, "seq", scatter_dimension=0, tiled=True)
     grad_hidden_norm, grad_second = rms_back(hidden_in, second_gain, grad_normed_two)
     grad_hidden_in = grad_out + grad_hidden_norm
     grad_mix = grad_hidden_in.astype(bf16)
-    *ff_grads, mlp_part, grad_block = feed_grads(
-        grad_mix, mlp_block, grad_block_two, w_down, hidden, grad_gate, grad_up, "head", 6
+    *ff_grads, grad_block = feed_grads(
+        grad_mix, mlp_block, grad_block_two, hidden, grad_gate, grad_up, "head", 6
     )
     grad_core, inner, pull, grad_gate_pre, grad_head, pulled = pl.pallas_call(
         functools.partial(core_grad_kernel, *sizes, chunks),
@@ -1374,8 +1664,6 @@
     later = from_later(
         jnp.concatenate([block_map[:, :, :key_width], pulled], axis=2).astype(bf16), "seq"
     )
-    mlp_part, later = lax.optimization_barrier((mlp_part, later))
-    mlp_out = lax.psum_scatter(mlp_part, "seq", scatter_dimension=0, tiled=True)
     grad_conv, grad_small, sums = pl.pallas_call(
         functools.partial(backward_kernel, *sizes, chunks, others),
         grid=(chunks,),
@@ -1399,74 +1687,76 @@
     edge = from_next(grad_conv[:HALO])
     step_rows = BLOCK // HALO
     last_halo = seq_rows // HALO - 1
+    later_rows = pl.BlockSpec(
+        (HALO, mixed_width), lambda step: (jnp.minimum((last_first(step) + 1) * step_rows, last_halo), 0)
+    )
     grad_pre, grad_taps, grad_rows, gain_sum = pl.pallas_call(
-        functools.partial(projection_grad_kernel, mixed_width, docs, chunks, taps),
+        functools.partial(projection_grad_kernel, mixed_width, docs, chunks, taps, cube),
         grid=(chunks,),
         in_specs=[
-            SCALARS, by_rows(mixed_width),
-            pl.BlockSpec(
-                (HALO, mixed_width), lambda step: (jnp.minimum((step + 1) * step_rows, last_halo), 0)
-            ),
-            whole(edge.shape), by_rows(mixed_width), by_rows(vw), by_rows(LANES),
-            whole(conv_all.shape), by_rows(model_width), *(whole(weight.shape) for weight in weights),
+            SCALARS, rows_back(mixed_width), later_rows, whole(edge.shape), rows_back(mixed_width), rows_back(vw),
+            rows_back(LANES), whole(conv_all.shape), rows_back(model_width),
+            *(held(weight.shape) for weight in weights),
         ],
-        out_specs=[by_rows(all_width), whole((8, mixed_width)), by_rows(model_width), whole((8, model_width))],
+        out_specs=[
+            rows_back(all_width), whole((8, mixed_width)),
+            whole((row_count, model_width)) if cube else rows_back(model_width), whole((8, model_width)),
+        ],
         out_shape=[
             struct((seq_rows, all_width), bf16), struct((8, mixed_width), f32),
-            struct((seq_rows, model_width), bf16), struct((8, model_width), f32),
+            struct((row_count, model_width), f32) if cube else struct((seq_rows, model_width), bf16),
+            struct((8, model_width), f32),
         ],
-        scratch_shapes=[pltpu.VMEM((BLOCK + HALO, mixed_width), f32)],
-        compiler_params=params(),
+        scratch_shapes=[pltpu.VMEM((BLOCK + HALO, mixed_width), f32)]
+        + (cube_scatter_scratch(row_count, model_width) if cube else []),
+        compiler_params=params(8 if cube else None),
         name="projection_grad",
     )(meta, grad_conv, grad_conv, edge, pre, grad_gate_pre, grad_small, conv_all, block_rows, *weights)
 
-    grad_normed = lax.psum_scatter(grad_rows, "head", scatter_dimension=0, tiled=True).astype(f32)
+    grad_pre, *ff_grads = lax.optimization_barrier((grad_pre, *ff_grads))
+    ff_grads = [lax.psum(part, "head") for part in ff_grads]
+    if cube:
+        grad_normed = grad_rows
+    else:
+        grad_normed = lax.psum_scatter(grad_rows, "head", scatter_dimension=0, tiled=True).astype(f32)
     grad_input_norm, _ = rms_back(inputs_f, first_gain, grad_normed)
     grad_inputs = grad_hidden_in + grad_input_norm
-    grad_w_all = dot_tn(block_rows, grad_pre).astype(bf16)
-
-    gains = cube_sum(
-        jnp.concatenate([gain_sum[0] / first_gain, grad_second, grad_head[0]]).reshape(2, -1).repeat(4, axis=0),
-        "head",
-        7,
-    )
-    mlp_out, *ff_grads = lax.optimization_barrier((mlp_out, *ff_grads))
-    ff_grads = [lax.psum(part, "head") for part in ff_grads]
-    grad_w_all, grad_w_output, small_sums, gains = line_sum(
+    gains = jnp.concatenate([gain_sum[0] / first_gain, grad_second, grad_head[0]]).reshape(2, -1)
+    grad_w_all, grad_w_output, small_sums, _, gains = line_sum(
+        block_rows,
+        grad_pre,
         (
-            grad_w_all,
             grad_w_output,
             jnp.pad(
-                jnp.concatenate([grad_taps, sums], axis=1), ((0, 24), (0, all_width - mixed_width - LANES))
+                jnp.concatenate([grad_taps, sums], axis=1), ((0, 24), (0, 0))
             ).astype(bf16),
-            jnp.pad(gains, ((0, 24), (0, 0))).astype(bf16),
+            jnp.pad(gains, ((0, 30), (0, 0))).astype(bf16),
         ),
         (32, 16, 16, 16),
         "seq",
         1,
     )
-    gains = jnp.concatenate([gains[0], gains[4]]).astype(f32)
+    gains = gains[:2].reshape(-1)
     first_part, second_part = gains[:model_width], gains[model_width : 2 * model_width]
     head_part = gains[2 * model_width :]
-    grad_w_all, *ff_grads = lax.optimization_barrier((grad_w_all, *ff_grads))
-    grad_w_down, grad_w_gate, grad_w_up = (part.astype(f32) for part in ff_grads)
-    grad_w_all = grad_w_all.astype(f32)
-    grad_w_output = grad_w_output.astype(f32)
+    grad_w_all, mlp_out, *ff_grads = lax.optimization_barrier((grad_w_all, mlp_out, *ff_grads))
+    grad_w_down, grad_w_gate, grad_w_up, grad_w_query, grad_w_key, grad_w_value, grad_w_outgate, grad_w_output = widen(
+        ff_grads, grad_w_all, (qw, qw, vw, vw), grad_w_output
+    )
+    grad_w_small = grad_w_all[:, mixed_width + vw :].astype(f32)
     grad_taps = small_sums[:taps, :mixed_width].astype(f32)
     sums = small_sums[:2, mixed_width : mixed_width + heads].astype(f32)
     output = (hidden_in + mlp_out.astype(f32)).astype(bf16)
-    gate_at = mixed_width
-    small_at = mixed_width + vw
     return (
         output,
         grad_inputs,
         first_part,
-        grad_w_all[:, :qw],
-        grad_w_all[:, qw : 2 * qw],
-        grad_w_all[:, 2 * qw : gate_at],
-        grad_w_all[:, gate_at:small_at],
-        grad_w_all[:, small_at : small_at + heads],
-        grad_w_all[:, small_at + heads : small_at + 2 * heads],
+        grad_w_query,
+        grad_w_key,
+        grad_w_value,
+        grad_w_outgate,
+        grad_w_small[:, :heads],
+        grad_w_small[:, heads : 2 * heads],
         grad_taps[:, :qw],
         grad_taps[:, qw : 2 * qw],
         grad_taps[:, 2 * qw :],

time: 925 us -> 792 us (0.86)
  Pallas kernels: 712 us -> 673 us
  matrix products: 41 us -> 11 us
  waiting for transfers between devices: 56.5 us -> 26.6 us
  other arithmetic: 52.9 us -> 29.9 us
    pallas_call x6 -> x4, Pallas kernels: 447 us -> 386 us  [the longest x1 235 us: line_sum(): pl.pallas_call(functools.partial(line_sum_kernel, axis, cube, counts, tup...]
    convert_element_type x6 -> x1, other arithmetic: 24.8 us -> 1.11 us  [shards(): grad_w_small = grad_w_all[:, mixed_width + vw:].astype(f32)]
    pallas_call x1, Pallas kernels: 31.8 us -> 53.2 us  [shards(): pl.pallas_call(functools.partial(projection_grad_kernel, mixed_width, doc...]
    dot_general x2 -> x1, matrix products: 30.9 us -> 11 us  [dot_tn(): lax.dot_general(left, right, (((0,), (0,)), ((), ())), preferred_element_...]
    ppermute x3, waiting for transfers between devices: 34.8 us -> 16.7 us  [from_later(): lax.ppermute(array, axis, [(i + by, i) for i in range(devices - by)])]
    reduce_scatter x1, waiting for transfers between devices: 12.6 us -> 0.01 us  [shards(): mlp_out = lax.psum_scatter(mlp_part, 'seq', scatter_dimension=0, tiled=True)]
    dot_general x1 -> x0, matrix products: 10.1 us -> none  [dot_nt(): lax.dot_general(left, right, (((1,), (1,)), ((), ())), preferred_element_...]
  transfers between devices with their start and end apart: 11 -> 10, of which waited for: 5 -> 5; matrix products, arithmetic and copies ran while one was open for 7% -> 5% of each run, Pallas kernels for 33% -> 65%
where the time goes in v3:
time: 792 us; the launch traced here: 785 us
  Pallas kernels  673 us (85%)
  other arithmetic  29.9 us (4%)
  waiting for transfers between devices  26.6 us (3%)
  starting transfers between devices  15.3 us (2%)
  local copies, waits for them, and re-layouts  14.6 us (2%)
  between operations  14.5 us (2%)
  matrix products  11 us (1%)
    pallas_call x1, Pallas kernels, line_sum(): pl.pallas_call(functools.partial(line_sum_kernel, axis, cube, counts, tup...  235 us
    pallas_call x1, Pallas kernels, feed(): pl.pallas_call(functools.partial(feed_kernel, axis, devices, rows), in_sp...  139 us
    pallas_call x1, Pallas kernels, shards(): pl.pallas_call(functools.partial(forward_kernel, *sizes, taps, chunks, cu...  76.5 us
    pallas_call x1, Pallas kernels, shards(): pl.pallas_call(functools.partial(projection_grad_kernel, mixed_width, doc...  53.2 us
    pallas_call x1, Pallas kernels, shards(): pl.pallas_call(functools.partial(output_kernel, *sizes, others, cube), gr...  49.2 us
    pallas_call x1, Pallas kernels, feed_grads(): pl.pallas_call(functools.partial(feed_grads_kernel, axis, cube), grid=(wi...  48.9 us
    pallas_call x1, Pallas kernels, widen(): pl.pallas_call(functools.partial(widen_kernel, cuts), grid=(steps,), in_s...  26 us
    pallas_call x1, Pallas kernels, shards(): pl.pallas_call(functools.partial(backward_kernel, *sizes, chunks, others)...  25.7 us
  transfers between devices with their start and end apart: 10, of which 5 were waited for; matrix products, arithmetic and copies ran while one was open for 5% of the time, Pallas kernels for 65%

profile of v3, /device:TPU:0, one launch (start us, length us, event | category | flops | bytes accessed | tf_op | source)
XLA Modules:
  0.0 784.7 jit_solution(3635798609008954460)
XLA Ops:
  7.3 0.7 fusion.20
  8.9 0.7 select_reduce_fusion.1
  9.8 2.5 fusion.7
  14.3 1.1 maximum_maximum_fusion.ws_ref
  15.4 1.3 fusion.2.rows_ref
  16.7 76.5 %mixer_forward.1 = (f32[2048,1024]{1,0:T(8,128)}, f32[2048,1024]{1,0:T(8,128)}, f32[2048,512]{1,0:T(8,128)}, f32[2048,128]{1,0:T(8,128)}, f32[2048,128]{1,0:T(8,...) custom-call(s32[4]{0:T(128)} %pad_add_fusion.meta, ...), custom_call_target="tpu_custom_call" | custom-call | tf_op jit(solution)/shard_map/mixer_forward/pallas_call | solution.py:1548
  93.2 1.0 convert_element_type.59
  94.2 3.5 collective-permute-start.2
  97.8 4.5 collective-permute-start.1
  102.3 1.6 collective-permute-start
  103.9 3.4 collective-permute-done.1
  107.3 2.1 collective-permute-done
  109.4 0.9 pad_maximum_fusion.maps_ref
  110.3 49.2 %mixer_output.1 = (f32[2048,512]{1,0:T(8,128)}, bf16[2048,512]{1,0:T(8,128)(2,1)}, bf16[8,2,256,256]{3,2,1,0:T(8,128)(2,1)}, f32[8,2,128,256]{3,2,1,0:T(8,128)}, f32[256,2048]{1,0:T(8,128)}) custom-call(s32[4]{0:T(128)} %pad_add_fusion.meta, bf16[3,2,128,384]{3,2,1,0:T(8,128)(2,1)} %pad_maximum_fusion.maps_ref, ...), custom_call_target="tpu_custom_call" | custom-call | tf_op jit(solution)/shard_map/mixer_output/pallas_call | solution.py:1600
  159.5 2.0 multiply_reduce_fusion.2
  161.5 1.2 multiply_convert_fusion.own_ref
  162.7 138.9 %feed.1 = (bf16[1024,2048]{1,0:T(8,128)(2,1)}, bf16[1024,1408]{1,0:T(8,128)(2,1)}, bf16[1024,1408]{1,0:T(8,128)(2,1)}, bf16[1024,1408]{1,0:T(8,128)(2,1)}, bf16[...) custom-call(bf16[256,2048]{1,0:T(8,128)(2,1)} %multiply_convert_fusion.own_ref, ...), custom_call_target="tpu_custom_call" | custom-call | tf_op jit(solution)/shard_map/feed/pallas_call | solution.py:1129
  301.9 2.3 multiply_reduce_fusion
  304.4 2.5 fusion.14
  306.9 48.9 %feed_grads.1 = (bf16[1408,2048]{1,0:T(8,128)(2,1)}, bf16[2048,1408]{1,0:T(8,128)(2,1)}, bf16[2048,1408]{1,0:T(8,128)(2,1)}, bf16[2048,2048]{1,0:T(8,128)(2,1)}) custom-call(bf16[256,2048]{1,0:T(8,128)(2,1)} %get-tuple-element.215.own_ref, bf16[1024,2048]{1,0:T(8,128)(2,1)} %get-tuple-element.116.blocks_ref, ...), custom_call_target="tpu_custom_call" | custom-call | tf_op jit(solution)/shard_map/feed_grads/pallas_call | solution.py:1291
  355.8 19.7 %mixer_core_grad.1 = (bf16[8,2,256,256]{3,2,1,0:T(8,128)(2,1)}, f32[8,2,256,256]{3,2,1,0:T(8,128)}, f32[8,2,128,256]{3,2,1,0:T(8,128)}, bf16[2048,512]{1,0:T(8,1...) custom-call(s32[4]{0:T(128)} %pad_add_fusion.meta, bf16[2048,2048]{1,0:T(8,128)(2,1)} %get-tuple-element.120.grad_ref, ...), custom_call_target="tpu_custom_call" | custom-call | tf_op jit(solution)/shard_map/mixer_core_grad/pallas_call | solution.py:1641
  375.4 1.0 convert.27
  376.5 1.3 collective-permute-start.5
  377.8 1.3 collective-permute-start.4
  379.1 1.3 collective-permute-start.3
  380.4 5.3 collective-permute-done.5
  385.7 11.4 %collective-permute-done.4 = bf16[2,128,384]{2,1,0:T(8,128)(2,1)S(1)} collective-permute-done((bf16[2,128,384]{2,1,0:T(8,128)(2,1)S(1)}, bf16[2,128,384]{2,1,0:T(8,128)(2,1)S(1)}, u32[]{:S(2)}, u32[]{:S(2)}) %collective-permute-start.4) | collective-permute-done | bytes 196640 | tf_op jit(solution)/shard_map/ppermute | solution.py:1464
  397.1 0.9 pad_maximum_fusion.1.maps_ref
  398.0 25.7 %mixer_backward.1 = (f32[2048,1024]{1,0:T(8,128)}, bf16[2048,128]{1,0:T(8,128)(2,1)}, f32[8,128]{1,0:T(8,128)}) custom-call(s32[4]{0:T(128)} %pad_add_fusion.meta, bf16[3,2,128,384]{3,2,1,0:T(8,128)(2,1)} %pad_maximum_fusion.1.maps_ref, bf16[2048,1024]{1,0:T(8,128)(2,1)} %get-tuple-element.110.qkv_ref, f32[2048,1024]{1,0:T(8,128)} %get-tuple-element.124.act_ref, ...), custom_call_target="tpu_custom_call" | custom-call | tf_op jit(solution)/shard_map/mixer_backward/pallas_call | solution.py:1667
  423.8 0.8 slice.96
  424.5 1.5 collective-permute-start.6
  426.0 4.3 collective-permute-done.6.edge_ref
  430.9 53.2 %projection_grad.1 = (bf16[2048,1664]{1,0:T(8,128)(2,1)}, f32[8,1024]{1,0:T(8,128)}, f32[256,2048]{1,0:T(8,128)}, f32[8,2048]{1,0:T(8,128)}) custom-call(s32[4]{0:T(128)} %pad_add_fusion.meta, f32[2048,1024]{1,0:T(8,128)} %get-tuple-element.132.grad_conv_ref.later_ref, f32[2048,1024]{1,0:T(8,128)} %get-tuple-element.132.grad_conv_ref.later_ref, ...), custom_call_target="tpu_custom_call" | custom-call | tf_op jit(solution)/shard_map/projection_grad/pallas_call | solution.py:1693
  484.2 0.7 fusion.12
  484.9 11.0 %convolution_convert_fusion.refs_2_ = bf16[512,2048]{1,0:T(8,128)(2,1)} fusion(bf16[2048,512]{1,0:T(8,128)(2,1)} %get-tuple-element.141, bf16[2048,2048]{1,0:T(8,128)(2,1)} %get-tuple-element.120.grad_ref), kind=kOutput, calls=%fused_computation.5 | convolution fusion | flops 4296015872 | bytes 12582912 | tf_op jit(solution)/shard_map/dot_general | solution.py:26
  495.9 0.8 slice.97
  496.8 0.7 pad.19.refs_4_
  498.1 234.7 %line_sum.1 = (bf16[2048,1664]{1,0:T(8,128)(2,1)}, bf16[512,2048]{1,0:T(8,128)(2,1)}, bf16[32,1152]{1,0:T(8,128)(2,1)}, bf16[32,2176]{1,0:T(8,128)(2,1)}, f32[8,2176]{1,0:T(8,128)}) custom-call(bf16[2048,2048]{1,0:T(8,128)(2,1)} %get-tuple-element.114.rows_ref.refs_0_, bf16[2048,1664]{1,0:T(8,128)(2,1)} %get-tuple-element.140.refs_1_, ...), custom_call_target="tpu_custom_call" | custom-call | flops 100000000 | bytes 40000000 | tf_op jit(solution)/shard_map/line_sum/pallas_call | solution.py:901
  732.9 0.7 slice_convert_fusion.1
  734.2 0.9 slice.99
  735.7 1.9 fusion.6
  737.6 0.7 slice_convert_fusion.3
  740.0 1.1 slice_convert_fusion
  741.1 1.6 fusion.15
  742.8 2.2 copy.48
  744.9 2.2 copy.47
  747.1 4.8 fusion.5
  751.9 26.0 %widen.1 = (f32[1408,2048]{1,0:T(8,128)}, f32[2048,1408]{1,0:T(8,128)}, f32[2048,1408]{1,0:T(8,128)}, f32[2048,256]{1,0:T(8,128)}, f32[2048,256]{1,0:T(8,128)}, ...) custom-call(bf16[1408,2048]{1,0:T(8,128)(2,1)} %get-tuple-element.154.down_in, ...), custom_call_target="tpu_custom_call" | custom-call | tf_op jit(solution)/shard_map/widen/pallas_call | solution.py:1437
  (83 shorter events, 7.7 us)
Async XLA Ops:
  7.2 5.2 copy-start.10
  7.2 5.5 copy-start.11
  7.2 155.5 %all-gather.2.cloned.1.call-start = ((), (), s32[]{:S(2)}) async-start(), calls=%async_computation.1 | async-start | bytes 5242880 | tf_op jit(solution)/shard_map/all_gather | solution.py:1589
  9.7 3.4 copy-start.16
  9.7 3.4 copy-start.17
  9.7 4.2 copy-start.14
  9.7 4.2 copy-start.15
  9.7 4.2 copy-start.12
  9.8 4.2 copy-start
  12.3 3.1 copy-start.4
  12.3 727.7 %reduce-scatter.2.cloned.1.call-start = ((), (), s32[]{:S(2)}) async-start(), calls=%async_computation.2 | async-start | bytes 5242880 | tf_op jit(solution)/shard_map/reduce_scatter | solution.py:1634
  13.3 3.4 copy-start.7
  14.0 2.7 copy-start.5
  94.2 9.7 %collective-permute-start.2 = (bf16[2,128,384]{2,1,0:T(8,128)(2,1)S(1)}, bf16[2,128,384]{2,1,0:T(8,128)(2,1)S(1)}, u32[]{:S(2)}, u32[]{:S(2)}) collective-permute-start(bf16[2,128,384]{2,1,0:T(8,128)(2,1)S(1)} %convert_element_type.59), channel_id=1, source_target_pairs={{0,8},{8,16},{16,24},{1,9},{9,17},{17,25},{2,10},{10,18},{18,26},{... | collective-permute-start | bytes 589832 | tf_op jit(solution)/shard_map/ppermute | solution.py:1455
  97.8 9.5 %collective-permute-start.1 = (bf16[2,128,384]{2,1,0:T(8,128)(2,1)S(1)}, bf16[2,128,384]{2,1,0:T(8,128)(2,1)S(1)}, u32[]{:S(2)}, u32[]{:S(2)}) collective-permute-start(bf16[2,128,384]{2,1,0:T(8,128)(2,1)S(1)} %convert_element_type.59), channel_id=1, source_target_pairs={{0,16},{8,24},{1,17},{9,25},{2,18},{10,26},{3,19},{11,27},{4,20},{... | collective-permute-start | bytes 589832 | tf_op jit(solution)/shard_map/ppermute | solution.py:1455
  102.3 7.1 collective-permute-start
  159.5 2.0 copy-start.6
  301.7 438.4 %all-reduce.6.cloned.1.call-start = ((), (), s32[]{:S(2)}) async-start(), calls=%async_computation.3 | async-start | bytes 34603008 | tf_op jit(solution)/shard_map/psum | solution.py:1717
  301.9 2.3 copy-start.2
  301.9 2.5 copy-start.3
  376.5 9.2 %collective-permute-start.5 = (bf16[2,128,384]{2,1,0:T(8,128)(2,1)S(1)}, bf16[2,128,384]{2,1,0:T(8,128)(2,1)S(1)}, u32[]{:S(2)}, u32[]{:S(2)}) collective-permute-start(bf16[2,128,384]{2,1,0:T(8,128)(2,1)S(1)} %pad_maximum_fusion.2), channel_id=1, source_target_pairs={{8,0},{16,8},{24,16},{9,1},{17,9},{25,17},{10,2},{18,10},{26,18},{... | collective-permute-start | bytes 589832 | tf_op jit(solution)/shard_map/ppermute | solution.py:1464
  377.8 19.3 %collective-permute-start.4 = (bf16[2,128,384]{2,1,0:T(8,128)(2,1)S(1)}, bf16[2,128,384]{2,1,0:T(8,128)(2,1)S(1)}, u32[]{:S(2)}, u32[]{:S(2)}) collective-permute-start(bf16[2,128,384]{2,1,0:T(8,128)(2,1)S(1)} %pad_maximum_fusion.2), channel_id=1, source_target_pairs={{16,0},{24,8},{17,1},{25,9},{18,2},{26,10},{19,3},{27,11},{20,4},{... | collective-permute-start | bytes 589832 | tf_op jit(solution)/shard_map/ppermute | solution.py:1464
  379.1 18.0 %collective-permute-start.3 = (bf16[2,128,384]{2,1,0:T(8,128)(2,1)S(1)}, bf16[2,128,384]{2,1,0:T(8,128)(2,1)S(1)}, u32[]{:S(2)}, u32[]{:S(2)}) collective-permute-start(bf16[2,128,384]{2,1,0:T(8,128)(2,1)S(1)} %pad_maximum_fusion.2), channel_id=1, source_target_pairs={{24,0},{25,1},{26,2},{27,3},{28,4},{29,5},{30,6},{31,7}} | collective-permute-start | bytes 589832 | tf_op jit(solution)/shard_map/ppermute | solution.py:1464
  424.5 5.8 collective-permute-start.6
  430.3 0.6 copy-start.8
  484.9 11.0 %copy-start.13 = (f32[8,128]{1,0:T(8,128)S(1)}, f32[8,128]{1,0:T(8,128)}, u32[]{:S(2)}) copy-start(f32[8,128]{1,0:T(8,128)} %get-tuple-element.143) | copy-start | bytes 12292
  484.9 11.9 %copy-start.9 = (f32[8,1024]{1,0:T(8,128)S(1)}, f32[8,1024]{1,0:T(8,128)}, u32[]{:S(2)}) copy-start(f32[8,1024]{1,0:T(8,128)} %get-tuple-element.142) | copy-start | bytes 98308
  498.1 237.6 %copy-start.1 = (bf16[256,2048]{1,0:T(8,128)(2,1)S(1)}, bf16[256,2048]{1,0:T(8,128)(2,1)}, u32[]{:S(2)}) copy-start(bf16[256,2048]{1,0:T(8,128)(2,1)} %param.25) | copy-start | bytes 3145732
Sparse Core Ops, SparseCore 0:
  12.4 83.4 all-gather.1
  301.8 75.0 reduce-scatter.1
  484.3 222.3 all-reduce.5

commit v4 on v3

--- a/solution.py
+++ b/solution.py
@@ -197,18 +197,10 @@
         barrier = pltpu.get_barrier_semaphore()
         for mask in (1, 2, 4, 6):
             pl.semaphore_signal(barrier, inc=1, device_id={self.axis: flip(self.place, mask)}, device_id_type=MESH)
-
-        @pl.when(self.receives())
-        def _():
-            pl.semaphore_signal(barrier, inc=1, device_id={self.line: self.group - 1}, device_id_type=MESH)
-
-        @pl.when(self.hands_on())
-        def _():
-            pl.semaphore_wait(barrier, 5)
-
-        @pl.when(jnp.logical_not(self.hands_on()))
-        def _():
-            pl.semaphore_wait(barrier, 4)
+        for by in range(1, self.groups):
+            other = lax.rem(self.group + by, self.groups)
+            pl.semaphore_signal(barrier, inc=1, device_id={self.line: other}, device_id_type=MESH)
+        pl.semaphore_wait(barrier, 3 + self.groups)
 
     def hands_on(self):
         return (self.place == self.last) & (self.group < self.groups - 1)
@@ -288,10 +280,12 @@
     starts_ref, map_ref, *refs,
 ):
     step = pl.program_id(0)
-    ext, state, drops, adds, throughs = refs[cube : cube + 5]
+    ext, state, drops, adds, throughs = refs[2 * cube : 2 * cube + 5]
     if cube:
         all_ref = refs[0]
-        held, copy_sem, edge_ref, line_sem, edge_send, edge_recv, cube_send, cube_recv = refs[6:]
+        earlier_ref, *refs = refs[1:]
+        held, copy_sem, edge_ref, line_sem, edge_send, edge_recv, cube_send, cube_recv = refs[5:13]
+        going, coming, map_sem = refs[13:]
         chunk = cube_order("head", step)
         rows_in = CubeGather("head", rows_ref, held, None, cube_send, cube_recv, STRIDE, LEAD)
         edges = EdgeRows("seq", "head", rows_ref, held, edge_ref, line_sem, edge_send, edge_recv)
@@ -424,6 +418,39 @@
         for head in range(heads):
             map_ref[head] = state[head]
         if cube:
+            groups, group = lax.axis_size("seq"), lax.axis_index("seq")
+
+            def hand_on(by, target):
+                slot = groups - 1 - by
+                return pltpu.make_async_remote_copy(
+                    going, coming.at[slot], map_sem.at[0, slot], map_sem.at[1, slot],
+                    device_id={"seq": target}, device_id_type=MESH,
+                )
+
+            for head in range(heads):
+                going[head] = state[head].astype(bf16)
+            for by in range(groups - 1, 0, -1):
+                @pl.when(group + by < groups)
+                def _():
+                    hand_on(by, group + by).start()
+
+            for by in range(groups - 1, 0, -1):
+                slot = groups - 1 - by
+
+                @pl.when(group >= by)
+                def _():
+                    hand_on(by, group - by).wait_recv()
+                    earlier_ref[slot] = coming[slot]
+
+                @pl.when(group < by)
+                def _():
+                    earlier_ref[slot] = jnp.zeros(earlier_ref.shape[1:], bf16)
+
+            for by in range(groups - 1, 0, -1):
+                @pl.when(group + by < groups)
+                def _():
+                    hand_on(by, group + by).wait_send()
+
             rows_in.last()
             edges.end()
             for block in range(chunks):
@@ -482,10 +509,10 @@
 def core_grad_kernel(
     heads, key_width, value_width, docs, chunks,
     meta, grad_ref, w_output_ref, core_ref, gate_ref, gain_ref, qkv_ref, scal_ref, w_in_ref, drop_ref,
-    grad_core_ref, inner_ref, pull_ref, grad_gate_ref, grad_gain_ref, total_ref,
+    grad_core_ref, inner_ref, pull_ref, grad_gate_ref, grad_gain_ref, total_ref, chunk=None, later=None,
 ):
     step = pl.program_id(0)
-    chunk = chunks - 1 - step
+    chunk = chunks - 1 - step if chunk is None else chunk
     qw = heads * key_width
     masks = Masks(meta, docs, chunk)
     scal = scal_ref[...]
@@ -525,6 +552,12 @@
             w_in_ref[0, head], inner.astype(bf16)
         )
         pull_ref[0, head] = pull
+        if later is not None:
+            pulls, drops, throughs = later
+            pulls[chunk, head] = pull
+            drops[chunk, head] = drop_ref[0, head].astype(bf16)
+            throughs[chunk, head] = jnp.broadcast_to(through, (8, LANES))
+            continue
         total = total_ref[head]
         total_ref[head] = (
             through * total - dot_tn(drop_ref[0, head].astype(bf16), total.astype(bf16)) + pull
@@ -535,11 +568,20 @@
     heads, key_width, value_width, docs, chunks, others,
     meta, maps_ref, qkv_ref, act_ref, scal_ref, small_ref, inv_ref, fresh_ref, state_ref,
     grad_core_ref, inner_ref, pull_ref, drop_ref, dvec_ref,
-    grad_conv_ref, grad_small_ref, sums_ref,
-    carried,
+    grad_conv_ref, grad_small_ref, sums_ref, edge_ref,
+    carried, edge_out, edge_in, edge_sem,
 ):
     step = pl.program_id(0)
     chunk = chunks - 1 - step
+    groups, group = lax.axis_size("seq"), lax.axis_index("seq")
+    edge = pltpu.make_async_remote_copy(
+        edge_out, edge_in, edge_sem.at[0], edge_sem.at[1],
+        device_id={"seq": jnp.maximum(group - 1, 0)}, device_id_type=MESH,
+    )
+
+    @pl.when(step == 0)
+    def _():
+        line_barrier("seq")
     qw = heads * key_width
 
     @pl.when(step == 0)
@@ -622,6 +664,27 @@
     strength = sigmoid(small_ref[...])
     grad_small_ref[...] = jnp.where(lane < heads, grad_z, betas * strength * (1.0 - strength)).astype(bf16)
 
+    @pl.when(step == chunks - 1)
+    def _():
+        edge_out[...] = grad_conv_ref[0:HALO, :]
+
+        @pl.when(group > 0)
+        def _():
+            edge.start()
+
+        @pl.when(group < groups - 1)
+        def _():
+            edge.wait_recv()
+            edge_ref[...] = edge_in[...]
+
+        @pl.when(group == groups - 1)
+        def _():
+            edge_ref[...] = jnp.zeros(edge_ref.shape, f32)
+
+        @pl.when(group > 0)
+        def _():
+            edge.wait_send()
+
 
 def projection_grad_kernel(
     mixed, docs, chunks, taps, cube,
@@ -656,15 +719,14 @@
         moved = ext[lag : lag + BLOCK, :] * keep
         total = total + conv_ref[lag : lag + 1, :] * moved
         grad_taps_ref[lag : lag + 1, :] += jnp.sum(pre * moved, axis=0, keepdims=True)
-    width = grad_gate_ref.shape[1]
     grad_pre_ref[:, :mixed] = total.astype(bf16)
-    grad_pre_ref[:, mixed : mixed + width] = grad_gate_ref[...]
-    grad_pre_ref[:, mixed + width :] = grad_small_ref[...]
+    grad_pre_ref[:, mixed:] = grad_small_ref[...]
     grad = jnp.zeros(grad_rows_ref.shape, f32)
     begin = 0
-    for ref in (wq_ref, wk_ref, wv_ref, wg_ref, ws_ref):
+    for ref in (wq_ref, wk_ref, wv_ref, ws_ref):
         grad = grad + dot_nt(grad_pre_ref[:, begin : begin + ref.shape[1]], ref[...])
         begin += ref.shape[1]
+    grad = grad + dot_nt(grad_gate_ref[...], wg_ref[...])
     gain_sum_ref[0:1, :] += jnp.sum(grad * rows_ref[...].astype(f32), axis=0, keepdims=True)
     if cube:
         scatter_block(step, CubeScatter("head", grad_rows_ref, *refs), grad)
@@ -947,10 +1009,11 @@
 ):
     given, kept, refs = refs[:4], refs[4:9], refs[9:]
     total_ref, *refs = refs
+    hidden_ref, *refs = refs
     inside, refs = refs[:8], refs[8:]
     inside = (*inside, inside[0])
     grads_ref, w_gate_ref, w_up_ref, w_down_ref = inside[:4]
-    blocks_ref, hidden_ref, grad_gate_ref, grad_up_ref, part_ref = inside[4:]
+    blocks_ref, turned_ref, grad_gate_ref, grad_up_ref, part_ref = inside[4:]
     parts, arrived, gather_send, gather_recv, chain_send, chain_recv, load_sem, store_sem = refs
     place = lax.axis_index(axis)
     piece = rows // 2
@@ -997,7 +1060,6 @@
         hop = (step + 1) // 2
         way = (step + 1) % 2
         owner = jnp.where(way == 0, place - hop, place + hop)
-        target = place + 1 - 2 * way
 
         @pl.when(step == 0)
         def _():
@@ -1010,26 +1072,34 @@
             for index in range(4):
                 load(index).wait()
 
+        @pl.when((step > 0) & (way == 0))
+        def _():
+            for side in range(2):
+                come = place - hop if side == 0 else place + hop
+                goes = place + 1 if side == 0 else place - 1
+
+                @pl.when((come >= 0) & (come < devices))
+                def _():
+                    for half in range(2):
+                        gather(come, hop - 1, side, half).wait_recv()
+
+                        @pl.when((goes >= 0) & (goes < devices))
+                        def _():
+                            gather(come, hop, side, half).start()
+
         @pl.when((owner >= 0) & (owner < devices))
         def _():
             here = full(owner)
             grad_hidden = dot_nt(grads_ref[here, :], w_down_ref[...])
-
-            @pl.when(step > 0)
-            def _():
-                for half in range(2):
-                    gather(owner, hop - 1, way, half).wait_recv()
-
-                    @pl.when((target >= 0) & (target < devices))
-                    def _():
-                        gather(owner, hop, way, half).start()
 
             block = blocks_ref[here, :]
             gate_pre = dot(block, w_gate_ref[...])
             up_pre = dot(block, w_up_ref[...])
             sigma = sigmoid(gate_pre)
             act = gate_pre * sigma
-            hidden_ref[here, :] = (act * up_pre).astype(bf16)
+            hidden = (act * up_pre).astype(bf16)
+            hidden_ref[here, :] = hidden
+            turned_ref[:, full(owner)] = hidden.T
             grad_gate_ref[here, :] = (grad_hidden * up_pre * (sigma * (1.0 + gate_pre * (1.0 - sigma)))).astype(bf16)
             grad_up_ref[here, :] = (grad_hidden * act).astype(bf16)
             grad = dot_nt(grad_gate_ref[here, :], w_gate_ref[...]) + dot_nt(grad_up_ref[here, :], w_up_ref[...])
@@ -1124,7 +1194,8 @@
     moves = pltpu.SemaphoreType.DMA((4 * devices,))
     chains = pltpu.SemaphoreType.DMA((8 * devices,))
     given = (grads, w_gate, w_up, w_down)
-    kept = [struct((devices * rows, width), bf16)] + [struct((devices * rows, units), bf16)] * 3
+    kept = [struct((devices * rows, width), bf16), struct((units, devices * rows), bf16)]
+    kept += [struct((devices * rows, units), bf16)] * 2
     kept += [struct((devices * rows, width), bf16)]
     return pl.pallas_call(
         functools.partial(feed_kernel, axis, devices, rows),
@@ -1132,6 +1203,7 @@
         out_specs=[ANYWHERE] * 5 + [vmem],
         out_shape=kept + [struct((rows, width), f32)],
         scratch_shapes=[
+            pltpu.VMEM((devices * rows, units), bf16),
             *(pltpu.VMEM(array.shape, array.dtype) for array in (*given, *kept[:4])),
             pltpu.VMEM((devices * rows, width), bf16), pltpu.VMEM(((devices + 1) * rows, width), bf16),
             moves, moves, chains, chains, pltpu.SemaphoreType.DMA((4,)), pltpu.SemaphoreType.DMA((5,)),
@@ -1230,77 +1302,107 @@
 CUBE_SEMAPHORES = [pltpu.SemaphoreType.DMA, pltpu.SemaphoreType.DMA((10, 4)), pltpu.SemaphoreType.DMA((16,))]
 
 
-def cube_gather_kernel(axis, own_ref, all_ref, *semaphores):
-    gather = CubeGather(axis, own_ref, all_ref, *semaphores)
-    gather.first()
-    gather.second()
-    gather.third()
-    gather.fourth()
-    gather.last()
-
-
-def cube_gather(own, axis, collective_id):
-    if lax.axis_size(axis) != 8:
-        return lax.all_gather(own, axis, axis=0, tiled=True)
-    rows, width = own.shape
-    return pl.pallas_call(
-        functools.partial(cube_gather_kernel, axis),
-        in_specs=[ANYWHERE],
-        out_specs=ANYWHERE,
-        out_shape=struct((8 * rows, width), own.dtype),
-        scratch_shapes=CUBE_SEMAPHORES,
-        compiler_params=pltpu.CompilerParams(
-            collective_id=collective_id, has_side_effects=True, vmem_limit_bytes=VMEM_LIMIT
-        ),
-        name="cube_gather",
-    )(own)
-
-
 def feed_grads_kernel(
-    axis, cube,
-    own_ref, blocks_ref, grads_ref, hidden_ref, grad_gate_ref, grad_up_ref,
-    *refs,
+    blocks_ref, grads_ref, hidden_ref, grad_gate_ref, grad_up_ref, down_ref, gate_ref, up_ref,
 ):
-    down_ref, gate_ref, up_ref = refs[:3]
-    step = pl.program_id(0)
-    steps = pl.num_programs(0)
-    if cube:
-        gather = CubeGather(axis, own_ref, refs[3], *refs[4:])
-        for at, phase in ((0, gather.first), (2, gather.second), (4, gather.third), (6, gather.fourth)):
-            @pl.when(step == at)
-            def _():
-                phase()
-
     gate_ref[...] = dot_tn(blocks_ref[...], grad_gate_ref[...]).astype(bf16)
     up_ref[...] = dot_tn(blocks_ref[...], grad_up_ref[...]).astype(bf16)
-    down_ref[...] = dot_tn(hidden_ref[...], grads_ref[...]).astype(bf16)
-    if cube:
-        @pl.when(step == steps - 1)
-        def _():
-            gather.last()
-
-
-def feed_grads(own, blocks, grads, hidden, grad_gate, grad_up, axis, collective_id):
-    cube = lax.axis_size(axis) == 8
+    down_ref[...] = dot(hidden_ref[...], grads_ref[...]).astype(bf16)
+
+
+def feed_grads(own, blocks, grads, hidden, grad_gate, grad_up, axis):
     rows, width = blocks.shape
-    units = hidden.shape[1]
+    units = hidden.shape[0]
     tall = pl.BlockSpec((rows, BLOCK), lambda step: (0, step))
     down = pl.BlockSpec((units, BLOCK), lambda step: (0, step))
     flat = pl.BlockSpec((BLOCK, units), lambda step: (step, 0))
     fixed = held((rows, units))
     results = pl.pallas_call(
-        functools.partial(feed_grads_kernel, axis, cube),
+        feed_grads_kernel,
         grid=(width // BLOCK,),
-        in_specs=[ANYWHERE, tall, tall, fixed, fixed, fixed],
-        out_specs=[down, flat, flat] + [ANYWHERE] * cube,
+        in_specs=[tall, tall, held(hidden.shape), fixed, fixed],
+        out_specs=[down, flat, flat],
         out_shape=[
             struct((units, width), bf16), struct((width, units), bf16), struct((width, units), bf16),
-        ] + [struct((8 * own.shape[0], width), bf16)] * cube,
-        scratch_shapes=CUBE_SEMAPHORES if cube else [],
-        compiler_params=params(collective_id if cube else None),
+        ],
+        compiler_params=params(),
         name="feed_grads",
-    )(own, blocks, grads, hidden, grad_gate, grad_up)
-    return results if cube else (*results, lax.all_gather(own, axis, axis=0, tiled=True))
+    )(blocks, grads, hidden, grad_gate, grad_up)
+    return (*results, lax.all_gather(own, axis, axis=0, tiled=True))
+
+
+def feed_core_kernel(
+    sizes, chunks, axis, tiles,
+    meta, own_ref, blocks_ref, grads_ref, hidden_ref, feed_gate_ref, feed_up_ref,
+    w_output_ref, core_ref, gate_ref, gain_ref, qkv_ref, scal_ref, w_in_ref, drop_ref,
+    down_out, gate_out, up_out, all_ref, *refs,
+):
+    outs, (rows_ref, copy_sem, send_sem, recv_sem, *later) = refs[:6], refs[6:]
+    step = pl.program_id(0)
+    gather = CubeGather(axis, own_ref, rows_ref, None, send_sem, recv_sem)
+    rows = own_ref.shape[0]
+
+    @pl.when(step == 0)
+    def _():
+        cube_barrier(axis, gather.place)
+        gather.first()
+        rows_ref[pl.ds(pl.multiple_of(gather.place * rows, rows), rows), :] = own_ref[...]
+
+    @pl.when(step == tiles - 1)
+    def _():
+        gather.second()
+        gather.third()
+
+    @pl.when(step == tiles + 3)
+    def _():
+        gather.fourth()
+
+    for mask in (1, 3, 5, 7):
+        @pl.when(step == (1 if mask == 1 else tiles + mask))
+        def _():
+            for half in range(2):
+                gather.wait(mask, half)
+
+    @pl.when((step >= 2) & (step < tiles + 2))
+    def _():
+        turned = blocks_ref[...].T
+        gate_out[...] = dot(turned, feed_gate_ref[...]).astype(bf16)
+        up_out[...] = dot(turned, feed_up_ref[...]).astype(bf16)
+        down_out[...] = dot(hidden_ref[...], grads_ref[...]).astype(bf16)
+
+    @pl.when((step < 2) | (step >= tiles + 2))
+    def _():
+        chunk = core_order(axis, step, tiles)
+        core_grad_kernel(
+            *sizes, chunks,
+            meta, rows_ref.at[pl.ds(pl.multiple_of(chunk * BLOCK, BLOCK), BLOCK), :], w_output_ref,
+            core_ref, gate_ref, gain_ref, qkv_ref, scal_ref, w_in_ref, drop_ref, *outs, chunk=chunk, later=later,
+        )
+
+    @pl.when(step == tiles + chunks - 1)
+    def _():
+        kept = pltpu.make_async_copy(rows_ref, all_ref, copy_sem)
+        kept.start()
+        total_ref = outs[5]
+        pulls, drops, throughs = later
+
+        def pass_on(at, carry):
+            chunk = chunks - 1 - at
+            for head in range(sizes[0]):
+                total = total_ref[head]
+                total_ref[head] = (
+                    throughs[chunk, head][0:1, 0:1] * total
+                    - dot_tn(drops[chunk, head], total.astype(bf16)) + pulls[chunk, head]
+                )
+            return carry
+
+        lax.fori_loop(0, chunks, pass_on, 0)
+        gather.last()
+        kept.wait()
+
+
+def core_order(axis, step, tiles):
+    return cube_order(axis, jnp.where(step < 2, step, jnp.maximum(step - tiles, 1)))
 
 
 class CubeScatter:
@@ -1416,29 +1518,42 @@
     )
 
 
-def widen_kernel(cuts, down_in, gate_in, up_in, all_in, output_in, down, gate, up, *refs):
-    *columns, output = refs
-    for source, result in ((down_in, down), (gate_in, gate), (up_in, up), (output_in, output)):
+def widen_kernel(cuts, total, *refs):
+    given, refs = refs[:total], refs[total:]
+    if cuts:
+        all_in, *refs = refs
+        begin = 0
+        for cut, result in zip(cuts, refs):
+            result[...] = all_in[:, begin : begin + cut].astype(f32)
+            begin += cut
+        refs = refs[len(cuts) :]
+        refs[-1][...] = all_in[:, begin:].astype(f32).T
+    for source, result in zip(given, refs):
         result[...] = source[...].astype(f32)
-    begin = 0
-    for cut, result in zip(cuts, columns):
-        result[...] = all_in[:, begin : begin + cut].astype(f32)
-        begin += cut
-
-
-def widen(ff_grads, grad_w_all, cuts, grad_w_output):
-    sources = (*ff_grads, grad_w_all, grad_w_output)
-    steps = 8 if ff_grads[0].shape[0] % 128 == 0 else 4
-    shapes = [array.shape for array in ff_grads] + [(grad_w_all.shape[0], cut) for cut in cuts] + [grad_w_output.shape]
+
+
+def widen(given, columns=None, cuts=()):
+    steps = 8 if given[0].shape[0] % 128 == 0 else 4
+    sources = list(given)
+    shapes = [array.shape for array in given]
 
     def part(shape):
         return pl.BlockSpec((shape[0] // steps, shape[1]), lambda step: (step, 0))
 
+    specs = [part(shape) for shape in shapes]
+    if cuts:
+        sources.append(columns)
+        rows, width = columns.shape
+        rest = width - sum(cuts)
+        cut_shapes = [(rows, cut) for cut in cuts]
+        specs = [part(shape) for shape in cut_shapes] + specs
+        specs.append(pl.BlockSpec((rest, rows // steps), lambda step: (0, step)))
+        shapes = cut_shapes + shapes + [(rest, rows)]
     return pl.pallas_call(
-        functools.partial(widen_kernel, cuts),
+        functools.partial(widen_kernel, cuts, len(given)),
         grid=(steps,),
         in_specs=[part(array.shape) for array in sources],
-        out_specs=[part(shape) for shape in shapes],
+        out_specs=specs,
         out_shape=[struct(shape, f32) for shape in shapes],
         compiler_params=params(),
         name="widen",
@@ -1516,7 +1631,7 @@
     grad_low = grad_out.astype(bf16)
     w_small = jnp.concatenate([w_decay, w_beta, jnp.zeros((model_width, LANES - 2 * heads), bf16)], axis=1)
     weights = (w_query, w_key, w_value, w_outgate, w_small)
-    all_width = mixed_width + vw + LANES
+    all_width = mixed_width + LANES
     conv_all = jnp.concatenate([conv_query, conv_key, conv_value], axis=1)
     dvec = jnp.zeros((8, LANES), f32)
     dvec = dvec.at[0, :heads].set(decay_bias).at[1, :heads].set(-jnp.exp(decay_log))
@@ -1558,7 +1673,7 @@
             chunk_out((heads, BLOCK, BLOCK)), chunk_out((heads, BLOCK, key_width)),
             chunk_out((heads, BLOCK, value_width)), chunk_out((heads, key_width, key_width)),
             whole((chunks,) + map_shape), whole(map_shape),
-        ] + [ANYWHERE] * cube,
+        ] + [ANYWHERE, whole((others,) + map_shape)] * cube,
         out_shape=[
             struct((seq_rows, mixed_width), f32), struct((seq_rows, mixed_width), f32),
             struct((seq_rows, vw), f32), struct((seq_rows, LANES), f32), struct((seq_rows, LANES), f32),
@@ -1567,7 +1682,7 @@
             struct((chunks, heads, BLOCK, value_width), f32),
             struct((chunks, heads, key_width, key_width), f32),
             struct((chunks,) + map_shape, f32), struct(map_shape, f32),
-        ] + [struct((seq_rows, model_width), bf16)] * cube,
+        ] + [struct((seq_rows, model_width), bf16), struct((others,) + map_shape, bf16)] * cube,
         scratch_shapes=[
             pltpu.VMEM((STRIDE, mixed_width), f32), pltpu.VMEM(map_shape, f32),
             pltpu.VMEM((chunks, heads, key_width, key_width), bf16),
@@ -1577,15 +1692,18 @@
             pltpu.VMEM((chunks * STRIDE, model_width), bf16), pltpu.SemaphoreType.DMA((chunks,)),
             pltpu.VMEM((LEAD, model_width), bf16), pltpu.SemaphoreType.DMA((2,)),
             pltpu.SemaphoreType.DMA((8,)), pltpu.SemaphoreType.DMA((8,)), *CUBE_SEMAPHORES[1:],
+            pltpu.VMEM(map_shape, bf16), pltpu.VMEM((others,) + map_shape, bf16),
+            pltpu.SemaphoreType.DMA((2, others)),
         ] * cube,
         compiler_params=params(2 if cube else None),
         name="mixer_forward",
     )(meta, rows_given, *weights, conv_all, dvec)
     (pre, conv, gate, small, scal, qkv, inverse, w_part, u_part, drop, starts, block_map) = results[:12]
     if cube:
-        block_rows = results[12]
-
-    earlier = from_earlier(block_map.astype(bf16), "seq")
+        block_rows, earlier = results[12:]
+    else:
+        earlier = from_earlier(block_map.astype(bf16), "seq")
+
     grad_block_two = lax.all_gather(grad_low, "seq", axis=0, tiled=True)
     gain_row = head_gain[None, :]
     def last_first(step):
@@ -1635,36 +1753,93 @@
     grad_hidden_norm, grad_second = rms_back(hidden_in, second_gain, grad_normed_two)
     grad_hidden_in = grad_out + grad_hidden_norm
     grad_mix = grad_hidden_in.astype(bf16)
-    *ff_grads, grad_block = feed_grads(
-        grad_mix, mlp_block, grad_block_two, hidden, grad_gate, grad_up, "head", 6
-    )
-    grad_core, inner, pull, grad_gate_pre, grad_head, pulled = pl.pallas_call(
-        functools.partial(core_grad_kernel, *sizes, chunks),
-        grid=(chunks,),
-        in_specs=[
-            SCALARS, by_rows(model_width, chunks), whole(w_output.shape), by_rows(vw, chunks), by_rows(vw, chunks),
-            whole(gain_row.shape), by_rows(mixed_width, chunks), by_rows(LANES, chunks),
-            by_chunk((heads, BLOCK, key_width), chunks), by_chunk((heads, key_width, key_width), chunks),
-        ],
-        out_specs=[
-            by_chunk((heads, BLOCK, value_width), chunks), by_chunk((heads, BLOCK, value_width), chunks),
-            by_chunk((heads, key_width, value_width), chunks), by_rows(vw, chunks),
-            whole((8, value_width)), whole((heads, key_width, value_width)),
-        ],
-        out_shape=[
-            struct((chunks, heads, BLOCK, value_width), bf16), struct((chunks, heads, BLOCK, value_width), f32),
-            struct((chunks, heads, key_width, value_width), f32), struct((seq_rows, vw), bf16),
-            struct((8, value_width), f32), struct((heads, key_width, value_width), f32),
-        ],
-        compiler_params=params(),
-        name="mixer_core_grad",
-    )(meta, grad_block, w_output, core, gate, gain_row, qkv, scal, w_part, drop)
+    core_shapes = [
+        struct((chunks, heads, BLOCK, value_width), bf16), struct((chunks, heads, BLOCK, value_width), f32),
+        struct((chunks, heads, key_width, value_width), f32), struct((seq_rows, vw), bf16),
+        struct((8, value_width), f32), struct((heads, key_width, value_width), f32),
+    ]
+    if cube:
+        tiles = model_width // BLOCK
+        units, mlp_rows = hidden.shape
+
+        def tile(step):
+            return jnp.clip(step - 2, 0, tiles - 1)
+
+        def core_chunk(step):
+            return core_order("head", step, tiles)
+
+        def core_rows(width):
+            return pl.BlockSpec((BLOCK, width), lambda step: (core_chunk(step), 0))
+
+        def core_blocks(shape):
+            return pl.BlockSpec((1,) + tuple(shape), lambda step: (core_chunk(step),) + (0,) * len(shape))
+
+        tall = pl.BlockSpec((mlp_rows, BLOCK), lambda step: (0, tile(step)))
+        down = pl.BlockSpec((units, BLOCK), lambda step: (0, tile(step)))
+        flat = pl.BlockSpec((BLOCK, units), lambda step: (tile(step), 0))
+        results = pl.pallas_call(
+            functools.partial(feed_core_kernel, sizes, chunks, "head", tiles),
+            grid=(tiles + chunks,),
+            in_specs=[
+                SCALARS, held(grad_mix.shape), tall, tall, *(held(array.shape) for array in (hidden, grad_gate, grad_up)),
+                held(w_output.shape), core_rows(vw), core_rows(vw), whole(gain_row.shape), core_rows(mixed_width),
+                core_rows(LANES), core_blocks((heads, BLOCK, key_width)), core_blocks((heads, key_width, key_width)),
+            ],
+            out_specs=[
+                down, flat, flat, ANYWHERE,
+                core_blocks((heads, BLOCK, value_width)), core_blocks((heads, BLOCK, value_width)),
+                core_blocks((heads, key_width, value_width)), core_rows(vw),
+                whole((8, value_width)), whole((heads, key_width, value_width)),
+            ],
+            out_shape=[
+                struct((units, model_width), bf16), struct((model_width, units), bf16),
+                struct((model_width, units), bf16), struct((seq_rows, model_width), bf16), *core_shapes,
+            ],
+            scratch_shapes=[
+                pltpu.VMEM((seq_rows, model_width), bf16), pltpu.SemaphoreType.DMA, *CUBE_SEMAPHORES[1:],
+                pltpu.VMEM((chunks, heads, key_width, value_width), f32),
+                pltpu.VMEM((chunks, heads, key_width, key_width), bf16),
+                pltpu.VMEM((chunks, heads, 8, LANES), f32),
+            ],
+            compiler_params=params(6),
+            name="feed_core",
+        )(
+            meta, grad_mix, mlp_block, grad_block_two, hidden, grad_gate, grad_up,
+            w_output, core, gate, gain_row, qkv, scal, w_part, drop,
+        )
+        ff_grads, grad_block = results[:3], results[3]
+        grad_core, inner, pull, grad_gate_pre, grad_head, pulled = results[4:]
+    else:
+        *ff_grads, grad_block = feed_grads(
+            grad_mix, mlp_block, grad_block_two, hidden, grad_gate, grad_up, "head"
+        )
+        grad_core, inner, pull, grad_gate_pre, grad_head, pulled = pl.pallas_call(
+            functools.partial(core_grad_kernel, *sizes, chunks),
+            grid=(chunks,),
+            in_specs=[
+                SCALARS, by_rows(model_width, chunks), whole(w_output.shape), by_rows(vw, chunks), by_rows(vw, chunks),
+                whole(gain_row.shape), by_rows(mixed_width, chunks), by_rows(LANES, chunks),
+                by_chunk((heads, BLOCK, key_width), chunks), by_chunk((heads, key_width, key_width), chunks),
+            ],
+            out_specs=[
+                by_chunk((heads, BLOCK, value_width), chunks), by_chunk((heads, BLOCK, value_width), chunks),
+                by_chunk((heads, key_width, value_width), chunks), by_rows(vw, chunks),
+                whole((8, value_width)), whole((heads, key_width, value_width)),
+            ],
+            out_shape=core_shapes,
+            compiler_params=params(),
+            name="mixer_core_grad",
+        )(meta, grad_block, w_output, core, gate, gain_row, qkv, scal, w_part, drop)
     grad_w_output = dot_tn(gated, grad_block).astype(bf16)
+    grad_w_outgate = dot_tn(block_rows, grad_gate_pre).astype(bf16)
 
     later = from_later(
         jnp.concatenate([block_map[:, :, :key_width], pulled], axis=2).astype(bf16), "seq"
     )
-    grad_conv, grad_small, sums = pl.pallas_call(
+    later, grad_w_output, grad_w_outgate = lax.optimization_barrier((later, grad_w_output, grad_w_outgate))
+    mlp_out, grad_w_outgate = lax.optimization_barrier((mlp_out, grad_w_outgate))
+    grad_w_outgate = lax.psum(grad_w_outgate, "seq")
+    grad_conv, grad_small, sums, edge = pl.pallas_call(
         functools.partial(backward_kernel, *sizes, chunks, others),
         grid=(chunks,),
         in_specs=[
@@ -1675,16 +1850,23 @@
             by_chunk((heads, key_width, value_width), chunks), by_chunk((heads, key_width, key_width), chunks),
             whole(dvec.shape),
         ],
-        out_specs=[by_rows(mixed_width, chunks), by_rows(LANES, chunks), whole((8, LANES))],
+        out_specs=[
+            by_rows(mixed_width, chunks), by_rows(LANES, chunks), whole((8, LANES)), whole((HALO, mixed_width)),
+        ],
         out_shape=[
             struct((seq_rows, mixed_width), f32), struct((seq_rows, LANES), bf16), struct((8, LANES), f32),
+            struct((HALO, mixed_width), f32),
         ],
-        scratch_shapes=[pltpu.VMEM((heads, key_width, value_width), f32)],
-        compiler_params=params(),
+        scratch_shapes=[
+            pltpu.VMEM((heads, key_width, value_width), f32), pltpu.VMEM((HALO, mixed_width), f32),
+            pltpu.VMEM((HALO, mixed_width), f32), pltpu.SemaphoreType.DMA((2,)),
+        ],
+        compiler_params=params(9),
         name="mixer_backward",
     )(meta, later, qkv, conv, scal, small, inverse, fresh, states, grad_core, inner, pull, drop, dvec)
 
-    edge = from_next(grad_conv[:HALO])
+    grad_small, *ff_grads = lax.optimization_barrier((grad_small, *ff_grads))
+    ff_grads = [lax.psum(part, "head") for part in ff_grads]
     step_rows = BLOCK // HALO
     last_halo = seq_rows // HALO - 1
     later_rows = pl.BlockSpec(
@@ -1713,8 +1895,6 @@
         name="projection_grad",
     )(meta, grad_conv, grad_conv, edge, pre, grad_gate_pre, grad_small, conv_all, block_rows, *weights)
 
-    grad_pre, *ff_grads = lax.optimization_barrier((grad_pre, *ff_grads))
-    ff_grads = [lax.psum(part, "head") for part in ff_grads]
     if cube:
         grad_normed = grad_rows
     else:
@@ -1739,11 +1919,13 @@
     gains = gains[:2].reshape(-1)
     first_part, second_part = gains[:model_width], gains[model_width : 2 * model_width]
     head_part = gains[2 * model_width :]
-    grad_w_all, mlp_out, *ff_grads = lax.optimization_barrier((grad_w_all, mlp_out, *ff_grads))
-    grad_w_down, grad_w_gate, grad_w_up, grad_w_query, grad_w_key, grad_w_value, grad_w_outgate, grad_w_output = widen(
-        ff_grads, grad_w_all, (qw, qw, vw, vw), grad_w_output
+    grad_w_query, grad_w_key, grad_w_value, grad_w_outgate, grad_w_output, grad_w_small = widen(
+        (grad_w_outgate, grad_w_output), grad_w_all, (qw, qw, vw)
     )
-    grad_w_small = grad_w_all[:, mixed_width + vw :].astype(f32)
+    grad_inputs, grad_w_query, mlp_out, *ff_grads = lax.optimization_barrier(
+        (grad_inputs, grad_w_query, mlp_out, *ff_grads)
+    )
+    grad_w_down, grad_w_gate, grad_w_up = widen(ff_grads)
     grad_taps = small_sums[:taps, :mixed_width].astype(f32)
     sums = small_sums[:2, mixed_width : mixed_width + heads].astype(f32)
     output = (hidden_in + mlp_out.astype(f32)).astype(bf16)
@@ -1755,8 +1937,8 @@
         grad_w_key,
         grad_w_value,
         grad_w_outgate,
-        grad_w_small[:, :heads],
-        grad_w_small[:, heads : 2 * heads],
+        grad_w_small[:heads].T,
+        grad_w_small[heads : 2 * heads].T,
         grad_taps[:, :qw],
         grad_taps[:, qw : 2 * qw],
         grad_taps[:, 2 * qw :],
@@ -1774,11 +1956,6 @@
 def from_previous(array):
     devices = lax.axis_size("seq")
     return lax.ppermute(array, "seq", [(i, i + 1) for i in range(devices - 1)])
-
-
-def from_next(array):
-    devices = lax.axis_size("seq")
-    return lax.ppermute(array, "seq", [(i + 1, i) for i in range(devices - 1)])
 
 
 def solution(mesh):

time: 792 us -> 745 us (0.941)
  Pallas kernels: 673 us -> 645 us
  waiting for transfers between devices: 26.6 us -> 11.4 us
  starting transfers between devices: 15.3 us -> 4.82 us
  matrix products: 11 us -> 19.8 us
    pallas_call x1, Pallas kernels: 235 us -> 193 us  [line_sum(): pl.pallas_call(functools.partial(line_sum_kernel, axis, cube, counts, tup...]
    pallas_call x1, Pallas kernels: 76.5 us -> 92.3 us  [shards(): pl.pallas_call(functools.partial(forward_kernel, *sizes, taps, chunks, cu...]
    ppermute x3, waiting for transfers between devices: 16.7 us -> 1.05 us  [from_later(): lax.ppermute(array, axis, [(i + by, i) for i in range(devices - by)])]
    ppermute x4 -> x0, starting transfers between devices: 11.2 us -> none  [the longest x3 9.68 us: from_earlier(): lax.ppermute(array, axis, [(i, i + by) for i in range(devices - by)])]
    psum x1, waiting for transfers between devices: 0.01 us -> 10.3 us  [shards(): ff_grads = [lax.psum(part, 'head') for part in ff_grads]]
    ppermute x4 -> x0, waiting for transfers between devices: 9.76 us -> none  [the longest x3 5.46 us: from_earlier(): lax.ppermute(array, axis, [(i, i + by) for i in range(devices - by)])]
    dot_general x1 -> x2, matrix products: 11 us -> 19.8 us  [dot_tn(): lax.dot_general(left, right, (((0,), (0,)), ((), ())), preferred_element_...]
  transfers between devices with their start and end apart: 10 -> 7, of which waited for: 5 -> 2; matrix products, arithmetic and copies ran while one was open for 5% -> 7% of each run, Pallas kernels for 65% -> 67%
where the time goes in v4:
time: 745 us; the launch traced here: 735 us
  Pallas kernels  645 us (87%)
  other arithmetic  29.7 us (4%)
  matrix products  19.8 us (3%)
  between operations  14.6 us (2%)
  waiting for transfers between devices  11.4 us (2%)
  local copies, waits for them, and re-layouts  9.73 us (1%)
    pallas_call x1, Pallas kernels, line_sum(): pl.pallas_call(functools.partial(line_sum_kernel, axis, cube, counts, tup...  193 us
    pallas_call x1, Pallas kernels, feed(): pl.pallas_call(functools.partial(feed_kernel, axis, devices, rows), in_sp...  134 us
    pallas_call x1, Pallas kernels, shards(): pl.pallas_call(functools.partial(forward_kernel, *sizes, taps, chunks, cu...  92.3 us
    pallas_call x1, Pallas kernels, shards(): pl.pallas_call(functools.partial(feed_core_kernel, sizes, chunks, 'head',...  59.2 us
    pallas_call x1, Pallas kernels, shards(): pl.pallas_call(functools.partial(projection_grad_kernel, mixed_width, doc...  54.2 us
    pallas_call x1, Pallas kernels, shards(): pl.pallas_call(functools.partial(output_kernel, *sizes, others, cube), gr...  49.6 us
    pallas_call x1, Pallas kernels, shards(): pl.pallas_call(functools.partial(backward_kernel, *sizes, chunks, others)...  32.9 us
    pallas_call x2, Pallas kernels, widen(): pl.pallas_call(functools.partial(widen_kernel, cuts, len(given)), grid=(s...  29.1 us
  transfers between devices with their start and end apart: 7, of which 2 were waited for; matrix products, arithmetic and copies ran while one was open for 7% of the time, Pallas kernels for 67%

profile of v4, /device:TPU:0, one launch (start us, length us, event | category | flops | bytes accessed | tf_op | source)
XLA Modules:
  0.0 734.9 jit_solution(10888260343999965534)
XLA Ops:
  7.3 0.7 fusion.21
  8.1 0.7 bitcast_subtract_fusion
  8.9 0.7 select_reduce_fusion.1
  9.8 2.5 fusion.7
  13.3 0.6 pad_add_fusion.meta
  14.3 1.1 maximum_maximum_fusion.ws_ref
  15.4 1.3 fusion.2.rows_ref
  16.7 92.3 %mixer_forward.1 = (f32[2048,1024]{1,0:T(8,128)}, f32[2048,1024]{1,0:T(8,128)}, f32[2048,512]{1,0:T(8,128)}, f32[2048,128]{1,0:T(8,128)}, f32[2048,128]{1,0:T(8,...) custom-call(s32[4]{0:T(128)} %pad_add_fusion.meta, ...), custom_call_target="tpu_custom_call" | custom-call | tf_op jit(solution)/shard_map/mixer_forward/pallas_call | solution.py:1663
  109.0 49.6 %mixer_output.1 = (f32[2048,512]{1,0:T(8,128)}, bf16[2048,512]{1,0:T(8,128)(2,1)}, bf16[8,2,256,256]{3,2,1,0:T(8,128)(2,1)}, f32[8,2,128,256]{3,2,1,0:T(8,128)}, f32[256,2048]{1,0:T(8,128)}) custom-call(s32[4]{0:T(128)} %pad_add_fusion.meta, bf16[3,2,128,384]{3,2,1,0:T(8,128)(2,1)} %get-tuple-element.115.maps_ref, ...), custom_call_target="tpu_custom_call" | custom-call | tf_op jit(solution)/shard_map/mixer_output/pallas_call | solution.py:1718
  158.6 2.0 multiply_reduce_fusion.2
  160.6 1.2 multiply_convert_fusion.own_ref
  161.8 134.4 %feed.1 = (bf16[1024,2048]{1,0:T(8,128)(2,1)}, bf16[1408,1024]{1,0:T(8,128)(2,1)}, bf16[1024,1408]{1,0:T(8,128)(2,1)}, bf16[1024,1408]{1,0:T(8,128)(2,1)}, bf16[...) custom-call(bf16[256,2048]{1,0:T(8,128)(2,1)} %multiply_convert_fusion.own_ref, ...), custom_call_target="tpu_custom_call" | custom-call | tf_op jit(solution)/shard_map/feed/pallas_call | solution.py:1200
  296.3 0.4 all-reduce.7.cloned.1.call-start
  296.8 0.9 slice.123
  297.7 2.3 multiply_reduce_fusion
  300.2 2.4 fusion.14
  302.6 59.2 %feed_core.1 = (bf16[1408,2048]{1,0:T(8,128)(2,1)}, bf16[2048,1408]{1,0:T(8,128)(2,1)}, bf16[2048,1408]{1,0:T(8,128)(2,1)}, bf16[2048,2048]{1,0:T(8,128)(2,1)}, ...) custom-call(s32[4]{0:T(128)} %pad_add_fusion.meta, ...), custom_call_target="tpu_custom_call" | custom-call | tf_op jit(solution)/shard_map/feed_core/pallas_call | solution.py:1780
  361.8 1.0 convert.30
  362.8 1.3 collective-permute-start.2
  364.1 1.3 collective-permute-start.1
  365.4 1.5 collective-permute-start
  366.8 9.9 %convolution_convert_fusion = bf16[2048,512]{1,0:T(8,128)(2,1)} fusion(bf16[2048,2048]{1,0:T(8,128)(2,1)} %get-tuple-element.134.rows_ref.refs_0_, bf16[2048,512]{1,0:T(8,128)(2,1)} %get-tuple-element.135.grad_gate_ref), kind=kOutput, calls=%fused_computation.5 | convolution fusion | flops 4296015872 | bytes 12582912 | tf_op jit(solution)/shard_map/dot_general | solution.py:26
  376.7 9.9 %convolution_convert_fusion.1.refs_2_ = bf16[512,2048]{1,0:T(8,128)(2,1)} fusion(bf16[2048,512]{1,0:T(8,128)(2,1)} %get-tuple-element.132, bf16[2048,2048]{1,0:T(8,128)(2,1)} %get-tuple-element.133), kind=kOutput, calls=%fused_computation.6 | convolution fusion | flops 4296015872 | bytes 12582912 | tf_op jit(solution)/shard_map/dot_general | solution.py:26
  386.6 1.0 collective-permute-done.1
  387.7 0.9 pad_maximum_fusion.maps_ref
  388.9 32.9 %mixer_backward.1 = (f32[2048,1024]{1,0:T(8,128)}, bf16[2048,128]{1,0:T(8,128)(2,1)}, f32[8,128]{1,0:T(8,128)}, f32[8,1024]{1,0:T(8,128)}) custom-call(s32[4]{0:T(128)} %pad_add_fusion.meta, bf16[3,2,128,384]{3,2,1,0:T(8,128)(2,1)} %pad_maximum_fusion.maps_ref, bf16[2048,1024]{1,0:T(8,128)(2,1)} %get-tuple-element.119.qkv_ref, ...), custom_call_target="tpu_custom_call" | custom-call | tf_op jit(solution)/shard_map/mixer_backward/pallas_call | solution.py:1842
  421.8 0.7 fusion.12
  422.5 54.2 %projection_grad.1 = (bf16[2048,1152]{1,0:T(8,128)(2,1)}, f32[8,1024]{1,0:T(8,128)}, f32[256,2048]{1,0:T(8,128)}, f32[8,2048]{1,0:T(8,128)}) custom-call(s32[4]{0:T(128)} %pad_add_fusion.meta, f32[2048,1024]{1,0:T(8,128)} %get-tuple-element.145.grad_conv_ref.later_ref, f32[2048,1024]{1,0:T(8,128)} %get-tuple-element.145.grad_conv_ref.later_ref, ...), custom_call_target="tpu_custom_call" | custom-call | tf_op jit(solution)/shard_map/projection_grad/pallas_call | solution.py:1875
  476.7 0.8 slice.90
  477.6 0.8 convert.31
  478.4 0.7 pad.19.refs_4_
  479.0 0.6 fusion.10.refs_3_
  479.7 193.2 %line_sum.1 = (bf16[2048,1152]{1,0:T(8,128)(2,1)}, bf16[512,2048]{1,0:T(8,128)(2,1)}, bf16[32,1152]{1,0:T(8,128)(2,1)}, bf16[32,2176]{1,0:T(8,128)(2,1)}, f32[8,2176]{1,0:T(8,128)}) custom-call(bf16[2048,2048]{1,0:T(8,128)(2,1)} %get-tuple-element.134.rows_ref.refs_0_, bf16[2048,1152]{1,0:T(8,128)(2,1)} %get-tuple-element.157.refs_1_, ...), custom_call_target="tpu_custom_call" | custom-call | flops 100000000 | bytes 40000000 | tf_op jit(solution)/shard_map/line_sum/pallas_call | solution.py:963
  672.9 0.7 slice_convert_fusion.1
  673.6 0.6 slice.110
  674.2 0.9 slice.92
  675.1 0.6 slice.111
  675.7 2.4 fusion.6
  678.1 0.7 slice_convert_fusion.3
  678.7 0.5 slice_bitcast_fusion.2
  679.3 0.6 fusion.16
  679.9 0.6 fusion.15
  680.5 4.1 fusion.5
  684.6 10.6 %widen.2 = (f32[2048,256]{1,0:T(8,128)}, f32[2048,256]{1,0:T(8,128)}, f32[2048,512]{1,0:T(8,128)}, f32[2048,512]{1,0:T(8,128)}, f32[512,2048]{1,0:T(8,128)}, /*index=5*/f32[128,2048]{1,0:T(8,128)}) custom-call(bf16[2048,512]{1,0:T(8,128)(2,1)} %all-reduce.7.cloned.1.call-done.refs_0_, bf16[512,2048]{1,0:T(8,128)(2,1)} %get-tuple-element.163.refs_1_, ...), custom_call_target="tpu_custom_call" | custom-call | tf_op jit(solution)/shard_map/widen/pallas_call | solution.py:1552
  695.2 10.3 %all-reduce.9.cloned.1.call-done = (bf16[1408,2048]{1,0:T(8,128)(2,1)}, bf16[2048,1408]{1,0:T(8,128)(2,1)}, bf16[2048,1408]{1,0:T(8,128)(2,1)}) async-done(((bf16[1408,2048]{1,0:T(8,128)(2,1)}, bf16[2048,1408]{1,0:T(8,128)(2,1)}, bf16[2048,1408]{1,0:T(8,128)(2,1)}), (bf16[1408,2048]{1,0:T(8,128)(2,1)}, bf16[2048,1408]{1,0:T(8,128)(2,1)}, bf16[2048,1408]{1,0:T(8,128)(2,1)})) %all-reduce.9.cloned.1.call-update) | async-done | bytes 17301520 | tf_op jit(solution)/shard_map/psum | solution.py:1869
  705.5 2.5 add_convert_fusion
  708.0 1.5 slice_bitcast_fusion
  709.5 18.5 %widen.3 = (f32[1408,2048]{1,0:T(8,128)}, f32[2048,1408]{1,0:T(8,128)}, f32[2048,1408]{1,0:T(8,128)}) custom-call(bf16[1408,2048]{1,0:T(8,128)(2,1)} %get-tuple-element.180.refs_0_, bf16[2048,1408]{1,0:T(8,128)(2,1)} %get-tuple-element.181.refs_1_, bf16[2048,1408]{1,0:T(8,128)(2,1)} %get-tuple-element.182.refs_2_), custom_call_target="tpu_custom_call" | custom-call | tf_op jit(solution)/shard_map/widen/pallas_call | solution.py:1552
  (72 shorter events, 2.3 us)
Async XLA Ops:
  7.2 5.2 copy-start.9
  7.2 5.5 copy-start.10
  7.2 154.6 %all-gather.2.cloned.1.call-start = ((), (), s32[]{:S(2)}) async-start(), calls=%async_computation.1 | async-start | bytes 5242880 | tf_op jit(solution)/shard_map/all_gather | solution.py:1707
  9.7 3.4 copy-start.15
  9.7 3.4 copy-start.16
  9.7 4.2 copy-start.13
  9.7 4.2 copy-start.14
  9.7 4.2 copy-start.11
  9.8 4.2 copy-start
  12.3 3.1 copy-start.5
  12.3 376.3 %reduce-scatter.2.cloned.1.call-start = ((), (), s32[]{:S(2)}) async-start(), calls=%async_computation.2 | async-start | bytes 5242880 | tf_op jit(solution)/shard_map/reduce_scatter | solution.py:1752
  13.3 3.4 copy-start.8
  14.0 2.7 copy-start.6
  109.0 49.6 %copy-start.1 = (bf16[256,2048]{1,0:T(8,128)(2,1)S(1)}, bf16[256,2048]{1,0:T(8,128)(2,1)}, u32[]{:S(2)}) copy-start(bf16[256,2048]{1,0:T(8,128)(2,1)} %param.25) | copy-start | bytes 3145732
  158.6 2.0 copy-start.7
  296.3 388.3 %all-reduce.7.cloned.1.call-start = ((), (), s32[]{:S(2)}) async-start(), calls=%async_computation.3 | async-start | bytes 4194304 | tf_op jit(solution)/shard_map/psum | solution.py:1841
  297.7 2.3 copy-start.3
  297.7 2.5 copy-start.4
  362.8 23.9 %collective-permute-start.2 = (bf16[2,128,384]{2,1,0:T(8,128)(2,1)S(1)}, bf16[2,128,384]{2,1,0:T(8,128)(2,1)S(1)}, u32[]{:S(2)}, u32[]{:S(2)}) collective-permute-start(bf16[2,128,384]{2,1,0:T(8,128)(2,1)S(1)} %pad_maximum_fusion.1), channel_id=1, source_target_pairs={{8,0},{16,8},{24,16},{9,1},{17,9},{25,17},{10,2},{18,10},{26,18},{... | collective-permute-start | bytes 589832 | tf_op jit(solution)/shard_map/ppermute | solution.py:1579
  364.1 23.6 %collective-permute-start.1 = (bf16[2,128,384]{2,1,0:T(8,128)(2,1)S(1)}, bf16[2,128,384]{2,1,0:T(8,128)(2,1)S(1)}, u32[]{:S(2)}, u32[]{:S(2)}) collective-permute-start(bf16[2,128,384]{2,1,0:T(8,128)(2,1)S(1)} %pad_maximum_fusion.1), channel_id=1, source_target_pairs={{16,0},{24,8},{17,1},{25,9},{18,2},{26,10},{19,3},{27,11},{20,4},{... | collective-permute-start | bytes 589832 | tf_op jit(solution)/shard_map/ppermute | solution.py:1579
  365.4 22.3 %collective-permute-start = (bf16[2,128,384]{2,1,0:T(8,128)(2,1)S(1)}, bf16[2,128,384]{2,1,0:T(8,128)(2,1)S(1)}, u32[]{:S(2)}, u32[]{:S(2)}) collective-permute-start(bf16[2,128,384]{2,1,0:T(8,128)(2,1)S(1)} %pad_maximum_fusion.1), channel_id=1, source_target_pairs={{24,0},{25,1},{26,2},{27,3},{28,4},{29,5},{30,6},{31,7}} | collective-permute-start | bytes 589832 | tf_op jit(solution)/shard_map/ppermute | solution.py:1579
  388.6 316.9 %all-reduce.9.cloned.1.call-start = ((), (), s32[]{:S(2)}) async-start(), calls=%async_computation.4 | async-start | bytes 34603008 | tf_op jit(solution)/shard_map/psum | solution.py:1869
  421.7 0.8 copy-start.12
  675.1 5.4 copy-start.2
Sparse Core Ops, SparseCore 0:
  12.4 83.4 all-gather.1
  296.4 77.6 reduce-scatter.1
  388.7 88.6 all-reduce.6
  481.5 223.9 all-reduce.8

commit v5 on v4

--- a/solution.py
+++ b/solution.py
@@ -459,10 +459,14 @@
 
 def output_kernel(
     heads, key_width, value_width, docs, others, cube,
-    meta, maps_ref, starts_ref, w_in_ref, u_ref, qkv_ref, scal_ref, gate_ref, gain_ref, w_output_ref,
-    core_ref, gated_ref, fresh_ref, state_ref, mixed_ref,
-    incoming, *refs,
+    meta, maps_ref, starts_ref, w_in_ref, u_ref, qkv_ref, scal_ref, gate_ref, gain_ref, w_output_ref, *refs,
 ):
+    if cube:
+        inputs_ref, next_gain_ref, *refs = refs
+    core_ref, gated_ref, fresh_ref, state_ref, mixed_ref, *refs = refs
+    if cube:
+        next_ref, *refs = refs
+    incoming, *refs = refs
     step = pl.program_id(0)
     chunk = cube_order("head", 7 - step) if cube else step
     qw = heads * key_width
@@ -503,7 +507,14 @@
         mixed_ref[...] = mixed.astype(bf16)
         return
 
-    scatter_block(step, CubeScatter("head", mixed_ref, *refs), mixed)
+    total, *refs = refs
+    scatter_block(step, CubeScatter("head", total, *refs), mixed)
+
+    @pl.when(step == 7)
+    def _():
+        hidden_in = inputs_ref[...].astype(f32) + total[...]
+        mixed_ref[...] = hidden_in
+        next_ref[...] = rms_scale(hidden_in, next_gain_ref[...]).astype(bf16)
 
 
 def core_grad_kernel(
@@ -565,23 +576,35 @@
 
 
 def backward_kernel(
-    heads, key_width, value_width, docs, chunks, others,
+    heads, key_width, value_width, docs, chunks, others, cube,
     meta, maps_ref, qkv_ref, act_ref, scal_ref, small_ref, inv_ref, fresh_ref, state_ref,
-    grad_core_ref, inner_ref, pull_ref, drop_ref, dvec_ref,
-    grad_conv_ref, grad_small_ref, sums_ref, edge_ref,
-    carried, edge_out, edge_in, edge_sem,
+    grad_core_ref, inner_ref, pull_ref, drop_ref, dvec_ref, *refs,
 ):
+    if cube:
+        feed_ref, *refs = refs
+    grad_conv_ref, grad_small_ref, sums_ref, edge_ref, *refs = refs
+    if cube:
+        feed_sum_ref, *refs = refs
+    carried, edge_out, edge_in, edge_sem, *refs = refs
     step = pl.program_id(0)
     chunk = chunks - 1 - step
+
+    @pl.when(step == 0)
+    def _():
+        line_barrier("seq", "head" if cube else None)
+
+    if cube:
+        rows = feed_ref.shape[0] // 8
+        total, *refs = refs
+        part = pl.ds(pl.multiple_of(cube_order("head", 7 - step) * rows, rows), rows)
+        scatter = CubeScatter("head", total, *refs)
+        scatter_block(step, scatter, feed_ref[part, :].astype(f32), inside=True)
     groups, group = lax.axis_size("seq"), lax.axis_index("seq")
     edge = pltpu.make_async_remote_copy(
         edge_out, edge_in, edge_sem.at[0], edge_sem.at[1],
         device_id={"seq": jnp.maximum(group - 1, 0)}, device_id_type=MESH,
     )
 
-    @pl.when(step == 0)
-    def _():
-        line_barrier("seq")
     qw = heads * key_width
 
     @pl.when(step == 0)
@@ -666,6 +689,9 @@
 
     @pl.when(step == chunks - 1)
     def _():
+        if cube:
+            scatter.finish()
+            feed_sum_ref[...] = total[...].astype(bf16)
         edge_out[...] = grad_conv_ref[0:HALO, :]
 
         @pl.when(group > 0)
@@ -719,14 +745,15 @@
         moved = ext[lag : lag + BLOCK, :] * keep
         total = total + conv_ref[lag : lag + 1, :] * moved
         grad_taps_ref[lag : lag + 1, :] += jnp.sum(pre * moved, axis=0, keepdims=True)
+    width = grad_gate_ref.shape[1]
     grad_pre_ref[:, :mixed] = total.astype(bf16)
-    grad_pre_ref[:, mixed:] = grad_small_ref[...]
+    grad_pre_ref[:, mixed : mixed + width] = grad_gate_ref[...]
+    grad_pre_ref[:, mixed + width :] = grad_small_ref[...]
     grad = jnp.zeros(grad_rows_ref.shape, f32)
     begin = 0
-    for ref in (wq_ref, wk_ref, wv_ref, ws_ref):
+    for ref in (wq_ref, wk_ref, wv_ref, wg_ref, ws_ref):
         grad = grad + dot_nt(grad_pre_ref[:, begin : begin + ref.shape[1]], ref[...])
         begin += ref.shape[1]
-    grad = grad + dot_nt(grad_gate_ref[...], wg_ref[...])
     gain_sum_ref[0:1, :] += jnp.sum(grad * rows_ref[...].astype(f32), axis=0, keepdims=True)
     if cube:
         scatter_block(step, CubeScatter("head", grad_rows_ref, *refs), grad)
@@ -773,6 +800,7 @@
 
     def __init__(self, axis, counts, depths, parts, passed, arrived, sums, reduce_sems, back_sems):
         self.axis, self.counts, self.depths = axis, counts, depths
+        self.single = [array.shape[0] == depth for array, depth in zip(sums, depths)]
         self.parts, self.passed, self.arrived, self.sums = parts, passed, arrived, sums
         self.sems = (reduce_sems, back_sems)
         self.devices, self.place = lax.axis_size(axis), lax.axis_index(axis)
@@ -806,7 +834,8 @@
             toward = place - 1 if half == 0 else place + 1
             away = place + 1 if half == 0 else place - 1
             for index in range(len(self.counts)):
-                handle(half, index, toward, away, place == ends[0], place == ends[1])
+                if half == 0 or not self.single[index]:
+                    handle(half, index, toward, away, place == ends[0], place == ends[1])
 
     def reduce(self, step):
         def handle(half, index, toward, away, begin, end):
@@ -877,11 +906,15 @@
 def line_sum_kernel(axis, cube, counts, depths, *refs):
     total = len(counts)
     rows_ref, grads_ref, *refs = refs
-    parts, sums, refs = refs[: total - 1], refs[total - 1 : 2 * total - 1], refs[2 * total - 1 :]
+    parts, refs = refs[: total - 2], refs[total - 2 :]
     if cube:
-        whole_ref, refs = refs[0], refs[1:]
-    product, *refs = refs
-    parts = (product, *parts)
+        block_ref, *refs = refs
+    sums, refs = refs[:total], refs[total:]
+    if cube:
+        whole_ref, blocks_ref, *refs = refs
+    product, turned, *refs = refs
+    parts = (product, turned, *parts)
+    width = product.shape[1]
     arrived, passed, refs = refs[:total], refs[total : 2 * total], refs[2 * total :]
     share = BLOCK // depths[0]
     tiles = counts[0] // share
@@ -889,14 +922,19 @@
     line_barrier(axis, "head" if cube else None)
 
     begin = max(counts)
-    final = CubeTotal(*refs[4 * total :]) if cube else None
+    if cube:
+        final = CubeTotal(*refs[4 * total : 4 * total + 4])
+        gather = CubeGather("head", block_ref, blocks_ref, *refs[4 * total + 4 :], enter=False)
+        gather.first()
+
+    turned[...] = dot_tn(grads_ref[:, width:], rows_ref[...])[: turned.shape[0], :].astype(bf16)
 
     def step_on(step, carry):
         @pl.when((step % share == 0) & (step < tiles * share))
         def _():
             for half in range(2):
                 columns = pl.ds(pl.multiple_of((half * tiles + step // share) * BLOCK, BLOCK), BLOCK)
-                product[columns, :] = dot_tn(rows_ref[:, columns], grads_ref[...]).astype(bf16)
+                product[columns, :] = dot_tn(rows_ref[:, columns], grads_ref[:, :width]).astype(bf16)
 
         @pl.when(step < line.steps)
         def _():
@@ -907,6 +945,11 @@
             line.back(step - begin)
 
         if cube:
+            for at, phase in ((begin // 2, gather.second), (begin * 3 // 4, gather.third), (begin, gather.fourth)):
+                @pl.when(step == at)
+                def _():
+                    phase()
+
             after = begin + line.skew * line.devices
             for stage in range(4):
                 @pl.when(step == after + 3 * stage)
@@ -923,6 +966,8 @@
     lax.fori_loop(0, begin + line.steps, step_on, 0)
     line.settle(0)
     line.settle(1)
+    if cube:
+        gather.last()
 
 
 class CubeTotal:
@@ -944,34 +989,38 @@
 
 
 def line_scratch(arrays, depths, moves):
-    counts = tuple(array.shape[0] // (2 * depth) for array, depth in zip(arrays, depths))
+    counts = tuple(max(array.shape[0] // (2 * depth), 1) for array, depth in zip(arrays, depths))
     semaphores = []
     for count in counts:
         semaphores += [pltpu.SemaphoreType.DMA((2 * count,))] * 2
     return counts, semaphores * moves
 
 
-def line_sum(rows, grads, given, depths, axis, collective_id):
+def line_sum(rows, grads, blocks, given, depths, axis, collective_id):
     cube = lax.axis_size("head") == 8
-    arrays = (struct((rows.shape[1], grads.shape[1]), bf16), *given)
+    arrays = (
+        struct((rows.shape[1], grads.shape[1] - LANES), bf16), struct((2 * HALO, rows.shape[1]), bf16), *given,
+    )
     counts, semaphores = line_scratch(arrays, depths, 2)
     vmem = pl.BlockSpec(memory_space=pltpu.VMEM)
-    scratch = [pltpu.VMEM(array.shape, bf16) for array in (arrays[0], *arrays, *arrays)] + semaphores
+    scratch = [pltpu.VMEM(array.shape, bf16) for array in (*arrays[:2], *arrays, *arrays)] + semaphores
     total = (8, arrays[-1].shape[1])
     if cube:
-        scratch += [pltpu.VMEM((3,) + total, f32)] * 2 + [pltpu.SemaphoreType.DMA((3,))] * 2
+        scratch += [pltpu.VMEM((3,) + total, f32)] * 2 + [pltpu.SemaphoreType.DMA((3,))] * 2 + CUBE_SEMAPHORES
     results = pl.pallas_call(
         functools.partial(line_sum_kernel, axis, cube, counts, tuple(depths)),
-        in_specs=[vmem] * (len(arrays) + 1),
-        out_specs=[vmem] * (len(arrays) + cube),
-        out_shape=[struct(array.shape, bf16) for array in arrays] + [struct(total, f32)] * cube,
+        in_specs=[vmem] * len(arrays) + [ANYWHERE] * cube,
+        out_specs=[vmem] * (len(arrays) + cube) + [ANYWHERE] * cube,
+        out_shape=[struct(array.shape, bf16) for array in arrays]
+        + [struct(total, f32)] * cube
+        + [struct((8 * block.shape[0], block.shape[1]), bf16) for block in blocks],
         scratch_shapes=scratch,
         compiler_params=pltpu.CompilerParams(
             collective_id=collective_id, has_side_effects=True, vmem_limit_bytes=VMEM_LIMIT
         ),
         cost_estimate=pl.CostEstimate(flops=10**8, bytes_accessed=40 * 10**6, transcendentals=0),
         name="line_sum",
-    )(rows, grads, *given)
+    )(rows, grads, *given, *blocks)
     if not cube:
         results = [*results, lax.psum(results[-1][:8].astype(f32), "head")]
     return results
@@ -1114,15 +1163,15 @@
 
         @pl.when((way == 1) & (step > 0))
         def _():
-            for turn in range(2):
-                side = jnp.where(2 * place < devices, turn, 1 - turn)
-                block = jnp.where(side == 1, devices - 1 - hop, hop)
-                begins = place == jnp.where(side == 1, devices - 1, 0)
-                valid = jnp.where(side == 1, block < place, block > place)
-
-                @pl.when(valid)
-                def _():
-                    for part in range(4):
+            for part in range(4):
+                for turn in range(2):
+                    side = jnp.where(2 * place < devices, turn, 1 - turn)
+                    block = jnp.where(side == 1, devices - 1 - hop, hop)
+                    begins = place == jnp.where(side == 1, devices - 1, 0)
+                    valid = jnp.where(side == 1, block < place, block > place)
+
+                    @pl.when(valid)
+                    def _():
                         @pl.when(jnp.logical_not(begins))
                         def _():
                             chain(block, side, part, place + 2 * side - 1).wait_recv()
@@ -1235,9 +1284,9 @@
     THIRD = ((2, 1, 1), (4, 0, 1))
     FOURTH = ((6, 0, 1), (6, 1, 1))
 
-    def __init__(self, axis, own_ref, all_ref, own_sem, send_sem, recv_sem, stride=None, lead=0):
+    def __init__(self, axis, own_ref, all_ref, own_sem, send_sem, recv_sem, stride=None, lead=0, enter=True):
         self.axis, self.own_ref, self.all_ref = axis, own_ref, all_ref
-        self.stride, self.lead = stride or own_ref.shape[0], lead
+        self.stride, self.lead, self.enter = stride or own_ref.shape[0], lead, enter
         self.own_sem, self.send_sem, self.recv_sem = own_sem, send_sem, recv_sem
         self.place = lax.axis_index(axis)
         self.rows = own_ref.shape[0]
@@ -1267,7 +1316,8 @@
 
     def first(self):
         if self.own_sem is not None:
-            cube_barrier(self.axis, self.place)
+            if self.enter:
+                cube_barrier(self.axis, self.place)
             self.own().start()
         for move in self.FIRST:
             self.copy(*move).start()
@@ -1333,20 +1383,25 @@
 
 def feed_core_kernel(
     sizes, chunks, axis, tiles,
-    meta, own_ref, blocks_ref, grads_ref, hidden_ref, feed_gate_ref, feed_up_ref,
+    meta, total_in, hidden_in, low_ref, next_gain_ref, blocks_ref, grads_ref, hidden_ref, feed_gate_ref, feed_up_ref,
     w_output_ref, core_ref, gate_ref, gain_ref, qkv_ref, scal_ref, w_in_ref, drop_ref,
     down_out, gate_out, up_out, all_ref, *refs,
 ):
-    outs, (rows_ref, copy_sem, send_sem, recv_sem, *later) = refs[:6], refs[6:]
+    outs, (grad_in_ref, gain_sum_ref, rows_ref, copy_sem, send_sem, recv_sem, *later) = refs[:6], refs[6:]
     step = pl.program_id(0)
-    gather = CubeGather(axis, own_ref, rows_ref, None, send_sem, recv_sem)
-    rows = own_ref.shape[0]
+    rows = total_in.shape[0]
+    own = pl.ds(pl.multiple_of(lax.axis_index(axis) * rows, rows), rows)
+    gather = CubeGather(axis, rows_ref.at[own, :], rows_ref, None, send_sem, recv_sem)
 
     @pl.when(step == 0)
     def _():
+        grad_norm, gain_sum = rms_back(hidden_in[...], next_gain_ref[...], total_in[...])
+        grad_in = low_ref[...].astype(f32) + grad_norm
+        grad_in_ref[...] = grad_in
+        gain_sum_ref[0:1, :] = gain_sum[None, :]
+        rows_ref[own, :] = grad_in.astype(bf16)
         cube_barrier(axis, gather.place)
         gather.first()
-        rows_ref[pl.ds(pl.multiple_of(gather.place * rows, rows), rows), :] = own_ref[...]
 
     @pl.when(step == tiles - 1)
     def _():
@@ -1449,6 +1504,9 @@
             self.given[pl.ds(mask // 2 * 2 * piece, 2 * piece), :] = block.astype(bf16)
             for half in range(2):
                 self.core_copy(mask, half).start()
+            if mask == 1:
+                self.send(2, 0, 4, self.waiting[0] + self.arrived(0, 0, 2))
+                self.send(1, 1, 2, self.waiting[1] + self.arrived(0, 1, 4))
             return
         parts = []
         for half in range(2):
@@ -1472,8 +1530,6 @@
 
     def finish(self):
         piece = self.piece
-        self.send(2, 0, 4, self.waiting[0] + self.arrived(0, 0, 2))
-        self.send(1, 1, 2, self.waiting[1] + self.arrived(0, 1, 4))
         self.total_ref[0:piece, :] += self.arrived(1, 0, 2)
         self.total_ref[piece:, :] += self.arrived(2, 1, 4)
         self.total_ref[0:piece, :] += self.arrived(2, 0, 4)
@@ -1485,19 +1541,21 @@
             self.chip_copy(index, half, toward).wait_send()
 
 
-def scatter_block(step, scatter, block):
-    @pl.when(step == 0)
-    def _():
-        cube_barrier("head", scatter.place)
+def scatter_block(step, scatter, block, inside=False):
+    if not inside:
+        @pl.when(step == 0)
+        def _():
+            cube_barrier("head", scatter.place)
 
     for mask in range(8):
         @pl.when(step == 7 - mask)
         def _():
             scatter.take(mask, block)
 
-    @pl.when(step == 7)
-    def _():
-        scatter.finish()
+    if not inside:
+        @pl.when(step == 7)
+        def _():
+            scatter.finish()
 
 
 def cube_scatter_scratch(rows, width):
@@ -1527,7 +1585,6 @@
             result[...] = all_in[:, begin : begin + cut].astype(f32)
             begin += cut
         refs = refs[len(cuts) :]
-        refs[-1][...] = all_in[:, begin:].astype(f32).T
     for source, result in zip(given, refs):
         result[...] = source[...].astype(f32)
 
@@ -1543,12 +1600,9 @@
     specs = [part(shape) for shape in shapes]
     if cuts:
         sources.append(columns)
-        rows, width = columns.shape
-        rest = width - sum(cuts)
-        cut_shapes = [(rows, cut) for cut in cuts]
+        cut_shapes = [(columns.shape[0], cut) for cut in cuts]
         specs = [part(shape) for shape in cut_shapes] + specs
-        specs.append(pl.BlockSpec((rest, rows // steps), lambda step: (0, step)))
-        shapes = cut_shapes + shapes + [(rest, rows)]
+        shapes = cut_shapes + shapes
     return pl.pallas_call(
         functools.partial(widen_kernel, cuts, len(given)),
         grid=(steps,),
@@ -1631,7 +1685,7 @@
     grad_low = grad_out.astype(bf16)
     w_small = jnp.concatenate([w_decay, w_beta, jnp.zeros((model_width, LANES - 2 * heads), bf16)], axis=1)
     weights = (w_query, w_key, w_value, w_outgate, w_small)
-    all_width = mixed_width + LANES
+    all_width = mixed_width + vw + LANES
     conv_all = jnp.concatenate([conv_query, conv_key, conv_value], axis=1)
     dvec = jnp.zeros((8, LANES), f32)
     dvec = dvec.at[0, :heads].set(decay_bias).at[1, :heads].set(-jnp.exp(decay_log))
@@ -1715,44 +1769,49 @@
     def chunk_back(shape):
         return pl.BlockSpec((1,) + tuple(shape), lambda step: (last_first(step),) + (0,) * len(shape))
 
-    core, gated, fresh, states, mixed_part = pl.pallas_call(
+    second_row = second_gain[None, :]
+    own_rows = (inputs, second_row) if cube else ()
+    core, gated, fresh, states, *mixed_parts = pl.pallas_call(
         functools.partial(output_kernel, *sizes, others, cube),
         grid=(chunks,),
         in_specs=[
             SCALARS, whole(earlier.shape), chunk_back(map_shape), chunk_back((heads, BLOCK, key_width)),
             chunk_back((heads, BLOCK, value_width)), rows_back(mixed_width), rows_back(LANES), rows_back(vw),
-            whole(gain_row.shape), held(w_output.shape),
+            whole(gain_row.shape), held(w_output.shape), *(held(array.shape) for array in own_rows),
         ],
         out_specs=[
             rows_back(vw), rows_back(vw), chunk_back((heads, BLOCK, value_width)),
             chunk_back((heads, key_width, value_width)),
-            whole((row_count, model_width)) if cube else rows_back(model_width),
+            *([whole((row_count, model_width))] * 2 if cube else [rows_back(model_width)]),
         ],
         out_shape=[
             struct((seq_rows, vw), f32), struct((seq_rows, vw), bf16),
             struct((chunks, heads, BLOCK, value_width), bf16),
             struct((chunks, heads, key_width, value_width), f32),
-            struct((row_count, model_width), f32) if cube else struct((seq_rows, model_width), bf16),
+            *(
+                [struct((row_count, model_width), f32), struct((row_count, model_width), bf16)]
+                if cube else [struct((seq_rows, model_width), bf16)]
+            ),
         ],
         scratch_shapes=[pltpu.VMEM((heads, key_width, value_width), f32)]
-        + (cube_scatter_scratch(row_count, model_width) if cube else []),
+        + (
+            [pltpu.VMEM((row_count, model_width), f32), *cube_scatter_scratch(row_count, model_width)]
+            if cube else []
+        ),
         compiler_params=params(5 if cube else None),
         name="mixer_output",
-    )(meta, earlier, starts, w_part, u_part, qkv, scal, gate, gain_row, w_output)
+    )(meta, earlier, starts, w_part, u_part, qkv, scal, gate, gain_row, w_output, *own_rows)
     if cube:
-        mixer_out = mixed_part
+        hidden_in, normed_two = mixed_parts
     else:
-        mixer_out = lax.psum_scatter(mixed_part, "head", scatter_dimension=0, tiled=True).astype(f32)
-
-    hidden_in = inputs_f + mixer_out
-    normed_two = rms_scale(hidden_in, second_gain).astype(bf16)
+        mixer_out = lax.psum_scatter(mixed_parts[0], "head", scatter_dimension=0, tiled=True).astype(f32)
+        hidden_in = inputs_f + mixer_out
+        normed_two = rms_scale(hidden_in, second_gain).astype(bf16)
+
     mlp_block, hidden, grad_gate, grad_up, mlp_part, grad_normed_two = feed(
         normed_two, grad_block_two, w_gate, w_up, w_down, "seq", 3
     )
     mlp_out = lax.psum_scatter(mlp_part, "seq", scatter_dimension=0, tiled=True)
-    grad_hidden_norm, grad_second = rms_back(hidden_in, second_gain, grad_normed_two)
-    grad_hidden_in = grad_out + grad_hidden_norm
-    grad_mix = grad_hidden_in.astype(bf16)
     core_shapes = [
         struct((chunks, heads, BLOCK, value_width), bf16), struct((chunks, heads, BLOCK, value_width), f32),
         struct((chunks, heads, key_width, value_width), f32), struct((seq_rows, vw), bf16),
@@ -1760,6 +1819,7 @@
     ]
     if cube:
         tiles = model_width // BLOCK
+        owned = (grad_normed_two, hidden_in, grad_low, second_row)
         units, mlp_rows = hidden.shape
 
         def tile(step):
@@ -1781,7 +1841,7 @@
             functools.partial(feed_core_kernel, sizes, chunks, "head", tiles),
             grid=(tiles + chunks,),
             in_specs=[
-                SCALARS, held(grad_mix.shape), tall, tall, *(held(array.shape) for array in (hidden, grad_gate, grad_up)),
+                SCALARS, *(held(array.shape) for array in owned), tall, tall, *(held(array.shape) for array in (hidden, grad_gate, grad_up)),
                 held(w_output.shape), core_rows(vw), core_rows(vw), whole(gain_row.shape), core_rows(mixed_width),
                 core_rows(LANES), core_blocks((heads, BLOCK, key_width)), core_blocks((heads, key_width, key_width)),
             ],
@@ -1790,10 +1850,12 @@
                 core_blocks((heads, BLOCK, value_width)), core_blocks((heads, BLOCK, value_width)),
                 core_blocks((heads, key_width, value_width)), core_rows(vw),
                 whole((8, value_width)), whole((heads, key_width, value_width)),
+                whole((row_count, model_width)), whole((8, model_width)),
             ],
             out_shape=[
                 struct((units, model_width), bf16), struct((model_width, units), bf16),
                 struct((model_width, units), bf16), struct((seq_rows, model_width), bf16), *core_shapes,
+                struct((row_count, model_width), f32), struct((8, model_width), f32),
             ],
             scratch_shapes=[
                 pltpu.VMEM((seq_rows, model_width), bf16), pltpu.SemaphoreType.DMA, *CUBE_SEMAPHORES[1:],
@@ -1804,12 +1866,16 @@
             compiler_params=params(6),
             name="feed_core",
         )(
-            meta, grad_mix, mlp_block, grad_block_two, hidden, grad_gate, grad_up,
+            meta, *owned, mlp_block, grad_block_two, hidden, grad_gate, grad_up,
             w_output, core, gate, gain_row, qkv, scal, w_part, drop,
         )
         ff_grads, grad_block = results[:3], results[3]
-        grad_core, inner, pull, grad_gate_pre, grad_head, pulled = results[4:]
+        grad_core, inner, pull, grad_gate_pre, grad_head, pulled, grad_hidden_in, grad_second = results[4:]
+        grad_second = grad_second[0]
     else:
+        grad_hidden_norm, grad_second = rms_back(hidden_in, second_gain, grad_normed_two)
+        grad_hidden_in = grad_out + grad_hidden_norm
+        grad_mix = grad_hidden_in.astype(bf16)
         *ff_grads, grad_block = feed_grads(
             grad_mix, mlp_block, grad_block_two, hidden, grad_gate, grad_up, "head"
         )
@@ -1831,16 +1897,15 @@
             name="mixer_core_grad",
         )(meta, grad_block, w_output, core, gate, gain_row, qkv, scal, w_part, drop)
     grad_w_output = dot_tn(gated, grad_block).astype(bf16)
-    grad_w_outgate = dot_tn(block_rows, grad_gate_pre).astype(bf16)
-
     later = from_later(
         jnp.concatenate([block_map[:, :, :key_width], pulled], axis=2).astype(bf16), "seq"
     )
-    later, grad_w_output, grad_w_outgate = lax.optimization_barrier((later, grad_w_output, grad_w_outgate))
-    mlp_out, grad_w_outgate = lax.optimization_barrier((mlp_out, grad_w_outgate))
-    grad_w_outgate = lax.psum(grad_w_outgate, "seq")
-    grad_conv, grad_small, sums, edge = pl.pallas_call(
-        functools.partial(backward_kernel, *sizes, chunks, others),
+    later, _ = lax.optimization_barrier((later, grad_w_output))
+    mlp_out, grad_w_output = lax.optimization_barrier((mlp_out, grad_w_output))
+    grad_w_output = lax.psum(grad_w_output, "seq")
+    feed_part = (ff_grads[1],) if cube else ()
+    grad_conv, grad_small, sums, edge, *feed_sum = pl.pallas_call(
+        functools.partial(backward_kernel, *sizes, chunks, others, cube),
         grid=(chunks,),
         in_specs=[
             SCALARS, whole(later.shape), by_rows(mixed_width, chunks), by_rows(mixed_width, chunks),
@@ -1848,23 +1913,35 @@
             by_chunk((heads, BLOCK, value_width), chunks), by_chunk((heads, key_width, value_width), chunks),
             by_chunk((heads, BLOCK, value_width), chunks), by_chunk((heads, BLOCK, value_width), chunks),
             by_chunk((heads, key_width, value_width), chunks), by_chunk((heads, key_width, key_width), chunks),
-            whole(dvec.shape),
+            whole(dvec.shape), *(held(array.shape) for array in feed_part),
         ],
         out_specs=[
             by_rows(mixed_width, chunks), by_rows(LANES, chunks), whole((8, LANES)), whole((HALO, mixed_width)),
+            *(whole((array.shape[0] // 8, array.shape[1])) for array in feed_part),
         ],
         out_shape=[
             struct((seq_rows, mixed_width), f32), struct((seq_rows, LANES), bf16), struct((8, LANES), f32),
             struct((HALO, mixed_width), f32),
+            *(struct((array.shape[0] // 8, array.shape[1]), bf16) for array in feed_part),
         ],
         scratch_shapes=[
             pltpu.VMEM((heads, key_width, value_width), f32), pltpu.VMEM((HALO, mixed_width), f32),
             pltpu.VMEM((HALO, mixed_width), f32), pltpu.SemaphoreType.DMA((2,)),
+            *(
+                scratch for array in feed_part for scratch in (
+                    pltpu.VMEM((array.shape[0] // 8, array.shape[1]), f32),
+                    *cube_scatter_scratch(array.shape[0] // 8, array.shape[1]),
+                )
+            ),
         ],
         compiler_params=params(9),
         name="mixer_backward",
-    )(meta, later, qkv, conv, scal, small, inverse, fresh, states, grad_core, inner, pull, drop, dvec)
-
+    )(
+        meta, later, qkv, conv, scal, small, inverse, fresh, states, grad_core, inner, pull, drop, dvec, *feed_part
+    )
+
+    if cube:
+        ff_grads = [ff_grads[0], ff_grads[2]]
     grad_small, *ff_grads = lax.optimization_barrier((grad_small, *ff_grads))
     ff_grads = [lax.psum(part, "head") for part in ff_grads]
     step_rows = BLOCK // HALO
@@ -1902,15 +1979,15 @@
     grad_input_norm, _ = rms_back(inputs_f, first_gain, grad_normed)
     grad_inputs = grad_hidden_in + grad_input_norm
     gains = jnp.concatenate([gain_sum[0] / first_gain, grad_second, grad_head[0]]).reshape(2, -1)
-    grad_w_all, grad_w_output, small_sums, _, gains = line_sum(
+    grad_w_all, grad_w_small, small_sums, _, gains, *gathered = line_sum(
         block_rows,
         grad_pre,
+        feed_sum,
         (
-            grad_w_output,
             jnp.pad(
-                jnp.concatenate([grad_taps, sums], axis=1), ((0, 24), (0, 0))
+                jnp.concatenate([grad_taps, sums], axis=1), ((0, 8), (0, 0))
             ).astype(bf16),
-            jnp.pad(gains, ((0, 30), (0, 0))).astype(bf16),
+            jnp.pad(gains, ((0, 14), (0, 0))).astype(bf16),
         ),
         (32, 16, 16, 16),
         "seq",
@@ -1919,13 +1996,15 @@
     gains = gains[:2].reshape(-1)
     first_part, second_part = gains[:model_width], gains[model_width : 2 * model_width]
     head_part = gains[2 * model_width :]
-    grad_w_query, grad_w_key, grad_w_value, grad_w_outgate, grad_w_output, grad_w_small = widen(
-        (grad_w_outgate, grad_w_output), grad_w_all, (qw, qw, vw)
+    if cube:
+        ff_grads = [ff_grads[0], *gathered, ff_grads[1]]
+    grad_w_all, grad_w_output = lax.optimization_barrier((grad_w_all, grad_w_output))
+    grad_w_all, grad_inputs, mlp_out, *ff_grads = lax.optimization_barrier(
+        (grad_w_all, grad_inputs, mlp_out, *ff_grads)
     )
-    grad_inputs, grad_w_query, mlp_out, *ff_grads = lax.optimization_barrier(
-        (grad_inputs, grad_w_query, mlp_out, *ff_grads)
-    )
-    grad_w_down, grad_w_gate, grad_w_up = widen(ff_grads)
+    (
+        grad_w_query, grad_w_key, grad_w_value, grad_w_outgate, grad_w_down, grad_w_gate, grad_w_up, grad_w_output,
+    ) = widen((*ff_grads, grad_w_output), grad_w_all, (qw, qw, vw, vw))
     grad_taps = small_sums[:taps, :mixed_width].astype(f32)
     sums = small_sums[:2, mixed_width : mixed_width + heads].astype(f32)
     output = (hidden_in + mlp_out.astype(f32)).astype(bf16)
@@ -1937,8 +2016,8 @@
         grad_w_key,
         grad_w_value,
         grad_w_outgate,
-        grad_w_small[:heads].T,
-        grad_w_small[heads : 2 * heads].T,
+        grad_w_small[:heads].astype(f32).T,
+        grad_w_small[heads : 2 * heads].astype(f32).T,
         grad_taps[:, :qw],
         grad_taps[:, qw : 2 * qw],
         grad_taps[:, 2 * qw :],

time: 745 us -> 717 us (0.962)
  matrix products: 19.8 us -> 9.12 us
  other arithmetic: 29.7 us -> 19.7 us
  Pallas kernels: 645 us -> 636 us
    pallas_call x1, Pallas kernels: 193 us -> 174 us  [line_sum(): pl.pallas_call(functools.partial(line_sum_kernel, axis, cube, counts, tup...]
    ppermute x3, waiting for transfers between devices: 1.05 us -> 17.4 us  [from_later(): lax.ppermute(array, axis, [(i + by, i) for i in range(devices - by)])]
    pallas_call x1, Pallas kernels: 32.9 us -> 45.1 us  [shards(): pl.pallas_call(functools.partial(backward_kernel, *sizes, chunks, others,...]
    dot_general x2 -> x1, matrix products: 19.8 us -> 9.12 us  [dot_tn(): lax.dot_general(left, right, (((0,), (0,)), ((), ())), preferred_element_...]
    psum x1, waiting for transfers between devices: 10.3 us -> 0.01 us  [shards(): ff_grads = [lax.psum(part, 'head') for part in ff_grads]]
    pallas_call x2 -> x1, Pallas kernels: 29.1 us -> 25.6 us  [widen(): pl.pallas_call(functools.partial(widen_kernel, cuts, len(given)), grid=(s...]
  transfers between devices with their start and end apart: 7 -> 7, of which waited for: 2 -> 2; matrix products, arithmetic and copies ran while one was open for 7% -> 4% of each run, Pallas kernels for 67% -> 68%
where the time goes in v5:
time: 717 us; the launch traced here: 710 us
  Pallas kernels  636 us (89%)
  other arithmetic  19.7 us (3%)
  waiting for transfers between devices  17.5 us (2%)
  between operations  14.4 us (2%)
  matrix products  9.12 us (1%)
  local copies, waits for them, and re-layouts  8.87 us (1%)
    pallas_call x1, Pallas kernels, line_sum(): pl.pallas_call(functools.partial(line_sum_kernel, axis, cube, counts, tup...  174 us
    pallas_call x1, Pallas kernels, feed(): pl.pallas_call(functools.partial(feed_kernel, axis, devices, rows), in_sp...  127 us
    pallas_call x1, Pallas kernels, shards(): pl.pallas_call(functools.partial(forward_kernel, *sizes, taps, chunks, cu...  92.3 us
    pallas_call x1, Pallas kernels, shards(): pl.pallas_call(functools.partial(feed_core_kernel, sizes, chunks, 'head',...  62.6 us
    pallas_call x1, Pallas kernels, shards(): pl.pallas_call(functools.partial(projection_grad_kernel, mixed_width, doc...  58.2 us
    pallas_call x1, Pallas kernels, shards(): pl.pallas_call(functools.partial(output_kernel, *sizes, others, cube), gr...  50.9 us
    pallas_call x1, Pallas kernels, shards(): pl.pallas_call(functools.partial(backward_kernel, *sizes, chunks, others,...  45.1 us
    pallas_call x1, Pallas kernels, widen(): pl.pallas_call(functools.partial(widen_kernel, cuts, len(given)), grid=(s...  25.6 us
  transfers between devices with their start and end apart: 7, of which 2 were waited for; matrix products, arithmetic and copies ran while one was open for 4% of the time, Pallas kernels for 68%

profile of v5, /device:TPU:0, one launch (start us, length us, event | category | flops | bytes accessed | tf_op | source)
XLA Modules:
  0.0 710.0 jit_solution(18094671264846661876)
XLA Ops:
  7.3 0.7 fusion.18
  7.9 0.2 reduce-window.9
  8.1 0.7 bitcast_subtract_fusion
  8.9 0.1 fusion.11
  8.9 0.7 select_reduce_fusion.1
  9.8 2.5 multiply_convert_fusion.low_ref
  12.4 0.3 copy.43
  12.7 0.3 copy.44
  13.1 0.2 scatter.9.dvec_ref
  13.3 0.6 pad_add_fusion.meta
  14.0 0.3 fusion
  14.3 1.1 maximum_maximum_fusion.ws_ref
  15.4 1.3 fusion.2.rows_ref
  16.7 92.3 %mixer_forward.1 = (f32[2048,1024]{1,0:T(8,128)}, f32[2048,1024]{1,0:T(8,128)}, f32[2048,512]{1,0:T(8,128)}, f32[2048,128]{1,0:T(8,128)}, f32[2048,128]{1,0:T(8,...) custom-call(s32[4]{0:T(128)} %pad_add_fusion.meta, ...), custom_call_target="tpu_custom_call" | custom-call | tf_op jit(solution)/shard_map/mixer_forward/pallas_call | solution.py:1717
  109.0 50.9 %mixer_output.1 = (f32[2048,512]{1,0:T(8,128)}, bf16[2048,512]{1,0:T(8,128)(2,1)}, bf16[8,2,256,256]{3,2,1,0:T(8,128)(2,1)}, f32[8,2,128,256]{3,2,1,0:T(8,128)},...) custom-call(s32[4]{0:T(128)} %pad_add_fusion.meta, bf16[3,2,128,384]{3,2,1,0:T(8,128)(2,1)} %get-tuple-element.118.maps_ref, ...), custom_call_target="tpu_custom_call" | custom-call | tf_op jit(solution)/shard_map/mixer_output/pallas_call | solution.py:1774
  159.9 127.3 %feed.1 = (bf16[1024,2048]{1,0:T(8,128)(2,1)}, bf16[1408,1024]{1,0:T(8,128)(2,1)}, bf16[1024,1408]{1,0:T(8,128)(2,1)}, bf16[1024,1408]{1,0:T(8,128)(2,1)}, bf16[...) custom-call(bf16[256,2048]{1,0:T(8,128)(2,1)} %get-tuple-element.128.own_ref, ...), custom_call_target="tpu_custom_call" | custom-call | tf_op jit(solution)/shard_map/feed/pallas_call | solution.py:1249
  287.3 0.9 slice.132
  288.3 62.6 %feed_core.1 = (bf16[1408,2048]{1,0:T(8,128)(2,1)}, bf16[2048,1408]{1,0:T(8,128)(2,1)}, bf16[2048,1408]{1,0:T(8,128)(2,1)}, bf16[2048,2048]{1,0:T(8,128)(2,1)}, ...) custom-call(s32[4]{0:T(128)} %pad_add_fusion.meta, ...), custom_call_target="tpu_custom_call" | custom-call | tf_op jit(solution)/shard_map/feed_core/pallas_call | solution.py:1840
  350.9 1.0 convert.34
  351.9 1.3 collective-permute-start.2
  353.2 1.3 collective-permute-start.1
  354.5 1.3 collective-permute-start
  355.8 9.1 %convolution_convert_fusion = bf16[512,2048]{1,0:T(8,128)(2,1)} fusion(bf16[2048,512]{1,0:T(8,128)(2,1)S(1)} %copy-done.14, bf16[2048,2048]{1,0:T(8,128)(2,1)} %get-tuple-element.138), kind=kOutput, calls=%fused_computation.4 | convolution fusion | flops 4296015872 | bytes 12582912 | tf_op jit(solution)/shard_map/dot_general | solution.py:26
  365.0 3.9 collective-permute-done.2
  368.8 13.6 %collective-permute-done.1 = bf16[2,128,384]{2,1,0:T(8,128)(2,1)S(1)} collective-permute-done((bf16[2,128,384]{2,1,0:T(8,128)(2,1)S(1)}, bf16[2,128,384]{2,1,0:T(8,128)(2,1)S(1)}, u32[]{:S(2)}, u32[]{:S(2)}) %collective-permute-start.1) | collective-permute-done | bytes 196640 | tf_op jit(solution)/shard_map/ppermute | solution.py:1633
  382.4 0.9 pad_maximum_fusion.maps_ref
  383.3 45.1 %mixer_backward.1 = (f32[2048,1024]{1,0:T(8,128)}, bf16[2048,128]{1,0:T(8,128)(2,1)}, f32[8,128]{1,0:T(8,128)}, f32[8,1024]{1,0:T(8,128)}, bf16[256,1408]{1,0:T(8,128)(2,1)}) custom-call(s32[4]{0:T(128)} %pad_add_fusion.meta, bf16[3,2,128,384]{3,2,1,0:T(8,128)(2,1)} %pad_maximum_fusion.maps_ref, bf16[2048,1024]{1,0:T(8,128)(2,1)} %get-tuple-element.122.qkv_ref, ...), custom_call_target="tpu_custom_call" | custom-call | tf_op jit(solution)/shard_map/mixer_backward/pallas_call | solution.py:1907
  428.5 0.7 fusion.12
  429.2 0.9 fusion.10
  430.1 58.2 %projection_grad.1 = (bf16[2048,1664]{1,0:T(8,128)(2,1)}, f32[8,1024]{1,0:T(8,128)}, f32[256,2048]{1,0:T(8,128)}, f32[8,2048]{1,0:T(8,128)}) custom-call(s32[4]{0:T(128)} %pad_add_fusion.meta, f32[2048,1024]{1,0:T(8,128)} %get-tuple-element.149.grad_conv_ref.later_ref, f32[2048,1024]{1,0:T(8,128)} %get-tuple-element.149.grad_conv_ref.later_ref, ...), custom_call_target="tpu_custom_call" | custom-call | tf_op jit(solution)/shard_map/projection_grad/pallas_call | solution.py:1952
  488.3 0.8 slice.94
  489.2 0.8 convert.35
  489.9 0.6 pad.19.refs_3_
  490.6 0.6 fusion.9.refs_2_
  491.2 174.3 %line_sum.1 = (bf16[2048,1536]{1,0:T(8,128)(2,1)}, bf16[16,2048]{1,0:T(8,128)(2,1)}, bf16[16,1152]{1,0:T(8,128)(2,1)}, bf16[16,2176]{1,0:T(8,128)(2,1)}, f32[8,2176]{1,0:T(8,128)}, /*index=5*/bf16[2048,1408]{1,0:T(8,128)(2,1)}) custom-call(bf16[2048,2048]{1,0:T(8,128)(2,1)} %get-tuple-element.126.rows_ref.refs_0_, ...), custom_call_target="tpu_custom_call" | custom-call | flops 100000000 | bytes 40000000 | tf_op jit(solution)/shard_map/line_sum/pallas_call | solution.py:1010
  665.6 0.7 slice_convert_fusion.2
  666.3 0.6 slice.116
  666.9 0.9 slice.97
  667.8 0.6 slice.117
  668.4 0.4 fusion.6
  668.7 0.7 slice_convert_fusion.4
  669.4 0.5 slice_bitcast_fusion
  669.9 0.6 fusion.15
  670.5 0.6 fusion.14
  671.1 1.5 convert_bitcast_fusion
  672.6 1.9 fusion.5
  674.5 3.1 add_convert_fusion
  677.6 25.6 %widen.1 = (f32[2048,256]{1,0:T(8,128)}, f32[2048,256]{1,0:T(8,128)}, f32[2048,512]{1,0:T(8,128)}, f32[2048,512]{1,0:T(8,128)}, f32[1408,2048]{1,0:T(8,128)}, /*...) custom-call(bf16[1408,2048]{1,0:T(8,128)(2,1)} %get-tuple-element.177.refs_0_, ...), custom_call_target="tpu_custom_call" | custom-call | tf_op jit(solution)/shard_map/widen/pallas_call | solution.py:1606
  (63 shorter events, 0.6 us)
Async XLA Ops:
  7.2 5.2 copy-start.7
  7.2 5.5 copy-start.8
  7.2 152.7 %all-gather.2.cloned.1.call-start = ((), (), s32[]{:S(2)}) async-start(), calls=%async_computation.1 | async-start | bytes 5242880 | tf_op jit(solution)/shard_map/all_gather | solution.py:1761
  9.7 3.4 copy-start.13
  9.7 3.4 copy-start.15
  9.7 4.2 copy-start.11
  9.7 4.2 copy-start.12
  9.7 4.2 copy-start.9
  9.8 4.2 copy-start
  12.3 3.1 copy-start.4
  12.3 370.9 %reduce-scatter.2.cloned.1.call-start = ((), (), s32[]{:S(2)}) async-start(), calls=%async_computation.2 | async-start | bytes 5242880 | tf_op jit(solution)/shard_map/reduce_scatter | solution.py:1814
  13.3 3.4 copy-start.6
  14.0 2.7 copy-start.5
  287.3 387.2 %all-reduce.7.cloned.1.call-start = ((), (), s32[]{:S(2)}) async-start(), calls=%async_computation.3 | async-start | bytes 4194304 | tf_op jit(solution)/shard_map/psum | solution.py:1905
  288.3 67.6 %copy-start.14 = (bf16[2048,512]{1,0:T(8,128)(2,1)S(1)}, bf16[2048,512]{1,0:T(8,128)(2,1)}, u32[]{:S(2)}) copy-start(bf16[2048,512]{1,0:T(8,128)(2,1)} %get-tuple-element.137) | copy-start | bytes 6291460
  351.9 16.9 %collective-permute-start.2 = (bf16[2,128,384]{2,1,0:T(8,128)(2,1)S(1)}, bf16[2,128,384]{2,1,0:T(8,128)(2,1)S(1)}, u32[]{:S(2)}, u32[]{:S(2)}) collective-permute-start(bf16[2,128,384]{2,1,0:T(8,128)(2,1)S(1)} %pad_maximum_fusion.1), channel_id=1, source_target_pairs={{8,0},{16,8},{24,16},{9,1},{17,9},{25,17},{10,2},{18,10},{26,18},{... | collective-permute-start | bytes 589832 | tf_op jit(solution)/shard_map/ppermute | solution.py:1633
  353.2 29.1 %collective-permute-start.1 = (bf16[2,128,384]{2,1,0:T(8,128)(2,1)S(1)}, bf16[2,128,384]{2,1,0:T(8,128)(2,1)S(1)}, u32[]{:S(2)}, u32[]{:S(2)}) collective-permute-start(bf16[2,128,384]{2,1,0:T(8,128)(2,1)S(1)} %pad_maximum_fusion.1), channel_id=1, source_target_pairs={{16,0},{24,8},{17,1},{25,9},{18,2},{26,10},{19,3},{27,11},{20,4},{... | collective-permute-start | bytes 589832 | tf_op jit(solution)/shard_map/ppermute | solution.py:1633
  354.5 27.8 %collective-permute-start = (bf16[2,128,384]{2,1,0:T(8,128)(2,1)S(1)}, bf16[2,128,384]{2,1,0:T(8,128)(2,1)S(1)}, u32[]{:S(2)}, u32[]{:S(2)}) collective-permute-start(bf16[2,128,384]{2,1,0:T(8,128)(2,1)S(1)} %pad_maximum_fusion.1), channel_id=1, source_target_pairs={{24,0},{25,1},{26,2},{27,3},{28,4},{29,5},{30,6},{31,7}} | collective-permute-start | bytes 589832 | tf_op jit(solution)/shard_map/ppermute | solution.py:1633
  383.3 291.2 %all-reduce.9.cloned.1.call-start = ((), (), s32[]{:S(2)}) async-start(), calls=%async_computation.4 | async-start | bytes 23068672 | tf_op jit(solution)/shard_map/psum | solution.py:1946
  428.4 1.6 copy-start.10
  491.2 177.2 %copy-start.1 = (bf16[256,2048]{1,0:T(8,128)(2,1)S(1)}, bf16[256,2048]{1,0:T(8,128)(2,1)}, u32[]{:S(2)}) copy-start(bf16[256,2048]{1,0:T(8,128)(2,1)} %refs_0_.1) | copy-start | bytes 3145732
  491.2 177.2 %copy-start.2 = (f32[256,2048]{1,0:T(8,128)S(1)}, f32[256,2048]{1,0:T(8,128)}, u32[]{:S(2)}) copy-start(f32[256,2048]{1,0:T(8,128)} %get-tuple-element.169) | copy-start | bytes 6291460
  667.8 4.8 copy-start.3
Sparse Core Ops, SparseCore 0:
  12.4 83.4 all-gather.1
  287.4 81.0 reduce-scatter.1
  383.4 85.2 all-reduce.6
  472.3 182.0 all-reduce.8

commit v6 on v5

--- a/solution.py
+++ b/solution.py
@@ -273,6 +273,57 @@
             self.copy(mask, 1).wait_send()
 
 
+class MapExchange:
+    def __init__(self, going, coming, behind, sem):
+        self.going, self.coming, self.behind, self.sem = going, coming, behind, sem
+        self.groups, self.group = lax.axis_size("seq"), lax.axis_index("seq")
+        self.width = going.shape[1]
+
+    def copy(self, kind, by, target):
+        slot = self.groups - 1 - by
+        passing = pl.ds(0, self.width)
+        span = pl.ds(self.width, self.going.shape[2] - self.width) if kind == 0 else passing
+        landing = self.behind.at[slot] if kind == 2 else self.coming.at[slot, :, :, span]
+        return pltpu.make_async_remote_copy(
+            self.going.at[:, :, span], landing, self.sem.at[2 * kind, slot], self.sem.at[2 * kind + 1, slot],
+            device_id={"seq": target}, device_id_type=MESH,
+        )
+
+    def moves(self):
+        group, groups = self.group, self.groups
+        for by in range(groups - 1, 0, -1):
+            yield 0, by, group + by, group + by < groups, group - by, group >= by
+            yield 1, by, group + by, (group + by < groups) & (group > 0), group - by, group > by
+            yield 2, by, group - by, group >= by, group + by, group + by < groups
+
+    def run(self):
+        for kind, by, target, sends, source, comes in self.moves():
+            @pl.when(sends)
+            def _():
+                self.copy(kind, by, target).start()
+
+        for kind, by, target, sends, source, comes in self.moves():
+            slot = self.groups - 1 - by
+
+            @pl.when(comes)
+            def _():
+                self.copy(kind, by, source).wait_recv()
+
+            @pl.when(jnp.logical_not(comes))
+            def _():
+                if kind == 0:
+                    self.coming[slot, :, :, self.width :] = jnp.zeros(self.coming.shape[1:3] + (self.going.shape[2] - self.width,), bf16)
+                elif kind == 1:
+                    self.coming[slot, :, :, : self.width] = jnp.zeros(self.behind.shape[1:], bf16)
+                else:
+                    self.behind[slot] = jnp.zeros(self.behind.shape[1:], bf16)
+
+        for kind, by, target, sends, source, comes in self.moves():
+            @pl.when(sends)
+            def _():
+                self.copy(kind, by, target).wait_send()
+
+
 def forward_kernel(
     heads, key_width, value_width, docs, taps, chunks, cube,
     meta, rows_ref, wq_ref, wk_ref, wv_ref, wg_ref, ws_ref, conv_ref, dvec_ref,
@@ -280,12 +331,12 @@
     starts_ref, map_ref, *refs,
 ):
     step = pl.program_id(0)
-    ext, state, drops, adds, throughs = refs[2 * cube : 2 * cube + 5]
+    ext, state, drops, adds, throughs = refs[3 * cube : 3 * cube + 5]
     if cube:
         all_ref = refs[0]
-        earlier_ref, *refs = refs[1:]
+        earlier_ref, later_ref, *refs = refs[1:]
         held, copy_sem, edge_ref, line_sem, edge_send, edge_recv, cube_send, cube_recv = refs[5:13]
-        going, coming, map_sem = refs[13:]
+        going, coming, behind, map_sem = refs[13:]
         chunk = cube_order("head", step)
         rows_in = CubeGather("head", rows_ref, held, None, cube_send, cube_recv, STRIDE, LEAD)
         edges = EdgeRows("seq", "head", rows_ref, held, edge_ref, line_sem, edge_send, edge_recv)
@@ -418,39 +469,12 @@
         for head in range(heads):
             map_ref[head] = state[head]
         if cube:
-            groups, group = lax.axis_size("seq"), lax.axis_index("seq")
-
-            def hand_on(by, target):
-                slot = groups - 1 - by
-                return pltpu.make_async_remote_copy(
-                    going, coming.at[slot], map_sem.at[0, slot], map_sem.at[1, slot],
-                    device_id={"seq": target}, device_id_type=MESH,
-                )
-
+            maps = MapExchange(going, coming, behind, map_sem)
             for head in range(heads):
                 going[head] = state[head].astype(bf16)
-            for by in range(groups - 1, 0, -1):
-                @pl.when(group + by < groups)
-                def _():
-                    hand_on(by, group + by).start()
-
-            for by in range(groups - 1, 0, -1):
-                slot = groups - 1 - by
-
-                @pl.when(group >= by)
-                def _():
-                    hand_on(by, group - by).wait_recv()
-                    earlier_ref[slot] = coming[slot]
-
-                @pl.when(group < by)
-                def _():
-                    earlier_ref[slot] = jnp.zeros(earlier_ref.shape[1:], bf16)
-
-            for by in range(groups - 1, 0, -1):
-                @pl.when(group + by < groups)
-                def _():
-                    hand_on(by, group + by).wait_send()
-
+            maps.run()
+            earlier_ref[...] = coming[...]
+            later_ref[...] = behind[...]
             rows_in.last()
             edges.end()
             for block in range(chunks):
@@ -577,7 +601,7 @@
 
 def backward_kernel(
     heads, key_width, value_width, docs, chunks, others, cube,
-    meta, maps_ref, qkv_ref, act_ref, scal_ref, small_ref, inv_ref, fresh_ref, state_ref,
+    meta, passing_ref, later_ref, qkv_ref, act_ref, scal_ref, small_ref, inv_ref, fresh_ref, state_ref,
     grad_core_ref, inner_ref, pull_ref, drop_ref, dvec_ref, *refs,
 ):
     if cube:
@@ -596,9 +620,13 @@
     if cube:
         rows = feed_ref.shape[0] // 8
         total, *refs = refs
-        part = pl.ds(pl.multiple_of(cube_order("head", 7 - step) * rows, rows), rows)
         scatter = CubeScatter("head", total, *refs)
-        scatter_block(step, scatter, feed_ref[part, :].astype(f32), inside=True)
+        for at, masks in enumerate(((7,), (6, 5), (4, 3), (2, 1), (0,))):
+            @pl.when(step == at)
+            def _():
+                for mask in masks:
+                    part = pl.ds(pl.multiple_of(flip(scatter.place, mask) * rows, rows), rows)
+                    scatter.take(mask, feed_ref[part, :].astype(f32))
     groups, group = lax.axis_size("seq"), lax.axis_index("seq")
     edge = pltpu.make_async_remote_copy(
         edge_out, edge_in, edge_sem.at[0], edge_sem.at[1],
@@ -613,9 +641,9 @@
         for head in range(heads):
             state = jnp.zeros((key_width, value_width), f32)
             for other in range(others):
-                passing = maps_ref[other, head, :, :key_width]
+                passing = passing_ref[other, head]
                 top, low = halves(state)
-                state = dot_tn(passing, top) + dot_tn(passing, low) + maps_ref[other, head, :, key_width:].astype(f32)
+                state = dot_tn(passing, top) + dot_tn(passing, low) + later_ref[other, head].astype(f32)
             carried[head] = state
 
     masks = Masks(meta, docs, chunk)
@@ -1053,7 +1081,7 @@
 
 
 def feed_kernel(
-    axis, devices, rows,
+    axis, devices, rows, pieces,
     own_ref, *refs,
 ):
     given, kept, refs = refs[:4], refs[4:9], refs[9:]
@@ -1091,15 +1119,17 @@
             gather_send.at[slot], gather_recv.at[slot], device_id={axis: target}, device_id_type=MESH,
         )
 
-    def quarter(block, part):
-        return pl.ds(pl.multiple_of(block * rows + part * (rows // 4), rows // 4), rows // 4)
+    bit = rows // pieces
+
+    def strip(block, part):
+        return pl.ds(pl.multiple_of(block * rows + part * bit, bit), bit)
 
     def chain(block, way, part, at):
         target = at + 1 - 2 * way
         landing = jnp.where((block == target) & (way == 0), devices, block)
-        slot = (way * devices + block) * 4 + part
+        slot = (way * devices + block) * pieces + part
         return pltpu.make_async_remote_copy(
-            parts.at[quarter(block, part), :], arrived.at[quarter(landing, part), :],
+            parts.at[strip(block, part), :], arrived.at[strip(landing, part), :],
             chain_send.at[slot], chain_recv.at[slot], device_id={axis: target}, device_id_type=MESH,
         )
 
@@ -1163,7 +1193,7 @@
 
         @pl.when((way == 1) & (step > 0))
         def _():
-            for part in range(4):
+            for part in range(pieces):
                 for turn in range(2):
                     side = jnp.where(2 * place < devices, turn, 1 - turn)
                     block = jnp.where(side == 1, devices - 1 - hop, hop)
@@ -1175,7 +1205,7 @@
                         @pl.when(jnp.logical_not(begins))
                         def _():
                             chain(block, side, part, place + 2 * side - 1).wait_recv()
-                            at = quarter(block, part)
+                            at = strip(block, part)
                             parts[at, :] = (parts[at, :].astype(f32) + arrived[at, :].astype(f32)).astype(bf16)
 
                         chain(block, side, part, place).start()
@@ -1197,10 +1227,10 @@
     for side, landing, comes in ((1, place, place < devices - 1), (0, devices, place > 0)):
         @pl.when(comes)
         def _():
-            for part in range(4):
+            for part in range(pieces):
                 chain(place, side, part, place + 2 * side - 1).wait_recv()
-                at = pl.ds(part * (rows // 4), rows // 4)
-                total_ref[at, :] += arrived[quarter(landing, part), :].astype(f32)
+                at = pl.ds(part * bit, bit)
+                total_ref[at, :] += arrived[strip(landing, part), :].astype(f32)
 
     def gather_end(step, carry):
         hop = step // 2
@@ -1220,12 +1250,12 @@
     def chain_end(block, carry):
         @pl.when(block < place)
         def _():
-            for part in range(4):
+            for part in range(pieces):
                 chain(block, 1, part, place).wait_send()
 
         @pl.when(block > place)
         def _():
-            for part in range(4):
+            for part in range(pieces):
                 chain(block, 0, part, place).wait_send()
 
         return carry
@@ -1241,13 +1271,14 @@
     units = w_gate.shape[1]
     vmem = pl.BlockSpec(memory_space=pltpu.VMEM)
     moves = pltpu.SemaphoreType.DMA((4 * devices,))
-    chains = pltpu.SemaphoreType.DMA((8 * devices,))
+    pieces = 4
+    chains = pltpu.SemaphoreType.DMA((2 * pieces * devices,))
     given = (grads, w_gate, w_up, w_down)
     kept = [struct((devices * rows, width), bf16), struct((units, devices * rows), bf16)]
     kept += [struct((devices * rows, units), bf16)] * 2
     kept += [struct((devices * rows, width), bf16)]
     return pl.pallas_call(
-        functools.partial(feed_kernel, axis, devices, rows),
+        functools.partial(feed_kernel, axis, devices, rows, pieces),
         in_specs=[vmem] + [ANYWHERE] * 4,
         out_specs=[ANYWHERE] * 5 + [vmem],
         out_shape=kept + [struct((rows, width), f32)],
@@ -1541,21 +1572,19 @@
             self.chip_copy(index, half, toward).wait_send()
 
 
-def scatter_block(step, scatter, block, inside=False):
-    if not inside:
-        @pl.when(step == 0)
-        def _():
-            cube_barrier("head", scatter.place)
+def scatter_block(step, scatter, block):
+    @pl.when(step == 0)
+    def _():
+        cube_barrier("head", scatter.place)
 
     for mask in range(8):
         @pl.when(step == 7 - mask)
         def _():
             scatter.take(mask, block)
 
-    if not inside:
-        @pl.when(step == 7)
-        def _():
-            scatter.finish()
+    @pl.when(step == 7)
+    def _():
+        scatter.finish()
 
 
 def cube_scatter_scratch(rows, width):
@@ -1576,42 +1605,58 @@
     )
 
 
-def widen_kernel(cuts, total, *refs):
+def finish_kernel(
+    cuts, total, grad_ref, inputs_ref, gain_ref, grad_hidden_ref, hidden_ref, mlp_ref, taps_ref, all_in, *refs,
+):
     given, refs = refs[:total], refs[total:]
-    if cuts:
-        all_in, *refs = refs
-        begin = 0
-        for cut, result in zip(cuts, refs):
-            result[...] = all_in[:, begin : begin + cut].astype(f32)
-            begin += cut
-        refs = refs[len(cuts) :]
-    for source, result in zip(given, refs):
+    output_ref, grad_inputs_ref, taps_q, taps_k, taps_v, *refs = refs
+    output_ref[...] = (hidden_ref[...] + mlp_ref[...].astype(f32)).astype(bf16)
+    values = inputs_ref[...].astype(f32)
+    scale = lax.rsqrt(jnp.mean(values * values, axis=-1, keepdims=True) + epsilon)
+    weighted = grad_ref[...] * gain_ref[...]
+    grad_inputs_ref[...] = grad_hidden_ref[...] + (
+        scale * weighted - values * scale**3 * jnp.mean(weighted * values, axis=-1, keepdims=True)
+    )
+    begin = 0
+    for result in (taps_q, taps_k, taps_v):
+        count, width = result.shape
+        result[...] = taps_ref[:, begin : begin + width].astype(f32)[:count, :]
+        begin += width
+    begin = 0
+    for cut, result in zip(cuts, refs):
+        result[...] = all_in[:, begin : begin + cut].astype(f32)
+        begin += cut
+    for source, result in zip(given, refs[len(cuts) :]):
         result[...] = source[...].astype(f32)
 
 
-def widen(given, columns=None, cuts=()):
+def finish(rows, gain, small, taps, columns, cuts, given):
     steps = 8 if given[0].shape[0] % 128 == 0 else 4
-    sources = list(given)
-    shapes = [array.shape for array in given]
 
     def part(shape):
         return pl.BlockSpec((shape[0] // steps, shape[1]), lambda step: (step, 0))
 
-    specs = [part(shape) for shape in shapes]
-    if cuts:
-        sources.append(columns)
-        cut_shapes = [(columns.shape[0], cut) for cut in cuts]
-        specs = [part(shape) for shape in cut_shapes] + specs
-        shapes = cut_shapes + shapes
+    grad, inputs, grad_hidden, hidden, mlp = rows
+    taps_shapes = [(taps, cut) for cut in cuts[:3]]
+    shapes = [(columns.shape[0], cut) for cut in cuts] + [array.shape for array in given]
     return pl.pallas_call(
-        functools.partial(widen_kernel, cuts, len(given)),
+        functools.partial(finish_kernel, cuts, len(given)),
         grid=(steps,),
-        in_specs=[part(array.shape) for array in sources],
-        out_specs=specs,
-        out_shape=[struct(shape, f32) for shape in shapes],
+        in_specs=[
+            part(grad.shape), part(inputs.shape), whole(gain.shape), part(grad_hidden.shape), part(hidden.shape),
+            part(mlp.shape), whole(small.shape), part(columns.shape), *(part(array.shape) for array in given),
+        ],
+        out_specs=[
+            part(inputs.shape), part(inputs.shape), *(whole(shape) for shape in taps_shapes),
+            *(part(shape) for shape in shapes),
+        ],
+        out_shape=[
+            struct(inputs.shape, bf16), struct(inputs.shape, f32), *(struct(shape, f32) for shape in taps_shapes),
+            *(struct(shape, f32) for shape in shapes),
+        ],
         compiler_params=params(),
-        name="widen",
-    )(*sources)
+        name="finish",
+    )(grad, inputs, gain, grad_hidden, hidden, mlp, small, columns, *given)
 
 
 def struct(shape, dtype):
@@ -1690,6 +1735,7 @@
     dvec = jnp.zeros((8, LANES), f32)
     dvec = dvec.at[0, :heads].set(decay_bias).at[1, :heads].set(-jnp.exp(decay_log))
     map_shape = (heads, key_width, key_width + value_width)
+    passing_shape = (others, heads, key_width, key_width)
 
     cube = head_total == 8 and chunks == 8 and row_count == BLOCK
     if cube:
@@ -1727,7 +1773,7 @@
             chunk_out((heads, BLOCK, BLOCK)), chunk_out((heads, BLOCK, key_width)),
             chunk_out((heads, BLOCK, value_width)), chunk_out((heads, key_width, key_width)),
             whole((chunks,) + map_shape), whole(map_shape),
-        ] + [ANYWHERE, whole((others,) + map_shape)] * cube,
+        ] + [ANYWHERE, whole((others,) + map_shape), whole(passing_shape)] * cube,
         out_shape=[
             struct((seq_rows, mixed_width), f32), struct((seq_rows, mixed_width), f32),
             struct((seq_rows, vw), f32), struct((seq_rows, LANES), f32), struct((seq_rows, LANES), f32),
@@ -1736,7 +1782,9 @@
             struct((chunks, heads, BLOCK, value_width), f32),
             struct((chunks, heads, key_width, key_width), f32),
             struct((chunks,) + map_shape, f32), struct(map_shape, f32),
-        ] + [struct((seq_rows, model_width), bf16), struct((others,) + map_shape, bf16)] * cube,
+        ] + [
+            struct((seq_rows, model_width), bf16), struct((others,) + map_shape, bf16), struct(passing_shape, bf16),
+        ] * cube,
         scratch_shapes=[
             pltpu.VMEM((STRIDE, mixed_width), f32), pltpu.VMEM(map_shape, f32),
             pltpu.VMEM((chunks, heads, key_width, key_width), bf16),
@@ -1746,17 +1794,18 @@
             pltpu.VMEM((chunks * STRIDE, model_width), bf16), pltpu.SemaphoreType.DMA((chunks,)),
             pltpu.VMEM((LEAD, model_width), bf16), pltpu.SemaphoreType.DMA((2,)),
             pltpu.SemaphoreType.DMA((8,)), pltpu.SemaphoreType.DMA((8,)), *CUBE_SEMAPHORES[1:],
-            pltpu.VMEM(map_shape, bf16), pltpu.VMEM((others,) + map_shape, bf16),
-            pltpu.SemaphoreType.DMA((2, others)),
+            pltpu.VMEM(map_shape, bf16), pltpu.VMEM((others,) + map_shape, bf16), pltpu.VMEM(passing_shape, bf16),
+            pltpu.SemaphoreType.DMA((6, others)),
         ] * cube,
         compiler_params=params(2 if cube else None),
         name="mixer_forward",
     )(meta, rows_given, *weights, conv_all, dvec)
     (pre, conv, gate, small, scal, qkv, inverse, w_part, u_part, drop, starts, block_map) = results[:12]
     if cube:
-        block_rows, earlier = results[12:]
+        block_rows, earlier, passing = results[12:]
     else:
         earlier = from_earlier(block_map.astype(bf16), "seq")
+        passing = from_later(block_map[:, :, :key_width].astype(bf16), "seq")
 
     grad_block_two = lax.all_gather(grad_low, "seq", axis=0, tiled=True)
     gain_row = head_gain[None, :]
@@ -1897,9 +1946,7 @@
             name="mixer_core_grad",
         )(meta, grad_block, w_output, core, gate, gain_row, qkv, scal, w_part, drop)
     grad_w_output = dot_tn(gated, grad_block).astype(bf16)
-    later = from_later(
-        jnp.concatenate([block_map[:, :, :key_width], pulled], axis=2).astype(bf16), "seq"
-    )
+    later = from_later(pulled.astype(bf16), "seq")
     later, _ = lax.optimization_barrier((later, grad_w_output))
     mlp_out, grad_w_output = lax.optimization_barrier((mlp_out, grad_w_output))
     grad_w_output = lax.psum(grad_w_output, "seq")
@@ -1908,7 +1955,8 @@
         functools.partial(backward_kernel, *sizes, chunks, others, cube),
         grid=(chunks,),
         in_specs=[
-            SCALARS, whole(later.shape), by_rows(mixed_width, chunks), by_rows(mixed_width, chunks),
+            SCALARS, whole(passing.shape), whole(later.shape), by_rows(mixed_width, chunks),
+            by_rows(mixed_width, chunks),
             by_rows(LANES, chunks), by_rows(LANES, chunks), by_chunk((heads, BLOCK, BLOCK), chunks),
             by_chunk((heads, BLOCK, value_width), chunks), by_chunk((heads, key_width, value_width), chunks),
             by_chunk((heads, BLOCK, value_width), chunks), by_chunk((heads, BLOCK, value_width), chunks),
@@ -1937,7 +1985,7 @@
         compiler_params=params(9),
         name="mixer_backward",
     )(
-        meta, later, qkv, conv, scal, small, inverse, fresh, states, grad_core, inner, pull, drop, dvec, *feed_part
+        meta, passing, later, qkv, conv, scal, small, inverse, fresh, states, grad_core, inner, pull, drop, dvec, *feed_part
     )
 
     if cube:
@@ -1976,8 +2024,6 @@
         grad_normed = grad_rows
     else:
         grad_normed = lax.psum_scatter(grad_rows, "head", scatter_dimension=0, tiled=True).astype(f32)
-    grad_input_norm, _ = rms_back(inputs_f, first_gain, grad_normed)
-    grad_inputs = grad_hidden_in + grad_input_norm
     gains = jnp.concatenate([gain_sum[0] / first_gain, grad_second, grad_head[0]]).reshape(2, -1)
     grad_w_all, grad_w_small, small_sums, _, gains, *gathered = line_sum(
         block_rows,
@@ -1999,15 +2045,15 @@
     if cube:
         ff_grads = [ff_grads[0], *gathered, ff_grads[1]]
     grad_w_all, grad_w_output = lax.optimization_barrier((grad_w_all, grad_w_output))
-    grad_w_all, grad_inputs, mlp_out, *ff_grads = lax.optimization_barrier(
-        (grad_w_all, grad_inputs, mlp_out, *ff_grads)
+    grad_w_all, mlp_out, *ff_grads = lax.optimization_barrier((grad_w_all, mlp_out, *ff_grads))
+    (
+        output, grad_inputs, grad_conv_query, grad_conv_key, grad_conv_value,
+        grad_w_query, grad_w_key, grad_w_value, grad_w_outgate, grad_w_down, grad_w_gate, grad_w_up, grad_w_output,
+    ) = finish(
+        (grad_normed, inputs, grad_hidden_in, hidden_in, mlp_out), first_gain[None, :], small_sums, taps,
+        grad_w_all, (qw, qw, vw, vw), (*ff_grads, grad_w_output),
     )
-    (
-        grad_w_query, grad_w_key, grad_w_value, grad_w_outgate, grad_w_down, grad_w_gate, grad_w_up, grad_w_output,
-    ) = widen((*ff_grads, grad_w_output), grad_w_all, (qw, qw, vw, vw))
-    grad_taps = small_sums[:taps, :mixed_width].astype(f32)
     sums = small_sums[:2, mixed_width : mixed_width + heads].astype(f32)
-    output = (hidden_in + mlp_out.astype(f32)).astype(bf16)
     return (
         output,
         grad_inputs,
@@ -2018,9 +2064,9 @@
         grad_w_outgate,
         grad_w_small[:heads].astype(f32).T,
         grad_w_small[heads : 2 * heads].astype(f32).T,
-        grad_taps[:, :qw],
-        grad_taps[:, qw : 2 * qw],
-        grad_taps[:, 2 * qw :],
+        grad_conv_query,
+        grad_conv_key,
+        grad_conv_value,
         sums[1],
         sums[0],
         head_part,

time: 717 us -> 698 us (0.974)
  no operation moved by 1% of the time
where the time goes in v6:
time: 698 us; the launch traced here: 691 us
  Pallas kernels  631 us (90%)
  between operations  14.3 us (2%)
  other arithmetic  13.4 us (2%)
  waiting for transfers between devices  12.3 us (2%)
  matrix products  9.12 us (1%)
    pallas_call x1, Pallas kernels, line_sum(): pl.pallas_call(functools.partial(line_sum_kernel, axis, cube, counts, tup...  174 us
    pallas_call x1, Pallas kernels, feed(): pl.pallas_call(functools.partial(feed_kernel, axis, devices, rows, pieces...  128 us
    pallas_call x1, Pallas kernels, shards(): pl.pallas_call(functools.partial(forward_kernel, *sizes, taps, chunks, cu...  88.4 us
    pallas_call x1, Pallas kernels, shards(): pl.pallas_call(functools.partial(feed_core_kernel, sizes, chunks, 'head',...  63.3 us
    pallas_call x1, Pallas kernels, shards(): pl.pallas_call(functools.partial(projection_grad_kernel, mixed_width, doc...  54.2 us
    pallas_call x1, Pallas kernels, shards(): pl.pallas_call(functools.partial(output_kernel, *sizes, others, cube), gr...  50.8 us
    pallas_call x1, Pallas kernels, shards(): pl.pallas_call(functools.partial(backward_kernel, *sizes, chunks, others,...  42 us
    pallas_call x1, Pallas kernels, finish(): pl.pallas_call(functools.partial(finish_kernel, cuts, len(given)), grid=(...  29.9 us
  transfers between devices with their start and end apart: 7, of which 2 were waited for; matrix products, arithmetic and copies ran while one was open for 4% of the time, Pallas kernels for 68%

profile of v6, /device:TPU:0, one launch (start us, length us, event | category | flops | bytes accessed | tf_op | source)
XLA Modules:
  0.0 691.1 jit_solution(17530585268666318340)
XLA Ops:
  7.3 0.0 all-gather.2.cloned.1.call-start
  7.3 0.8 fusion.13
  8.1 0.2 reduce-window.9
  8.3 0.7 bitcast_subtract_fusion
  8.9 0.1 slice.76
  9.0 0.1 fusion.7
  9.1 0.7 select_reduce_fusion.1
  9.8 2.4 multiply_convert_fusion.low_ref
  12.3 0.0 reduce-scatter.2.cloned.1.call-start
  12.4 0.3 copy.43
  12.7 0.3 copy.44
  13.0 0.1 pad.30.clone
  13.1 0.2 scatter.9.dvec_ref
  13.3 0.6 pad_add_fusion.meta
  14.0 0.3 fusion
  14.3 1.1 maximum_maximum_fusion.ws_ref
  15.4 1.3 fusion.2.rows_ref
  16.7 88.4 %mixer_forward.1 = (f32[2048,1024]{1,0:T(8,128)}, f32[2048,1024]{1,0:T(8,128)}, f32[2048,512]{1,0:T(8,128)}, f32[2048,128]{1,0:T(8,128)}, f32[2048,128]{1,0:T(8,...) custom-call(s32[4]{0:T(128)} %pad_add_fusion.meta, ...), custom_call_target="tpu_custom_call" | custom-call | tf_op jit(solution)/shard_map/mixer_forward/pallas_call | solution.py:1763
  105.1 50.8 %mixer_output.1 = (f32[2048,512]{1,0:T(8,128)}, bf16[2048,512]{1,0:T(8,128)(2,1)}, bf16[8,2,256,256]{3,2,1,0:T(8,128)(2,1)}, f32[8,2,128,256]{3,2,1,0:T(8,128)},...) custom-call(s32[4]{0:T(128)} %pad_add_fusion.meta, bf16[3,2,128,384]{3,2,1,0:T(8,128)(2,1)} %get-tuple-element.123.maps_ref, ...), custom_call_target="tpu_custom_call" | custom-call | tf_op jit(solution)/shard_map/mixer_output/pallas_call | solution.py:1823
  155.9 0.0 all-gather.2.cloned.1.call-done.refs_0_.grads_ref
  155.9 128.4 %feed.1 = (bf16[1024,2048]{1,0:T(8,128)(2,1)}, bf16[1408,1024]{1,0:T(8,128)(2,1)}, bf16[1024,1408]{1,0:T(8,128)(2,1)}, bf16[1024,1408]{1,0:T(8,128)(2,1)}, bf16[...) custom-call(bf16[256,2048]{1,0:T(8,128)(2,1)} %get-tuple-element.130.own_ref, ...), custom_call_target="tpu_custom_call" | custom-call | tf_op jit(solution)/shard_map/feed/pallas_call | solution.py:1280
  284.4 0.0 all-reduce.7.cloned.1.call-start
  284.4 63.3 %feed_core.1 = (bf16[1408,2048]{1,0:T(8,128)(2,1)}, bf16[2048,1408]{1,0:T(8,128)(2,1)}, bf16[2048,1408]{1,0:T(8,128)(2,1)}, bf16[2048,2048]{1,0:T(8,128)(2,1)}, ...) custom-call(s32[4]{0:T(128)} %pad_add_fusion.meta, ...), custom_call_target="tpu_custom_call" | custom-call | tf_op jit(solution)/shard_map/feed_core/pallas_call | solution.py:1889
  347.7 1.0 convert_element_type.46
  348.7 1.3 collective-permute-start.2
  350.0 1.3 collective-permute-start.1
  351.3 1.3 collective-permute-start
  352.6 9.1 %convolution_convert_fusion = bf16[512,2048]{1,0:T(8,128)(2,1)} fusion(bf16[2048,512]{1,0:T(8,128)(2,1)S(1)} %copy-done.11, bf16[2048,2048]{1,0:T(8,128)(2,1)} %get-tuple-element.141), kind=kOutput, calls=%fused_computation | convolution fusion | flops 4296015872 | bytes 12582912 | tf_op jit(solution)/shard_map/dot_general | solution.py:26
  361.7 2.5 collective-permute-done.2
  364.2 9.6 %collective-permute-done.1 = bf16[2,128,256]{2,1,0:T(8,128)(2,1)S(1)} collective-permute-done((bf16[2,128,256]{2,1,0:T(8,128)(2,1)S(1)}, bf16[2,128,256]{2,1,0:T(8,128)(2,1)S(1)}, u32[]{:S(2)}, u32[]{:S(2)}) %collective-permute-start.1) | collective-permute-done | bytes 131104 | tf_op jit(solution)/shard_map/ppermute | solution.py:1678
  373.9 0.8 pad_maximum_fusion.later_ref
  374.7 0.0 all-reduce.9.cloned.1.call-start
  374.7 42.0 %mixer_backward.1 = (f32[2048,1024]{1,0:T(8,128)}, bf16[2048,128]{1,0:T(8,128)(2,1)}, f32[8,128]{1,0:T(8,128)}, f32[8,1024]{1,0:T(8,128)}, bf16[256,1408]{1,0:T(8,128)(2,1)}) custom-call(s32[4]{0:T(128)} %pad_add_fusion.meta, bf16[3,2,128,128]{3,2,1,0:T(8,128)(2,1)} %get-tuple-element.122.passing_ref, bf16[3,2,128,256]{3,2,1,0:T(8,128)(2,1)} %pad_maximum_fusion.later_ref, ...), custom_call_target="tpu_custom_call" | custom-call | tf_op jit(solution)/shard_map/mixer_backward/pallas_call | solution.py:1954
  416.8 0.7 fusion.8
  417.5 0.9 fusion.6
  418.4 54.2 %projection_grad.1 = (bf16[2048,1664]{1,0:T(8,128)(2,1)}, f32[8,1024]{1,0:T(8,128)}, f32[256,2048]{1,0:T(8,128)}, f32[8,2048]{1,0:T(8,128)}) custom-call(s32[4]{0:T(128)} %pad_add_fusion.meta, f32[2048,1024]{1,0:T(8,128)} %get-tuple-element.152.grad_conv_ref.later_ref, f32[2048,1024]{1,0:T(8,128)} %get-tuple-element.152.grad_conv_ref.later_ref, ...), custom_call_target="tpu_custom_call" | custom-call | tf_op jit(solution)/shard_map/projection_grad/pallas_call | solution.py:2000
  472.7 0.8 slice.77
  473.6 0.8 convert.26
  474.3 0.6 pad.19.refs_3_
  475.0 0.6 fusion.5.refs_2_
  475.6 174.1 %line_sum.1 = (bf16[2048,1536]{1,0:T(8,128)(2,1)}, bf16[16,2048]{1,0:T(8,128)(2,1)}, bf16[16,1152]{1,0:T(8,128)(2,1)}, bf16[16,2176]{1,0:T(8,128)(2,1)}, f32[8,2176]{1,0:T(8,128)}, /*index=5*/bf16[2048,1408]{1,0:T(8,128)(2,1)}) custom-call(bf16[2048,2048]{1,0:T(8,128)(2,1)} %get-tuple-element.160.rows_ref.refs_0_, ...), custom_call_target="tpu_custom_call" | custom-call | flops 100000000 | bytes 40000000 | tf_op jit(solution)/shard_map/line_sum/pallas_call | solution.py:1038
  649.7 0.9 slice.80
  650.6 0.6 slice.92
  651.2 0.7 slice_convert_fusion.2
  651.8 0.5 slice_bitcast_fusion
  652.4 0.6 fusion.10
  653.0 1.5 convert_bitcast_fusion
  654.4 29.9 %finish.1 = (bf16[256,2048]{1,0:T(8,128)(2,1)}, f32[256,2048]{1,0:T(8,128)}, f32[4,256]{1,0:T(4,128)}, f32[4,256]{1,0:T(4,128)}, f32[4,512]{1,0:T(4,128)}, /*ind...) custom-call(f32[256,2048]{1,0:T(8,128)} %get-tuple-element.161.grad_, ...), custom_call_target="tpu_custom_call" | custom-call | tf_op jit(solution)/shard_map/finish/pallas_call | solution.py:1642
  (48 shorter events, 0.2 us)
Async XLA Ops:
  7.2 5.2 copy-start.4
  7.2 5.5 copy-start.5
  7.2 5.9 copy-start.10
  7.2 5.9 copy-start.12
  7.2 6.7 copy-start.8
  7.2 6.7 copy-start.9
  7.3 6.7 copy-start.6
  7.3 6.7 copy-start
  7.3 148.7 %all-gather.2.cloned.1.call-start = ((), (), s32[]{:S(2)}) async-start(), calls=%async_computation.1 | async-start | bytes 5242880 | tf_op jit(solution)/shard_map/all_gather | solution.py:1810
  12.3 3.1 copy-start.2
  12.3 362.4 %reduce-scatter.2.cloned.1.call-start = ((), (), s32[]{:S(2)}) async-start(), calls=%async_computation.2 | async-start | bytes 5242880 | tf_op jit(solution)/shard_map/reduce_scatter | solution.py:1863
  13.3 3.4 copy-start.3
  14.0 2.7 copy-start.1
  284.4 370.0 %all-reduce.7.cloned.1.call-start = ((), (), s32[]{:S(2)}) async-start(), calls=%async_computation.3 | async-start | bytes 4194304 | tf_op jit(solution)/shard_map/psum | solution.py:1952
  284.4 68.2 %copy-start.11 = (bf16[2048,512]{1,0:T(8,128)(2,1)S(1)}, bf16[2048,512]{1,0:T(8,128)(2,1)}, u32[]{:S(2)}) copy-start(bf16[2048,512]{1,0:T(8,128)(2,1)} %get-tuple-element.140) | copy-start | bytes 6291460
  348.7 15.6 %collective-permute-start.2 = (bf16[2,128,256]{2,1,0:T(8,128)(2,1)S(1)}, bf16[2,128,256]{2,1,0:T(8,128)(2,1)S(1)}, u32[]{:S(2)}, u32[]{:S(2)}) collective-permute-start(bf16[2,128,256]{2,1,0:T(8,128)(2,1)S(1)} %convert_element_type.46), channel_id=1, source_target_pairs={{8,0},{16,8},{24,16},{9,1},{17,9},{25,17},{10,2},{18,10},{26,18},{... | collective-permute-start | bytes 393224 | tf_op jit(solution)/shard_map/ppermute | solution.py:1678
  350.0 23.9 %collective-permute-start.1 = (bf16[2,128,256]{2,1,0:T(8,128)(2,1)S(1)}, bf16[2,128,256]{2,1,0:T(8,128)(2,1)S(1)}, u32[]{:S(2)}, u32[]{:S(2)}) collective-permute-start(bf16[2,128,256]{2,1,0:T(8,128)(2,1)S(1)} %convert_element_type.46), channel_id=1, source_target_pairs={{16,0},{24,8},{17,1},{25,9},{18,2},{26,10},{19,3},{27,11},{20,4},{... | collective-permute-start | bytes 393224 | tf_op jit(solution)/shard_map/ppermute | solution.py:1678
  351.3 22.6 %collective-permute-start = (bf16[2,128,256]{2,1,0:T(8,128)(2,1)S(1)}, bf16[2,128,256]{2,1,0:T(8,128)(2,1)S(1)}, u32[]{:S(2)}, u32[]{:S(2)}) collective-permute-start(bf16[2,128,256]{2,1,0:T(8,128)(2,1)S(1)} %convert_element_type.46), channel_id=1, source_target_pairs={{24,0},{25,1},{26,2},{27,3},{28,4},{29,5},{30,6},{31,7}} | collective-permute-start | bytes 393224 | tf_op jit(solution)/shard_map/ppermute | solution.py:1678
  374.7 279.7 %all-reduce.9.cloned.1.call-start = ((), (), s32[]{:S(2)}) async-start(), calls=%async_computation.4 | async-start | bytes 23068672 | tf_op jit(solution)/shard_map/psum | solution.py:1994
  416.8 1.6 copy-start.7
Sparse Core Ops, SparseCore 0:
  12.4 88.9 all-gather.1
  284.5 81.6 reduce-scatter.1
  374.8 85.9 all-reduce.6
  464.4 184.7 all-reduce.8

commit v7 on v6

--- a/solution.py
+++ b/solution.py
@@ -108,6 +108,13 @@
     for doc in range(1, docs):
         begin = jnp.where(places >= meta[1 + doc], meta[1 + doc], begin)
     return places - begin
+
+
+def valid_of(meta, docs, places):
+    left = meta[1] + meta[1 + docs] - places
+    for doc in range(1, docs):
+        left = jnp.where(places >= meta[1 + doc], meta[1 + doc] + meta[1 + docs + doc] - places, left)
+    return jnp.where(left > 0, 1.0, 0.0)
 
 
 class Masks:
@@ -1081,8 +1088,8 @@
 
 
 def feed_kernel(
-    axis, devices, rows, pieces,
-    own_ref, *refs,
+    axis, devices, rows, pieces, docs,
+    meta, own_ref, *refs,
 ):
     given, kept, refs = refs[:4], refs[4:9], refs[9:]
     total_ref, *refs = refs
@@ -1169,16 +1176,17 @@
         @pl.when((owner >= 0) & (owner < devices))
         def _():
             here = full(owner)
-            grad_hidden = dot_nt(grads_ref[here, :], w_down_ref[...])
-
+            first = (owner * lax.axis_size("head") + lax.axis_index("head")) * rows
+            valid = valid_of(meta, docs, first + lax.broadcasted_iota(jnp.int32, (rows, 1), 0))
+            grad_hidden = valid * dot_nt(grads_ref[here, :], w_down_ref[...])
             block = blocks_ref[here, :]
             gate_pre = dot(block, w_gate_ref[...])
             up_pre = dot(block, w_up_ref[...])
             sigma = sigmoid(gate_pre)
             act = gate_pre * sigma
-            hidden = (act * up_pre).astype(bf16)
-            hidden_ref[here, :] = hidden
-            turned_ref[:, full(owner)] = hidden.T
+            hidden = act * up_pre
+            hidden_ref[here, :] = hidden.astype(bf16)
+            turned_ref[:, full(owner)] = (valid * hidden).astype(bf16).T
             grad_gate_ref[here, :] = (grad_hidden * up_pre * (sigma * (1.0 + gate_pre * (1.0 - sigma)))).astype(bf16)
             grad_up_ref[here, :] = (grad_hidden * act).astype(bf16)
             grad = dot_nt(grad_gate_ref[here, :], w_gate_ref[...]) + dot_nt(grad_up_ref[here, :], w_up_ref[...])
@@ -1265,7 +1273,7 @@
         store(index).wait()
 
 
-def feed(own, grads, w_gate, w_up, w_down, axis, collective_id):
+def feed(meta, docs, own, grads, w_gate, w_up, w_down, axis, collective_id):
     devices = lax.axis_size(axis)
     rows, width = own.shape
     units = w_gate.shape[1]
@@ -1278,8 +1286,8 @@
     kept += [struct((devices * rows, units), bf16)] * 2
     kept += [struct((devices * rows, width), bf16)]
     return pl.pallas_call(
-        functools.partial(feed_kernel, axis, devices, rows, pieces),
-        in_specs=[vmem] + [ANYWHERE] * 4,
+        functools.partial(feed_kernel, axis, devices, rows, pieces, docs),
+        in_specs=[SCALARS, vmem] + [ANYWHERE] * 4,
         out_specs=[ANYWHERE] * 5 + [vmem],
         out_shape=kept + [struct((rows, width), f32)],
         scratch_shapes=[
@@ -1292,7 +1300,7 @@
             collective_id=collective_id, has_side_effects=True, vmem_limit_bytes=61 * 1024 * 1024
         ),
         name="feed",
-    )(own, grads, w_gate, w_up, w_down)
+    )(meta, own, grads, w_gate, w_up, w_down)
 
 
 def flip(index, mask):
@@ -1427,7 +1435,9 @@
     @pl.when(step == 0)
     def _():
         grad_norm, gain_sum = rms_back(hidden_in[...], next_gain_ref[...], total_in[...])
-        grad_in = low_ref[...].astype(f32) + grad_norm
+        first = meta[0] + lax.axis_index(axis) * rows
+        valid = valid_of(meta, sizes[3], first + lax.broadcasted_iota(jnp.int32, (rows, 1), 0))
+        grad_in = valid * low_ref[...].astype(f32) + grad_norm
         grad_in_ref[...] = grad_in
         gain_sum_ref[0:1, :] = gain_sum[None, :]
         rows_ref[own, :] = grad_in.astype(bf16)
@@ -1722,12 +1732,9 @@
     inputs_f = inputs.astype(f32)
     normed = rms_scale(inputs_f, first_gain).astype(bf16)
     meta = jnp.concatenate(
-        [(seq_index * seq_rows).astype(jnp.int32)[None], slot_starts(doc_lengths)]
+        [(seq_index * seq_rows).astype(jnp.int32)[None], slot_starts(doc_lengths), doc_lengths]
     )
-    _, own_valid = layout(doc_lengths, (seq_index * head_total + head_index) * row_count, row_count)
-
-    grad_out = cotangent.astype(f32) * own_valid.astype(f32)[:, None]
-    grad_low = grad_out.astype(bf16)
+
     w_small = jnp.concatenate([w_decay, w_beta, jnp.zeros((model_width, LANES - 2 * heads), bf16)], axis=1)
     weights = (w_query, w_key, w_value, w_outgate, w_small)
     all_width = mixed_width + vw + LANES
@@ -1807,7 +1814,7 @@
         earlier = from_earlier(block_map.astype(bf16), "seq")
         passing = from_later(block_map[:, :, :key_width].astype(bf16), "seq")
 
-    grad_block_two = lax.all_gather(grad_low, "seq", axis=0, tiled=True)
+    grad_block_two = lax.all_gather(cotangent, "seq", axis=0, tiled=True)
     gain_row = head_gain[None, :]
     def last_first(step):
         return cube_order("head", 7 - step) if cube else step
@@ -1858,7 +1865,7 @@
         normed_two = rms_scale(hidden_in, second_gain).astype(bf16)
 
     mlp_block, hidden, grad_gate, grad_up, mlp_part, grad_normed_two = feed(
-        normed_two, grad_block_two, w_gate, w_up, w_down, "seq", 3
+        meta, docs, normed_two, grad_block_two, w_gate, w_up, w_down, "seq", 3
     )
     mlp_out = lax.psum_scatter(mlp_part, "seq", scatter_dimension=0, tiled=True)
     core_shapes = [
@@ -1868,7 +1875,7 @@
     ]
     if cube:
         tiles = model_width // BLOCK
-        owned = (grad_normed_two, hidden_in, grad_low, second_row)
+        owned = (grad_normed_two, hidden_in, cotangent, second_row)
         units, mlp_rows = hidden.shape
 
         def tile(step):
@@ -1923,7 +1930,8 @@
         grad_second = grad_second[0]
     else:
         grad_hidden_norm, grad_second = rms_back(hidden_in, second_gain, grad_normed_two)
-        grad_hidden_in = grad_out + grad_hidden_norm
+        _, own_valid = layout(doc_lengths, (seq_index * head_total + head_index) * row_count, row_count)
+        grad_hidden_in = cotangent.astype(f32) * own_valid.astype(f32)[:, None] + grad_hidden_norm
         grad_mix = grad_hidden_in.astype(bf16)
         *ff_grads, grad_block = feed_grads(
             grad_mix, mlp_block, grad_block_two, hidden, grad_gate, grad_up, "head"

time: 698 us -> 699 us (level)
  transfers between devices with their start and end apart: 7 -> 7, of which waited for: 2 -> 2; matrix products, arithmetic and copies ran while one was open for 4% -> 5% of each run, Pallas kernels for 68% -> 68%
where the time goes in v7:
time: 699 us; the launch traced here: 692 us
  Pallas kernels  629 us (90%)
  between operations  14.2 us (2%)
  other arithmetic  12.6 us (2%)
  waiting for transfers between devices  11.6 us (2%)
  local copies, waits for them, and re-layouts  10.6 us (2%)
  matrix products  9.12 us (1%)
    pallas_call x1, Pallas kernels, line_sum(): pl.pallas_call(functools.partial(line_sum_kernel, axis, cube, counts, tup...  175 us
    pallas_call x1, Pallas kernels, feed(): pl.pallas_call(functools.partial(feed_kernel, axis, devices, rows, pieces...  128 us
    pallas_call x1, Pallas kernels, shards(): pl.pallas_call(functools.partial(forward_kernel, *sizes, taps, chunks, cu...  86.4 us
    pallas_call x1, Pallas kernels, shards(): pl.pallas_call(functools.partial(feed_core_kernel, sizes, chunks, 'head',...  65 us
    pallas_call x1, Pallas kernels, shards(): pl.pallas_call(functools.partial(projection_grad_kernel, mixed_width, doc...  54.2 us
    pallas_call x1, Pallas kernels, shards(): pl.pallas_call(functools.partial(output_kernel, *sizes, others, cube), gr...  49.5 us
    pallas_call x1, Pallas kernels, shards(): pl.pallas_call(functools.partial(backward_kernel, *sizes, chunks, others,...  41.4 us
    pallas_call x1, Pallas kernels, finish(): pl.pallas_call(functools.partial(finish_kernel, cuts, len(given)), grid=(...  29.9 us
  transfers between devices with their start and end apart: 7, of which 2 were waited for; matrix products, arithmetic and copies ran while one was open for 5% of the time, Pallas kernels for 68%

profile of v7, /device:TPU:0, one launch (start us, length us, event | category | flops | bytes accessed | tf_op | source)
XLA Modules:
  0.0 691.6 jit_solution(15581322213996257482)
XLA Ops:
  7.3 0.7 all-gather.2.cloned.1.call-update
  7.9 0.0 reduce-scatter.2.cloned.1.call-start
  8.0 1.0 copy.41
  9.0 1.0 copy.42
  10.0 0.7 fusion.12
  10.7 0.2 reduce-window.9
  10.9 0.1 pad.30.clone
  11.0 0.7 scatter.6
  11.6 0.7 negate_bitcast_fusion
  12.3 0.1 scatter.9.dvec_ref
  12.4 0.7 bitcast_subtract_fusion
  13.1 1.2 pad_add_fusion.meta
  14.3 0.7 constant_dynamic-update-slice_fusion.2
  15.0 0.7 constant_dynamic-update-slice_fusion.1
  15.7 0.7 constant_dynamic-update-slice_fusion.conv_ref
  16.4 1.5 fusion
  17.9 1.1 maximum_maximum_fusion.ws_ref
  19.0 1.3 fusion.2.rows_ref
  20.3 86.4 %mixer_forward.1 = (f32[2048,1024]{1,0:T(8,128)}, f32[2048,1024]{1,0:T(8,128)}, f32[2048,512]{1,0:T(8,128)}, f32[2048,128]{1,0:T(8,128)}, f32[2048,128]{1,0:T(8,...) custom-call(s32[7]{0:T(128)} %pad_add_fusion.meta, ...), custom_call_target="tpu_custom_call" | custom-call | tf_op jit(solution)/shard_map/mixer_forward/pallas_call | solution.py:1770
  106.8 49.5 %mixer_output.1 = (f32[2048,512]{1,0:T(8,128)}, bf16[2048,512]{1,0:T(8,128)(2,1)}, bf16[8,2,256,256]{3,2,1,0:T(8,128)(2,1)}, f32[8,2,128,256]{3,2,1,0:T(8,128)},...) custom-call(s32[7]{0:T(128)} %pad_add_fusion.meta, bf16[3,2,128,384]{3,2,1,0:T(8,128)(2,1)} %get-tuple-element.123.maps_ref, ...), custom_call_target="tpu_custom_call" | custom-call | tf_op jit(solution)/shard_map/mixer_output/pallas_call | solution.py:1830
  156.3 128.1 %feed.1 = (bf16[1024,2048]{1,0:T(8,128)(2,1)}, bf16[1408,1024]{1,0:T(8,128)(2,1)}, bf16[1024,1408]{1,0:T(8,128)(2,1)}, bf16[1024,1408]{1,0:T(8,128)(2,1)}, bf16[...) custom-call(s32[7]{0:T(128)} %pad_add_fusion.meta, bf16[256,2048]{1,0:T(8,128)(2,1)} %get-tuple-element.130.own_ref, ...), custom_call_target="tpu_custom_call" | custom-call | tf_op jit(solution)/shard_map/feed/pallas_call | solution.py:1288
  284.4 0.0 all-reduce.7.cloned.1.call-start
  284.5 65.0 %feed_core.1 = (bf16[1408,2048]{1,0:T(8,128)(2,1)}, bf16[2048,1408]{1,0:T(8,128)(2,1)}, bf16[2048,1408]{1,0:T(8,128)(2,1)}, bf16[2048,2048]{1,0:T(8,128)(2,1)}, ...) custom-call(s32[7]{0:T(128)} %pad_add_fusion.meta, ...), custom_call_target="tpu_custom_call" | custom-call | tf_op jit(solution)/shard_map/feed_core/pallas_call | solution.py:1896
  349.5 1.0 convert_element_type.25
  350.4 1.3 collective-permute-start.2
  351.7 1.3 collective-permute-start.1
  353.0 1.3 collective-permute-start
  354.3 9.1 %convolution_convert_fusion = bf16[512,2048]{1,0:T(8,128)(2,1)} fusion(bf16[2048,512]{1,0:T(8,128)(2,1)S(1)} %copy-done.5, bf16[2048,2048]{1,0:T(8,128)(2,1)} %get-tuple-element.141), kind=kOutput, calls=%fused_computation | convolution fusion | flops 4296015872 | bytes 12582912 | tf_op jit(solution)/shard_map/dot_general | solution.py:26
  363.5 1.5 collective-permute-done.2
  365.0 9.3 %collective-permute-done.1 = bf16[2,128,256]{2,1,0:T(8,128)(2,1)S(1)} collective-permute-done((bf16[2,128,256]{2,1,0:T(8,128)(2,1)S(1)}, bf16[2,128,256]{2,1,0:T(8,128)(2,1)S(1)}, u32[]{:S(2)}, u32[]{:S(2)}) %collective-permute-start.1) | collective-permute-done | bytes 131104 | tf_op jit(solution)/shard_map/ppermute | solution.py:1688
  374.3 0.8 pad_maximum_fusion.later_ref
  375.1 0.0 all-reduce.9.cloned.1.call-start
  375.2 41.4 %mixer_backward.1 = (f32[2048,1024]{1,0:T(8,128)}, bf16[2048,128]{1,0:T(8,128)(2,1)}, f32[8,128]{1,0:T(8,128)}, f32[8,1024]{1,0:T(8,128)}, bf16[256,1408]{1,0:T(8,128)(2,1)}) custom-call(s32[7]{0:T(128)} %pad_add_fusion.meta, bf16[3,2,128,128]{3,2,1,0:T(8,128)(2,1)} %get-tuple-element.122.passing_ref, bf16[3,2,128,256]{3,2,1,0:T(8,128)(2,1)} %pad_maximum_fusion.later_ref, ...), custom_call_target="tpu_custom_call" | custom-call | tf_op jit(solution)/shard_map/mixer_backward/pallas_call | solution.py:1962
  416.6 0.7 fusion.7
  417.3 0.9 fusion.6
  418.2 54.2 %projection_grad.1 = (bf16[2048,1664]{1,0:T(8,128)(2,1)}, f32[8,1024]{1,0:T(8,128)}, f32[256,2048]{1,0:T(8,128)}, f32[8,2048]{1,0:T(8,128)}) custom-call(s32[7]{0:T(128)} %pad_add_fusion.meta, f32[2048,1024]{1,0:T(8,128)} %get-tuple-element.152.grad_conv_ref.later_ref, f32[2048,1024]{1,0:T(8,128)} %get-tuple-element.152.grad_conv_ref.later_ref, ...), custom_call_target="tpu_custom_call" | custom-call | tf_op jit(solution)/shard_map/projection_grad/pallas_call | solution.py:2008
  472.5 0.8 slice.73
  473.4 0.8 convert.26
  474.1 0.6 pad.19.refs_3_
  474.8 0.6 fusion.5.refs_2_
  475.4 174.7 %line_sum.1 = (bf16[2048,1536]{1,0:T(8,128)(2,1)}, bf16[16,2048]{1,0:T(8,128)(2,1)}, bf16[16,1152]{1,0:T(8,128)(2,1)}, bf16[16,2176]{1,0:T(8,128)(2,1)}, f32[8,2176]{1,0:T(8,128)}, /*index=5*/bf16[2048,1408]{1,0:T(8,128)(2,1)}) custom-call(bf16[2048,2048]{1,0:T(8,128)(2,1)} %get-tuple-element.160.rows_ref.refs_0_, ...), custom_call_target="tpu_custom_call" | custom-call | flops 100000000 | bytes 40000000 | tf_op jit(solution)/shard_map/line_sum/pallas_call | solution.py:1045
  650.2 0.9 slice.76
  651.1 0.6 slice.88
  651.6 0.7 slice_convert_fusion.2
  652.3 0.5 slice_bitcast_fusion
  652.8 0.6 fusion.9
  653.4 1.5 convert_bitcast_fusion
  654.9 29.9 %finish.1 = (bf16[256,2048]{1,0:T(8,128)(2,1)}, f32[256,2048]{1,0:T(8,128)}, f32[4,256]{1,0:T(4,128)}, f32[4,256]{1,0:T(4,128)}, f32[4,512]{1,0:T(4,128)}, /*ind...) custom-call(f32[256,2048]{1,0:T(8,128)} %get-tuple-element.161.grad_, ...), custom_call_target="tpu_custom_call" | custom-call | tf_op jit(solution)/shard_map/finish/pallas_call | solution.py:1652
  (28 shorter events, 0.2 us)
Async XLA Ops:
  7.2 11.9 %copy-start = (bf16[256,2048]{1,0:T(8,128)(2,1)S(1)}, bf16[256,2048]{1,0:T(8,128)(2,1)}, u32[]{:S(2)}) copy-start(bf16[256,2048]{1,0:T(8,128)(2,1)} %inputs_ref.1) | copy-start | bytes 3145732
  7.2 11.8 %copy-start.2 = (f32[2048]{0:T(1024)S(1)}, f32[2048]{0:T(1024)}, u32[]{:S(2)}) copy-start(f32[2048]{0:T(1024)} %param.27) | copy-start | bytes 24580
  7.2 149.1 %all-gather.2.cloned.1.call-start = ((), (), s32[]{:S(2)}) async-start(), calls=%async_computation.1 | async-start | bytes 5242880 | tf_op jit(solution)/shard_map/all_gather | solution.py:1817
  7.9 367.2 %reduce-scatter.2.cloned.1.call-start = ((), (), s32[]{:S(2)}) async-start(), calls=%async_computation.2 | async-start | bytes 5242880 | tf_op jit(solution)/shard_map/reduce_scatter | solution.py:1870
  12.4 7.9 %copy-start.3 = (f32[8,128]{1,0:T(8,128)}, f32[8,128]{1,0:T(8,128)S(1)}, u32[]{:S(2)}) copy-start(f32[8,128]{1,0:T(8,128)S(1)} %scatter.9.dvec_ref) | copy-start | bytes 12292
  16.4 3.9 copy-start.1
  284.4 370.4 %all-reduce.7.cloned.1.call-start = ((), (), s32[]{:S(2)}) async-start(), calls=%async_computation.3 | async-start | bytes 4194304 | tf_op jit(solution)/shard_map/psum | solution.py:1960
  284.5 69.8 %copy-start.5 = (bf16[2048,512]{1,0:T(8,128)(2,1)S(1)}, bf16[2048,512]{1,0:T(8,128)(2,1)}, u32[]{:S(2)}) copy-start(bf16[2048,512]{1,0:T(8,128)(2,1)} %get-tuple-element.140) | copy-start | bytes 6291460
  350.4 14.5 %collective-permute-start.2 = (bf16[2,128,256]{2,1,0:T(8,128)(2,1)S(1)}, bf16[2,128,256]{2,1,0:T(8,128)(2,1)S(1)}, u32[]{:S(2)}, u32[]{:S(2)}) collective-permute-start(bf16[2,128,256]{2,1,0:T(8,128)(2,1)S(1)} %convert_element_type.25), channel_id=1, source_target_pairs={{8,0},{16,8},{24,16},{9,1},{17,9},{25,17},{10,2},{18,10},{26,18},{... | collective-permute-start | bytes 393224 | tf_op jit(solution)/shard_map/ppermute | solution.py:1688
  351.7 22.6 %collective-permute-start.1 = (bf16[2,128,256]{2,1,0:T(8,128)(2,1)S(1)}, bf16[2,128,256]{2,1,0:T(8,128)(2,1)S(1)}, u32[]{:S(2)}, u32[]{:S(2)}) collective-permute-start(bf16[2,128,256]{2,1,0:T(8,128)(2,1)S(1)} %convert_element_type.25), channel_id=1, source_target_pairs={{16,0},{24,8},{17,1},{25,9},{18,2},{26,10},{19,3},{27,11},{20,4},{... | collective-permute-start | bytes 393224 | tf_op jit(solution)/shard_map/ppermute | solution.py:1688
  353.0 21.3 %collective-permute-start = (bf16[2,128,256]{2,1,0:T(8,128)(2,1)S(1)}, bf16[2,128,256]{2,1,0:T(8,128)(2,1)S(1)}, u32[]{:S(2)}, u32[]{:S(2)}) collective-permute-start(bf16[2,128,256]{2,1,0:T(8,128)(2,1)S(1)} %convert_element_type.25), channel_id=1, source_target_pairs={{24,0},{25,1},{26,2},{27,3},{28,4},{29,5},{30,6},{31,7}} | collective-permute-start | bytes 393224 | tf_op jit(solution)/shard_map/ppermute | solution.py:1688
  375.1 279.7 %all-reduce.9.cloned.1.call-start = ((), (), s32[]{:S(2)}) async-start(), calls=%async_computation.4 | async-start | bytes 23068672 | tf_op jit(solution)/shard_map/psum | solution.py:2002
  416.6 1.6 copy-start.4
Sparse Core Ops, SparseCore 0:
  9.6 83.5 all-gather.1
  284.6 80.4 reduce-scatter.1
  375.3 85.2 all-reduce.6
  464.2 184.0 all-reduce.8
